TPU v7x, 512 devices: a whole 4x4x16 slice. The times are simulated.
512 devices in a mesh: dp: 32 (over z_lo, x), tensor: 16 (over y, z_hi, core).
Axes of the slice: x: 4, y: 4, z: 16 (z_hi: 2, z_lo: 8; z = z_hi * 8 + z_lo), core: 2. Of those that a mesh axis runs over, the one named last changes fastest.
Arguments:
- x_panel: bfloat16 [16384, 4096], P('dp', 'tensor'), may hold values from -6 to 6
- grad_hidden: bfloat16 [16384, 14336], P('dp', 'tensor'), may hold values from -0.046875 to 0.046875
- gate_blocks: bfloat16 [112, 8, 128, 128], P('tensor'), may hold values from -0.1875 to 0.1875
- up_blocks: bfloat16 [112, 8, 128, 128], P('tensor'), may hold values from -0.1875 to 0.1875
- block_rows: int32 [112, 8], P('tensor'), may hold values from 0 to 31, as said below
- block_owner: int32 [112, 8], P('tensor'), may hold values from 0 to 31, as said below
Outputs:
- grad_owned: float32 [16, 32, 2, 2, 128, 128], P('tensor', 'dp')
Inputs may be any that keep to these rules, and one draw needn't show every extreme that they name: `block_rows`: the 8 block rows of one block column are distinct. `block_owner`: within each group of 7 consecutive block columns every dp index owns at most 2 blocks, and some index owns exactly 2.
All inputs are finite; a program needn't handle non-finite values.
Results may differ from a plain program's by a relative error of at most 0.013.
Values may be sent and summed in bfloat16 or wider, within the bound.
No kernel may reach another device: no remote copies, remote signals or barrier semaphores. Data moves between devices by JAX's collectives and lax.ppermute only.
A program may use at most 64 MiB of HBM per device.

v0:
```python
import jax
import jax.numpy as jnp
from jax import lax
from jax.sharding import PartitionSpec as P


def silu_parts(gate_pre):
    sigmoid_v = jax.nn.sigmoid(gate_pre)
    return (gate_pre * sigmoid_v, sigmoid_v * (1.0 + gate_pre * (1.0 - sigmoid_v)))


def body(x_panel, grad_hidden, gate_blocks, up_blocks, block_rows, block_owner):
    gathered = lax.all_gather(x_panel, "tensor", axis=1, tiled=True)
    token_count = gathered.shape[0]
    column_count = gate_blocks.shape[0]
    depth = gate_blocks.shape[1]
    block_size = gate_blocks.shape[2]
    row_total = gathered.shape[1] // block_size
    picked = gathered.reshape(token_count, row_total, block_size)[:, block_rows, :]
    gate_pre = jnp.einsum("tckb,ckbe->tce", picked, gate_blocks, preferred_element_type=jnp.float32)
    up_pre = jnp.einsum("tckb,ckbe->tce", picked, up_blocks, preferred_element_type=jnp.float32)
    activation, derivative = silu_parts(gate_pre)
    grad_f32 = grad_hidden.reshape(token_count, column_count, block_size).astype(jnp.float32)
    grad_gate_act = (grad_f32 * up_pre * derivative).astype(jnp.bfloat16)
    grad_up_act = (grad_f32 * activation).astype(jnp.bfloat16)
    paired = jnp.stack([grad_gate_act, grad_up_act], 2)
    partial_value = jnp.einsum(
        "tckb,tcme->ckmbe", picked, paired, preferred_element_type=jnp.float32
    )
    partial_value = partial_value.astype(jnp.bfloat16)
    owner_count = lax.axis_size("dp")
    block_count = column_count * depth
    capacity = block_count // owner_count + 1
    flat_owner = block_owner.reshape(block_count)
    onehot = (flat_owner[:, None] == jnp.arange(owner_count, dtype=jnp.int32)[None, :]).astype(
        jnp.int32
    )
    before = jnp.cumsum(onehot, 0) - onehot
    slot_index = jnp.sum(onehot * before, 1)
    target = flat_owner * capacity + slot_index
    packed = jnp.zeros((owner_count * capacity, 2, block_size, block_size), jnp.bfloat16)
    packed = packed.at[target].set(partial_value.reshape(block_count, 2, block_size, block_size))
    arrived = lax.all_to_all(
        packed.reshape(owner_count, capacity, 2, block_size, block_size),
        "dp",
        split_axis=0,
        concat_axis=0,
        tiled=True,
    )
    summed = jnp.sum(arrived.astype(jnp.float32), 0)
    return summed.reshape(1, 1, capacity, 2, block_size, block_size)


def solution(mesh):
    in_specs = (
        P("dp", "tensor"),
        P("dp", "tensor"),
        P("tensor", None, None, None),
        P("tensor", None, None, None),
        P("tensor", None),
        P("tensor", None),
    )
    out_specs = P("tensor", "dp", None, None, None, None)
    return jax.shard_map(body, mesh=mesh, in_specs=in_specs, out_specs=out_specs, check_vma=False)
```

profile of v0, /device:TPU:6, one launch (start us, length us, event | category | flops | bytes accessed | tf_op | source)
XLA Modules:
  0.0 383.6 jit_solution(14458488507015758200)
XLA Ops:
  6.5 0.0 copy-start
  6.5 0.0 all-gather.2.cloned.1.call-start
  6.5 1.9 copy.22
  8.5 0.0 all-gather.2.cloned.1.call-update
  8.5 0.7 compare_select_fusion
  9.2 0.1 reshape.52
  9.3 1.5 copy.21
  10.7 0.0 copy-start.3
  10.7 1.6 copy.24
  12.3 0.0 copy-done.3
  12.3 0.1 eq.15
  12.4 0.1 mul.39
  12.5 0.1 fusion.12
  12.6 0.1 reduce_window_sum.11
  12.7 0.2 select_reduce_fusion
  12.9 119.8 %all-gather.2.cloned.1.call-done = bf16[512,4096]{0,1:T(8,128)(2,1)} async-done(((bf16[512,256]{0,1:T(8,128)(2,1)}), bf16[512,4096]{0,1:T(8,128)(2,1)}) %all-gather.2.cloned.1.call-update) | async-done | bytes 4194320 | tf_op jit(solution)/shard_map/all_gather | solution.py:13
  132.7 6.4 %copy.23 = bf16[512,32,128]{2,0,1:T(8,128)(2,1)} copy(bf16[512,32,128]{0,2,1:T(8,128)(2,1)} %bitcast.81) | data formatting | bytes 8388608 | tf_op jit(solution)/shard_map/reshape | solution.py:19
  139.2 7.5 %gather_fusion = bf16[56,512,128]{2,1,0:T(8,128)(2,1)} fusion(bf16[512,32,128]{2,0,1:T(8,128)(2,1)} %copy.23, s32[1024]{0:T(1024)S(1)} %pad_clamp_fusion), kind=kCustom, calls=%fused_computation | custom fusion | bytes 14680288 | tf_op jit(solution)/shard_map/gather | solution.py:19
  146.6 0.0 copy-done
  146.6 5.3 %fusion.14 = f32[7,512,128,1]{2,1,3,0:T(8,128)S(1)} fusion(bf16[512,7,8,128]{3,0,2,1:T(8,128)(2,1)} %bitcast.78, bf16[7,8,128,128]{3,2,1,0:T(8,128)(2,1)S(1)} %copy-done), kind=kOutput, calls=%fused_computation.30 | convolution fusion | flops 939524096 | bytes 11010048 | tf_op jit(solution)/shard_map/tckb,ckbe->tce/dot_general | solution.py:20
  151.9 0.0 copy-done.1
  151.9 0.0 copy-start.4
  151.9 0.5 fusion.11
  152.4 0.0 copy-done.2
  152.4 1.1 copy-done.4
  153.5 2.1 fusion.10
  155.7 3.9 %convert_bitcast_fusion = bf16[7,8,2,128,128]{3,4,1,2,0:T(8,128)(2,1)} fusion(bf16[512,7,8,128,1]{3,0,2,4,1:T(8,128)(2,1)S(1)} %bitcast.80, bf16[512,7,1,128]{3,0,1,2:T(8,128)(2,1)S(1)} %fusion.11, bf16[512,7,1,128]{3,0,1,2:T(8,128)(2,1)S(1)} %fusion.10), kind=kOutput, calls=%fused_computation.3 | convolution fusion | flops 1881800704 | bytes 12845056 | tf_op jit(solution)/shard_map/tckb,tcme->ckmbe/dot_general | solution.py:27
  159.6 6.2 %copy.27 = bf16[7,8,2,128,128]{4,3,2,1,0:T(8,128)(2,1)} copy(bf16[7,8,2,128,128]{3,4,1,2,0:T(8,128)(2,1)} %convert_bitcast_fusion) | data formatting | bytes 7340032 | tf_op jit(solution)/shard_map/convert_element_type | solution.py:30
  165.8 3.0 broadcast_in_dim.8
  168.8 11.5 %scatter_fusion = bf16[64,2,128,128]{3,2,1,0:T(8,128)(2,1)} fusion(bf16[64,2,128,128]{3,2,1,0:T(8,128)(2,1)} %broadcast_in_dim.8, s32[56]{0:T(128)S(1)} %fusion.13, bf16[56,2,128,128]{3,2,1,0:T(8,128)(2,1)} %bitcast.77), kind=kCustom, calls=%fused_computation.1 | custom fusion | bytes 11010272 | tf_op jit(solution)/shard_map/scatter | solution.py:42
  180.3 194.9 %all_to_all.5 = bf16[32,2,2,128,128]{4,3,2,1,0:T(8,128)(2,1)S(1)} all-to-all(bf16[32,2,2,128,128]{4,3,2,1,0:T(8,128)(2,1)} %bitcast.76), channel_id=1, replica_groups=mesh['dp'=32,'tensor'=16] {'dp'}, dimensions={0} | all-to-all | bytes 8388608 | tf_op jit(solution)/shard_map/all_to_all | solution.py:43
  375.2 1.5 convert_reduce_fusion
  (5 shorter events, 0.0 us)
Async XLA Ops:
  6.5 140.1 %copy-start = (bf16[7,8,128,128]{3,2,1,0:T(8,128)(2,1)S(1)}, bf16[7,8,128,128]{3,2,1,0:T(8,128)(2,1)}, u32[]{:S(2)}) copy-start(bf16[7,8,128,128]{3,2,1,0:T(8,128)(2,1)} %param.8) | copy-start | bytes 5505028
  6.5 126.2 %all-gather.2.cloned.1.call-start = ((), (), s32[]{:S(2)}) async-start(), calls=%async_computation.1 | async-start | bytes 4456448 | tf_op jit(solution)/shard_map/all_gather | solution.py:13
  10.7 1.6 copy-start.3
  146.6 5.3 %copy-start.1 = (f32[512,7,128]{2,0,1:T(8,128)S(1)}, f32[512,7,128]{2,0,1:T(8,128)}, u32[]{:S(2)}) copy-start(f32[512,7,128]{2,0,1:T(8,128)} %copy.24) | copy-start | bytes 5505028
  146.6 5.8 %copy-start.2 = (bf16[56,512,128]{2,1,0:T(8,128)(2,1)S(1)}, bf16[56,512,128]{2,1,0:T(8,128)(2,1)}, u32[]{:S(2)}) copy-start(bf16[56,512,128]{2,1,0:T(8,128)(2,1)} %gather_fusion) | copy-start | bytes 22020100
  151.9 1.6 copy-start.4
Sparse Core Ops, SparseCore 0:
  10.6 122.0 all-gather.1
where the time goes:
time: 385 us; the launch traced here: 384 us
  blocking collectives  195 us (51%)
  waiting for transfers between devices  120 us (31%)
  local copies, waits for them, and re-layouts  41 us (11%)
  between operations  13.5 us (4%)
  matrix products  11.3 us (3%)
    all_to_all x1, blocking collectives, body(): lax.all_to_all(packed.reshape(owner_count, capacity, 2, block_size, block...  195 us
    all_gather x1, waiting for transfers between devices, body(): gathered = lax.all_gather(x_panel, 'tensor', axis=1, tiled=True)  120 us
    scatter x1, local copies, waits for them, and re-layouts, body(): packed.at[target]  11.5 us
  transfers between devices with their start and end apart: 1, of which 1 were waited for; matrix products, arithmetic and copies ran while one was open for 1% of the time, Pallas kernels for 0%

commit v1 on v0

v1 whole, which is shorter than its diff:
```python
import functools

import jax
import jax.numpy as jnp
from jax import lax
from jax.experimental import pallas as pl
from jax.experimental.pallas import tpu as pltpu
from jax.sharding import Mesh, PartitionSpec as P

BS = 128
KB = 8
COLS = 7
BLOCKS = COLS * KB
TOK = 512
ROWS = 32
NX, NZ, CAP = 4, 8, 2
GROUP = NZ * CAP
AXES = {"zl": 8, "x": 4, "y": 4, "zh": 2, "core": 2}
VMEM = pl.BlockSpec(memory_space=pltpu.VMEM)
SMEM = pl.BlockSpec(memory_space=pltpu.SMEM)


def shift(value, axis, step):
    size = AXES[axis]
    return lax.ppermute(value, axis, [(i, (i + step) % size) for i in range(size)])


def flip(value, axis, bit):
    return lax.ppermute(value, axis, [(i, i ^ bit) for i in range(AXES[axis])])


def call(kernel, out_shape, in_specs, out_specs, scratch=(), flops=0, bytes_accessed=0):
    return pl.pallas_call(
        kernel,
        out_shape=out_shape,
        in_specs=in_specs,
        out_specs=out_specs,
        scratch_shapes=list(scratch),
        compiler_params=pltpu.CompilerParams(vmem_limit_bytes=40 * 1024 * 1024),
        cost_estimate=pl.CostEstimate(flops=flops, bytes_accessed=bytes_accessed, transcendentals=0),
    )


def table_kernel(owner_ref, table_ref, seen_ref):
    my_x = lax.axis_index("x")
    my_z = lax.axis_index("zl")

    def clear(i, carry):
        table_ref[i] = jnp.int32(-1)
        return carry

    lax.fori_loop(0, NX * GROUP, clear, 0)

    def clear_seen(i, carry):
        seen_ref[i] = jnp.int32(0)
        return carry

    lax.fori_loop(0, NX * NZ, clear_seen, 0)

    def place(i, carry):
        owner = owner_ref[i // KB, i % KB]
        slot = seen_ref[owner]
        seen_ref[owner] = slot + 1
        rel_x = (owner % NX - my_x + NX) % NX
        rel_z = (owner // NX) ^ my_z
        rel_z = (rel_z & 1) * 4 + (rel_z & 2) + (rel_z >> 2)
        table_ref[rel_x * GROUP + rel_z * CAP + slot] = i
        return carry

    lax.fori_loop(0, BLOCKS, place, 0)


def forward_kernel(a_ref, ac_ref, b_ref, bc_ref, w_ref, g_ref, rows_ref, x_ref, act_ref, picked_ref):
    zh = lax.axis_index("zh")
    core = lax.axis_index("core")
    for ref, z, c in ((a_ref, zh, core), (ac_ref, zh, 1 - core), (b_ref, 1 - zh, core), (bc_ref, 1 - zh, 1 - core)):
        for y in range(4):
            at = (y * 4 + z * 2 + c) * 2
            x_ref[at] = ref[y, :BS]
            x_ref[at + 1] = ref[y, BS:]

    def column(c, carry):
        for k in range(KB):
            picked_ref[k * BS:(k + 1) * BS] = x_ref[rows_ref[c, k]]
        pre = jnp.dot(w_ref[c], picked_ref[...], preferred_element_type=jnp.float32)
        gate, up = pre[:BS], pre[BS:]
        s = jax.nn.sigmoid(gate)
        h = g_ref[c].astype(jnp.float32)
        act_ref[c, :BS] = (h * up * (s * (1.0 + gate * (1.0 - s)))).astype(jnp.bfloat16)
        act_ref[c, BS:] = (h * (gate * s)).astype(jnp.bfloat16)
        return carry

    lax.fori_loop(0, COLS, column, 0)


def backward_kernel(group, dtype, x_ref, act_ref, rows_ref, table_ref, lo_ref, hi_ref):
    for i in range(GROUP):
        block = table_ref[group * GROUP + i]
        at = jnp.maximum(block, 0)
        c = at // KB
        value = lax.dot_general(
            x_ref[rows_ref[c, at % KB]], act_ref[c], (((1,), (1,)), ((), ())), preferred_element_type=jnp.float32
        )
        value = jnp.where(block >= 0, value, 0.0).astype(dtype)
        ref = lo_ref if i < GROUP // 2 else hi_ref
        row = (i % (GROUP // 2)) * 2 * BS
        ref[row:row + BS] = value[:, :BS]
        ref[row + BS:row + 2 * BS] = value[:, BS:]


def body(x_panel, grad_hidden, gate_blocks, up_blocks, block_rows, block_owner):
    bf16, f32 = jnp.bfloat16, jnp.float32
    table = call(
        table_kernel, jax.ShapeDtypeStruct((NX * GROUP,), jnp.int32), [SMEM], SMEM,
        [pltpu.SMEM((NX * NZ,), jnp.int32)],
    )(block_owner)
    own = x_panel.T
    far = flip(own, "zh", 1)
    weights = jnp.concatenate(
        [w.transpose(0, 3, 1, 2).reshape(COLS, BS, KB * BS) for w in (gate_blocks, up_blocks)], 1
    )
    hidden = grad_hidden.T.reshape(COLS, BS, TOK)
    a = lax.all_to_all(jnp.broadcast_to(own[None], (4,) + own.shape), "y", 0, 0, tiled=True)
    ac = flip(a, "core", 1)
    b = lax.all_to_all(jnp.broadcast_to(far[None], (4,) + far.shape), "y", 0, 0, tiled=True)
    bc = flip(b, "core", 1)

    x_all, act = call(
        forward_kernel,
        (jax.ShapeDtypeStruct((ROWS, BS, TOK), bf16), jax.ShapeDtypeStruct((COLS, 2 * BS, TOK), bf16)),
        [VMEM] * 6 + [SMEM], (VMEM, VMEM), [pltpu.VMEM((KB * BS, TOK), bf16)],
        flops=2 * COLS * KB * BS * 2 * BS * TOK, bytes_accessed=14 * 2**20,
    )(a, ac, b, bc, weights, hidden, block_rows)

    def backward(group, dtype):
        half = jax.ShapeDtypeStruct((GROUP * BS, BS), dtype)
        return call(
            functools.partial(backward_kernel, group, dtype), (half, half), [VMEM, VMEM, SMEM, SMEM], (VMEM, VMEM),
            flops=2 * GROUP * BS * 2 * BS * TOK, bytes_accessed=7 * 2**20,
        )(x_all, act, block_rows, table)

    p2a, p2b = backward(2, bf16)
    r2a = shift(p2a, "x", 1)
    r2b = shift(p2b, "x", -1)
    p1a, p1b = backward(1, bf16)
    r1b = shift(p1b, "x", 1)
    p3a, p3b = backward(3, bf16)
    r3a = shift(p3a, "x", -1)
    p0a, p0b = backward(0, f32)
    r1a = shift((p1a.astype(f32) + r2a.astype(f32)).astype(bf16), "x", 1)
    r3b = shift((p3b.astype(f32) + r2b.astype(f32)).astype(bf16), "x", -1)
    send = (p0b + r1b.astype(f32) + r3b.astype(f32)).astype(bf16)
    got = flip(send, "zl", 1)
    keep = p0a + r1a.astype(f32) + r3a.astype(f32) + got.astype(f32)
    half = keep.shape[0] // 2
    got = flip(keep[half:].astype(bf16), "zl", 2)
    keep = keep[:half] + got.astype(f32)
    half = half // 2
    got = flip(keep[half:].astype(bf16), "zl", 4)
    keep = keep[:half] + got.astype(f32)
    return keep.reshape(1, 1, CAP, 2, BS, BS)


def solution(mesh):
    fine = Mesh(mesh.devices.reshape(tuple(AXES.values())), tuple(AXES))
    dp, tensor = ("zl", "x"), ("y", "zh", "core")
    in_specs = (
        P(dp, tensor),
        P(dp, tensor),
        P(tensor, None, None, None),
        P(tensor, None, None, None),
        P(tensor, None),
        P(tensor, None),
    )
    out_specs = P(tensor, dp, None, None, None, None)
    return jax.shard_map(body, mesh=fine, in_specs=in_specs, out_specs=out_specs, check_vma=False)
```

time: 385 us -> 184 us (0.48)
  blocking collectives: 195 us -> 0 us
  starting transfers between devices: 0.01 us -> 77.8 us
  waiting for transfers between devices: 120 us -> 67.2 us
  local copies, waits for them, and re-layouts: 41 us -> 14.8 us
  Pallas kernels: 0 us -> 18.9 us
  between operations: 13.5 us -> 0.27 us
  matrix products: 11.3 us -> 0 us
    all_to_all x1 -> x0, blocking collectives: 195 us -> none  [body(): lax.all_to_all(packed.reshape(owner_count, capacity, 2, block_size, block...]
    all_gather x1 -> x0, waiting for transfers between devices: 120 us -> none  [body(): gathered = lax.all_gather(x_panel, 'tensor', axis=1, tiled=True)]
    ppermute x0 -> x12, starting transfers between devices: none -> 68.8 us  [the longest x6 48.5 us: flip(): return lax.ppermute(value, axis, [(i, i ^ bit) for i in range(AXES[axis])])]
    ppermute x0 -> x12, waiting for transfers between devices: none -> 55.5 us  [the longest x6 41.2 us: flip(): return lax.ppermute(value, axis, [(i, i ^ bit) for i in range(AXES[axis])])]
    pallas_call x0 -> x6, Pallas kernels: none -> 18.9 us  [the longest x4 8.38 us: backward(): call(functools.partial(backward_kernel, group, dtype), (half, half), [VME...]
    all_to_all x0 -> x2, waiting for transfers between devices: none -> 11.7 us  [the longest x1 11.7 us: body(): lax.all_to_all(jnp.broadcast_to(far[None], (4,) + far.shape), 'y', 0, 0,...]
    scatter x1 -> x0, local copies, waits for them, and re-layouts: 11.5 us -> none  [body(): packed.at[target]]
    dot_general x3 -> x0, matrix products: 11.3 us -> none  [the longest x1 5.28 us: body(): jnp.einsum('tckb,ckbe->tce', picked, gate_blocks, preferred_element_type=...]
  transfers between devices with their start and end apart: 1 -> 14, of which waited for: 1 -> 8; matrix products, arithmetic and copies ran while one was open for 1% -> 7% of each run, Pallas kernels for 0% -> 5%
where the time goes in v1:
time: 184 us; the launch traced here: 183 us
  starting transfers between devices  77.8 us (42%)
  waiting for transfers between devices  67.2 us (37%)
  Pallas kernels  18.9 us (10%)
  local copies, waits for them, and re-layouts  14.8 us (8%)
  other arithmetic  3.88 us (2%)
    ppermute x6, starting transfers between devices, flip(): return lax.ppermute(value, axis, [(i, i ^ bit) for i in range(AXES[axis])])  48.5 us
    ppermute x6, waiting for transfers between devices, flip(): return lax.ppermute(value, axis, [(i, i ^ bit) for i in range(AXES[axis])])  41.2 us
    ppermute x6, starting transfers between devices, shift(): lax.ppermute(value, axis, [(i, (i + step) % size) for i in range(size)])  20.3 us
    ppermute x6, waiting for transfers between devices, shift(): lax.ppermute(value, axis, [(i, (i + step) % size) for i in range(size)])  14.3 us
    all_to_all x1, waiting for transfers between devices, body(): lax.all_to_all(jnp.broadcast_to(far[None], (4,) + far.shape), 'y', 0, 0,...  11.7 us
    pallas_call x4, Pallas kernels, backward(): call(functools.partial(backward_kernel, group, dtype), (half, half), [VME...  8.38 us
    reshape x2, local copies, waits for them, and re-layouts, body(): w.transpose(0, 3, 1, 2).reshape(COLS, BS, KB * BS)  7.68 us
    pallas_call x1, Pallas kernels, body(): call(forward_kernel, (jax.ShapeDtypeStruct((ROWS, BS, TOK), bf16), jax.Sh...  7.07 us
  transfers between devices with their start and end apart: 14, of which 8 were waited for; matrix products, arithmetic and copies ran while one was open for 7% of the time, Pallas kernels for 5%

profile of v1, /device:TPU:6, one launch (start us, length us, event | category | flops | bytes accessed | tf_op | source)
XLA Modules:
  0.0 182.9 jit_solution(1537941979936460191)
XLA Ops:
  2.2 4.5 %all-to-all-start = ((bf16[4,256,512]{2,1,0:T(8,128)(2,1)}), bf16[4,256,512]{2,1,0:T(8,128)(2,1)S(1)}, u32[]{:S(2)}, u32[]{:S(2)}) async-start(bf16[4,256,512]{2,1,0:T(8,128)(2,1)} %broadcast_in_dim.4), calls=%async_computation | async-start | bytes 2097152 | tf_op jit(solution)/shard_map/all_to_all | solution.py:123
  6.7 15.7 %collective-permute-start.1 = (bf16[256,512]{0,1:T(8,128)(2,1)S(1)}, bf16[256,512]{0,1:T(8,128)(2,1)S(1)}, u32[]{:S(2)}, u32[]{:S(2)}) collective-permute-start(bf16[256,512]{0,1:T(8,128)(2,1)S(1)} %bitcast.15), channel_id=1, source_target_pairs={{0,2},{2,0},{1,3},{3,1},{4,6},{6,4},{5,7},{7,5},{8,10},{10,8},{9,1... | collective-permute-start | bytes 786440 | tf_op jit(solution)/shard_map/ppermute | solution.py:29
  22.4 6.3 %collective-permute-done.1 = bf16[256,512]{0,1:T(8,128)(2,1)S(1)} collective-permute-done((bf16[256,512]{0,1:T(8,128)(2,1)S(1)}, bf16[256,512]{0,1:T(8,128)(2,1)S(1)}, u32[]{:S(2)}, u32[]{:S(2)}) %collective-permute-start.1) | collective-permute-done | bytes 262176 | tf_op jit(solution)/shard_map/ppermute | solution.py:29
  30.0 4.5 %all-to-all-start.1 = ((bf16[4,256,512]{2,1,0:T(8,128)(2,1)}), bf16[4,256,512]{2,1,0:T(8,128)(2,1)S(1)}, u32[]{:S(2)}, u32[]{:S(2)}) async-start(bf16[4,256,512]{2,1,0:T(8,128)(2,1)} %broadcast_in_dim.5), calls=%async_computation.1 | async-start | bytes 2097152 | tf_op jit(solution)/shard_map/all_to_all | solution.py:125
  34.5 1.9 %collective-permute-start = (bf16[4,256,512]{2,1,0:T(8,128)(2,1)S(1)}, bf16[4,256,512]{2,1,0:T(8,128)(2,1)}, u32[]{:S(2)}, u32[]{:S(2)}) collective-permute-start(bf16[4,256,512]{2,1,0:T(8,128)(2,1)S(1)} %all-to-all-done.a_ref), channel_id=1, source_target_pairs={{0,1},{1,0},{2,3},{3,2},{4,5},{5,4},{6,7},{7,6},{8,9},{9,8},{10,11... | collective-permute-start | bytes 3145736 | tf_op jit(solution)/shard_map/ppermute | solution.py:29
  36.4 11.7 %all-to-all-done.1.b_ref = bf16[4,256,512]{2,1,0:T(8,128)(2,1)S(1)} async-done(((bf16[4,256,512]{2,1,0:T(8,128)(2,1)}), bf16[4,256,512]{2,1,0:T(8,128)(2,1)S(1)}, u32[]{:S(2)}, u32[]{:S(2)}) %all-to-all-start.1) | async-done | bytes 1048608 | tf_op jit(solution)/shard_map/all_to_all | solution.py:125
  48.1 1.9 %collective-permute-start.2 = (bf16[4,256,512]{2,1,0:T(8,128)(2,1)S(1)}, bf16[4,256,512]{2,1,0:T(8,128)(2,1)}, u32[]{:S(2)}, u32[]{:S(2)}) collective-permute-start(bf16[4,256,512]{2,1,0:T(8,128)(2,1)S(1)} %all-to-all-done.1.b_ref), channel_id=1, source_target_pairs={{0,1},{1,0},{2,3},{3,2},{4,5},{5,4},{6,7},{7,6},{8,9},{9,8},{10,11... | collective-permute-start | bytes 3145736 | tf_op jit(solution)/shard_map/ppermute | solution.py:29
  50.0 3.8 %copy.12 = bf16[7,128,1024]{2,1,0:T(8,128)(2,1)} copy(bf16[7,128,1024]{1,2,0:T(8,128)(2,1)} %bitcast.11) | data formatting | bytes 3670016 | tf_op jit(solution)/shard_map/reshape | solution.py:120
  53.9 3.8 %copy.13 = bf16[7,128,1024]{2,1,0:T(8,128)(2,1)} copy(bf16[7,128,1024]{1,2,0:T(8,128)(2,1)} %bitcast.12) | data formatting | bytes 3670016 | tf_op jit(solution)/shard_map/reshape | solution.py:120
  57.7 1.5 copy.11
  59.2 3.5 %shard_map.65.table_ref = s32[64]{0:T(128)S(1)} custom-call(s32[7,8]{1,0:T(8,128)S(1)} %copy-done.2), custom_call_target="tpu_custom_call" | custom-call | tf_op jit(solution)/shard_map/pallas_call | solution.py:113
  62.7 2.4 %pad_maximum_fusion.w_ref = bf16[7,256,1024]{2,1,0:T(8,128)(2,1)S(1)} fusion(bf16[7,128,1024]{2,1,0:T(8,128)(2,1)} %copy.13, bf16[7,128,1024]{2,1,0:T(8,128)(2,1)} %copy.12), kind=kLoop, calls=%fused_computation | loop fusion | flops 7340032 | bytes 7340032 | tf_op jit(solution)/shard_map/concatenate | solution.py:119
  65.1 7.1 %shard_map.64 = (bf16[32,128,512]{2,1,0:T(8,128)(2,1)}, bf16[7,256,512]{2,1,0:T(8,128)(2,1)S(1)}) custom-call(bf16[4,256,512]{2,1,0:T(8,128)(2,1)S(1)} %all-to-all-done.a_ref, bf16[4,256,512]{2,1,0:T(8,128)(2,1)} %collective-permute-done.ac_ref, bf16[4,256,512]{2,1,0:T(8,128)(2,1)S(1)} %all-to-all-done.1.b_ref, ...), custom_call_target="tpu_custom_call" | custom-call | flops 1879048192 | bytes 14680064 | tf_op jit(solution)/shard_map/pallas_call | solution.py:128
  72.2 2.2 %copy-done = bf16[32,128,512]{2,1,0:T(8,128)(2,1)S(1)} copy-done((bf16[32,128,512]{2,1,0:T(8,128)(2,1)S(1)}, bf16[32,128,512]{2,1,0:T(8,128)(2,1)}, u32[]{:S(2)}) %copy-start) | copy-done | bytes 4194328
  74.4 2.1 %shard_map.68 = (bf16[2048,128]{1,0:T(8,128)(2,1)S(1)}, bf16[2048,128]{1,0:T(8,128)(2,1)S(1)}) custom-call(bf16[32,128,512]{2,1,0:T(8,128)(2,1)S(1)} %copy-done, bf16[7,256,512]{2,1,0:T(8,128)(2,1)S(1)} %get-tuple-element.16.act_ref, s32[7,8]{1,0:T(8,128)S(1)} %copy-done.1, s32[64]{0:T(128)S(1)} %shard_map.65.table_ref), custom_call_target="tpu_custom_call" | custom-call | flops 536870912 | bytes 7340032 | tf_op jit(solution)/shard_map/pallas_call | solution.py:137
  76.5 2.7 %collective-permute-start.7 = (bf16[2048,128]{1,0:T(8,128)(2,1)S(1)}, bf16[2048,128]{1,0:T(8,128)(2,1)S(1)}, u32[]{:S(2)}, u32[]{:S(2)}) collective-permute-start(bf16[2048,128]{1,0:T(8,128)(2,1)S(1)} %get-tuple-element.24), channel_id=1, source_target_pairs={{0,48},{16,0},{32,16},{48,32},{1,49},{17,1},{33,17},{49,33},{2,50}... | collective-permute-start | bytes 1572872 | tf_op jit(solution)/shard_map/ppermute | solution.py:25
  79.2 2.1 %shard_map.67 = (bf16[2048,128]{1,0:T(8,128)(2,1)S(1)}, bf16[2048,128]{1,0:T(8,128)(2,1)S(1)}) custom-call(bf16[32,128,512]{2,1,0:T(8,128)(2,1)S(1)} %copy-done, bf16[7,256,512]{2,1,0:T(8,128)(2,1)S(1)} %get-tuple-element.16.act_ref, s32[7,8]{1,0:T(8,128)S(1)} %copy-done.1, s32[64]{0:T(128)S(1)} %shard_map.65.table_ref), custom_call_target="tpu_custom_call" | custom-call | flops 536870912 | bytes 7340032 | tf_op jit(solution)/shard_map/pallas_call | solution.py:137
  81.3 4.3 %collective-permute-start.6 = (bf16[2048,128]{1,0:T(8,128)(2,1)S(1)}, bf16[2048,128]{1,0:T(8,128)(2,1)S(1)}, u32[]{:S(2)}, u32[]{:S(2)}) collective-permute-start(bf16[2048,128]{1,0:T(8,128)(2,1)S(1)} %get-tuple-element.22), channel_id=1, source_target_pairs={{0,16},{16,32},{32,48},{48,0},{1,17},{17,33},{33,49},{49,1},{2,18}... | collective-permute-start | bytes 1572872 | tf_op jit(solution)/shard_map/ppermute | solution.py:25
  85.7 1.9 %collective-permute-start.3 = (bf16[2048,128]{1,0:T(8,128)(2,1)S(1)}, bf16[2048,128]{1,0:T(8,128)(2,1)S(1)}, u32[]{:S(2)}, u32[]{:S(2)}) collective-permute-start(bf16[2048,128]{1,0:T(8,128)(2,1)S(1)} %get-tuple-element.19), channel_id=1, source_target_pairs={{0,16},{16,32},{32,48},{48,0},{1,17},{17,33},{33,49},{49,1},{2,18}... | collective-permute-start | bytes 1572872 | tf_op jit(solution)/shard_map/ppermute | solution.py:25
  87.6 2.1 %shard_map.69 = (bf16[2048,128]{1,0:T(8,128)(2,1)S(1)}, bf16[2048,128]{1,0:T(8,128)(2,1)S(1)}) custom-call(bf16[32,128,512]{2,1,0:T(8,128)(2,1)S(1)} %copy-done, bf16[7,256,512]{2,1,0:T(8,128)(2,1)S(1)} %get-tuple-element.16.act_ref, s32[7,8]{1,0:T(8,128)S(1)} %copy-done.1, s32[64]{0:T(128)S(1)} %shard_map.65.table_ref), custom_call_target="tpu_custom_call" | custom-call | flops 536870912 | bytes 7340032 | tf_op jit(solution)/shard_map/pallas_call | solution.py:137
  89.7 3.9 %collective-permute-start.5 = (bf16[2048,128]{1,0:T(8,128)(2,1)S(1)}, bf16[2048,128]{1,0:T(8,128)(2,1)S(1)}, u32[]{:S(2)}, u32[]{:S(2)}) collective-permute-start(bf16[2048,128]{1,0:T(8,128)(2,1)S(1)} %get-tuple-element.20), channel_id=1, source_target_pairs={{0,48},{16,0},{32,16},{48,32},{1,49},{17,1},{33,17},{49,33},{2,50}... | collective-permute-start | bytes 1572872 | tf_op jit(solution)/shard_map/ppermute | solution.py:25
  94.1 1.9 %collective-permute-start.8 = (bf16[2048,128]{1,0:T(8,128)(2,1)S(1)}, bf16[2048,128]{1,0:T(8,128)(2,1)S(1)}, u32[]{:S(2)}, u32[]{:S(2)}) collective-permute-start(bf16[2048,128]{1,0:T(8,128)(2,1)S(1)} %add_convert_fusion.1), channel_id=1, source_target_pairs={{0,48},{16,0},{32,16},{48,32},{1,49},{17,1},{33,17},{49,33},{2,50}... | collective-permute-start | bytes 1572872 | tf_op jit(solution)/shard_map/ppermute | solution.py:25
  96.0 2.1 %shard_map.66 = (f32[2048,128]{1,0:T(8,128)S(1)}, f32[2048,128]{1,0:T(8,128)S(1)}) custom-call(bf16[32,128,512]{2,1,0:T(8,128)(2,1)S(1)} %copy-done, bf16[7,256,512]{2,1,0:T(8,128)(2,1)S(1)} %get-tuple-element.16.act_ref, s32[7,8]{1,0:T(8,128)S(1)} %copy-done.1, s32[64]{0:T(128)S(1)} %shard_map.65.table_ref), custom_call_target="tpu_custom_call" | custom-call | flops 536870912 | bytes 7340032 | tf_op jit(solution)/shard_map/pallas_call | solution.py:137
  98.1 10.4 %collective-permute-done.3 = bf16[2048,128]{1,0:T(8,128)(2,1)S(1)} collective-permute-done((bf16[2048,128]{1,0:T(8,128)(2,1)S(1)}, bf16[2048,128]{1,0:T(8,128)(2,1)S(1)}, u32[]{:S(2)}, u32[]{:S(2)}) %collective-permute-start.3) | collective-permute-done | bytes 524320 | tf_op jit(solution)/shard_map/ppermute | solution.py:25
  108.7 5.5 %collective-permute-start.4 = (bf16[2048,128]{1,0:T(8,128)(2,1)S(1)}, bf16[2048,128]{1,0:T(8,128)(2,1)S(1)}, u32[]{:S(2)}, u32[]{:S(2)}) collective-permute-start(bf16[2048,128]{1,0:T(8,128)(2,1)S(1)} %add_convert_fusion.2), channel_id=1, source_target_pairs={{0,16},{16,32},{32,48},{48,0},{1,17},{17,33},{33,49},{49,1},{2,18}... | collective-permute-start | bytes 1572872 | tf_op jit(solution)/shard_map/ppermute | solution.py:25
  114.2 3.6 %collective-permute-done.8 = bf16[2048,128]{1,0:T(8,128)(2,1)S(1)} collective-permute-done((bf16[2048,128]{1,0:T(8,128)(2,1)S(1)}, bf16[2048,128]{1,0:T(8,128)(2,1)S(1)}, u32[]{:S(2)}, u32[]{:S(2)}) %collective-permute-start.8) | collective-permute-done | bytes 524320 | tf_op jit(solution)/shard_map/ppermute | solution.py:25
  118.0 20.2 %collective-permute-start.9 = (bf16[2048,128]{1,0:T(8,128)(2,1)S(1)}, bf16[2048,128]{1,0:T(8,128)(2,1)S(1)}, u32[]{:S(2)}, u32[]{:S(2)}) collective-permute-start(bf16[2048,128]{1,0:T(8,128)(2,1)S(1)} %add_convert_fusion), channel_id=1, source_target_pairs={{0,64},{64,0},{128,192},{192,128},{256,320},{320,256},{384,448},{4... | collective-permute-start | bytes 1572872 | tf_op jit(solution)/shard_map/ppermute | solution.py:29
  138.2 11.1 %collective-permute-done.9 = bf16[2048,128]{1,0:T(8,128)(2,1)S(1)} collective-permute-done((bf16[2048,128]{1,0:T(8,128)(2,1)S(1)}, bf16[2048,128]{1,0:T(8,128)(2,1)S(1)}, u32[]{:S(2)}, u32[]{:S(2)}) %collective-permute-start.9) | collective-permute-done | bytes 524320 | tf_op jit(solution)/shard_map/ppermute | solution.py:29
  149.6 1.9 %collective-permute-start.10 = (bf16[1024,128]{1,0:T(8,128)(2,1)S(1)}, bf16[1024,128]{1,0:T(8,128)(2,1)S(1)}, u32[]{:S(2)}, u32[]{:S(2)}) collective-permute-start(bf16[1024,128]{1,0:T(8,128)(2,1)S(1)} %slice.26), channel_id=1, source_target_pairs={{0,128},{64,192},{128,0},{192,64},{256,384},{320,448},{384,256},{4... | collective-permute-start | bytes 786440 | tf_op jit(solution)/shard_map/ppermute | solution.py:29
  151.5 13.1 %collective-permute-done.10 = bf16[1024,128]{1,0:T(8,128)(2,1)S(1)} collective-permute-done((bf16[1024,128]{1,0:T(8,128)(2,1)S(1)}, bf16[1024,128]{1,0:T(8,128)(2,1)S(1)}, u32[]{:S(2)}, u32[]{:S(2)}) %collective-permute-start.10) | collective-permute-done | bytes 262176 | tf_op jit(solution)/shard_map/ppermute | solution.py:29
  164.8 6.8 %collective-permute-start.11 = (bf16[512,128]{1,0:T(8,128)(2,1)S(1)}, bf16[512,128]{1,0:T(8,128)(2,1)S(1)}, u32[]{:S(2)}, u32[]{:S(2)}) collective-permute-start(bf16[512,128]{1,0:T(8,128)(2,1)S(1)} %slice.27), channel_id=1, source_target_pairs={{0,256},{64,320},{128,384},{192,448},{256,0},{320,64},{384,128},{4... | collective-permute-start | bytes 393224 | tf_op jit(solution)/shard_map/ppermute | solution.py:29
  171.6 10.6 %collective-permute-done.11 = bf16[512,128]{1,0:T(8,128)(2,1)S(1)} collective-permute-done((bf16[512,128]{1,0:T(8,128)(2,1)S(1)}, bf16[512,128]{1,0:T(8,128)(2,1)S(1)}, u32[]{:S(2)}, u32[]{:S(2)}) %collective-permute-start.11) | collective-permute-done | bytes 131104 | tf_op jit(solution)/shard_map/ppermute | solution.py:29
  (26 shorter events, 5.3 us)
Async XLA Ops:
  0.0 6.7 %copy-start.3 = (bf16[512,256]{1,0:T(8,128)(2,1)S(1)}, bf16[512,256]{1,0:T(8,128)(2,1)}, u32[]{:S(2)}) copy-start(bf16[512,256]{1,0:T(8,128)(2,1)} %param.6) | copy-start | bytes 786436
  2.2 26.6 %all-to-all-start = ((bf16[4,256,512]{2,1,0:T(8,128)(2,1)}), bf16[4,256,512]{2,1,0:T(8,128)(2,1)S(1)}, u32[]{:S(2)}, u32[]{:S(2)}) async-start(bf16[4,256,512]{2,1,0:T(8,128)(2,1)} %broadcast_in_dim.4), calls=%async_computation | async-start | bytes 2097152 | tf_op jit(solution)/shard_map/all_to_all | solution.py:123
  6.7 22.0 %collective-permute-start.1 = (bf16[256,512]{0,1:T(8,128)(2,1)S(1)}, bf16[256,512]{0,1:T(8,128)(2,1)S(1)}, u32[]{:S(2)}, u32[]{:S(2)}) collective-permute-start(bf16[256,512]{0,1:T(8,128)(2,1)S(1)} %bitcast.15), channel_id=1, source_target_pairs={{0,2},{2,0},{1,3},{3,1},{4,6},{6,4},{5,7},{7,5},{8,10},{10,8},{9,1... | collective-permute-start | bytes 786440 | tf_op jit(solution)/shard_map/ppermute | solution.py:29
  30.0 18.1 %all-to-all-start.1 = ((bf16[4,256,512]{2,1,0:T(8,128)(2,1)}), bf16[4,256,512]{2,1,0:T(8,128)(2,1)S(1)}, u32[]{:S(2)}, u32[]{:S(2)}) async-start(bf16[4,256,512]{2,1,0:T(8,128)(2,1)} %broadcast_in_dim.5), calls=%async_computation.1 | async-start | bytes 2097152 | tf_op jit(solution)/shard_map/all_to_all | solution.py:125
  34.5 30.6 %collective-permute-start = (bf16[4,256,512]{2,1,0:T(8,128)(2,1)S(1)}, bf16[4,256,512]{2,1,0:T(8,128)(2,1)}, u32[]{:S(2)}, u32[]{:S(2)}) collective-permute-start(bf16[4,256,512]{2,1,0:T(8,128)(2,1)S(1)} %all-to-all-done.a_ref), channel_id=1, source_target_pairs={{0,1},{1,0},{2,3},{3,2},{4,5},{5,4},{6,7},{7,6},{8,9},{9,8},{10,11... | collective-permute-start | bytes 3145736 | tf_op jit(solution)/shard_map/ppermute | solution.py:29
  48.1 17.0 %collective-permute-start.2 = (bf16[4,256,512]{2,1,0:T(8,128)(2,1)S(1)}, bf16[4,256,512]{2,1,0:T(8,128)(2,1)}, u32[]{:S(2)}, u32[]{:S(2)}) collective-permute-start(bf16[4,256,512]{2,1,0:T(8,128)(2,1)S(1)} %all-to-all-done.1.b_ref), channel_id=1, source_target_pairs={{0,1},{1,0},{2,3},{3,2},{4,5},{5,4},{6,7},{7,6},{8,9},{9,8},{10,11... | collective-permute-start | bytes 3145736 | tf_op jit(solution)/shard_map/ppermute | solution.py:29
  53.9 5.3 %copy-start.2 = (s32[7,8]{1,0:T(8,128)S(1)}, s32[7,8]{1,0:T(8,128)}, u32[]{:S(2)}) copy-start(s32[7,8]{1,0:T(8,128)} %owner_ref.1) | copy-start | bytes 676
  62.7 2.5 %copy-start.1 = (s32[7,8]{1,0:T(8,128)S(1)}, s32[7,8]{1,0:T(8,128)}, u32[]{:S(2)}) copy-start(s32[7,8]{1,0:T(8,128)} %rows_ref.9) | copy-start | bytes 676
  72.2 2.2 %copy-start = (bf16[32,128,512]{2,1,0:T(8,128)(2,1)S(1)}, bf16[32,128,512]{2,1,0:T(8,128)(2,1)}, u32[]{:S(2)}) copy-start(bf16[32,128,512]{2,1,0:T(8,128)(2,1)} %get-tuple-element.15.x_ref) | copy-start | bytes 12582916
  76.5 17.4 %collective-permute-start.7 = (bf16[2048,128]{1,0:T(8,128)(2,1)S(1)}, bf16[2048,128]{1,0:T(8,128)(2,1)S(1)}, u32[]{:S(2)}, u32[]{:S(2)}) collective-permute-start(bf16[2048,128]{1,0:T(8,128)(2,1)S(1)} %get-tuple-element.24), channel_id=1, source_target_pairs={{0,48},{16,0},{32,16},{48,32},{1,49},{17,1},{33,17},{49,33},{2,50}... | collective-permute-start | bytes 1572872 | tf_op jit(solution)/shard_map/ppermute | solution.py:25
  81.3 32.9 %collective-permute-start.6 = (bf16[2048,128]{1,0:T(8,128)(2,1)S(1)}, bf16[2048,128]{1,0:T(8,128)(2,1)S(1)}, u32[]{:S(2)}, u32[]{:S(2)}) collective-permute-start(bf16[2048,128]{1,0:T(8,128)(2,1)S(1)} %get-tuple-element.22), channel_id=1, source_target_pairs={{0,16},{16,32},{32,48},{48,0},{1,17},{17,33},{33,49},{49,1},{2,18}... | collective-permute-start | bytes 1572872 | tf_op jit(solution)/shard_map/ppermute | solution.py:25
  85.7 22.9 %collective-permute-start.3 = (bf16[2048,128]{1,0:T(8,128)(2,1)S(1)}, bf16[2048,128]{1,0:T(8,128)(2,1)S(1)}, u32[]{:S(2)}, u32[]{:S(2)}) collective-permute-start(bf16[2048,128]{1,0:T(8,128)(2,1)S(1)} %get-tuple-element.19), channel_id=1, source_target_pairs={{0,16},{16,32},{32,48},{48,0},{1,17},{17,33},{33,49},{49,1},{2,18}... | collective-permute-start | bytes 1572872 | tf_op jit(solution)/shard_map/ppermute | solution.py:25
  89.7 48.5 %collective-permute-start.5 = (bf16[2048,128]{1,0:T(8,128)(2,1)S(1)}, bf16[2048,128]{1,0:T(8,128)(2,1)S(1)}, u32[]{:S(2)}, u32[]{:S(2)}) collective-permute-start(bf16[2048,128]{1,0:T(8,128)(2,1)S(1)} %get-tuple-element.20), channel_id=1, source_target_pairs={{0,48},{16,0},{32,16},{48,32},{1,49},{17,1},{33,17},{49,33},{2,50}... | collective-permute-start | bytes 1572872 | tf_op jit(solution)/shard_map/ppermute | solution.py:25
  94.1 23.7 %collective-permute-start.8 = (bf16[2048,128]{1,0:T(8,128)(2,1)S(1)}, bf16[2048,128]{1,0:T(8,128)(2,1)S(1)}, u32[]{:S(2)}, u32[]{:S(2)}) collective-permute-start(bf16[2048,128]{1,0:T(8,128)(2,1)S(1)} %add_convert_fusion.1), channel_id=1, source_target_pairs={{0,48},{16,0},{32,16},{48,32},{1,49},{17,1},{33,17},{49,33},{2,50}... | collective-permute-start | bytes 1572872 | tf_op jit(solution)/shard_map/ppermute | solution.py:25
  108.7 29.6 %collective-permute-start.4 = (bf16[2048,128]{1,0:T(8,128)(2,1)S(1)}, bf16[2048,128]{1,0:T(8,128)(2,1)S(1)}, u32[]{:S(2)}, u32[]{:S(2)}) collective-permute-start(bf16[2048,128]{1,0:T(8,128)(2,1)S(1)} %add_convert_fusion.2), channel_id=1, source_target_pairs={{0,16},{16,32},{32,48},{48,0},{1,17},{17,33},{33,49},{49,1},{2,18}... | collective-permute-start | bytes 1572872 | tf_op jit(solution)/shard_map/ppermute | solution.py:25
  118.0 31.4 %collective-permute-start.9 = (bf16[2048,128]{1,0:T(8,128)(2,1)S(1)}, bf16[2048,128]{1,0:T(8,128)(2,1)S(1)}, u32[]{:S(2)}, u32[]{:S(2)}) collective-permute-start(bf16[2048,128]{1,0:T(8,128)(2,1)S(1)} %add_convert_fusion), channel_id=1, source_target_pairs={{0,64},{64,0},{128,192},{192,128},{256,320},{320,256},{384,448},{4... | collective-permute-start | bytes 1572872 | tf_op jit(solution)/shard_map/ppermute | solution.py:29
  149.6 15.1 %collective-permute-start.10 = (bf16[1024,128]{1,0:T(8,128)(2,1)S(1)}, bf16[1024,128]{1,0:T(8,128)(2,1)S(1)}, u32[]{:S(2)}, u32[]{:S(2)}) collective-permute-start(bf16[1024,128]{1,0:T(8,128)(2,1)S(1)} %slice.26), channel_id=1, source_target_pairs={{0,128},{64,192},{128,0},{192,64},{256,384},{320,448},{384,256},{4... | collective-permute-start | bytes 786440 | tf_op jit(solution)/shard_map/ppermute | solution.py:29
  164.8 17.4 %collective-permute-start.11 = (bf16[512,128]{1,0:T(8,128)(2,1)S(1)}, bf16[512,128]{1,0:T(8,128)(2,1)S(1)}, u32[]{:S(2)}, u32[]{:S(2)}) collective-permute-start(bf16[512,128]{1,0:T(8,128)(2,1)S(1)} %slice.27), channel_id=1, source_target_pairs={{0,256},{64,320},{128,384},{192,448},{256,0},{320,64},{384,128},{4... | collective-permute-start | bytes 393224 | tf_op jit(solution)/shard_map/ppermute | solution.py:29

commit v2 on v1

--- a/solution.py
+++ b/solution.py
@@ -25,6 +25,14 @@
     return lax.ppermute(value, axis, [(i, (i + step) % size) for i in range(size)])
 
 
+def climb(value, step):
+    perm = []
+    for z in range(16):
+        to = (z + step) % 16
+        perm.append((z % 8 * 2 + z // 8, to % 8 * 2 + to // 8))
+    return lax.ppermute(value, ("zl", "zh"), perm)
+
+
 def flip(value, axis, bit):
     return lax.ppermute(value, axis, [(i, i ^ bit) for i in range(AXES[axis])])
 
@@ -36,7 +44,7 @@
         in_specs=in_specs,
         out_specs=out_specs,
         scratch_shapes=list(scratch),
-        compiler_params=pltpu.CompilerParams(vmem_limit_bytes=40 * 1024 * 1024),
+        compiler_params=pltpu.CompilerParams(vmem_limit_bytes=8 * 1024 * 1024),
         cost_estimate=pl.CostEstimate(flops=flops, bytes_accessed=bytes_accessed, transcendentals=0),
     )
 
@@ -90,7 +98,7 @@
         act_ref[c, BS:] = (h * (gate * s)).astype(jnp.bfloat16)
         return carry
 
-    lax.fori_loop(0, COLS, column, 0)
+    lax.fori_loop(0, COLS, column, 0, unroll=True)
 
 
 def backward_kernel(group, dtype, x_ref, act_ref, rows_ref, table_ref, lo_ref, hi_ref):
@@ -115,13 +123,16 @@
         [pltpu.SMEM((NX * NZ,), jnp.int32)],
     )(block_owner)
     own = x_panel.T
-    far = flip(own, "zh", 1)
-    weights = jnp.concatenate(
-        [w.transpose(0, 3, 1, 2).reshape(COLS, BS, KB * BS) for w in (gate_blocks, up_blocks)], 1
-    )
-    hidden = grad_hidden.T.reshape(COLS, BS, TOK)
+    up, down = climb(own[:BS], 4), climb(own[BS:], -4)
     a = lax.all_to_all(jnp.broadcast_to(own[None], (4,) + own.shape), "y", 0, 0, tiled=True)
     ac = flip(a, "core", 1)
+    gate_t, up_t = (w.transpose(0, 3, 1, 2).reshape(COLS, BS, KB * BS) for w in (gate_blocks, up_blocks))
+    up, down, gate_t = lax.optimization_barrier((up, down, gate_t))
+    up, down = climb(up, 4), climb(down, -4)
+    weights = jnp.concatenate([gate_t, up_t], 1)
+    hidden = grad_hidden.T.reshape(COLS, BS, TOK)
+    up, down, weights, hidden, table = lax.optimization_barrier((up, down, weights, hidden, table))
+    far = jnp.concatenate([up, down], 0)
     b = lax.all_to_all(jnp.broadcast_to(far[None], (4,) + far.shape), "y", 0, 0, tiled=True)
     bc = flip(b, "core", 1)
 

time: 184 us -> 179 us (0.973)
  starting transfers between devices: 77.8 us -> 71.1 us
  waiting for transfers between devices: 67.2 us -> 71.3 us
  Pallas kernels: 18.9 us -> 16 us
  other arithmetic: 3.88 us -> 5.87 us
    ppermute x6 -> x5, starting transfers between devices: 48.5 us -> 17.4 us  [flip(): return lax.ppermute(value, axis, [(i, i ^ bit) for i in range(AXES[axis])])]
    ppermute x0 -> x4, starting transfers between devices: none -> 24.4 us  [climb(): return lax.ppermute(value, ('zl', 'zh'), perm)]
    ppermute x0 -> x4, waiting for transfers between devices: none -> 8.56 us  [climb(): return lax.ppermute(value, ('zl', 'zh'), perm)]
    ppermute x6 -> x5, waiting for transfers between devices: 41.2 us -> 34.4 us  [flip(): return lax.ppermute(value, axis, [(i, i ^ bit) for i in range(AXES[axis])])]
    pallas_call x1, Pallas kernels: 7.07 us -> 4.15 us  [body(): call(forward_kernel, (jax.ShapeDtypeStruct((ROWS, BS, TOK), bf16), jax.Sh...]
    concatenate x1 -> x2, other arithmetic: 2.43 us -> 4.42 us  [the longest x1 4.39 us: body(): weights = jnp.concatenate([gate_t, up_t], 1)]
  transfers between devices with their start and end apart: 14 -> 17, of which waited for: 8 -> 12; matrix products, arithmetic and copies ran while one was open for 7% -> 7% of each run, Pallas kernels for 5% -> 5%
where the time goes in v2:
time: 179 us
  waiting for transfers between devices  71.3 us (40%)
  starting transfers between devices  71.1 us (40%)
  Pallas kernels  16 us (9%)
  local copies, waits for them, and re-layouts  13.9 us (8%)
  other arithmetic  5.87 us (3%)
    ppermute x5, waiting for transfers between devices, flip(): return lax.ppermute(value, axis, [(i, i ^ bit) for i in range(AXES[axis])])  34.4 us
    ppermute x4, starting transfers between devices, climb(): return lax.ppermute(value, ('zl', 'zh'), perm)  24.4 us
    ppermute x6, starting transfers between devices, shift(): lax.ppermute(value, axis, [(i, (i + step) % size) for i in range(size)])  20.5 us
    ppermute x5, starting transfers between devices, flip(): return lax.ppermute(value, axis, [(i, i ^ bit) for i in range(AXES[axis])])  17.4 us
    ppermute x6, waiting for transfers between devices, shift(): lax.ppermute(value, axis, [(i, (i + step) % size) for i in range(size)])  16 us
    all_to_all x1, waiting for transfers between devices, body(): lax.all_to_all(jnp.broadcast_to(far[None], (4,) + far.shape), 'y', 0, 0,...  12.3 us
    ppermute x4, waiting for transfers between devices, climb(): return lax.ppermute(value, ('zl', 'zh'), perm)  8.56 us
    pallas_call x4, Pallas kernels, backward(): call(functools.partial(backward_kernel, group, dtype), (half, half), [VME...  8.39 us
  transfers between devices with their start and end apart: 17, of which 12 were waited for; matrix products, arithmetic and copies ran while one was open for 7% of the time, Pallas kernels for 5%

profile of v2, /device:TPU:6, one launch (start us, length us, event | category | flops | bytes accessed | tf_op | source)
XLA Modules:
  0.0 178.5 jit_solution(7205416317508175498)
XLA Ops:
  2.4 4.5 %all-to-all-start = ((bf16[4,256,512]{2,1,0:T(8,128)(2,1)}), bf16[4,256,512]{2,1,0:T(8,128)(2,1)S(1)}, u32[]{:S(2)}, u32[]{:S(2)}) async-start(bf16[4,256,512]{2,1,0:T(8,128)(2,1)} %broadcast_in_dim.4), calls=%async_computation | async-start | bytes 2097152 | tf_op jit(solution)/shard_map/all_to_all | solution.py:127
  6.9 12.7 %collective-permute-start.2 = (bf16[128,512]{0,1:T(8,128)(2,1)S(1)}, bf16[128,512]{0,1:T(8,128)(2,1)S(1)}, u32[]{:S(2)}, u32[]{:S(2)}) collective-permute-start(bf16[128,512]{0,1:T(8,128)(2,1)S(1)} %get-tuple-element.41), channel_id=1, source_target_pairs={{0,258},{64,322},{128,386},{192,450},{256,0},{320,64},{384,128},{4... | collective-permute-start | bytes 393224 | tf_op jit(solution)/shard_map/ppermute | solution.py:33
  21.5 3.5 %shard_map.64.table_ref = s32[64]{0:T(128)S(1)} custom-call(s32[7,8]{1,0:T(8,128)S(1)} %copy-done.2), custom_call_target="tpu_custom_call" | custom-call | tf_op jit(solution)/shard_map/pallas_call | solution.py:121
  25.6 3.8 %copy.12 = bf16[7,128,1024]{2,1,0:T(8,128)(2,1)} copy(bf16[7,128,1024]{1,2,0:T(8,128)(2,1)} %bitcast.11) | data formatting | bytes 3670016 | tf_op jit(solution)/shard_map/reshape | solution.py:129
  29.4 3.8 %copy.13 = bf16[7,128,1024]{2,1,0:T(8,128)(2,1)} copy(bf16[7,128,1024]{1,2,0:T(8,128)(2,1)} %bitcast.12) | data formatting | bytes 3670016 | tf_op jit(solution)/shard_map/reshape | solution.py:129
  33.8 4.9 %collective-permute-start.3 = (bf16[128,512]{0,1:T(8,128)(2,1)S(1)}, bf16[128,512]{0,1:T(8,128)(2,1)S(1)}, u32[]{:S(2)}, u32[]{:S(2)}) collective-permute-start(bf16[128,512]{0,1:T(8,128)(2,1)S(1)} %collective-permute-done.1), channel_id=1, source_target_pairs={{0,256},{64,320},{128,384},{192,448},{256,2},{320,66},{384,130},{4... | collective-permute-start | bytes 393224 | tf_op jit(solution)/shard_map/ppermute | solution.py:33
  38.7 4.8 %collective-permute-start.4 = (bf16[128,512]{0,1:T(8,128)(2,1)S(1)}, bf16[128,512]{0,1:T(8,128)(2,1)S(1)}, u32[]{:S(2)}, u32[]{:S(2)}) collective-permute-start(bf16[128,512]{0,1:T(8,128)(2,1)S(1)} %collective-permute-done.2), channel_id=1, source_target_pairs={{0,258},{64,322},{128,386},{192,450},{256,0},{320,64},{384,128},{4... | collective-permute-start | bytes 393224 | tf_op jit(solution)/shard_map/ppermute | solution.py:33
  43.5 4.4 %pad_maximum_fusion.w_ref = bf16[7,256,1024]{2,1,0:T(8,128)(2,1)} fusion(bf16[7,128,1024]{2,1,0:T(8,128)(2,1)} %copy.13, bf16[7,128,1024]{2,1,0:T(8,128)(2,1)} %copy.12), kind=kLoop, calls=%fused_computation | loop fusion | flops 7340032 | bytes 7340032 | tf_op jit(solution)/shard_map/concatenate | solution.py:132
  47.9 8.0 %collective-permute-done.4 = bf16[128,512]{0,1:T(8,128)(2,1)S(1)} collective-permute-done((bf16[128,512]{0,1:T(8,128)(2,1)S(1)}, bf16[128,512]{0,1:T(8,128)(2,1)S(1)}, u32[]{:S(2)}, u32[]{:S(2)}) %collective-permute-start.4) | collective-permute-done | bytes 131104 | tf_op jit(solution)/shard_map/ppermute | solution.py:33
  57.2 4.4 %all-to-all-start.1 = ((bf16[4,256,512]{2,1,0:T(8,128)(2,1)}), bf16[4,256,512]{2,1,0:T(8,128)(2,1)S(1)}, u32[]{:S(2)}, u32[]{:S(2)}) async-start(bf16[4,256,512]{2,1,0:T(8,128)(2,1)} %broadcast_in_dim.5), calls=%async_computation.1 | async-start | bytes 2097152 | tf_op jit(solution)/shard_map/all_to_all | solution.py:136
  63.5 12.3 %all-to-all-done.1.b_ref = bf16[4,256,512]{2,1,0:T(8,128)(2,1)S(1)} async-done(((bf16[4,256,512]{2,1,0:T(8,128)(2,1)}), bf16[4,256,512]{2,1,0:T(8,128)(2,1)S(1)}, u32[]{:S(2)}, u32[]{:S(2)}) %all-to-all-start.1) | async-done | bytes 1048608 | tf_op jit(solution)/shard_map/all_to_all | solution.py:136
  77.8 2.6 %collective-permute-done.5.bc_ref = bf16[4,256,512]{2,1,0:T(8,128)(2,1)S(1)} collective-permute-done((bf16[4,256,512]{2,1,0:T(8,128)(2,1)S(1)}, bf16[4,256,512]{2,1,0:T(8,128)(2,1)S(1)}, u32[]{:S(2)}, u32[]{:S(2)}) %collective-permute-start.5) | collective-permute-done | bytes 1048608 | tf_op jit(solution)/shard_map/ppermute | solution.py:37
  80.4 2.0 %copy-done = bf16[7,256,1024]{2,1,0:T(8,128)(2,1)S(1)} copy-done((bf16[7,256,1024]{2,1,0:T(8,128)(2,1)S(1)}, bf16[7,256,1024]{2,1,0:T(8,128)(2,1)}, u32[]{:S(2)}) %copy-start) | copy-done | bytes 3670040
  82.4 4.2 %shard_map.65 = (bf16[32,128,512]{2,1,0:T(8,128)(2,1)S(1)}, bf16[7,256,512]{2,1,0:T(8,128)(2,1)S(1)}) custom-call(bf16[4,256,512]{2,1,0:T(8,128)(2,1)S(1)} %all-to-all-done.a_ref, bf16[4,256,512]{2,1,0:T(8,128)(2,1)} %collective-permute-done.ac_ref, bf16[4,256,512]{2,1,0:T(8,128)(2,1)S(1)} %all-to-all-done.1.b_ref, ...), custom_call_target="tpu_custom_call" | custom-call | flops 1879048192 | bytes 14680064 | tf_op jit(solution)/shard_map/pallas_call | solution.py:139
  86.6 2.1 %shard_map.68 = (bf16[2048,128]{1,0:T(8,128)(2,1)S(1)}, bf16[2048,128]{1,0:T(8,128)(2,1)S(1)}) custom-call(bf16[32,128,512]{2,1,0:T(8,128)(2,1)S(1)} %get-tuple-element.30.x_ref, bf16[7,256,512]{2,1,0:T(8,128)(2,1)S(1)} %get-tuple-element.31.act_ref, s32[7,8]{1,0:T(8,128)S(1)} %copy-done.1, s32[64]{0:T(128)S(1)} %shard_map.64.table_ref), custom_call_target="tpu_custom_call" | custom-call | flops 536870912 | bytes 7340032 | tf_op jit(solution)/shard_map/pallas_call | solution.py:148
  88.7 2.7 %collective-permute-start.10 = (bf16[2048,128]{1,0:T(8,128)(2,1)S(1)}, bf16[2048,128]{1,0:T(8,128)(2,1)S(1)}, u32[]{:S(2)}, u32[]{:S(2)}) collective-permute-start(bf16[2048,128]{1,0:T(8,128)(2,1)S(1)} %get-tuple-element.40), channel_id=1, source_target_pairs={{0,48},{16,0},{32,16},{48,32},{1,49},{17,1},{33,17},{49,33},{2,50}... | collective-permute-start | bytes 1572872 | tf_op jit(solution)/shard_map/ppermute | solution.py:25
  91.4 2.1 %shard_map.69 = (bf16[2048,128]{1,0:T(8,128)(2,1)S(1)}, bf16[2048,128]{1,0:T(8,128)(2,1)S(1)}) custom-call(bf16[32,128,512]{2,1,0:T(8,128)(2,1)S(1)} %get-tuple-element.30.x_ref, bf16[7,256,512]{2,1,0:T(8,128)(2,1)S(1)} %get-tuple-element.31.act_ref, s32[7,8]{1,0:T(8,128)S(1)} %copy-done.1, s32[64]{0:T(128)S(1)} %shard_map.64.table_ref), custom_call_target="tpu_custom_call" | custom-call | flops 536870912 | bytes 7340032 | tf_op jit(solution)/shard_map/pallas_call | solution.py:148
  93.5 2.5 %collective-permute-start.8 = (bf16[2048,128]{1,0:T(8,128)(2,1)S(1)}, bf16[2048,128]{1,0:T(8,128)(2,1)S(1)}, u32[]{:S(2)}, u32[]{:S(2)}) collective-permute-start(bf16[2048,128]{1,0:T(8,128)(2,1)S(1)} %get-tuple-element.36), channel_id=1, source_target_pairs={{0,48},{16,0},{32,16},{48,32},{1,49},{17,1},{33,17},{49,33},{2,50}... | collective-permute-start | bytes 1572872 | tf_op jit(solution)/shard_map/ppermute | solution.py:25
  96.0 4.6 %collective-permute-start.6 = (bf16[2048,128]{1,0:T(8,128)(2,1)S(1)}, bf16[2048,128]{1,0:T(8,128)(2,1)S(1)}, u32[]{:S(2)}, u32[]{:S(2)}) collective-permute-start(bf16[2048,128]{1,0:T(8,128)(2,1)S(1)} %get-tuple-element.35), channel_id=1, source_target_pairs={{0,16},{16,32},{32,48},{48,0},{1,17},{17,33},{33,49},{49,1},{2,18}... | collective-permute-start | bytes 1572872 | tf_op jit(solution)/shard_map/ppermute | solution.py:25
  100.6 2.1 %shard_map.67 = (bf16[2048,128]{1,0:T(8,128)(2,1)S(1)}, bf16[2048,128]{1,0:T(8,128)(2,1)S(1)}) custom-call(bf16[32,128,512]{2,1,0:T(8,128)(2,1)S(1)} %get-tuple-element.30.x_ref, bf16[7,256,512]{2,1,0:T(8,128)(2,1)S(1)} %get-tuple-element.31.act_ref, s32[7,8]{1,0:T(8,128)S(1)} %copy-done.1, s32[64]{0:T(128)S(1)} %shard_map.64.table_ref), custom_call_target="tpu_custom_call" | custom-call | flops 536870912 | bytes 7340032 | tf_op jit(solution)/shard_map/pallas_call | solution.py:148
  102.7 3.1 %collective-permute-start.9 = (bf16[2048,128]{1,0:T(8,128)(2,1)S(1)}, bf16[2048,128]{1,0:T(8,128)(2,1)S(1)}, u32[]{:S(2)}, u32[]{:S(2)}) collective-permute-start(bf16[2048,128]{1,0:T(8,128)(2,1)S(1)} %get-tuple-element.38), channel_id=1, source_target_pairs={{0,16},{16,32},{32,48},{48,0},{1,17},{17,33},{33,49},{49,1},{2,18}... | collective-permute-start | bytes 1572872 | tf_op jit(solution)/shard_map/ppermute | solution.py:25
  108.7 2.1 %shard_map.66 = (f32[2048,128]{1,0:T(8,128)S(1)}, f32[2048,128]{1,0:T(8,128)S(1)}) custom-call(bf16[32,128,512]{2,1,0:T(8,128)(2,1)S(1)} %get-tuple-element.30.x_ref, bf16[7,256,512]{2,1,0:T(8,128)(2,1)S(1)} %get-tuple-element.31.act_ref, s32[7,8]{1,0:T(8,128)S(1)} %copy-done.1, s32[64]{0:T(128)S(1)} %shard_map.64.table_ref), custom_call_target="tpu_custom_call" | custom-call | flops 536870912 | bytes 7340032 | tf_op jit(solution)/shard_map/pallas_call | solution.py:148
  110.8 2.1 %collective-permute-done.6 = bf16[2048,128]{1,0:T(8,128)(2,1)S(1)} collective-permute-done((bf16[2048,128]{1,0:T(8,128)(2,1)S(1)}, bf16[2048,128]{1,0:T(8,128)(2,1)S(1)}, u32[]{:S(2)}, u32[]{:S(2)}) %collective-permute-start.6) | collective-permute-done | bytes 524320 | tf_op jit(solution)/shard_map/ppermute | solution.py:25
  113.1 5.6 %collective-permute-start.7 = (bf16[2048,128]{1,0:T(8,128)(2,1)S(1)}, bf16[2048,128]{1,0:T(8,128)(2,1)S(1)}, u32[]{:S(2)}, u32[]{:S(2)}) collective-permute-start(bf16[2048,128]{1,0:T(8,128)(2,1)S(1)} %add_convert_fusion.2), channel_id=1, source_target_pairs={{0,16},{16,32},{32,48},{48,0},{1,17},{17,33},{33,49},{49,1},{2,18}... | collective-permute-start | bytes 1572872 | tf_op jit(solution)/shard_map/ppermute | solution.py:25
  118.7 5.5 %collective-permute-done.9 = bf16[2048,128]{1,0:T(8,128)(2,1)S(1)} collective-permute-done((bf16[2048,128]{1,0:T(8,128)(2,1)S(1)}, bf16[2048,128]{1,0:T(8,128)(2,1)S(1)}, u32[]{:S(2)}, u32[]{:S(2)}) %collective-permute-start.9) | collective-permute-done | bytes 524320 | tf_op jit(solution)/shard_map/ppermute | solution.py:25
  124.2 4.0 %collective-permute-done.11 = bf16[2048,128]{1,0:T(8,128)(2,1)S(1)} collective-permute-done((bf16[2048,128]{1,0:T(8,128)(2,1)S(1)}, bf16[2048,128]{1,0:T(8,128)(2,1)S(1)}, u32[]{:S(2)}, u32[]{:S(2)}) %collective-permute-start.11) | collective-permute-done | bytes 524320 | tf_op jit(solution)/shard_map/ppermute | solution.py:25
  130.4 3.7 %collective-permute-done.7 = bf16[2048,128]{1,0:T(8,128)(2,1)S(1)} collective-permute-done((bf16[2048,128]{1,0:T(8,128)(2,1)S(1)}, bf16[2048,128]{1,0:T(8,128)(2,1)S(1)}, u32[]{:S(2)}, u32[]{:S(2)}) %collective-permute-start.7) | collective-permute-done | bytes 524320 | tf_op jit(solution)/shard_map/ppermute | solution.py:25
  134.0 9.4 %collective-permute-done.12 = bf16[2048,128]{1,0:T(8,128)(2,1)S(1)} collective-permute-done((bf16[2048,128]{1,0:T(8,128)(2,1)S(1)}, bf16[2048,128]{1,0:T(8,128)(2,1)S(1)}, u32[]{:S(2)}, u32[]{:S(2)}) %collective-permute-start.12) | collective-permute-done | bytes 524320 | tf_op jit(solution)/shard_map/ppermute | solution.py:37
  143.7 2.8 %collective-permute-start.13 = (bf16[1024,128]{1,0:T(8,128)(2,1)S(1)}, bf16[1024,128]{1,0:T(8,128)(2,1)S(1)}, u32[]{:S(2)}, u32[]{:S(2)}) collective-permute-start(bf16[1024,128]{1,0:T(8,128)(2,1)S(1)} %slice.36), channel_id=1, source_target_pairs={{0,128},{64,192},{128,0},{192,64},{256,384},{320,448},{384,256},{4... | collective-permute-start | bytes 786440 | tf_op jit(solution)/shard_map/ppermute | solution.py:37
  146.5 12.2 %collective-permute-done.13 = bf16[1024,128]{1,0:T(8,128)(2,1)S(1)} collective-permute-done((bf16[1024,128]{1,0:T(8,128)(2,1)S(1)}, bf16[1024,128]{1,0:T(8,128)(2,1)S(1)}, u32[]{:S(2)}, u32[]{:S(2)}) %collective-permute-start.13) | collective-permute-done | bytes 262176 | tf_op jit(solution)/shard_map/ppermute | solution.py:37
  158.8 8.9 %collective-permute-start.14 = (bf16[512,128]{1,0:T(8,128)(2,1)S(1)}, bf16[512,128]{1,0:T(8,128)(2,1)S(1)}, u32[]{:S(2)}, u32[]{:S(2)}) collective-permute-start(bf16[512,128]{1,0:T(8,128)(2,1)S(1)} %slice.37), channel_id=1, source_target_pairs={{0,256},{64,320},{128,384},{192,448},{256,0},{320,64},{384,128},{4... | collective-permute-start | bytes 393224 | tf_op jit(solution)/shard_map/ppermute | solution.py:37
  167.7 10.1 %collective-permute-done.14 = bf16[512,128]{1,0:T(8,128)(2,1)S(1)} collective-permute-done((bf16[512,128]{1,0:T(8,128)(2,1)S(1)}, bf16[512,128]{1,0:T(8,128)(2,1)S(1)}, u32[]{:S(2)}, u32[]{:S(2)}) %collective-permute-start.14) | collective-permute-done | bytes 131104 | tf_op jit(solution)/shard_map/ppermute | solution.py:37
  (36 shorter events, 16.6 us)
Async XLA Ops:
  0.0 6.8 %copy-start.3 = (bf16[512,256]{1,0:T(8,128)(2,1)S(1)}, bf16[512,256]{1,0:T(8,128)(2,1)}, u32[]{:S(2)}) copy-start(bf16[512,256]{1,0:T(8,128)(2,1)} %param.6) | copy-start | bytes 786436
  0.0 21.5 %copy-start.2 = (s32[7,8]{1,0:T(8,128)S(1)}, s32[7,8]{1,0:T(8,128)}, u32[]{:S(2)}) copy-start(s32[7,8]{1,0:T(8,128)} %owner_ref.1) | copy-start | bytes 676
  0.0 25.0 %copy-start.4 = (bf16[512,896]{1,0:T(8,128)(2,1)S(1)}, bf16[512,896]{1,0:T(8,128)(2,1)}, u32[]{:S(2)}) copy-start(bf16[512,896]{1,0:T(8,128)(2,1)} %param.7) | copy-start | bytes 2752516
  2.4 53.8 %all-to-all-start = ((bf16[4,256,512]{2,1,0:T(8,128)(2,1)}), bf16[4,256,512]{2,1,0:T(8,128)(2,1)S(1)}, u32[]{:S(2)}, u32[]{:S(2)}) async-start(bf16[4,256,512]{2,1,0:T(8,128)(2,1)} %broadcast_in_dim.4), calls=%async_computation | async-start | bytes 2097152 | tf_op jit(solution)/shard_map/all_to_all | solution.py:127
  6.9 26.4 %collective-permute-start.2 = (bf16[128,512]{0,1:T(8,128)(2,1)S(1)}, bf16[128,512]{0,1:T(8,128)(2,1)S(1)}, u32[]{:S(2)}, u32[]{:S(2)}) collective-permute-start(bf16[128,512]{0,1:T(8,128)(2,1)S(1)} %get-tuple-element.41), channel_id=1, source_target_pairs={{0,258},{64,322},{128,386},{192,450},{256,0},{320,64},{384,128},{4... | collective-permute-start | bytes 393224 | tf_op jit(solution)/shard_map/ppermute | solution.py:33
  19.6 14.2 %collective-permute-start.1 = (bf16[128,512]{0,1:T(8,128)(2,1)S(1)}, bf16[128,512]{0,1:T(8,128)(2,1)S(1)}, u32[]{:S(2)}, u32[]{:S(2)}) collective-permute-start(bf16[128,512]{0,1:T(8,128)(2,1)S(1)} %get-tuple-element.42), channel_id=1, source_target_pairs={{0,256},{64,320},{128,384},{192,448},{256,2},{320,66},{384,130},{4... | collective-permute-start | bytes 393224 | tf_op jit(solution)/shard_map/ppermute | solution.py:33
  33.8 14.1 %collective-permute-start.3 = (bf16[128,512]{0,1:T(8,128)(2,1)S(1)}, bf16[128,512]{0,1:T(8,128)(2,1)S(1)}, u32[]{:S(2)}, u32[]{:S(2)}) collective-permute-start(bf16[128,512]{0,1:T(8,128)(2,1)S(1)} %collective-permute-done.1), channel_id=1, source_target_pairs={{0,256},{64,320},{128,384},{192,448},{256,2},{320,66},{384,130},{4... | collective-permute-start | bytes 393224 | tf_op jit(solution)/shard_map/ppermute | solution.py:33
  38.7 17.2 %collective-permute-start.4 = (bf16[128,512]{0,1:T(8,128)(2,1)S(1)}, bf16[128,512]{0,1:T(8,128)(2,1)S(1)}, u32[]{:S(2)}, u32[]{:S(2)}) collective-permute-start(bf16[128,512]{0,1:T(8,128)(2,1)S(1)} %collective-permute-done.2), channel_id=1, source_target_pairs={{0,258},{64,322},{128,386},{192,450},{256,0},{320,64},{384,128},{4... | collective-permute-start | bytes 393224 | tf_op jit(solution)/shard_map/ppermute | solution.py:33
  47.9 32.5 %copy-start.1 = (s32[7,8]{1,0:T(8,128)S(1)}, s32[7,8]{1,0:T(8,128)}, u32[]{:S(2)}) copy-start(s32[7,8]{1,0:T(8,128)} %rows_ref.9) | copy-start | bytes 676
  57.2 18.6 %all-to-all-start.1 = ((bf16[4,256,512]{2,1,0:T(8,128)(2,1)}), bf16[4,256,512]{2,1,0:T(8,128)(2,1)S(1)}, u32[]{:S(2)}, u32[]{:S(2)}) async-start(bf16[4,256,512]{2,1,0:T(8,128)(2,1)} %broadcast_in_dim.5), calls=%async_computation.1 | async-start | bytes 2097152 | tf_op jit(solution)/shard_map/all_to_all | solution.py:136
  61.6 16.2 %collective-permute-start = (bf16[4,256,512]{2,1,0:T(8,128)(2,1)S(1)}, bf16[4,256,512]{2,1,0:T(8,128)(2,1)}, u32[]{:S(2)}, u32[]{:S(2)}) collective-permute-start(bf16[4,256,512]{2,1,0:T(8,128)(2,1)S(1)} %all-to-all-done.a_ref), channel_id=1, source_target_pairs={{0,1},{1,0},{2,3},{3,2},{4,5},{5,4},{6,7},{7,6},{8,9},{9,8},{10,11... | collective-permute-start | bytes 3145736 | tf_op jit(solution)/shard_map/ppermute | solution.py:37
  75.8 4.5 %collective-permute-start.5 = (bf16[4,256,512]{2,1,0:T(8,128)(2,1)S(1)}, bf16[4,256,512]{2,1,0:T(8,128)(2,1)S(1)}, u32[]{:S(2)}, u32[]{:S(2)}) collective-permute-start(bf16[4,256,512]{2,1,0:T(8,128)(2,1)S(1)} %all-to-all-done.1.b_ref), channel_id=1, source_target_pairs={{0,1},{1,0},{2,3},{3,2},{4,5},{5,4},{6,7},{7,6},{8,9},{9,8},{10,11... | collective-permute-start | bytes 3145736 | tf_op jit(solution)/shard_map/ppermute | solution.py:37
  80.4 2.0 %copy-start = (bf16[7,256,1024]{2,1,0:T(8,128)(2,1)S(1)}, bf16[7,256,1024]{2,1,0:T(8,128)(2,1)}, u32[]{:S(2)}) copy-start(bf16[7,256,1024]{2,1,0:T(8,128)(2,1)} %pad_maximum_fusion.w_ref) | copy-start | bytes 11010052
  88.7 17.9 %collective-permute-start.10 = (bf16[2048,128]{1,0:T(8,128)(2,1)S(1)}, bf16[2048,128]{1,0:T(8,128)(2,1)S(1)}, u32[]{:S(2)}, u32[]{:S(2)}) collective-permute-start(bf16[2048,128]{1,0:T(8,128)(2,1)S(1)} %get-tuple-element.40), channel_id=1, source_target_pairs={{0,48},{16,0},{32,16},{48,32},{1,49},{17,1},{33,17},{49,33},{2,50}... | collective-permute-start | bytes 1572872 | tf_op jit(solution)/shard_map/ppermute | solution.py:25
  93.5 36.8 %collective-permute-start.8 = (bf16[2048,128]{1,0:T(8,128)(2,1)S(1)}, bf16[2048,128]{1,0:T(8,128)(2,1)S(1)}, u32[]{:S(2)}, u32[]{:S(2)}) collective-permute-start(bf16[2048,128]{1,0:T(8,128)(2,1)S(1)} %get-tuple-element.36), channel_id=1, source_target_pairs={{0,48},{16,0},{32,16},{48,32},{1,49},{17,1},{33,17},{49,33},{2,50}... | collective-permute-start | bytes 1572872 | tf_op jit(solution)/shard_map/ppermute | solution.py:25
  96.0 16.9 %collective-permute-start.6 = (bf16[2048,128]{1,0:T(8,128)(2,1)S(1)}, bf16[2048,128]{1,0:T(8,128)(2,1)S(1)}, u32[]{:S(2)}, u32[]{:S(2)}) collective-permute-start(bf16[2048,128]{1,0:T(8,128)(2,1)S(1)} %get-tuple-element.35), channel_id=1, source_target_pairs={{0,16},{16,32},{32,48},{48,0},{1,17},{17,33},{33,49},{49,1},{2,18}... | collective-permute-start | bytes 1572872 | tf_op jit(solution)/shard_map/ppermute | solution.py:25
  102.7 21.5 %collective-permute-start.9 = (bf16[2048,128]{1,0:T(8,128)(2,1)S(1)}, bf16[2048,128]{1,0:T(8,128)(2,1)S(1)}, u32[]{:S(2)}, u32[]{:S(2)}) collective-permute-start(bf16[2048,128]{1,0:T(8,128)(2,1)S(1)} %get-tuple-element.38), channel_id=1, source_target_pairs={{0,16},{16,32},{32,48},{48,0},{1,17},{17,33},{33,49},{49,1},{2,18}... | collective-permute-start | bytes 1572872 | tf_op jit(solution)/shard_map/ppermute | solution.py:25
  106.7 21.5 %collective-permute-start.11 = (bf16[2048,128]{1,0:T(8,128)(2,1)S(1)}, bf16[2048,128]{1,0:T(8,128)(2,1)S(1)}, u32[]{:S(2)}, u32[]{:S(2)}) collective-permute-start(bf16[2048,128]{1,0:T(8,128)(2,1)S(1)} %add_convert_fusion.1), channel_id=1, source_target_pairs={{0,48},{16,0},{32,16},{48,32},{1,49},{17,1},{33,17},{49,33},{2,50}... | collective-permute-start | bytes 1572872 | tf_op jit(solution)/shard_map/ppermute | solution.py:25
  113.1 20.9 %collective-permute-start.7 = (bf16[2048,128]{1,0:T(8,128)(2,1)S(1)}, bf16[2048,128]{1,0:T(8,128)(2,1)S(1)}, u32[]{:S(2)}, u32[]{:S(2)}) collective-permute-start(bf16[2048,128]{1,0:T(8,128)(2,1)S(1)} %add_convert_fusion.2), channel_id=1, source_target_pairs={{0,16},{16,32},{32,48},{48,0},{1,17},{17,33},{33,49},{49,1},{2,18}... | collective-permute-start | bytes 1572872 | tf_op jit(solution)/shard_map/ppermute | solution.py:25
  128.4 15.0 %collective-permute-start.12 = (bf16[2048,128]{1,0:T(8,128)(2,1)S(1)}, bf16[2048,128]{1,0:T(8,128)(2,1)S(1)}, u32[]{:S(2)}, u32[]{:S(2)}) collective-permute-start(bf16[2048,128]{1,0:T(8,128)(2,1)S(1)} %add_convert_fusion), channel_id=1, source_target_pairs={{0,64},{64,0},{128,192},{192,128},{256,320},{320,256},{384,448},{4... | collective-permute-start | bytes 1572872 | tf_op jit(solution)/shard_map/ppermute | solution.py:37
  143.7 15.0 %collective-permute-start.13 = (bf16[1024,128]{1,0:T(8,128)(2,1)S(1)}, bf16[1024,128]{1,0:T(8,128)(2,1)S(1)}, u32[]{:S(2)}, u32[]{:S(2)}) collective-permute-start(bf16[1024,128]{1,0:T(8,128)(2,1)S(1)} %slice.36), channel_id=1, source_target_pairs={{0,128},{64,192},{128,0},{192,64},{256,384},{320,448},{384,256},{4... | collective-permute-start | bytes 786440 | tf_op jit(solution)/shard_map/ppermute | solution.py:37
  158.8 19.0 %collective-permute-start.14 = (bf16[512,128]{1,0:T(8,128)(2,1)S(1)}, bf16[512,128]{1,0:T(8,128)(2,1)S(1)}, u32[]{:S(2)}, u32[]{:S(2)}) collective-permute-start(bf16[512,128]{1,0:T(8,128)(2,1)S(1)} %slice.37), channel_id=1, source_target_pairs={{0,256},{64,320},{128,384},{192,448},{256,0},{320,64},{384,128},{4... | collective-permute-start | bytes 393224 | tf_op jit(solution)/shard_map/ppermute | solution.py:37

commit v3 on v2

v3 whole, which is shorter than its diff:
```python
import functools

import jax
import jax.numpy as jnp
from jax import lax
from jax.experimental import pallas as pl
from jax.experimental.pallas import tpu as pltpu
from jax.sharding import Mesh, PartitionSpec as P

BS = 128
KB = 8
COLS = 7
BLOCKS = COLS * KB
TOK = 512
ROWS = 32
NX, NZ, CAP = 4, 8, 2
AXES = {"zl": 8, "x": 4, "y": 4, "zh": 2, "core": 2}
VMEM = pl.BlockSpec(memory_space=pltpu.VMEM)
SMEM = pl.BlockSpec(memory_space=pltpu.SMEM)


def climb(value, step):
    perm = []
    for z in range(16):
        to = (z + step) % 16
        perm.append((z % 8 * 2 + z // 8, to % 8 * 2 + to // 8))
    return lax.ppermute(value, ("zl", "zh"), perm)


def flip(value, axis, bit):
    return lax.ppermute(value, axis, [(i, i ^ bit) for i in range(AXES[axis])])


def call(kernel, out_shape, in_specs, out_specs, scratch=(), flops=0, bytes_accessed=0):
    return pl.pallas_call(
        kernel,
        out_shape=out_shape,
        in_specs=in_specs,
        out_specs=out_specs,
        scratch_shapes=list(scratch),
        compiler_params=pltpu.CompilerParams(vmem_limit_bytes=8 * 1024 * 1024),
        cost_estimate=pl.CostEstimate(flops=flops, bytes_accessed=bytes_accessed, transcendentals=0),
    )


def table_kernel(owner_ref, table_ref, seen_ref):
    my_z = lax.axis_index("zl")

    def clear(i, carry):
        table_ref[i] = jnp.int32(-1)
        return carry

    lax.fori_loop(0, NX * NZ * CAP, clear, 0)

    def clear_seen(i, carry):
        seen_ref[i] = jnp.int32(0)
        return carry

    lax.fori_loop(0, NX * NZ, clear_seen, 0)

    def place(i, carry):
        owner = owner_ref[i // KB, i % KB]
        slot = seen_ref[owner]
        seen_ref[owner] = slot + 1
        x = owner % NX
        rel_z = (owner // NX) ^ my_z
        odd = rel_z & 1
        rest = (rel_z & 2) + (rel_z >> 2)
        first = x * NZ + odd * 4 + rest
        second = NX * NZ + (1 - odd) * (NX * 4) + x * 4 + rest
        table_ref[jnp.where(slot == 0, first, second)] = i
        return carry

    lax.fori_loop(0, BLOCKS, place, 0)


def forward_kernel(a_ref, ac_ref, b_ref, bc_ref, gate_ref, up_ref, g_ref, rows_ref, x_ref, act_ref, picked_ref):
    zh = lax.axis_index("zh")
    core = lax.axis_index("core")
    for ref, z, c in ((a_ref, zh, core), (ac_ref, zh, 1 - core), (b_ref, 1 - zh, core), (bc_ref, 1 - zh, 1 - core)):
        for y in range(4):
            at = (y * 4 + z * 2 + c) * 2
            x_ref[at] = ref[y, :BS]
            x_ref[at + 1] = ref[y, BS:]

    def column(c, carry):
        for k in range(KB):
            picked_ref[k * BS:(k + 1) * BS] = x_ref[rows_ref[c, k]]
        weights = jnp.concatenate([gate_ref[c], up_ref[c]], 0)
        pre = jnp.dot(weights, picked_ref[...], preferred_element_type=jnp.float32)
        gate, up = pre[:BS], pre[BS:]
        s = jax.nn.sigmoid(gate)
        h = g_ref[c].astype(jnp.float32)
        act_ref[c, :BS] = (h * up * (s * (1.0 + gate * (1.0 - s)))).astype(jnp.bfloat16)
        act_ref[c, BS:] = (h * (gate * s)).astype(jnp.bfloat16)
        return carry

    lax.fori_loop(0, COLS, column, 0, unroll=True)


def backward_kernel(first, count, dtype, x_ref, act_ref, rows_ref, table_ref, out_ref):
    for i in range(count):
        block = table_ref[first + i]
        at = jnp.maximum(block, 0)
        c = at // KB
        value = lax.dot_general(
            x_ref[rows_ref[c, at % KB]], act_ref[c], (((1,), (1,)), ((), ())), preferred_element_type=jnp.float32
        )
        value = jnp.where(block >= 0, value, 0.0).astype(dtype)
        out_ref[2 * i * BS:(2 * i + 1) * BS] = value[:, :BS]
        out_ref[(2 * i + 1) * BS:(2 * i + 2) * BS] = value[:, BS:]


def body(x_panel, grad_hidden, gate_blocks, up_blocks, block_rows, block_owner):
    bf16, f32 = jnp.bfloat16, jnp.float32
    table = call(
        table_kernel, jax.ShapeDtypeStruct((NX * NZ * CAP,), jnp.int32), [SMEM], SMEM,
        [pltpu.SMEM((NX * NZ,), jnp.int32)],
    )(block_owner)
    own = x_panel.T
    up, down = climb(own[:BS], 4), climb(own[BS:], -4)
    gate_t, up_t = (w.transpose(0, 3, 1, 2).reshape(COLS, BS, KB * BS) for w in (gate_blocks, up_blocks))
    hidden = grad_hidden.T.reshape(COLS, BS, TOK)
    own, gate_t = lax.optimization_barrier((own, gate_t))
    a = lax.all_to_all(jnp.broadcast_to(own[None], (4,) + own.shape), "y", 0, 0, tiled=True)
    ac = flip(a, "core", 1)
    up, down = climb(up, 4), climb(down, -4)
    up, down, up_t, hidden = lax.optimization_barrier((up, down, up_t, hidden))
    far = jnp.concatenate([up, down], 0)
    b = lax.all_to_all(jnp.broadcast_to(far[None], (4,) + far.shape), "y", 0, 0, tiled=True)
    b, table = lax.optimization_barrier((b, table))
    bc = flip(b, "core", 1)

    x_all, act = call(
        forward_kernel,
        (jax.ShapeDtypeStruct((ROWS, BS, TOK), bf16), jax.ShapeDtypeStruct((COLS, 2 * BS, TOK), bf16)),
        [VMEM] * 7 + [SMEM], (VMEM, VMEM), [pltpu.VMEM((KB * BS, TOK), bf16)],
        flops=2 * COLS * KB * BS * 2 * BS * TOK, bytes_accessed=14 * 2**20,
    )(a, ac, b, bc, gate_t, up_t, hidden, block_rows)

    def backward(first, count, dtype):
        return call(
            functools.partial(backward_kernel, first, count, dtype),
            jax.ShapeDtypeStruct((count * 2 * BS, BS), dtype), [VMEM, VMEM, SMEM, SMEM], VMEM,
            flops=2 * count * BS * 2 * BS * TOK, bytes_accessed=7 * 2**20,
        )(x_all, act, block_rows, table)

    def over_x(value):
        value = value.reshape(NX, value.shape[0] // NX, BS)
        return lax.all_to_all(value, "x", 0, 0, tiled=True)

    def halve(keep, bit):
        half = keep.shape[0] // 2
        got = flip(keep[half:].astype(bf16), "zl", bit)
        return keep[:half] + got.astype(f32)

    got = flip(backward(NX * NZ, NX * 4, bf16), "zl", 1)
    first = over_x(backward(0, NX * NZ, bf16))
    second = (backward(NX * NZ + NX * 4, NX * 4, f32) + got.astype(f32)).astype(bf16)
    first, second = lax.optimization_barrier((first, second))
    second = over_x(second)
    half = first.shape[1] // 2
    got = flip(jnp.sum(first[:, half:].astype(f32), 0).astype(bf16), "zl", 1)
    first = jnp.sum(first[:, :half].astype(f32), 0) + got.astype(f32)
    first = halve(halve(first, 2), 4)
    second = halve(halve(jnp.sum(second.astype(f32), 0), 2), 4)
    return jnp.concatenate([first, second], 0).reshape(1, 1, CAP, 2, BS, BS)


def solution(mesh):
    fine = Mesh(mesh.devices.reshape(tuple(AXES.values())), tuple(AXES))
    dp, tensor = ("zl", "x"), ("y", "zh", "core")
    in_specs = (
        P(dp, tensor),
        P(dp, tensor),
        P(tensor, None, None, None),
        P(tensor, None, None, None),
        P(tensor, None),
        P(tensor, None),
    )
    out_specs = P(tensor, dp, None, None, None, None)
    return jax.shard_map(body, mesh=fine, in_specs=in_specs, out_specs=out_specs, check_vma=False)
```

time: 179 us -> 180 us (level)
  waiting for transfers between devices: 71.3 us -> 63.9 us
  local copies, waits for them, and re-layouts: 13.9 us -> 21.2 us
    ppermute x6 -> x0, starting transfers between devices: 20.5 us -> none  [shift(): lax.ppermute(value, axis, [(i, (i + step) % size) for i in range(size)])]
    ppermute x6 -> x0, waiting for transfers between devices: 16 us -> none  [shift(): lax.ppermute(value, axis, [(i, (i + step) % size) for i in range(size)])]
    all_to_all x0 -> x2, starting transfers between devices: none -> 10.6 us  [over_x(): return lax.all_to_all(value, 'x', 0, 0, tiled=True)]
    ppermute x4, waiting for transfers between devices: 8.56 us -> 18.6 us  [climb(): return lax.ppermute(value, ('zl', 'zh'), perm)]
    ppermute x5 -> x8, starting transfers between devices: 17.4 us -> 25.9 us  [flip(): return lax.ppermute(value, axis, [(i, i ^ bit) for i in range(AXES[axis])])]
    unnamed x10 -> x24, local copies, waits for them, and re-layouts: 2.05 us -> 9.97 us
    all_to_all x0 -> x2, waiting for transfers between devices: none -> 7.07 us  [over_x(): return lax.all_to_all(value, 'x', 0, 0, tiled=True)]
    ppermute x5 -> x8, waiting for transfers between devices: 34.4 us -> 28.4 us  [flip(): return lax.ppermute(value, axis, [(i, i ^ bit) for i in range(AXES[axis])])]
  transfers between devices with their start and end apart: 17 -> 16, of which waited for: 12 -> 10; matrix products, arithmetic and copies ran while one was open for 7% -> 6% of each run, Pallas kernels for 5% -> 5%
where the time goes in v3:
time: 180 us; the launch traced here: 179 us
  starting transfers between devices  71.8 us (40%)
  waiting for transfers between devices  63.9 us (36%)
  local copies, waits for them, and re-layouts  21.2 us (12%)
  Pallas kernels  15.2 us (8%)
  other arithmetic  6.25 us (3%)
    ppermute x8, waiting for transfers between devices, flip(): return lax.ppermute(value, axis, [(i, i ^ bit) for i in range(AXES[axis])])  28.4 us
    ppermute x4, starting transfers between devices, climb(): return lax.ppermute(value, ('zl', 'zh'), perm)  26.2 us
    ppermute x8, starting transfers between devices, flip(): return lax.ppermute(value, axis, [(i, i ^ bit) for i in range(AXES[axis])])  25.9 us
    ppermute x4, waiting for transfers between devices, climb(): return lax.ppermute(value, ('zl', 'zh'), perm)  18.6 us
    all_to_all x2, starting transfers between devices, over_x(): return lax.all_to_all(value, 'x', 0, 0, tiled=True)  10.6 us
    unnamed x24, local copies, waits for them, and re-layouts  9.97 us
    all_to_all x1, waiting for transfers between devices, body(): lax.all_to_all(jnp.broadcast_to(far[None], (4,) + far.shape), 'y', 0, 0,...  9.86 us
    pallas_call x3, Pallas kernels, backward(): call(functools.partial(backward_kernel, first, count, dtype), jax.ShapeDt...  7.64 us
  transfers between devices with their start and end apart: 16, of which 10 were waited for; matrix products, arithmetic and copies ran while one was open for 6% of the time, Pallas kernels for 5%

profile of v3, /device:TPU:6, one launch (start us, length us, event | category | flops | bytes accessed | tf_op | source)
XLA Modules:
  0.0 178.7 jit_solution(9106327044577901345)
XLA Ops:
  0.0 3.9 %copy.12.gate_ref = bf16[7,128,1024]{2,1,0:T(8,128)(2,1)} copy(bf16[7,128,1024]{1,2,0:T(8,128)(2,1)} %bitcast.14) | data formatting | bytes 3670016 | tf_op jit(solution)/shard_map/reshape | solution.py:122
  5.1 4.6 %all-to-all-start = ((bf16[4,256,512]{2,1,0:T(8,128)(2,1)}), bf16[4,256,512]{2,1,0:T(8,128)(2,1)S(1)}, u32[]{:S(2)}, u32[]{:S(2)}) async-start(bf16[4,256,512]{2,1,0:T(8,128)(2,1)} %broadcast_in_dim.4), calls=%async_computation | async-start | bytes 2097152 | tf_op jit(solution)/shard_map/all_to_all | solution.py:125
  9.7 12.7 %collective-permute-start.3 = (bf16[128,512]{0,1:T(8,128)(2,1)S(1)}, bf16[128,512]{0,1:T(8,128)(2,1)S(1)}, u32[]{:S(2)}, u32[]{:S(2)}) collective-permute-start(bf16[128,512]{0,1:T(8,128)(2,1)S(1)} %get-tuple-element.29), channel_id=1, source_target_pairs={{0,258},{64,322},{128,386},{192,450},{256,0},{320,64},{384,128},{4... | collective-permute-start | bytes 393224 | tf_op jit(solution)/shard_map/ppermute | solution.py:27
  22.4 1.9 %collective-permute-start.1 = (bf16[128,512]{0,1:T(8,128)(2,1)S(1)}, bf16[128,512]{0,1:T(8,128)(2,1)S(1)}, u32[]{:S(2)}, u32[]{:S(2)}) collective-permute-start(bf16[128,512]{0,1:T(8,128)(2,1)S(1)} %get-tuple-element.30), channel_id=1, source_target_pairs={{0,256},{64,320},{128,384},{192,448},{256,2},{320,66},{384,130},{4... | collective-permute-start | bytes 393224 | tf_op jit(solution)/shard_map/ppermute | solution.py:27
  24.4 9.0 %collective-permute-done.3 = bf16[128,512]{0,1:T(8,128)(2,1)S(1)} collective-permute-done((bf16[128,512]{0,1:T(8,128)(2,1)S(1)}, bf16[128,512]{0,1:T(8,128)(2,1)S(1)}, u32[]{:S(2)}, u32[]{:S(2)}) %collective-permute-start.3) | collective-permute-done | bytes 131104 | tf_op jit(solution)/shard_map/ppermute | solution.py:27
  33.4 9.7 %collective-permute-start.4 = (bf16[128,512]{0,1:T(8,128)(2,1)S(1)}, bf16[128,512]{0,1:T(8,128)(2,1)S(1)}, u32[]{:S(2)}, u32[]{:S(2)}) collective-permute-start(bf16[128,512]{0,1:T(8,128)(2,1)S(1)} %collective-permute-done.3), channel_id=1, source_target_pairs={{0,258},{64,322},{128,386},{192,450},{256,0},{320,64},{384,128},{4... | collective-permute-start | bytes 393224 | tf_op jit(solution)/shard_map/ppermute | solution.py:27
  45.0 2.2 %copy.10 = bf16[896,512]{1,0:T(8,128)(2,1)} copy(bf16[896,512]{0,1:T(8,128)(2,1)} %bitcast.18) | data formatting | bytes 1835008 | tf_op jit(solution)/shard_map/transpose | solution.py:123
  47.2 2.6 %copy.13.up_ref = bf16[7,128,1024]{2,1,0:T(8,128)(2,1)} copy(bf16[7,128,1024]{1,2,0:T(8,128)(2,1)S(1)} %bitcast.15) | data formatting | bytes 3670016 | tf_op jit(solution)/shard_map/reshape | solution.py:122
  49.9 9.6 %collective-permute-done.2 = bf16[128,512]{0,1:T(8,128)(2,1)S(1)} collective-permute-done((bf16[128,512]{0,1:T(8,128)(2,1)S(1)}, bf16[128,512]{0,1:T(8,128)(2,1)S(1)}, u32[]{:S(2)}, u32[]{:S(2)}) %collective-permute-start.2) | collective-permute-done | bytes 131104 | tf_op jit(solution)/shard_map/ppermute | solution.py:27
  60.7 4.5 %all-to-all-start.1 = ((bf16[4,256,512]{2,1,0:T(8,128)(2,1)}), bf16[4,256,512]{2,1,0:T(8,128)(2,1)S(1)}, u32[]{:S(2)}, u32[]{:S(2)}) async-start(bf16[4,256,512]{2,1,0:T(8,128)(2,1)} %broadcast_in_dim.5), calls=%async_computation.1 | async-start | bytes 2097152 | tf_op jit(solution)/shard_map/all_to_all | solution.py:130
  65.2 3.5 %shard_map.64.table_ref = s32[64]{0:T(128)S(1)} custom-call(s32[7,8]{1,0:T(8,128)S(1)} %copy-done.9), custom_call_target="tpu_custom_call" | custom-call | tf_op jit(solution)/shard_map/pallas_call | solution.py:116
  68.7 1.9 %collective-permute-start = (bf16[4,256,512]{2,1,0:T(8,128)(2,1)S(1)}, bf16[4,256,512]{2,1,0:T(8,128)(2,1)}, u32[]{:S(2)}, u32[]{:S(2)}) collective-permute-start(bf16[4,256,512]{2,1,0:T(8,128)(2,1)S(1)} %all-to-all-done.a_ref), channel_id=1, source_target_pairs={{0,1},{1,0},{2,3},{3,2},{4,5},{5,4},{6,7},{7,6},{8,9},{9,8},{10,11... | collective-permute-start | bytes 3145736 | tf_op jit(solution)/shard_map/ppermute | solution.py:31
  70.7 9.9 %all-to-all-done.1.b_ref = bf16[4,256,512]{2,1,0:T(8,128)(2,1)S(1)} async-done(((bf16[4,256,512]{2,1,0:T(8,128)(2,1)}), bf16[4,256,512]{2,1,0:T(8,128)(2,1)S(1)}, u32[]{:S(2)}, u32[]{:S(2)}) %all-to-all-start.1) | async-done | bytes 1048608 | tf_op jit(solution)/shard_map/all_to_all | solution.py:130
  90.5 4.1 %shard_map.65 = (bf16[32,128,512]{2,1,0:T(8,128)(2,1)S(1)}, bf16[7,256,512]{2,1,0:T(8,128)(2,1)S(1)}) custom-call(bf16[4,256,512]{2,1,0:T(8,128)(2,1)S(1)} %all-to-all-done.a_ref, bf16[4,256,512]{2,1,0:T(8,128)(2,1)} %collective-permute-done.ac_ref, bf16[4,256,512]{2,1,0:T(8,128)(2,1)S(1)} %copy-done.6, ...), custom_call_target="tpu_custom_call" | custom-call | flops 1879048192 | bytes 14680064 | tf_op jit(solution)/shard_map/pallas_call | solution.py:134
  94.6 2.1 %shard_map.68 = bf16[4096,128]{1,0:T(8,128)(2,1)S(1)} custom-call(bf16[32,128,512]{2,1,0:T(8,128)(2,1)S(1)} %get-tuple-element.24.x_ref, bf16[7,256,512]{2,1,0:T(8,128)(2,1)S(1)} %get-tuple-element.25.act_ref, s32[7,8]{1,0:T(8,128)S(1)} %copy-done.8, s32[64]{0:T(128)S(1)} %shard_map.64.table_ref), custom_call_target="tpu_custom_call" | custom-call | flops 536870912 | bytes 7340032 | tf_op jit(solution)/shard_map/pallas_call | solution.py:142
  96.7 1.9 %collective-permute-start.6 = (bf16[4096,128]{1,0:T(8,128)(2,1)S(1)}, bf16[4096,128]{1,0:T(8,128)(2,1)}, u32[]{:S(2)}, u32[]{:S(2)}) collective-permute-start(bf16[4096,128]{1,0:T(8,128)(2,1)S(1)} %shard_map.68), channel_id=1, source_target_pairs={{0,64},{64,0},{128,192},{192,128},{256,320},{320,256},{384,448},{4... | collective-permute-start | bytes 3145736 | tf_op jit(solution)/shard_map/ppermute | solution.py:31
  98.6 3.4 %shard_map.66 = bf16[8192,128]{1,0:T(8,128)(2,1)S(1)} custom-call(bf16[32,128,512]{2,1,0:T(8,128)(2,1)S(1)} %get-tuple-element.24.x_ref, bf16[7,256,512]{2,1,0:T(8,128)(2,1)S(1)} %get-tuple-element.25.act_ref, s32[7,8]{1,0:T(8,128)S(1)} %copy-done.8, s32[64]{0:T(128)S(1)} %shard_map.64.table_ref), custom_call_target="tpu_custom_call" | custom-call | flops 1073741824 | bytes 7340032 | tf_op jit(solution)/shard_map/pallas_call | solution.py:142
  103.5 5.0 %all-to-all-start.2 = ((bf16[4,2048,128]{2,1,0:T(8,128)(2,1)}), bf16[4,2048,128]{2,1,0:T(8,128)(2,1)}, u32[]{:S(2)}, u32[]{:S(2)}) async-start(bf16[4,2048,128]{2,1,0:T(8,128)(2,1)} %bitcast.12), calls=%async_computation.2 | async-start | bytes 4194304 | tf_op jit(solution)/shard_map/all_to_all | solution.py:150
  108.5 2.2 %copy-done.1 = bf16[32,128,512]{2,1,0:T(8,128)(2,1)S(1)} copy-done((bf16[32,128,512]{2,1,0:T(8,128)(2,1)S(1)}, bf16[32,128,512]{2,1,0:T(8,128)(2,1)}, u32[]{:S(2)}) %copy-start.1) | copy-done | bytes 4194328
  110.7 2.1 %shard_map.67 = f32[4096,128]{1,0:T(8,128)S(1)} custom-call(bf16[32,128,512]{2,1,0:T(8,128)(2,1)S(1)} %copy-done.1, bf16[7,256,512]{2,1,0:T(8,128)(2,1)S(1)} %get-tuple-element.25.act_ref, s32[7,8]{1,0:T(8,128)S(1)} %copy-done.8, s32[64]{0:T(128)S(1)} %shard_map.64.table_ref), custom_call_target="tpu_custom_call" | custom-call | flops 536870912 | bytes 7340032 | tf_op jit(solution)/shard_map/pallas_call | solution.py:142
  112.8 11.1 %collective-permute-done.6 = bf16[4096,128]{1,0:T(8,128)(2,1)} collective-permute-done((bf16[4096,128]{1,0:T(8,128)(2,1)S(1)}, bf16[4096,128]{1,0:T(8,128)(2,1)}, u32[]{:S(2)}, u32[]{:S(2)}) %collective-permute-start.6) | collective-permute-done | bytes 1048608 | tf_op jit(solution)/shard_map/ppermute | solution.py:31
  123.9 2.4 %add_convert_fusion = bf16[4096,128]{1,0:T(8,128)(2,1)} fusion(f32[4096,128]{1,0:T(8,128)S(1)} %shard_map.67, bf16[4096,128]{1,0:T(8,128)(2,1)} %collective-permute-done.6), kind=kLoop, calls=%fused_computation.2 | loop fusion | flops 1572864 | bytes 4194304 | tf_op jit(solution)/shard_map/convert_element_type | solution.py:159
  126.3 7.1 %all-to-all-done.2 = bf16[4,2048,128]{2,1,0:T(8,128)(2,1)} async-done(((bf16[4,2048,128]{2,1,0:T(8,128)(2,1)}), bf16[4,2048,128]{2,1,0:T(8,128)(2,1)}, u32[]{:S(2)}, u32[]{:S(2)}) %all-to-all-start.2) | async-done | bytes 2097184 | tf_op jit(solution)/shard_map/all_to_all | solution.py:150
  133.4 5.6 %all-to-all-start.3 = ((bf16[4,1024,128]{2,1,0:T(8,128)(2,1)}), bf16[4,1024,128]{2,1,0:T(8,128)(2,1)S(1)}, u32[]{:S(2)}, u32[]{:S(2)}) async-start(bf16[4,1024,128]{2,1,0:T(8,128)(2,1)} %bitcast.8), calls=%async_computation.3 | async-start | bytes 2097152 | tf_op jit(solution)/shard_map/all_to_all | solution.py:150
  140.3 3.6 %collective-permute-start.7 = (bf16[1024,128]{1,0:T(8,128)(2,1)S(1)}, bf16[1024,128]{1,0:T(8,128)(2,1)S(1)}, u32[]{:S(2)}, u32[]{:S(2)}) collective-permute-start(bf16[1024,128]{1,0:T(8,128)(2,1)S(1)} %slice_reduce_fusion), channel_id=1, source_target_pairs={{0,64},{64,0},{128,192},{192,128},{256,320},{320,256},{384,448},{4... | collective-permute-start | bytes 786440 | tf_op jit(solution)/shard_map/ppermute | solution.py:31
  145.4 4.0 %collective-permute-done.7 = bf16[1024,128]{1,0:T(8,128)(2,1)S(1)} collective-permute-done((bf16[1024,128]{1,0:T(8,128)(2,1)S(1)}, bf16[1024,128]{1,0:T(8,128)(2,1)S(1)}, u32[]{:S(2)}, u32[]{:S(2)}) %collective-permute-start.7) | collective-permute-done | bytes 262176 | tf_op jit(solution)/shard_map/ppermute | solution.py:31
  149.5 2.8 %collective-permute-start.8 = (bf16[512,128]{1,0:T(8,128)(2,1)S(1)}, bf16[512,128]{1,0:T(8,128)(2,1)S(1)}, u32[]{:S(2)}, u32[]{:S(2)}) collective-permute-start(bf16[512,128]{1,0:T(8,128)(2,1)S(1)} %slice.73), channel_id=1, source_target_pairs={{0,128},{64,192},{128,0},{192,64},{256,384},{320,448},{384,256},{4... | collective-permute-start | bytes 393224 | tf_op jit(solution)/shard_map/ppermute | solution.py:31
  152.5 3.9 %collective-permute-start.10 = (bf16[512,128]{1,0:T(8,128)(2,1)S(1)}, bf16[512,128]{1,0:T(8,128)(2,1)S(1)}, u32[]{:S(2)}, u32[]{:S(2)}) collective-permute-start(bf16[512,128]{1,0:T(8,128)(2,1)S(1)} %slice.72), channel_id=1, source_target_pairs={{0,128},{64,192},{128,0},{192,64},{256,384},{320,448},{384,256},{4... | collective-permute-start | bytes 393224 | tf_op jit(solution)/shard_map/ppermute | solution.py:31
  156.5 6.4 %collective-permute-done.8 = bf16[512,128]{1,0:T(8,128)(2,1)S(1)} collective-permute-done((bf16[512,128]{1,0:T(8,128)(2,1)S(1)}, bf16[512,128]{1,0:T(8,128)(2,1)S(1)}, u32[]{:S(2)}, u32[]{:S(2)}) %collective-permute-start.8) | collective-permute-done | bytes 131104 | tf_op jit(solution)/shard_map/ppermute | solution.py:31
  162.9 1.9 %collective-permute-start.9 = (bf16[256,128]{1,0:T(8,128)(2,1)S(1)}, bf16[256,128]{1,0:T(8,128)(2,1)S(1)}, u32[]{:S(2)}, u32[]{:S(2)}) collective-permute-start(bf16[256,128]{1,0:T(8,128)(2,1)S(1)} %slice.75), channel_id=1, source_target_pairs={{0,256},{64,320},{128,384},{192,448},{256,0},{320,64},{384,128},{4... | collective-permute-start | bytes 196616 | tf_op jit(solution)/shard_map/ppermute | solution.py:31
  164.9 7.8 %collective-permute-start.11 = (bf16[256,128]{1,0:T(8,128)(2,1)S(1)}, bf16[256,128]{1,0:T(8,128)(2,1)S(1)}, u32[]{:S(2)}, u32[]{:S(2)}) collective-permute-start(bf16[256,128]{1,0:T(8,128)(2,1)S(1)} %slice.74), channel_id=1, source_target_pairs={{0,256},{64,320},{128,384},{192,448},{256,0},{320,64},{384,128},{4... | collective-permute-start | bytes 196616 | tf_op jit(solution)/shard_map/ppermute | solution.py:31
  172.7 4.5 %collective-permute-done.9 = bf16[256,128]{1,0:T(8,128)(2,1)S(1)} collective-permute-done((bf16[256,128]{1,0:T(8,128)(2,1)S(1)}, bf16[256,128]{1,0:T(8,128)(2,1)S(1)}, u32[]{:S(2)}, u32[]{:S(2)}) %collective-permute-start.9) | collective-permute-done | bytes 65568 | tf_op jit(solution)/shard_map/ppermute | solution.py:31
  (52 shorter events, 20.2 us)
Async XLA Ops:
  0.0 3.9 %copy-start.11 = (bf16[512,256]{1,0:T(8,128)(2,1)S(1)}, bf16[512,256]{1,0:T(8,128)(2,1)}, u32[]{:S(2)}) copy-start(bf16[512,256]{1,0:T(8,128)(2,1)} %param.6) | copy-start | bytes 786436
  5.1 42.2 %copy-start.10 = (bf16[7,8,128,128]{3,2,1,0:T(8,128)(2,1)S(1)}, bf16[7,8,128,128]{3,2,1,0:T(8,128)(2,1)}, u32[]{:S(2)}) copy-start(bf16[7,8,128,128]{3,2,1,0:T(8,128)(2,1)} %param.9) | copy-start | bytes 5505028
  5.1 54.6 %all-to-all-start = ((bf16[4,256,512]{2,1,0:T(8,128)(2,1)}), bf16[4,256,512]{2,1,0:T(8,128)(2,1)S(1)}, u32[]{:S(2)}, u32[]{:S(2)}) async-start(bf16[4,256,512]{2,1,0:T(8,128)(2,1)} %broadcast_in_dim.4), calls=%async_computation | async-start | bytes 2097152 | tf_op jit(solution)/shard_map/all_to_all | solution.py:125
  9.7 23.7 %collective-permute-start.3 = (bf16[128,512]{0,1:T(8,128)(2,1)S(1)}, bf16[128,512]{0,1:T(8,128)(2,1)S(1)}, u32[]{:S(2)}, u32[]{:S(2)}) collective-permute-start(bf16[128,512]{0,1:T(8,128)(2,1)S(1)} %get-tuple-element.29), channel_id=1, source_target_pairs={{0,258},{64,322},{128,386},{192,450},{256,0},{320,64},{384,128},{4... | collective-permute-start | bytes 393224 | tf_op jit(solution)/shard_map/ppermute | solution.py:27
  22.4 20.6 %collective-permute-start.1 = (bf16[128,512]{0,1:T(8,128)(2,1)S(1)}, bf16[128,512]{0,1:T(8,128)(2,1)S(1)}, u32[]{:S(2)}, u32[]{:S(2)}) collective-permute-start(bf16[128,512]{0,1:T(8,128)(2,1)S(1)} %get-tuple-element.30), channel_id=1, source_target_pairs={{0,256},{64,320},{128,384},{192,448},{256,2},{320,66},{384,130},{4... | collective-permute-start | bytes 393224 | tf_op jit(solution)/shard_map/ppermute | solution.py:27
  33.4 16.5 %collective-permute-start.4 = (bf16[128,512]{0,1:T(8,128)(2,1)S(1)}, bf16[128,512]{0,1:T(8,128)(2,1)S(1)}, u32[]{:S(2)}, u32[]{:S(2)}) collective-permute-start(bf16[128,512]{0,1:T(8,128)(2,1)S(1)} %collective-permute-done.3), channel_id=1, source_target_pairs={{0,258},{64,322},{128,386},{192,450},{256,0},{320,64},{384,128},{4... | collective-permute-start | bytes 393224 | tf_op jit(solution)/shard_map/ppermute | solution.py:27
  43.1 16.4 %collective-permute-start.2 = (bf16[128,512]{0,1:T(8,128)(2,1)S(1)}, bf16[128,512]{0,1:T(8,128)(2,1)S(1)}, u32[]{:S(2)}, u32[]{:S(2)}) collective-permute-start(bf16[128,512]{0,1:T(8,128)(2,1)S(1)} %collective-permute-done.1), channel_id=1, source_target_pairs={{0,256},{64,320},{128,384},{192,448},{256,2},{320,66},{384,130},{4... | collective-permute-start | bytes 393224 | tf_op jit(solution)/shard_map/ppermute | solution.py:27
  59.5 5.8 %copy-start.9 = (s32[7,8]{1,0:T(8,128)S(1)}, s32[7,8]{1,0:T(8,128)}, u32[]{:S(2)}) copy-start(s32[7,8]{1,0:T(8,128)} %owner_ref.1) | copy-start | bytes 676
  59.5 25.6 %copy-start.8 = (s32[7,8]{1,0:T(8,128)S(1)}, s32[7,8]{1,0:T(8,128)}, u32[]{:S(2)}) copy-start(s32[7,8]{1,0:T(8,128)} %rows_ref.7) | copy-start | bytes 676
  60.7 19.8 %all-to-all-start.1 = ((bf16[4,256,512]{2,1,0:T(8,128)(2,1)}), bf16[4,256,512]{2,1,0:T(8,128)(2,1)S(1)}, u32[]{:S(2)}, u32[]{:S(2)}) async-start(bf16[4,256,512]{2,1,0:T(8,128)(2,1)} %broadcast_in_dim.5), calls=%async_computation.1 | async-start | bytes 2097152 | tf_op jit(solution)/shard_map/all_to_all | solution.py:130
  68.7 14.7 %collective-permute-start = (bf16[4,256,512]{2,1,0:T(8,128)(2,1)S(1)}, bf16[4,256,512]{2,1,0:T(8,128)(2,1)}, u32[]{:S(2)}, u32[]{:S(2)}) collective-permute-start(bf16[4,256,512]{2,1,0:T(8,128)(2,1)S(1)} %all-to-all-done.a_ref), channel_id=1, source_target_pairs={{0,1},{1,0},{2,3},{3,2},{4,5},{5,4},{6,7},{7,6},{8,9},{9,8},{10,11... | collective-permute-start | bytes 3145736 | tf_op jit(solution)/shard_map/ppermute | solution.py:31
  80.5 4.5 %collective-permute-start.5 = (bf16[4,256,512]{2,1,0:T(8,128)(2,1)S(1)}, bf16[4,256,512]{2,1,0:T(8,128)(2,1)S(1)}, u32[]{:S(2)}, u32[]{:S(2)}) collective-permute-start(bf16[4,256,512]{2,1,0:T(8,128)(2,1)S(1)} %all-to-all-done.1.b_ref), channel_id=1, source_target_pairs={{0,1},{1,0},{2,3},{3,2},{4,5},{5,4},{6,7},{7,6},{8,9},{9,8},{10,11... | collective-permute-start | bytes 3145736 | tf_op jit(solution)/shard_map/ppermute | solution.py:31
  82.4 1.0 copy-start.5
  85.1 1.5 copy-start.3
  86.6 1.5 copy-start.4
  88.1 1.2 copy-start.6
  89.3 1.2 copy-start.7
  94.6 4.0 %copy-start = (bf16[32,128,512]{2,1,0:T(8,128)(2,1)}, bf16[32,128,512]{2,1,0:T(8,128)(2,1)S(1)}, u32[]{:S(2)}) copy-start(bf16[32,128,512]{2,1,0:T(8,128)(2,1)S(1)} %get-tuple-element.24.x_ref) | copy-start | bytes 12582916
  96.7 27.2 %collective-permute-start.6 = (bf16[4096,128]{1,0:T(8,128)(2,1)S(1)}, bf16[4096,128]{1,0:T(8,128)(2,1)}, u32[]{:S(2)}, u32[]{:S(2)}) collective-permute-start(bf16[4096,128]{1,0:T(8,128)(2,1)S(1)} %shard_map.68), channel_id=1, source_target_pairs={{0,64},{64,0},{128,192},{192,128},{256,320},{320,256},{384,448},{4... | collective-permute-start | bytes 3145736 | tf_op jit(solution)/shard_map/ppermute | solution.py:31
  102.1 1.4 copy-start.2
  103.5 29.9 %all-to-all-start.2 = ((bf16[4,2048,128]{2,1,0:T(8,128)(2,1)}), bf16[4,2048,128]{2,1,0:T(8,128)(2,1)}, u32[]{:S(2)}, u32[]{:S(2)}) async-start(bf16[4,2048,128]{2,1,0:T(8,128)(2,1)} %bitcast.12), calls=%async_computation.2 | async-start | bytes 4194304 | tf_op jit(solution)/shard_map/all_to_all | solution.py:150
  108.5 2.2 %copy-start.1 = (bf16[32,128,512]{2,1,0:T(8,128)(2,1)S(1)}, bf16[32,128,512]{2,1,0:T(8,128)(2,1)}, u32[]{:S(2)}) copy-start(bf16[32,128,512]{2,1,0:T(8,128)(2,1)} %copy-done) | copy-start | bytes 12582916
  133.4 18.9 %all-to-all-start.3 = ((bf16[4,1024,128]{2,1,0:T(8,128)(2,1)}), bf16[4,1024,128]{2,1,0:T(8,128)(2,1)S(1)}, u32[]{:S(2)}, u32[]{:S(2)}) async-start(bf16[4,1024,128]{2,1,0:T(8,128)(2,1)} %bitcast.8), calls=%async_computation.3 | async-start | bytes 2097152 | tf_op jit(solution)/shard_map/all_to_all | solution.py:150
  140.3 9.1 %collective-permute-start.7 = (bf16[1024,128]{1,0:T(8,128)(2,1)S(1)}, bf16[1024,128]{1,0:T(8,128)(2,1)S(1)}, u32[]{:S(2)}, u32[]{:S(2)}) collective-permute-start(bf16[1024,128]{1,0:T(8,128)(2,1)S(1)} %slice_reduce_fusion), channel_id=1, source_target_pairs={{0,64},{64,0},{128,192},{192,128},{256,320},{320,256},{384,448},{4... | collective-permute-start | bytes 786440 | tf_op jit(solution)/shard_map/ppermute | solution.py:31
  149.5 13.3 %collective-permute-start.8 = (bf16[512,128]{1,0:T(8,128)(2,1)S(1)}, bf16[512,128]{1,0:T(8,128)(2,1)S(1)}, u32[]{:S(2)}, u32[]{:S(2)}) collective-permute-start(bf16[512,128]{1,0:T(8,128)(2,1)S(1)} %slice.73), channel_id=1, source_target_pairs={{0,128},{64,192},{128,0},{192,64},{256,384},{320,448},{384,256},{4... | collective-permute-start | bytes 393224 | tf_op jit(solution)/shard_map/ppermute | solution.py:31
  152.5 12.3 %collective-permute-start.10 = (bf16[512,128]{1,0:T(8,128)(2,1)S(1)}, bf16[512,128]{1,0:T(8,128)(2,1)S(1)}, u32[]{:S(2)}, u32[]{:S(2)}) collective-permute-start(bf16[512,128]{1,0:T(8,128)(2,1)S(1)} %slice.72), channel_id=1, source_target_pairs={{0,128},{64,192},{128,0},{192,64},{256,384},{320,448},{384,256},{4... | collective-permute-start | bytes 393224 | tf_op jit(solution)/shard_map/ppermute | solution.py:31
  162.9 14.4 %collective-permute-start.9 = (bf16[256,128]{1,0:T(8,128)(2,1)S(1)}, bf16[256,128]{1,0:T(8,128)(2,1)S(1)}, u32[]{:S(2)}, u32[]{:S(2)}) collective-permute-start(bf16[256,128]{1,0:T(8,128)(2,1)S(1)} %slice.75), channel_id=1, source_target_pairs={{0,256},{64,320},{128,384},{192,448},{256,0},{320,64},{384,128},{4... | collective-permute-start | bytes 196616 | tf_op jit(solution)/shard_map/ppermute | solution.py:31
  164.9 13.1 %collective-permute-start.11 = (bf16[256,128]{1,0:T(8,128)(2,1)S(1)}, bf16[256,128]{1,0:T(8,128)(2,1)S(1)}, u32[]{:S(2)}, u32[]{:S(2)}) collective-permute-start(bf16[256,128]{1,0:T(8,128)(2,1)S(1)} %slice.74), channel_id=1, source_target_pairs={{0,256},{64,320},{128,384},{192,448},{256,0},{320,64},{384,128},{4... | collective-permute-start | bytes 196616 | tf_op jit(solution)/shard_map/ppermute | solution.py:31

commit v4 on v3

--- a/solution.py
+++ b/solution.py
@@ -15,16 +15,15 @@
 ROWS = 32
 NX, NZ, CAP = 4, 8, 2
 AXES = {"zl": 8, "x": 4, "y": 4, "zh": 2, "core": 2}
+Y_STEPS = (0, 1, -1, 2)
 VMEM = pl.BlockSpec(memory_space=pltpu.VMEM)
+ANY = pl.BlockSpec(memory_space=pl.ANY)
 SMEM = pl.BlockSpec(memory_space=pltpu.SMEM)
 
 
-def climb(value, step):
-    perm = []
-    for z in range(16):
-        to = (z + step) % 16
-        perm.append((z % 8 * 2 + z // 8, to % 8 * 2 + to // 8))
-    return lax.ppermute(value, ("zl", "zh"), perm)
+def shift(value, axis, step):
+    size = AXES[axis]
+    return lax.ppermute(value, axis, [(i, (i + step) % size) for i in range(size)])
 
 
 def flip(value, axis, bit):
@@ -43,7 +42,7 @@
     )
 
 
-def table_kernel(owner_ref, table_ref, seen_ref):
+def table_kernel(owner_ref, gate_ref, up_ref, hidden_ref, table_ref, seen_ref):
     my_z = lax.axis_index("zl")
 
     def clear(i, carry):
@@ -77,11 +76,15 @@
 def forward_kernel(a_ref, ac_ref, b_ref, bc_ref, gate_ref, up_ref, g_ref, rows_ref, x_ref, act_ref, picked_ref):
     zh = lax.axis_index("zh")
     core = lax.axis_index("core")
-    for ref, z, c in ((a_ref, zh, core), (ac_ref, zh, 1 - core), (b_ref, 1 - zh, core), (bc_ref, 1 - zh, 1 - core)):
-        for y in range(4):
-            at = (y * 4 + z * 2 + c) * 2
-            x_ref[at] = ref[y, :BS]
-            x_ref[at + 1] = ref[y, BS:]
+    me = lax.axis_index("y")
+    for c, near_ref, far_ref in ((core, a_ref, b_ref), (1 - core, ac_ref, bc_ref)):
+        for i, step in enumerate(Y_STEPS):
+            at = ((me - step + 4) % 4 * 4 + zh * 2 + c) * 2
+            x_ref[at] = near_ref[i, :BS]
+            x_ref[at + 1] = near_ref[i, BS:]
+            at = (i * 4 + (1 - zh) * 2 + c) * 2
+            x_ref[at] = far_ref[i, :BS]
+            x_ref[at + 1] = far_ref[i, BS:]
 
     def column(c, carry):
         for k in range(KB):
@@ -111,24 +114,31 @@
         out_ref[(2 * i + 1) * BS:(2 * i + 2) * BS] = value[:, BS:]
 
 
+def sum_kernel(got_ref, order_ref, send_ref, keep_ref):
+    half = got_ref.shape[1] // 2
+    for ref, at in ((keep_ref, 0), (send_ref, half)):
+        rows = slice(at, at + half)
+        total = got_ref[0, rows].astype(jnp.float32)
+        for i in range(1, NX):
+            total += got_ref[i, rows].astype(jnp.float32)
+        ref[...] = total.astype(ref.dtype)
+
+
 def body(x_panel, grad_hidden, gate_blocks, up_blocks, block_rows, block_owner):
     bf16, f32 = jnp.bfloat16, jnp.float32
-    table = call(
-        table_kernel, jax.ShapeDtypeStruct((NX * NZ * CAP,), jnp.int32), [SMEM], SMEM,
-        [pltpu.SMEM((NX * NZ,), jnp.int32)],
-    )(block_owner)
     own = x_panel.T
-    up, down = climb(own[:BS], 4), climb(own[BS:], -4)
+    far = flip(own, "zh", 1)
     gate_t, up_t = (w.transpose(0, 3, 1, 2).reshape(COLS, BS, KB * BS) for w in (gate_blocks, up_blocks))
     hidden = grad_hidden.T.reshape(COLS, BS, TOK)
-    own, gate_t = lax.optimization_barrier((own, gate_t))
-    a = lax.all_to_all(jnp.broadcast_to(own[None], (4,) + own.shape), "y", 0, 0, tiled=True)
+    a = jnp.stack([own] + [shift(own, "y", step) for step in Y_STEPS[1:]])
     ac = flip(a, "core", 1)
-    up, down = climb(up, 4), climb(down, -4)
-    up, down, up_t, hidden = lax.optimization_barrier((up, down, up_t, hidden))
-    far = jnp.concatenate([up, down], 0)
+    corners = [v[0, :8] for v in (gate_t, up_t, hidden)]
+    table = call(
+        table_kernel, jax.ShapeDtypeStruct((NX * NZ * CAP,), jnp.int32), [SMEM] + [ANY] * 3, SMEM,
+        [pltpu.SMEM((NX * NZ,), jnp.int32)],
+    )(block_owner, *corners)
+    far, table = lax.optimization_barrier((far, table))
     b = lax.all_to_all(jnp.broadcast_to(far[None], (4,) + far.shape), "y", 0, 0, tiled=True)
-    b, table = lax.optimization_barrier((b, table))
     bc = flip(b, "core", 1)
 
     x_all, act = call(
@@ -149,22 +159,22 @@
         value = value.reshape(NX, value.shape[0] // NX, BS)
         return lax.all_to_all(value, "x", 0, 0, tiled=True)
 
-    def halve(keep, bit):
-        half = keep.shape[0] // 2
-        got = flip(keep[half:].astype(bf16), "zl", bit)
-        return keep[:half] + got.astype(f32)
-
     got = flip(backward(NX * NZ, NX * 4, bf16), "zl", 1)
     first = over_x(backward(0, NX * NZ, bf16))
     second = (backward(NX * NZ + NX * 4, NX * 4, f32) + got.astype(f32)).astype(bf16)
-    first, second = lax.optimization_barrier((first, second))
+    half = first.shape[1] // 2
+    send, first = call(
+        sum_kernel, (jax.ShapeDtypeStruct((half, BS), bf16), jax.ShapeDtypeStruct((half, BS), f32)),
+        [VMEM, ANY], (VMEM, VMEM), bytes_accessed=3 * 2**20,
+    )(first, second)
     second = over_x(second)
-    half = first.shape[1] // 2
-    got = flip(jnp.sum(first[:, half:].astype(f32), 0).astype(bf16), "zl", 1)
-    first = jnp.sum(first[:, :half].astype(f32), 0) + got.astype(f32)
-    first = halve(halve(first, 2), 4)
-    second = halve(halve(jnp.sum(second.astype(f32), 0), 2), 4)
-    return jnp.concatenate([first, second], 0).reshape(1, 1, CAP, 2, BS, BS)
+    first = first + flip(send, "zl", 1).astype(f32)
+    both = [first, jnp.sum(second.astype(f32), 0)]
+    for bit in (2, 4):
+        half = half // 2
+        got = flip(jnp.concatenate([v[half:].astype(bf16) for v in both], 0), "zl", bit)
+        both = [v[:half] + got[i * half:(i + 1) * half].astype(f32) for i, v in enumerate(both)]
+    return jnp.concatenate(both, 0).reshape(1, 1, CAP, 2, BS, BS)
 
 
 def solution(mesh):

time: 180 us -> 184 us (1.022)
  the two profiles are of different devices: /device:TPU:6 before, /device:TPU:1 now
where the time goes in v4:
time: 184 us; the launch traced here: 183 us
  waiting for transfers between devices  74.8 us (41%)
  starting transfers between devices  64.5 us (35%)
  local copies, waits for them, and re-layouts  22.5 us (12%)
  Pallas kernels  17.1 us (9%)
  other arithmetic  3.58 us (2%)
    ppermute x7, starting transfers between devices, flip(): return lax.ppermute(value, axis, [(i, i ^ bit) for i in range(AXES[axis])])  42.1 us
    ppermute x7, waiting for transfers between devices, flip(): return lax.ppermute(value, axis, [(i, i ^ bit) for i in range(AXES[axis])])  39 us
    all_to_all x2, waiting for transfers between devices, over_x(): return lax.all_to_all(value, 'x', 0, 0, tiled=True)  19.2 us
    ppermute x3, waiting for transfers between devices, shift(): lax.ppermute(value, axis, [(i, (i + step) % size) for i in range(size)])  16.6 us
    unnamed x25, local copies, waits for them, and re-layouts  12 us
    ppermute x3, starting transfers between devices, shift(): lax.ppermute(value, axis, [(i, (i + step) % size) for i in range(size)])  10.1 us
    all_to_all x2, starting transfers between devices, over_x(): return lax.all_to_all(value, 'x', 0, 0, tiled=True)  7.99 us
    pallas_call x3, Pallas kernels, backward(): call(functools.partial(backward_kernel, first, count, dtype), jax.ShapeDt...  7.63 us
  transfers between devices with their start and end apart: 13, of which 9 were waited for; matrix products, arithmetic and copies ran while one was open for 7% of the time, Pallas kernels for 6%

profile of v4, /device:TPU:1, one launch (start us, length us, event | category | flops | bytes accessed | tf_op | source)
XLA Modules:
  0.0 182.9 jit_solution(16823444144834515220)
XLA Ops:
  1.1 16.3 %collective-permute-start.4 = (bf16[256,512]{1,0:T(8,128)(2,1)S(1)}, bf16[256,512]{1,0:T(8,128)(2,1)S(1)}, u32[]{:S(2)}, u32[]{:S(2)}) collective-permute-start(bf16[256,512]{1,0:T(8,128)(2,1)S(1)} %bitcast.28), channel_id=1, source_target_pairs={{0,2},{2,0},{1,3},{3,1},{4,6},{6,4},{5,7},{7,5},{8,10},{10,8},{9,1... | collective-permute-start | bytes 786440 | tf_op jit(solution)/shard_map/ppermute | solution.py:30
  19.8 2.9 %copy.11.gate_ref = bf16[7,128,1024]{2,1,0:T(8,128)(2,1)S(1)} copy(bf16[7,128,1024]{1,2,0:T(8,128)(2,1)} %bitcast.26) | data formatting | bytes 3670016 | tf_op jit(solution)/shard_map/reshape | solution.py:131
  22.7 4.4 %copy.12.up_ref = bf16[7,128,1024]{2,1,0:T(8,128)(2,1)} copy(bf16[7,128,1024]{1,2,0:T(8,128)(2,1)} %bitcast.27) | data formatting | bytes 3670016 | tf_op jit(solution)/shard_map/reshape | solution.py:131
  27.8 3.5 %shard_map.64.table_ref = s32[64]{0:T(128)S(1)} custom-call(s32[7,8]{1,0:T(8,128)S(1)} %copy-done.11, bf16[8,1024]{1,0:T(8,128)(2,1)S(1)} %get-tuple-element.22.gate_ref, bf16[8,1024]{1,0:T(8,128)(2,1)S(1)} %get-tuple-element.21.up_ref, bf16[8,512]{1,0:T(8,128)(2,1)S(1)} %slice_bitcast_fusion.2.hidden_ref), custom_call_target="tpu_custom_call" | custom-call | tf_op jit(solution)/shard_map/pallas_call | solution.py:136
  32.4 4.3 %all-to-all-start = ((bf16[4,256,512]{2,1,0:T(8,128)(2,1)}), bf16[4,256,512]{2,1,0:T(8,128)(2,1)S(1)}, u32[]{:S(2)}, u32[]{:S(2)}) async-start(bf16[4,256,512]{2,1,0:T(8,128)(2,1)} %broadcast_in_dim.2), calls=%async_computation | async-start | bytes 2097152 | tf_op jit(solution)/shard_map/all_to_all | solution.py:141
  36.7 4.9 %collective-permute-start.2 = (bf16[256,512]{1,0:T(8,128)(2,1)S(1)}, bf16[256,512]{1,0:T(8,128)(2,1)S(1)}, u32[]{:S(2)}, u32[]{:S(2)}) collective-permute-start(bf16[256,512]{1,0:T(8,128)(2,1)S(1)} %bitcast.29), channel_id=1, source_target_pairs={{0,8},{4,12},{8,0},{12,4},{1,9},{5,13},{9,1},{13,5},{2,10},{6,14},... | collective-permute-start | bytes 786440 | tf_op jit(solution)/shard_map/ppermute | solution.py:26
  41.5 2.8 %collective-permute-start.1 = (bf16[256,512]{1,0:T(8,128)(2,1)S(1)}, bf16[256,512]{1,0:T(8,128)(2,1)S(1)}, u32[]{:S(2)}, u32[]{:S(2)}) collective-permute-start(bf16[256,512]{1,0:T(8,128)(2,1)S(1)} %bitcast.30), channel_id=1, source_target_pairs={{0,12},{4,0},{8,4},{12,8},{1,13},{5,1},{9,5},{13,9},{2,14},{6,2},{... | collective-permute-start | bytes 786440 | tf_op jit(solution)/shard_map/ppermute | solution.py:26
  44.4 2.5 %collective-permute-start = (bf16[256,512]{1,0:T(8,128)(2,1)S(1)}, bf16[256,512]{1,0:T(8,128)(2,1)S(1)}, u32[]{:S(2)}, u32[]{:S(2)}) collective-permute-start(bf16[256,512]{1,0:T(8,128)(2,1)S(1)} %bitcast.31), channel_id=1, source_target_pairs={{0,4},{4,8},{8,12},{12,0},{1,5},{5,9},{9,13},{13,1},{2,6},{6,10},{... | collective-permute-start | bytes 786440 | tf_op jit(solution)/shard_map/ppermute | solution.py:26
  46.8 9.4 %collective-permute-done.2 = bf16[256,512]{1,0:T(8,128)(2,1)S(1)} collective-permute-done((bf16[256,512]{1,0:T(8,128)(2,1)S(1)}, bf16[256,512]{1,0:T(8,128)(2,1)S(1)}, u32[]{:S(2)}, u32[]{:S(2)}) %collective-permute-start.2) | collective-permute-done | bytes 262176 | tf_op jit(solution)/shard_map/ppermute | solution.py:26
  56.2 4.1 %collective-permute-done.1 = bf16[256,512]{1,0:T(8,128)(2,1)S(1)} collective-permute-done((bf16[256,512]{1,0:T(8,128)(2,1)S(1)}, bf16[256,512]{1,0:T(8,128)(2,1)S(1)}, u32[]{:S(2)}, u32[]{:S(2)}) %collective-permute-start.1) | collective-permute-done | bytes 262176 | tf_op jit(solution)/shard_map/ppermute | solution.py:26
  60.3 3.1 %collective-permute-done = bf16[256,512]{1,0:T(8,128)(2,1)S(1)} collective-permute-done((bf16[256,512]{1,0:T(8,128)(2,1)S(1)}, bf16[256,512]{1,0:T(8,128)(2,1)S(1)}, u32[]{:S(2)}, u32[]{:S(2)}) %collective-permute-start) | collective-permute-done | bytes 262176 | tf_op jit(solution)/shard_map/ppermute | solution.py:26
  63.6 2.4 %collective-permute-start.3 = (bf16[4,256,512]{2,1,0:T(8,128)(2,1)S(1)}, bf16[4,256,512]{2,1,0:T(8,128)(2,1)}, u32[]{:S(2)}, u32[]{:S(2)}) collective-permute-start(bf16[4,256,512]{2,1,0:T(8,128)(2,1)S(1)} %pad_maximum_fusion.a_ref), channel_id=1, source_target_pairs={{0,1},{1,0},{2,3},{3,2},{4,5},{5,4},{6,7},{7,6},{8,9},{9,8},{10,11... | collective-permute-start | bytes 3145736 | tf_op jit(solution)/shard_map/ppermute | solution.py:30
  67.0 1.9 %collective-permute-start.5 = (bf16[4,256,512]{2,1,0:T(8,128)(2,1)S(1)}, bf16[4,256,512]{2,1,0:T(8,128)(2,1)S(1)}, u32[]{:S(2)}, u32[]{:S(2)}) collective-permute-start(bf16[4,256,512]{2,1,0:T(8,128)(2,1)S(1)} %all-to-all-done.b_ref), channel_id=1, source_target_pairs={{0,1},{1,0},{2,3},{3,2},{4,5},{5,4},{6,7},{7,6},{8,9},{9,8},{10,11... | collective-permute-start | bytes 3145736 | tf_op jit(solution)/shard_map/ppermute | solution.py:30
  69.0 2.6 %collective-permute-done.5.bc_ref = bf16[4,256,512]{2,1,0:T(8,128)(2,1)S(1)} collective-permute-done((bf16[4,256,512]{2,1,0:T(8,128)(2,1)S(1)}, bf16[4,256,512]{2,1,0:T(8,128)(2,1)S(1)}, u32[]{:S(2)}, u32[]{:S(2)}) %collective-permute-start.5) | collective-permute-done | bytes 1048608 | tf_op jit(solution)/shard_map/ppermute | solution.py:30
  77.0 4.1 %shard_map.65 = (bf16[32,128,512]{2,1,0:T(8,128)(2,1)S(1)}, bf16[7,256,512]{2,1,0:T(8,128)(2,1)S(1)}) custom-call(bf16[4,256,512]{2,1,0:T(8,128)(2,1)S(1)} %copy-done.7, bf16[4,256,512]{2,1,0:T(8,128)(2,1)} %collective-permute-done.3.ac_ref, bf16[4,256,512]{2,1,0:T(8,128)(2,1)S(1)} %all-to-all-done.b_ref, ...), custom_call_target="tpu_custom_call" | custom-call | flops 1879048192 | bytes 14680064 | tf_op jit(solution)/shard_map/pallas_call | solution.py:144
  81.1 2.1 %shard_map.68 = bf16[4096,128]{1,0:T(8,128)(2,1)S(1)} custom-call(bf16[32,128,512]{2,1,0:T(8,128)(2,1)S(1)} %get-tuple-element.12.x_ref, bf16[7,256,512]{2,1,0:T(8,128)(2,1)S(1)} %get-tuple-element.13.act_ref, s32[7,8]{1,0:T(8,128)S(1)} %copy-done.10, s32[64]{0:T(128)S(1)} %shard_map.64.table_ref), custom_call_target="tpu_custom_call" | custom-call | flops 536870912 | bytes 7340032 | tf_op jit(solution)/shard_map/pallas_call | solution.py:152
  83.2 11.7 %collective-permute-start.6 = (bf16[4096,128]{1,0:T(8,128)(2,1)S(1)}, bf16[4096,128]{1,0:T(8,128)(2,1)}, u32[]{:S(2)}, u32[]{:S(2)}) collective-permute-start(bf16[4096,128]{1,0:T(8,128)(2,1)S(1)} %shard_map.68), channel_id=1, source_target_pairs={{0,64},{64,0},{128,192},{192,128},{256,320},{320,256},{384,448},{4... | collective-permute-start | bytes 3145736 | tf_op jit(solution)/shard_map/ppermute | solution.py:30
  94.9 3.4 %shard_map.66 = bf16[8192,128]{1,0:T(8,128)(2,1)S(1)} custom-call(bf16[32,128,512]{2,1,0:T(8,128)(2,1)S(1)} %get-tuple-element.12.x_ref, bf16[7,256,512]{2,1,0:T(8,128)(2,1)S(1)} %get-tuple-element.13.act_ref, s32[7,8]{1,0:T(8,128)S(1)} %copy-done.10, s32[64]{0:T(128)S(1)} %shard_map.64.table_ref), custom_call_target="tpu_custom_call" | custom-call | flops 1073741824 | bytes 7340032 | tf_op jit(solution)/shard_map/pallas_call | solution.py:152
  99.7 4.5 %all-to-all-start.1 = ((bf16[4,2048,128]{2,1,0:T(8,128)(2,1)}), bf16[4,2048,128]{2,1,0:T(8,128)(2,1)}, u32[]{:S(2)}, u32[]{:S(2)}) async-start(bf16[4,2048,128]{2,1,0:T(8,128)(2,1)} %bitcast.23), calls=%async_computation.1 | async-start | bytes 4194304 | tf_op jit(solution)/shard_map/all_to_all | solution.py:160
  104.2 2.2 %copy-done.1 = bf16[32,128,512]{2,1,0:T(8,128)(2,1)S(1)} copy-done((bf16[32,128,512]{2,1,0:T(8,128)(2,1)S(1)}, bf16[32,128,512]{2,1,0:T(8,128)(2,1)}, u32[]{:S(2)}) %copy-start.1) | copy-done | bytes 4194328
  106.4 2.1 %shard_map.67 = f32[4096,128]{1,0:T(8,128)S(1)} custom-call(bf16[32,128,512]{2,1,0:T(8,128)(2,1)S(1)} %copy-done.1, bf16[7,256,512]{2,1,0:T(8,128)(2,1)S(1)} %get-tuple-element.13.act_ref, s32[7,8]{1,0:T(8,128)S(1)} %copy-done.10, s32[64]{0:T(128)S(1)} %shard_map.64.table_ref), custom_call_target="tpu_custom_call" | custom-call | flops 536870912 | bytes 7340032 | tf_op jit(solution)/shard_map/pallas_call | solution.py:152
  108.5 9.9 %collective-permute-done.6 = bf16[4096,128]{1,0:T(8,128)(2,1)} collective-permute-done((bf16[4096,128]{1,0:T(8,128)(2,1)S(1)}, bf16[4096,128]{1,0:T(8,128)(2,1)}, u32[]{:S(2)}, u32[]{:S(2)}) %collective-permute-start.6) | collective-permute-done | bytes 1048608 | tf_op jit(solution)/shard_map/ppermute | solution.py:30
  118.4 2.4 %add_convert_fusion.order_ref = bf16[4096,128]{1,0:T(8,128)(2,1)} fusion(f32[4096,128]{1,0:T(8,128)S(1)} %shard_map.67, bf16[4096,128]{1,0:T(8,128)(2,1)} %collective-permute-done.6), kind=kLoop, calls=%fused_computation.1 | loop fusion | flops 1572864 | bytes 4194304 | tf_op jit(solution)/shard_map/convert_element_type | solution.py:164
  120.8 9.5 %all-to-all-done.1.got_ref = bf16[4,2048,128]{2,1,0:T(8,128)(2,1)} async-done(((bf16[4,2048,128]{2,1,0:T(8,128)(2,1)}), bf16[4,2048,128]{2,1,0:T(8,128)(2,1)}, u32[]{:S(2)}, u32[]{:S(2)}) %all-to-all-start.1) | async-done | bytes 2097184 | tf_op jit(solution)/shard_map/all_to_all | solution.py:160
  130.3 3.5 %all-to-all-start.2 = ((bf16[4,1024,128]{2,1,0:T(8,128)(2,1)}), bf16[4,1024,128]{2,1,0:T(8,128)(2,1)S(1)}, u32[]{:S(2)}, u32[]{:S(2)}) async-start(bf16[4,1024,128]{2,1,0:T(8,128)(2,1)} %bitcast.15), calls=%async_computation.2 | async-start | bytes 2097152 | tf_op jit(solution)/shard_map/all_to_all | solution.py:160
  133.8 1.8 %shard_map.69 = (bf16[1024,128]{1,0:T(8,128)(2,1)S(1)}, f32[1024,128]{1,0:T(8,128)S(1)}) custom-call(bf16[4,2048,128]{2,1,0:T(8,128)(2,1)} %all-to-all-done.1.got_ref, bf16[4096,128]{1,0:T(8,128)(2,1)} %add_convert_fusion.order_ref), custom_call_target="tpu_custom_call" | custom-call | bytes 3145728 | tf_op jit(solution)/shard_map/pallas_call | solution.py:166
  135.7 2.2 %collective-permute-start.7 = (bf16[1024,128]{1,0:T(8,128)(2,1)S(1)}, bf16[1024,128]{1,0:T(8,128)(2,1)S(1)}, u32[]{:S(2)}, u32[]{:S(2)}) collective-permute-start(bf16[1024,128]{1,0:T(8,128)(2,1)S(1)} %get-tuple-element.16), channel_id=1, source_target_pairs={{0,64},{64,0},{128,192},{192,128},{256,320},{320,256},{384,448},{4... | collective-permute-start | bytes 786440 | tf_op jit(solution)/shard_map/ppermute | solution.py:30
  137.9 9.7 %all-to-all-done.2 = bf16[4,1024,128]{2,1,0:T(8,128)(2,1)S(1)} async-done(((bf16[4,1024,128]{2,1,0:T(8,128)(2,1)}), bf16[4,1024,128]{2,1,0:T(8,128)(2,1)S(1)}, u32[]{:S(2)}, u32[]{:S(2)}) %all-to-all-start.2) | async-done | bytes 1048608 | tf_op jit(solution)/shard_map/all_to_all | solution.py:160
  147.9 1.9 %collective-permute-start.8 = (bf16[1024,128]{1,0:T(8,128)(2,1)S(1)}, bf16[1024,128]{1,0:T(8,128)(2,1)S(1)}, u32[]{:S(2)}, u32[]{:S(2)}) collective-permute-start(bf16[1024,128]{1,0:T(8,128)(2,1)S(1)} %pad_maximum_fusion.1), channel_id=1, source_target_pairs={{0,128},{64,192},{128,0},{192,64},{256,384},{320,448},{384,256},{4... | collective-permute-start | bytes 786440 | tf_op jit(solution)/shard_map/ppermute | solution.py:30
  149.8 14.3 %collective-permute-done.8 = bf16[1024,128]{1,0:T(8,128)(2,1)S(1)} collective-permute-done((bf16[1024,128]{1,0:T(8,128)(2,1)S(1)}, bf16[1024,128]{1,0:T(8,128)(2,1)S(1)}, u32[]{:S(2)}, u32[]{:S(2)}) %collective-permute-start.8) | collective-permute-done | bytes 262176 | tf_op jit(solution)/shard_map/ppermute | solution.py:30
  164.2 5.7 %collective-permute-start.9 = (bf16[512,128]{1,0:T(8,128)(2,1)S(1)}, bf16[512,128]{1,0:T(8,128)(2,1)S(1)}, u32[]{:S(2)}, u32[]{:S(2)}) collective-permute-start(bf16[512,128]{1,0:T(8,128)(2,1)S(1)} %pad_maximum_fusion.3), channel_id=1, source_target_pairs={{0,256},{64,320},{128,384},{192,448},{256,0},{320,64},{384,128},{4... | collective-permute-start | bytes 393224 | tf_op jit(solution)/shard_map/ppermute | solution.py:30
  169.9 12.3 %collective-permute-done.9 = bf16[512,128]{1,0:T(8,128)(2,1)S(1)} collective-permute-done((bf16[512,128]{1,0:T(8,128)(2,1)S(1)}, bf16[512,128]{1,0:T(8,128)(2,1)S(1)}, u32[]{:S(2)}, u32[]{:S(2)}) %collective-permute-start.9) | collective-permute-done | bytes 131104 | tf_op jit(solution)/shard_map/ppermute | solution.py:30
  (44 shorter events, 14.3 us)
Async XLA Ops:
  1.1 30.2 %collective-permute-start.4 = (bf16[256,512]{1,0:T(8,128)(2,1)S(1)}, bf16[256,512]{1,0:T(8,128)(2,1)S(1)}, u32[]{:S(2)}, u32[]{:S(2)}) collective-permute-start(bf16[256,512]{1,0:T(8,128)(2,1)S(1)} %bitcast.28), channel_id=1, source_target_pairs={{0,2},{2,0},{1,3},{3,1},{4,6},{6,4},{5,7},{7,5},{8,10},{10,8},{9,1... | collective-permute-start | bytes 786440 | tf_op jit(solution)/shard_map/ppermute | solution.py:30
  18.9 0.9 copy-start.8
  22.7 9.7 %copy-start.3 = (bf16[7,128,1024]{2,1,0:T(8,128)(2,1)}, bf16[7,128,1024]{2,1,0:T(8,128)(2,1)S(1)}, u32[]{:S(2)}) copy-start(bf16[7,128,1024]{2,1,0:T(8,128)(2,1)S(1)} %copy.11.gate_ref) | copy-start | bytes 5505028
  22.7 5.1 %copy-start.11 = (s32[7,8]{1,0:T(8,128)S(1)}, s32[7,8]{1,0:T(8,128)}, u32[]{:S(2)}) copy-start(s32[7,8]{1,0:T(8,128)} %owner_ref.1) | copy-start | bytes 676
  32.4 39.2 %copy-start.10 = (s32[7,8]{1,0:T(8,128)S(1)}, s32[7,8]{1,0:T(8,128)}, u32[]{:S(2)}) copy-start(s32[7,8]{1,0:T(8,128)} %rows_ref.7) | copy-start | bytes 676
  32.4 34.7 %all-to-all-start = ((bf16[4,256,512]{2,1,0:T(8,128)(2,1)}), bf16[4,256,512]{2,1,0:T(8,128)(2,1)S(1)}, u32[]{:S(2)}, u32[]{:S(2)}) async-start(bf16[4,256,512]{2,1,0:T(8,128)(2,1)} %broadcast_in_dim.2), calls=%async_computation | async-start | bytes 2097152 | tf_op jit(solution)/shard_map/all_to_all | solution.py:141
  36.7 19.5 %collective-permute-start.2 = (bf16[256,512]{1,0:T(8,128)(2,1)S(1)}, bf16[256,512]{1,0:T(8,128)(2,1)S(1)}, u32[]{:S(2)}, u32[]{:S(2)}) collective-permute-start(bf16[256,512]{1,0:T(8,128)(2,1)S(1)} %bitcast.29), channel_id=1, source_target_pairs={{0,8},{4,12},{8,0},{12,4},{1,9},{5,13},{9,1},{13,5},{2,10},{6,14},... | collective-permute-start | bytes 786440 | tf_op jit(solution)/shard_map/ppermute | solution.py:26
  41.5 18.8 %collective-permute-start.1 = (bf16[256,512]{1,0:T(8,128)(2,1)S(1)}, bf16[256,512]{1,0:T(8,128)(2,1)S(1)}, u32[]{:S(2)}, u32[]{:S(2)}) collective-permute-start(bf16[256,512]{1,0:T(8,128)(2,1)S(1)} %bitcast.30), channel_id=1, source_target_pairs={{0,12},{4,0},{8,4},{12,8},{1,13},{5,1},{9,5},{13,9},{2,14},{6,2},{... | collective-permute-start | bytes 786440 | tf_op jit(solution)/shard_map/ppermute | solution.py:26
  44.4 19.1 %collective-permute-start = (bf16[256,512]{1,0:T(8,128)(2,1)S(1)}, bf16[256,512]{1,0:T(8,128)(2,1)S(1)}, u32[]{:S(2)}, u32[]{:S(2)}) collective-permute-start(bf16[256,512]{1,0:T(8,128)(2,1)S(1)} %bitcast.31), channel_id=1, source_target_pairs={{0,4},{4,8},{8,12},{12,0},{1,5},{5,9},{9,13},{13,1},{2,6},{6,10},{... | collective-permute-start | bytes 786440 | tf_op jit(solution)/shard_map/ppermute | solution.py:26
  63.6 5.3 %collective-permute-start.3 = (bf16[4,256,512]{2,1,0:T(8,128)(2,1)S(1)}, bf16[4,256,512]{2,1,0:T(8,128)(2,1)}, u32[]{:S(2)}, u32[]{:S(2)}) collective-permute-start(bf16[4,256,512]{2,1,0:T(8,128)(2,1)S(1)} %pad_maximum_fusion.a_ref), channel_id=1, source_target_pairs={{0,1},{1,0},{2,3},{3,2},{4,5},{5,4},{6,7},{7,6},{8,9},{9,8},{10,11... | collective-permute-start | bytes 3145736 | tf_op jit(solution)/shard_map/ppermute | solution.py:30
  66.0 1.0 copy-start.6
  67.0 4.5 %collective-permute-start.5 = (bf16[4,256,512]{2,1,0:T(8,128)(2,1)S(1)}, bf16[4,256,512]{2,1,0:T(8,128)(2,1)S(1)}, u32[]{:S(2)}, u32[]{:S(2)}) collective-permute-start(bf16[4,256,512]{2,1,0:T(8,128)(2,1)S(1)} %all-to-all-done.b_ref), channel_id=1, source_target_pairs={{0,1},{1,0},{2,3},{3,2},{4,5},{5,4},{6,7},{7,6},{8,9},{9,8},{10,11... | collective-permute-start | bytes 3145736 | tf_op jit(solution)/shard_map/ppermute | solution.py:30
  71.6 1.5 copy-start.4
  73.1 1.5 copy-start.5
  74.6 1.2 copy-start.7
  75.8 1.2 copy-start.9
  81.1 13.8 %copy-start = (bf16[32,128,512]{2,1,0:T(8,128)(2,1)}, bf16[32,128,512]{2,1,0:T(8,128)(2,1)S(1)}, u32[]{:S(2)}) copy-start(bf16[32,128,512]{2,1,0:T(8,128)(2,1)S(1)} %get-tuple-element.12.x_ref) | copy-start | bytes 12582916
  83.2 35.2 %collective-permute-start.6 = (bf16[4096,128]{1,0:T(8,128)(2,1)S(1)}, bf16[4096,128]{1,0:T(8,128)(2,1)}, u32[]{:S(2)}, u32[]{:S(2)}) collective-permute-start(bf16[4096,128]{1,0:T(8,128)(2,1)S(1)} %shard_map.68), channel_id=1, source_target_pairs={{0,64},{64,0},{128,192},{192,128},{256,320},{320,256},{384,448},{4... | collective-permute-start | bytes 3145736 | tf_op jit(solution)/shard_map/ppermute | solution.py:30
  98.3 1.4 copy-start.2
  99.7 30.6 %all-to-all-start.1 = ((bf16[4,2048,128]{2,1,0:T(8,128)(2,1)}), bf16[4,2048,128]{2,1,0:T(8,128)(2,1)}, u32[]{:S(2)}, u32[]{:S(2)}) async-start(bf16[4,2048,128]{2,1,0:T(8,128)(2,1)} %bitcast.23), calls=%async_computation.1 | async-start | bytes 4194304 | tf_op jit(solution)/shard_map/all_to_all | solution.py:160
  104.2 2.2 %copy-start.1 = (bf16[32,128,512]{2,1,0:T(8,128)(2,1)S(1)}, bf16[32,128,512]{2,1,0:T(8,128)(2,1)}, u32[]{:S(2)}) copy-start(bf16[32,128,512]{2,1,0:T(8,128)(2,1)} %copy-done) | copy-start | bytes 12582916
  130.3 17.3 %all-to-all-start.2 = ((bf16[4,1024,128]{2,1,0:T(8,128)(2,1)}), bf16[4,1024,128]{2,1,0:T(8,128)(2,1)S(1)}, u32[]{:S(2)}, u32[]{:S(2)}) async-start(bf16[4,1024,128]{2,1,0:T(8,128)(2,1)} %bitcast.15), calls=%async_computation.2 | async-start | bytes 2097152 | tf_op jit(solution)/shard_map/all_to_all | solution.py:160
  135.7 12.2 %collective-permute-start.7 = (bf16[1024,128]{1,0:T(8,128)(2,1)S(1)}, bf16[1024,128]{1,0:T(8,128)(2,1)S(1)}, u32[]{:S(2)}, u32[]{:S(2)}) collective-permute-start(bf16[1024,128]{1,0:T(8,128)(2,1)S(1)} %get-tuple-element.16), channel_id=1, source_target_pairs={{0,64},{64,0},{128,192},{192,128},{256,320},{320,256},{384,448},{4... | collective-permute-start | bytes 786440 | tf_op jit(solution)/shard_map/ppermute | solution.py:30
  147.9 16.2 %collective-permute-start.8 = (bf16[1024,128]{1,0:T(8,128)(2,1)S(1)}, bf16[1024,128]{1,0:T(8,128)(2,1)S(1)}, u32[]{:S(2)}, u32[]{:S(2)}) collective-permute-start(bf16[1024,128]{1,0:T(8,128)(2,1)S(1)} %pad_maximum_fusion.1), channel_id=1, source_target_pairs={{0,128},{64,192},{128,0},{192,64},{256,384},{320,448},{384,256},{4... | collective-permute-start | bytes 786440 | tf_op jit(solution)/shard_map/ppermute | solution.py:30
  164.2 18.0 %collective-permute-start.9 = (bf16[512,128]{1,0:T(8,128)(2,1)S(1)}, bf16[512,128]{1,0:T(8,128)(2,1)S(1)}, u32[]{:S(2)}, u32[]{:S(2)}) collective-permute-start(bf16[512,128]{1,0:T(8,128)(2,1)S(1)} %pad_maximum_fusion.3), channel_id=1, source_target_pairs={{0,256},{64,320},{128,384},{192,448},{256,0},{320,64},{384,128},{4... | collective-permute-start | bytes 393224 | tf_op jit(solution)/shard_map/ppermute | solution.py:30

commit v5 on v4

v5 whole, which is shorter than its diff:
```python
import functools

import jax
import jax.numpy as jnp
from jax import lax
from jax.experimental import pallas as pl
from jax.experimental.pallas import tpu as pltpu
from jax.sharding import Mesh, PartitionSpec as P

BS = 128
KB = 8
COLS = 7
BLOCKS = COLS * KB
TOK = 512
ROWS = 32
NX, NZ, CAP = 4, 8, 2
AXES = {"z4": 4, "z2": 2, "x": 4, "y": 4, "zh": 2, "core": 2}
VMEM = pl.BlockSpec(memory_space=pltpu.VMEM)
ANY = pl.BlockSpec(memory_space=pl.ANY)
SMEM = pl.BlockSpec(memory_space=pltpu.SMEM)


def swap(value, axis):
    return lax.ppermute(value, axis, [(0, 1), (1, 0)])


def spread(value, axis):
    return lax.all_to_all(jnp.broadcast_to(value[None], (AXES[axis],) + value.shape), axis, 0, 0, tiled=True)


def call(kernel, out_shape, in_specs, out_specs, scratch=(), flops=0, bytes_accessed=0):
    return pl.pallas_call(
        kernel,
        out_shape=out_shape,
        in_specs=in_specs,
        out_specs=out_specs,
        scratch_shapes=list(scratch),
        compiler_params=pltpu.CompilerParams(vmem_limit_bytes=40 * 1024 * 1024),
        cost_estimate=pl.CostEstimate(flops=flops, bytes_accessed=bytes_accessed, transcendentals=0),
    )


def place_kernel(owner_ref, gate_ref, up_ref, hidden_ref, near_ref, place_ref, seen_ref):
    my_z = lax.axis_index("z2")

    def clear(i, carry):
        seen_ref[i] = jnp.int32(0)
        return carry

    lax.fori_loop(0, NX * NZ, clear, 0)

    def place(i, carry):
        owner = owner_ref[i // KB, i % KB]
        slot = seen_ref[owner]
        seen_ref[owner] = slot + 1
        x = owner % NX
        z = owner // NX
        other = (z & 1) ^ my_z
        first = x * NZ + other * 4 + (z >> 1)
        second = NX * NZ + (1 - other) * (NX * 4) + x * 4 + (z >> 1)
        place_ref[i] = jnp.where(slot == 0, first, second)
        return carry

    lax.fori_loop(0, BLOCKS, place, 0)


def block_kernel(
    a_ref, ac_ref, b_ref, bc_ref, gate_ref, up_ref, hidden_ref, rows_ref, place_ref,
    first_ref, send_ref, keep_ref, x_ref, w_ref, h_ref, picked_ref, out_ref, x_sem, w_sem, out_sem,
):
    zh = lax.axis_index("zh")
    core = lax.axis_index("core")
    x_copies = []
    for i, (ref, z, c) in enumerate(
        ((a_ref, zh, core), (ac_ref, zh, 1 - core), (b_ref, 1 - zh, core), (bc_ref, 1 - zh, 1 - core))
    ):
        for y in range(4):
            at = (y * 4 + z * 2 + c) * 2
            x_copies.append(pltpu.make_async_copy(ref.at[y], x_ref.at[pl.ds(at, 2)], x_sem.at[i * 4 + y]))
    w_copies = []
    for c in range(COLS):
        w_copies.append((
            pltpu.make_async_copy(gate_ref.at[c], w_ref.at[c, pl.ds(0, BS)], w_sem.at[3 * c]),
            pltpu.make_async_copy(up_ref.at[c], w_ref.at[c, pl.ds(BS, BS)], w_sem.at[3 * c + 1]),
            pltpu.make_async_copy(hidden_ref.at[c], h_ref.at[c], w_sem.at[3 * c + 2]),
        ))
    for copy in x_copies:
        copy.start()
    for copies in w_copies:
        for copy in copies:
            copy.start()
    out_ref[...] = jnp.zeros_like(out_ref)
    for copy in x_copies:
        copy.wait()
    for c in range(COLS):
        for k in range(KB):
            picked_ref[k * BS:(k + 1) * BS] = x_ref[rows_ref[c, k]]
        for copy in w_copies[c]:
            copy.wait()
        picked = picked_ref[...]
        pre = jnp.dot(w_ref[c], picked, preferred_element_type=jnp.float32)
        gate, up = pre[:BS], pre[BS:]
        s = jax.nn.sigmoid(gate)
        h = h_ref[c].astype(jnp.float32)
        grad_gate = (h * up * (s * (1.0 + gate * (1.0 - s)))).astype(jnp.bfloat16)
        grad_up = (h * (gate * s)).astype(jnp.bfloat16)
        for m, act in enumerate((grad_gate, grad_up)):
            value = lax.dot_general(
                picked, act, (((1,), (1,)), ((), ())), preferred_element_type=jnp.float32
            ).astype(jnp.bfloat16)
            for k in range(KB):
                out_ref[place_ref[c * KB + k], m * BS:(m + 1) * BS] = value[k * BS:(k + 1) * BS]
    out_copies = []
    at = 0
    for i, ref in enumerate((send_ref, first_ref, keep_ref)):
        at = (NX * NZ, 0, NX * NZ + NX * 4)[i]
        out_copies.append(pltpu.make_async_copy(out_ref.at[pl.ds(at, ref.shape[0])], ref, out_sem.at[i]))
    for copy in out_copies:
        copy.start()
    for copy in out_copies:
        copy.wait()


def sum_kernel(got_ref, order_ref, send_ref, keep_ref):
    half = got_ref.shape[1] // 2
    for ref, at in ((keep_ref, 0), (send_ref, half)):
        rows = slice(at, at + half)
        total = got_ref[0, rows].astype(jnp.float32)
        for i in range(1, NX):
            total += got_ref[i, rows].astype(jnp.float32)
        ref[...] = total.astype(ref.dtype)


def body(x_panel, grad_hidden, gate_blocks, up_blocks, block_rows, block_owner):
    bf16, f32 = jnp.bfloat16, jnp.float32
    own = x_panel.T.reshape(2, BS, TOK)
    far = swap(own, "zh")
    a = spread(own, "y")
    gate_t, up_t = (w.transpose(0, 3, 1, 2).reshape(COLS, BS, KB * BS) for w in (gate_blocks, up_blocks))
    hidden = grad_hidden.T.reshape(COLS, BS, TOK)
    corners = [v[0, :8] for v in (gate_t, up_t, hidden, a[0])]
    place = call(
        place_kernel, jax.ShapeDtypeStruct((BLOCKS,), jnp.int32), [SMEM] + [ANY] * 4, SMEM,
        [pltpu.SMEM((NX * NZ,), jnp.int32)],
    )(block_owner, *corners)
    ac = swap(a, "core")
    far, place = lax.optimization_barrier((far, place))
    b = spread(far, "y")
    bc = swap(b, "core")

    halves = [jax.ShapeDtypeStruct((count, 2 * BS, BS), bf16) for count in (NX * NZ, NX * 4, NX * 4)]
    first, send, keep = call(
        block_kernel, halves, [ANY] * 7 + [SMEM, SMEM], [ANY] * 3,
        [
            pltpu.VMEM((ROWS, BS, TOK), bf16),
            pltpu.VMEM((COLS, 2 * BS, KB * BS), bf16),
            pltpu.VMEM((COLS, BS, TOK), bf16),
            pltpu.VMEM((KB * BS, TOK), bf16),
            pltpu.VMEM((NX * NZ * CAP, 2 * BS, BS), bf16),
            pltpu.SemaphoreType.DMA((16,)),
            pltpu.SemaphoreType.DMA((3 * COLS,)),
            pltpu.SemaphoreType.DMA((3,)),
        ],
        flops=8 * BLOCKS * BS * BS * TOK, bytes_accessed=14 * 2**20,
    )(a, ac, b, bc, gate_t, up_t, hidden, block_rows, place)

    def over_x(value):
        return lax.all_to_all(value.reshape(NX, -1, BS), "x", 0, 0, tiled=True)

    got = swap(send.reshape(-1, BS), "z2")
    first = over_x(first)
    second = (keep.reshape(-1, BS).astype(f32) + got.astype(f32)).astype(bf16)
    half = first.shape[1] // 2
    send, first = call(
        sum_kernel, (jax.ShapeDtypeStruct((half, BS), bf16), jax.ShapeDtypeStruct((half, BS), f32)),
        [VMEM, ANY], (VMEM, VMEM), bytes_accessed=3 * 2**20,
    )(first, second)
    second = over_x(second)
    first = first + swap(send, "z2").astype(f32)
    second = jnp.sum(second.astype(f32), 0)
    both = jnp.concatenate([v.astype(bf16).reshape(4, 2 * BS, BS) for v in (first, second)], 1)
    got = lax.all_to_all(both, "z4", 0, 0, tiled=True)
    return jnp.sum(got.astype(f32), 0).reshape(1, 1, CAP, 2, BS, BS)


def solution(mesh):
    fine = Mesh(mesh.devices.reshape(tuple(AXES.values())), tuple(AXES))
    dp, tensor = ("z4", "z2", "x"), ("y", "zh", "core")
    in_specs = (
        P(dp, tensor),
        P(dp, tensor),
        P(tensor, None, None, None),
        P(tensor, None, None, None),
        P(tensor, None),
        P(tensor, None),
    )
    out_specs = P(tensor, dp, None, None, None, None)
    return jax.shard_map(body, mesh=fine, in_specs=in_specs, out_specs=out_specs, check_vma=False)
```

time: 184 us -> 178 us (0.967)
  the two profiles are of different devices: /device:TPU:1 before, /device:TPU:6 now
where the time goes in v5:
time: 178 us; the launch traced here: 175 us
  starting transfers between devices  55.4 us (31%)
  waiting for transfers between devices  46.8 us (26%)
  blocking collectives  34.2 us (19%)
  local copies, waits for them, and re-layouts  17.8 us (10%)
  Pallas kernels  15.6 us (9%)
  other arithmetic  4.83 us (3%)
    ppermute x5, starting transfers between devices, swap(): return lax.ppermute(value, axis, [(0, 1), (1, 0)])  34.9 us
    all_to_all x1, blocking collectives, body(): got = lax.all_to_all(both, 'z4', 0, 0, tiled=True)  34.2 us
    ppermute x5, waiting for transfers between devices, swap(): return lax.ppermute(value, axis, [(0, 1), (1, 0)])  21.7 us
    all_to_all x2, waiting for transfers between devices, over_x(): return lax.all_to_all(value.reshape(NX, -1, BS), 'x', 0, 0, tiled=True)  12.7 us
    pallas_call x1, Pallas kernels, body(): call(block_kernel, halves, [ANY] * 7 + [SMEM, SMEM], [ANY] * 3, [pltpu.VM...  12.6 us
    all_to_all x2, waiting for transfers between devices, spread(): lax.all_to_all(jnp.broadcast_to(value[None], (AXES[axis],) + value.shape)...  12.4 us
    all_to_all x2, starting transfers between devices, over_x(): return lax.all_to_all(value.reshape(NX, -1, BS), 'x', 0, 0, tiled=True)  11.2 us
    all_to_all x2, starting transfers between devices, spread(): lax.all_to_all(jnp.broadcast_to(value[None], (AXES[axis],) + value.shape)...  9.26 us
  transfers between devices with their start and end apart: 9, of which 5 were waited for; matrix products, arithmetic and copies ran while one was open for 8% of the time, Pallas kernels for 2%

profile of v5, /device:TPU:6, one launch (start us, length us, event | category | flops | bytes accessed | tf_op | source)
XLA Modules:
  0.0 174.8 jit_solution(3064450682095972597)
XLA Ops:
  0.0 1.1 copy.12
  1.1 1.1 broadcast_in_dim.14
  2.2 4.5 %all-to-all-start = ((bf16[4,2,128,512]{3,2,1,0:T(8,128)(2,1)}), bf16[4,2,128,512]{3,2,1,0:T(8,128)(2,1)S(1)}, u32[]{:S(2)}, u32[]{:S(2)}) async-start(bf16[4,2,128,512]{3,2,1,0:T(8,128)(2,1)} %broadcast_in_dim.14), calls=%async_computation | async-start | bytes 2097152 | tf_op jit(solution)/shard_map/all_to_all | solution.py:28
  6.6 15.7 %collective-permute-start.1 = (bf16[2,128,512]{2,1,0:T(8,128)(2,1)S(1)}, bf16[2,128,512]{2,1,0:T(8,128)(2,1)S(1)}, u32[]{:S(2)}, u32[]{:S(2)}) collective-permute-start(bf16[2,128,512]{2,1,0:T(8,128)(2,1)S(1)} %bitcast.35), channel_id=1, source_target_pairs={{0,2},{2,0},{1,3},{3,1},{4,6},{6,4},{5,7},{7,5},{8,10},{10,8},{9,1... | collective-permute-start | bytes 786440 | tf_op jit(solution)/shard_map/ppermute | solution.py:24
  22.4 1.3 copy.11
  23.7 2.9 %copy.13.gate_ref = bf16[7,128,1024]{2,1,0:T(8,128)(2,1)S(1)} copy(bf16[7,128,1024]{1,2,0:T(8,128)(2,1)} %bitcast.32) | data formatting | bytes 3670016 | tf_op jit(solution)/shard_map/reshape | solution.py:139
  26.6 3.8 %copy.14.up_ref = bf16[7,128,1024]{2,1,0:T(8,128)(2,1)} copy(bf16[7,128,1024]{1,2,0:T(8,128)(2,1)} %bitcast.33) | data formatting | bytes 3670016 | tf_op jit(solution)/shard_map/reshape | solution.py:139
  30.5 0.7 slice_bitcast_fusion.4.hidden_ref
  31.2 0.7 slice_bitcast_fusion.1
  31.9 2.8 %shard_map.64.place_ref = s32[56]{0:T(128)S(1)} custom-call(s32[7,8]{1,0:T(8,128)S(1)} %copy-done.5, bf16[8,1024]{1,0:T(8,128)(2,1)S(1)} %get-tuple-element.20.gate_ref, bf16[8,1024]{1,0:T(8,128)(2,1)S(1)} %get-tuple-element.19.up_ref, bf16[8,512]{1,0:T(8,128)(2,1)S(1)} %slice_bitcast_fusion.4.hidden_ref, bf16[8,512]{1,0:T(8,128)(2,1)S(1)} %slice_bitcast_fusion.3.near_ref), custom_call_target="tpu_custom_call" | custom-call | tf_op jit(solution)/shard_map/pallas_call | solution.py:142
  34.7 1.1 broadcast_in_dim.15
  35.8 4.8 %all-to-all-start.1 = ((bf16[4,2,128,512]{3,2,1,0:T(8,128)(2,1)}), bf16[4,2,128,512]{3,2,1,0:T(8,128)(2,1)}, u32[]{:S(2)}, u32[]{:S(2)}) async-start(bf16[4,2,128,512]{3,2,1,0:T(8,128)(2,1)} %broadcast_in_dim.15), calls=%async_computation.1 | async-start | bytes 2097152 | tf_op jit(solution)/shard_map/all_to_all | solution.py:28
  40.6 1.9 %collective-permute-start = (bf16[4,2,128,512]{3,2,1,0:T(8,128)(2,1)S(1)}, bf16[4,2,128,512]{3,2,1,0:T(8,128)(2,1)}, u32[]{:S(2)}, u32[]{:S(2)}) collective-permute-start(bf16[4,2,128,512]{3,2,1,0:T(8,128)(2,1)S(1)} %all-to-all-done.a_ref), channel_id=1, source_target_pairs={{0,1},{1,0},{2,3},{3,2},{4,5},{5,4},{6,7},{7,6},{8,9},{9,8},{10,11... | collective-permute-start | bytes 3145736 | tf_op jit(solution)/shard_map/ppermute | solution.py:24
  42.5 12.4 %all-to-all-done.1.b_ref = bf16[4,2,128,512]{3,2,1,0:T(8,128)(2,1)} async-done(((bf16[4,2,128,512]{3,2,1,0:T(8,128)(2,1)}), bf16[4,2,128,512]{3,2,1,0:T(8,128)(2,1)}, u32[]{:S(2)}, u32[]{:S(2)}) %all-to-all-start.1) | async-done | bytes 1048608 | tf_op jit(solution)/shard_map/all_to_all | solution.py:28
  55.0 1.9 %collective-permute-start.2 = (bf16[4,2,128,512]{3,2,1,0:T(8,128)(2,1)}, bf16[4,2,128,512]{3,2,1,0:T(8,128)(2,1)S(1)}, u32[]{:S(2)}, u32[]{:S(2)}) collective-permute-start(bf16[4,2,128,512]{3,2,1,0:T(8,128)(2,1)} %all-to-all-done.1.b_ref), channel_id=1, source_target_pairs={{0,1},{1,0},{2,3},{3,2},{4,5},{5,4},{6,7},{7,6},{8,9},{9,8},{10,11... | collective-permute-start | bytes 3145736 | tf_op jit(solution)/shard_map/ppermute | solution.py:24
  56.9 2.8 %collective-permute-done.2.bc_ref = bf16[4,2,128,512]{3,2,1,0:T(8,128)(2,1)S(1)} collective-permute-done((bf16[4,2,128,512]{3,2,1,0:T(8,128)(2,1)}, bf16[4,2,128,512]{3,2,1,0:T(8,128)(2,1)S(1)}, u32[]{:S(2)}, u32[]{:S(2)}) %collective-permute-start.2) | collective-permute-done | bytes 1048608 | tf_op jit(solution)/shard_map/ppermute | solution.py:24
  59.7 1.5 copy-done.1
  61.2 1.2 copy-done.4
  62.4 12.6 %shard_map.65 = (bf16[32,256,128]{2,1,0:T(8,128)(2,1)S(1)}, bf16[16,256,128]{2,1,0:T(8,128)(2,1)}, bf16[16,256,128]{2,1,0:T(8,128)(2,1)S(1)}) custom-call(bf16[4,2,128,512]{3,2,1,0:T(8,128)(2,1)S(1)} %all-to-all-done.a_ref, bf16[4,2,128,512]{3,2,1,0:T(8,128)(2,1)} %collective-permute-done.ac_ref, bf16[4,2,128,512]{3,2,1,0:T(8,128)(2,1)} %all-to-all-done.1.b_ref, ...), custom_call_target="tpu_custom_call" | custom-call | flops 3758096384 | bytes 14680064 | tf_op jit(solution)/shard_map/pallas_call | solution.py:152
  75.0 1.3 copy-done
  76.3 1.0 copy-done.2
  77.3 13.2 %collective-permute-start.3 = (bf16[4096,128]{1,0:T(8,128)(2,1)}, bf16[4096,128]{1,0:T(8,128)(2,1)}, u32[]{:S(2)}, u32[]{:S(2)}) collective-permute-start(bf16[4096,128]{1,0:T(8,128)(2,1)} %bitcast.15), channel_id=1, source_target_pairs={{0,64},{64,0},{1,65},{65,1},{2,66},{66,2},{3,67},{67,3},{4,68},{68... | collective-permute-start | bytes 3145736 | tf_op jit(solution)/shard_map/ppermute | solution.py:24
  90.6 4.9 %all-to-all-start.2 = ((bf16[4,2048,128]{2,1,0:T(8,128)(2,1)}), bf16[4,2048,128]{2,1,0:T(8,128)(2,1)S(1)}, u32[]{:S(2)}, u32[]{:S(2)}) async-start(bf16[4,2048,128]{2,1,0:T(8,128)(2,1)} %bitcast.29), calls=%async_computation.2 | async-start | bytes 4194304 | tf_op jit(solution)/shard_map/all_to_all | solution.py:168
  95.5 18.8 %collective-permute-done.3 = bf16[4096,128]{1,0:T(8,128)(2,1)} collective-permute-done((bf16[4096,128]{1,0:T(8,128)(2,1)}, bf16[4096,128]{1,0:T(8,128)(2,1)}, u32[]{:S(2)}, u32[]{:S(2)}) %collective-permute-start.3) | collective-permute-done | bytes 1048608 | tf_op jit(solution)/shard_map/ppermute | solution.py:24
  114.3 2.5 %fusion.order_ref = bf16[4096,128]{1,0:T(8,128)(2,1)} fusion(bf16[4096,128]{1,0:T(8,128)(2,1)} %collective-permute-done.3, bf16[16,256,128]{2,1,0:T(8,128)(2,1)S(1)} %copy-done.3), kind=kLoop, calls=%fused_computation.1 | loop fusion | flops 2097152 | bytes 3145728 | tf_op jit(solution)/shard_map/convert_element_type | solution.py:172
  116.8 2.9 %all-to-all-done.2.got_ref = bf16[4,2048,128]{2,1,0:T(8,128)(2,1)S(1)} async-done(((bf16[4,2048,128]{2,1,0:T(8,128)(2,1)}), bf16[4,2048,128]{2,1,0:T(8,128)(2,1)S(1)}, u32[]{:S(2)}, u32[]{:S(2)}) %all-to-all-start.2) | async-done | bytes 2097184 | tf_op jit(solution)/shard_map/all_to_all | solution.py:168
  119.8 6.3 %all-to-all-start.3 = ((bf16[4,1024,128]{2,1,0:T(8,128)(2,1)}), bf16[4,1024,128]{2,1,0:T(8,128)(2,1)}, u32[]{:S(2)}, u32[]{:S(2)}) async-start(bf16[4,1024,128]{2,1,0:T(8,128)(2,1)} %bitcast.17), calls=%async_computation.3 | async-start | bytes 2097152 | tf_op jit(solution)/shard_map/all_to_all | solution.py:168
  126.3 2.2 %collective-permute-start.4 = (bf16[1024,128]{1,0:T(8,128)(2,1)S(1)}, bf16[1024,128]{1,0:T(8,128)(2,1)S(1)}, u32[]{:S(2)}, u32[]{:S(2)}) collective-permute-start(bf16[1024,128]{1,0:T(8,128)(2,1)S(1)} %get-tuple-element.18), channel_id=1, source_target_pairs={{0,64},{64,0},{1,65},{65,1},{2,66},{66,2},{3,67},{67,3},{4,68},{68... | collective-permute-start | bytes 786440 | tf_op jit(solution)/shard_map/ppermute | solution.py:24
  128.5 9.8 %all-to-all-done.3 = bf16[4,1024,128]{2,1,0:T(8,128)(2,1)} async-done(((bf16[4,1024,128]{2,1,0:T(8,128)(2,1)}), bf16[4,1024,128]{2,1,0:T(8,128)(2,1)}, u32[]{:S(2)}, u32[]{:S(2)}) %all-to-all-start.3) | async-done | bytes 1048608 | tf_op jit(solution)/shard_map/all_to_all | solution.py:168
  138.3 1.5 reduce_sum.21
  139.9 34.2 %all_to_all.25 = bf16[4,512,128]{2,1,0:T(8,128)(2,1)S(1)} all-to-all(bf16[4,512,128]{2,1,0:T(8,128)(2,1)S(1)} %pad_maximum_fusion), channel_id=1, replica_groups=mesh['z4'=4,'z2'=2,'x'=4,'y'=4,'zh'=2,'core'=2] {'z4'}, dimensions={0} | all-to-all | bytes 1048576 | tf_op jit(solution)/shard_map/all_to_all | solution.py:182
  174.1 0.8 convert_reduce_fusion
  (21 shorter events, 0.4 us)
Async XLA Ops:
  1.1 21.3 %copy-start.7 = (bf16[512,896]{1,0:T(8,128)(2,1)S(1)}, bf16[512,896]{1,0:T(8,128)(2,1)}, u32[]{:S(2)}) copy-start(bf16[512,896]{1,0:T(8,128)(2,1)} %param.7) | copy-start | bytes 2752516
  2.2 29.7 %all-to-all-start = ((bf16[4,2,128,512]{3,2,1,0:T(8,128)(2,1)}), bf16[4,2,128,512]{3,2,1,0:T(8,128)(2,1)S(1)}, u32[]{:S(2)}, u32[]{:S(2)}) async-start(bf16[4,2,128,512]{3,2,1,0:T(8,128)(2,1)} %broadcast_in_dim.14), calls=%async_computation | async-start | bytes 2097152 | tf_op jit(solution)/shard_map/all_to_all | solution.py:28
  6.6 28.1 %collective-permute-start.1 = (bf16[2,128,512]{2,1,0:T(8,128)(2,1)S(1)}, bf16[2,128,512]{2,1,0:T(8,128)(2,1)S(1)}, u32[]{:S(2)}, u32[]{:S(2)}) collective-permute-start(bf16[2,128,512]{2,1,0:T(8,128)(2,1)S(1)} %bitcast.35), channel_id=1, source_target_pairs={{0,2},{2,0},{1,3},{3,1},{4,6},{6,4},{5,7},{7,5},{8,10},{10,8},{9,1... | collective-permute-start | bytes 786440 | tf_op jit(solution)/shard_map/ppermute | solution.py:24
  26.6 5.3 %copy-start.5 = (s32[7,8]{1,0:T(8,128)S(1)}, s32[7,8]{1,0:T(8,128)}, u32[]{:S(2)}) copy-start(s32[7,8]{1,0:T(8,128)} %owner_ref.1) | copy-start | bytes 676
  31.9 27.8 %copy-start.6 = (s32[7,8]{1,0:T(8,128)S(1)}, s32[7,8]{1,0:T(8,128)}, u32[]{:S(2)}) copy-start(s32[7,8]{1,0:T(8,128)} %rows_ref.1) | copy-start | bytes 676
  35.8 19.2 %all-to-all-start.1 = ((bf16[4,2,128,512]{3,2,1,0:T(8,128)(2,1)}), bf16[4,2,128,512]{3,2,1,0:T(8,128)(2,1)}, u32[]{:S(2)}, u32[]{:S(2)}) async-start(bf16[4,2,128,512]{3,2,1,0:T(8,128)(2,1)} %broadcast_in_dim.15), calls=%async_computation.1 | async-start | bytes 2097152 | tf_op jit(solution)/shard_map/all_to_all | solution.py:28
  40.6 16.3 %collective-permute-start = (bf16[4,2,128,512]{3,2,1,0:T(8,128)(2,1)S(1)}, bf16[4,2,128,512]{3,2,1,0:T(8,128)(2,1)}, u32[]{:S(2)}, u32[]{:S(2)}) collective-permute-start(bf16[4,2,128,512]{3,2,1,0:T(8,128)(2,1)S(1)} %all-to-all-done.a_ref), channel_id=1, source_target_pairs={{0,1},{1,0},{2,3},{3,2},{4,5},{5,4},{6,7},{7,6},{8,9},{9,8},{10,11... | collective-permute-start | bytes 3145736 | tf_op jit(solution)/shard_map/ppermute | solution.py:24
  55.0 4.8 %collective-permute-start.2 = (bf16[4,2,128,512]{3,2,1,0:T(8,128)(2,1)}, bf16[4,2,128,512]{3,2,1,0:T(8,128)(2,1)S(1)}, u32[]{:S(2)}, u32[]{:S(2)}) collective-permute-start(bf16[4,2,128,512]{3,2,1,0:T(8,128)(2,1)} %all-to-all-done.1.b_ref), channel_id=1, source_target_pairs={{0,1},{1,0},{2,3},{3,2},{4,5},{5,4},{6,7},{7,6},{8,9},{9,8},{10,11... | collective-permute-start | bytes 3145736 | tf_op jit(solution)/shard_map/ppermute | solution.py:24
  59.7 1.5 copy-start.1
  61.2 1.2 copy-start.4
  75.0 1.3 copy-start
  76.3 1.0 copy-start.2
  77.3 37.0 %collective-permute-start.3 = (bf16[4096,128]{1,0:T(8,128)(2,1)}, bf16[4096,128]{1,0:T(8,128)(2,1)}, u32[]{:S(2)}, u32[]{:S(2)}) collective-permute-start(bf16[4096,128]{1,0:T(8,128)(2,1)} %bitcast.15), channel_id=1, source_target_pairs={{0,64},{64,0},{1,65},{65,1},{2,66},{66,2},{3,67},{67,3},{4,68},{68... | collective-permute-start | bytes 3145736 | tf_op jit(solution)/shard_map/ppermute | solution.py:24
  90.5 23.8 %copy-start.3 = (bf16[16,256,128]{2,1,0:T(8,128)(2,1)S(1)}, bf16[16,256,128]{2,1,0:T(8,128)(2,1)}, u32[]{:S(2)}) copy-start(bf16[16,256,128]{2,1,0:T(8,128)(2,1)} %copy-done.2) | copy-start | bytes 3145732
  90.6 29.2 %all-to-all-start.2 = ((bf16[4,2048,128]{2,1,0:T(8,128)(2,1)}), bf16[4,2048,128]{2,1,0:T(8,128)(2,1)S(1)}, u32[]{:S(2)}, u32[]{:S(2)}) async-start(bf16[4,2048,128]{2,1,0:T(8,128)(2,1)} %bitcast.29), calls=%async_computation.2 | async-start | bytes 4194304 | tf_op jit(solution)/shard_map/all_to_all | solution.py:168
  119.8 18.5 %all-to-all-start.3 = ((bf16[4,1024,128]{2,1,0:T(8,128)(2,1)}), bf16[4,1024,128]{2,1,0:T(8,128)(2,1)}, u32[]{:S(2)}, u32[]{:S(2)}) async-start(bf16[4,1024,128]{2,1,0:T(8,128)(2,1)} %bitcast.17), calls=%async_computation.3 | async-start | bytes 2097152 | tf_op jit(solution)/shard_map/all_to_all | solution.py:168
  126.3 13.5 %collective-permute-start.4 = (bf16[1024,128]{1,0:T(8,128)(2,1)S(1)}, bf16[1024,128]{1,0:T(8,128)(2,1)S(1)}, u32[]{:S(2)}, u32[]{:S(2)}) collective-permute-start(bf16[1024,128]{1,0:T(8,128)(2,1)S(1)} %get-tuple-element.18), channel_id=1, source_target_pairs={{0,64},{64,0},{1,65},{65,1},{2,66},{66,2},{3,67},{67,3},{4,68},{68... | collective-permute-start | bytes 786440 | tf_op jit(solution)/shard_map/ppermute | solution.py:24

commit v6 on v5

v6 whole, which is shorter than its diff:
```python
import functools

import jax
import jax.numpy as jnp
from jax import lax
from jax.experimental import pallas as pl
from jax.experimental.pallas import tpu as pltpu
from jax.sharding import Mesh, PartitionSpec as P

BS = 128
KB = 8
COLS = 7
BLOCKS = COLS * KB
TOK = 512
ROWS = 32
NX, NZ, CAP = 4, 8, 2
AXES = {"z8": 2, "z4": 2, "z2": 2, "x": 4, "y": 4, "zh": 2, "core": 2}
VMEM = pl.BlockSpec(memory_space=pltpu.VMEM)
HBM = pl.BlockSpec(memory_space=pltpu.HBM)
ANY = pl.BlockSpec(memory_space=pl.ANY)
SMEM = pl.BlockSpec(memory_space=pltpu.SMEM)


def swap(value, axis):
    return lax.ppermute(value, axis, [(0, 1), (1, 0)])


def shift(value, axis, step):
    size = AXES[axis]
    return lax.ppermute(value, axis, [(i, (i + step) % size) for i in range(size)])


def spread(value, axis):
    return lax.all_to_all(jnp.broadcast_to(value[None], (AXES[axis],) + value.shape), axis, 0, 0, tiled=True)


def call(kernel, out_shape, in_specs, out_specs, scratch=(), flops=0, bytes_accessed=0):
    return pl.pallas_call(
        kernel,
        out_shape=out_shape,
        in_specs=in_specs,
        out_specs=out_specs,
        scratch_shapes=list(scratch),
        compiler_params=pltpu.CompilerParams(vmem_limit_bytes=40 * 1024 * 1024),
        cost_estimate=pl.CostEstimate(flops=flops, bytes_accessed=bytes_accessed, transcendentals=0),
    )


def place_kernel(owner_ref, gate_ref, up_ref, hidden_ref, near_ref, place_ref, seen_ref):
    my_x = lax.axis_index("x")
    my_z = lax.axis_index("z8") * 4 + lax.axis_index("z4") * 2 + lax.axis_index("z2")

    def clear(i, carry):
        seen_ref[i] = jnp.int32(0)
        return carry

    lax.fori_loop(0, NX * NZ, clear, 0)

    def place(i, carry):
        owner = owner_ref[i // KB, i % KB]
        slot = seen_ref[owner]
        seen_ref[owner] = slot + 1
        x = (owner % NX - my_x + NX) % NX
        z = (owner // NX) ^ my_z
        other = z & 1
        rest = (z & 2) + (z >> 2)
        first = x * NZ + other * 4 + rest
        second = NX * NZ + (1 - other) * (NX * 4) + x * 4 + rest
        place_ref[i] = jnp.where(slot == 0, first, second)
        return carry

    lax.fori_loop(0, BLOCKS, place, 0)


def block_kernel(
    a_ref, ac_ref, b_ref, bc_ref, gate_ref, up_ref, hidden_ref, rows_ref, place_ref,
    send_ref, first0_ref, first1_ref, first2_ref, first3_ref, keep_ref, x_ref, w_ref, h_ref, picked_ref, out_ref, x_sem, w_sem, out_sem,
):
    zh = lax.axis_index("zh")
    core = lax.axis_index("core")
    x_copies = []
    for i, (ref, z, c) in enumerate(
        ((a_ref, zh, core), (ac_ref, zh, 1 - core), (b_ref, 1 - zh, core), (bc_ref, 1 - zh, 1 - core))
    ):
        for y in range(4):
            at = (y * 4 + z * 2 + c) * 2
            x_copies.append(pltpu.make_async_copy(ref.at[y], x_ref.at[pl.ds(at, 2)], x_sem.at[i * 4 + y]))
    w_copies = []
    for c in range(COLS):
        w_copies.append((
            pltpu.make_async_copy(gate_ref.at[c], w_ref.at[c, pl.ds(0, BS)], w_sem.at[3 * c]),
            pltpu.make_async_copy(up_ref.at[c], w_ref.at[c, pl.ds(BS, BS)], w_sem.at[3 * c + 1]),
            pltpu.make_async_copy(hidden_ref.at[c], h_ref.at[c], w_sem.at[3 * c + 2]),
        ))
    for copy in x_copies:
        copy.start()
    for copies in w_copies:
        for copy in copies:
            copy.start()
    out_ref[...] = jnp.zeros_like(out_ref)
    for copy in x_copies:
        copy.wait()
    for c in range(COLS):
        now_ref = picked_ref.at[c % 2]
        for k in range(KB):
            now_ref[k * BS:(k + 1) * BS] = x_ref[rows_ref[c, k]]
        for copy in w_copies[c]:
            copy.wait()
        picked = now_ref[...]
        pre = jnp.dot(w_ref[c], picked, preferred_element_type=jnp.float32)
        gate, up = pre[:BS], pre[BS:]
        s = jax.nn.sigmoid(gate)
        h = h_ref[c].astype(jnp.float32)
        grad_gate = (h * up * (s * (1.0 + gate * (1.0 - s)))).astype(jnp.bfloat16)
        grad_up = (h * (gate * s)).astype(jnp.bfloat16)
        value = lax.dot_general(
            picked, jnp.concatenate([grad_gate, grad_up], 0), (((1,), (1,)), ((), ())),
            preferred_element_type=jnp.float32,
        ).astype(jnp.bfloat16)
        for k in range(KB):
            for m in range(2):
                out_ref[place_ref[c * KB + k], m * BS:(m + 1) * BS] = value[k * BS:(k + 1) * BS, m * BS:(m + 1) * BS]
    places = [NX * NZ] + [i * NZ for i in range(NX)] + [NX * NZ + NX * 4]
    out_copies = []
    for i, ref in enumerate((send_ref, first0_ref, first1_ref, first2_ref, first3_ref, keep_ref)):
        out_copies.append(pltpu.make_async_copy(out_ref.at[pl.ds(places[i], ref.shape[0])], ref, out_sem.at[i]))
    for copy in out_copies:
        copy.start()
    for copy in out_copies:
        copy.wait()


def body(x_panel, grad_hidden, gate_blocks, up_blocks, block_rows, block_owner):
    bf16, f32 = jnp.bfloat16, jnp.float32
    own = x_panel.T.reshape(2, BS, TOK)
    far = swap(own, "zh")
    a = spread(own, "y")
    gate_t, up_t = (w.transpose(0, 3, 1, 2).reshape(COLS, BS, KB * BS) for w in (gate_blocks, up_blocks))
    hidden = grad_hidden.T.reshape(COLS, BS, TOK)
    corners = [v[0, :8] for v in (gate_t, up_t, hidden, a[0])]
    place = call(
        place_kernel, jax.ShapeDtypeStruct((BLOCKS,), jnp.int32), [SMEM] + [ANY] * 4, SMEM,
        [pltpu.SMEM((NX * NZ,), jnp.int32)],
    )(block_owner, *corners)
    ac = swap(a, "core")
    far, place = lax.optimization_barrier((far, place))
    b = spread(far, "y")
    bc = swap(b, "core")

    counts = (NX * 4, NZ, NZ, NZ, NZ, NX * 4)
    send, *firsts, keep = call(
        block_kernel, [jax.ShapeDtypeStruct((count, 2 * BS, BS), bf16) for count in counts],
        [HBM] * 7 + [SMEM, SMEM], [ANY] * 6,
        [
            pltpu.VMEM((ROWS, BS, TOK), bf16),
            pltpu.VMEM((COLS, 2 * BS, KB * BS), bf16),
            pltpu.VMEM((COLS, BS, TOK), bf16),
            pltpu.VMEM((2, KB * BS, TOK), bf16),
            pltpu.VMEM((NX * NZ * CAP, 2 * BS, BS), bf16),
            pltpu.SemaphoreType.DMA((16,)),
            pltpu.SemaphoreType.DMA((3 * COLS,)),
            pltpu.SemaphoreType.DMA((6,)),
        ],
        flops=8 * BLOCKS * BS * BS * TOK, bytes_accessed=14 * 2**20,
    )(a, ac, b, bc, gate_t, up_t, hidden, block_rows, place)

    def over_x(parts):
        parts = [parts[0]] + [shift(parts[i], "x", i) for i in range(1, NX)]
        return sum(part.astype(f32) for part in parts)

    def halve(keep, axis):
        half = keep.shape[0] // 2
        return keep[:half] + swap(keep[half:].astype(bf16), axis).astype(f32)

    got = swap(send.reshape(-1, BS), "z2").reshape(NX, -1, BS)
    keep = keep.reshape(NX, -1, BS)
    first = over_x([part.reshape(-1, BS) for part in firsts])
    second = over_x([(keep[i].astype(f32) + got[i].astype(f32)).astype(bf16) for i in range(NX)])
    first = halve(halve(halve(first, "z2"), "z4"), "z8")
    second = halve(halve(second, "z4"), "z8")
    return jnp.concatenate([first, second], 0).reshape(1, 1, CAP, 2, BS, BS)


def solution(mesh):
    fine = Mesh(mesh.devices.reshape(tuple(AXES.values())), tuple(AXES))
    dp, tensor = ("z8", "z4", "z2", "x"), ("y", "zh", "core")
    in_specs = (
        P(dp, tensor),
        P(dp, tensor),
        P(tensor, None, None, None),
        P(tensor, None, None, None),
        P(tensor, None),
        P(tensor, None),
    )
    out_specs = P(tensor, dp, None, None, None, None)
    return jax.shard_map(body, mesh=fine, in_specs=in_specs, out_specs=out_specs, check_vma=False)
```

time: 178 us -> 165 us (0.927)
  starting transfers between devices: 55.4 us -> 92.4 us
  blocking collectives: 34.2 us -> 0 us
  waiting for transfers between devices: 46.8 us -> 39 us
  other arithmetic: 4.83 us -> 1.55 us
  local copies, waits for them, and re-layouts: 17.8 us -> 15.6 us
    all_to_all x1 -> x0, blocking collectives: 34.2 us -> none  [body(): got = lax.all_to_all(both, 'z4', 0, 0, tiled=True)]
    ppermute x5 -> x9, starting transfers between devices: 34.9 us -> 62.9 us  [swap(): return lax.ppermute(value, axis, [(0, 1), (1, 0)])]
    ppermute x0 -> x6, starting transfers between devices: none -> 20.2 us  [shift(): lax.ppermute(value, axis, [(i, (i + step) % size) for i in range(size)])]
    ppermute x0 -> x6, waiting for transfers between devices: none -> 15.9 us  [shift(): lax.ppermute(value, axis, [(i, (i + step) % size) for i in range(size)])]
    all_to_all x2 -> x0, waiting for transfers between devices: 12.7 us -> none  [over_x(): return lax.all_to_all(value.reshape(NX, -1, BS), 'x', 0, 0, tiled=True)]
    all_to_all x2 -> x0, starting transfers between devices: 11.2 us -> none  [over_x(): return lax.all_to_all(value.reshape(NX, -1, BS), 'x', 0, 0, tiled=True)]
    ppermute x5 -> x9, waiting for transfers between devices: 21.7 us -> 10.7 us  [swap(): return lax.ppermute(value, axis, [(0, 1), (1, 0)])]
    unnamed x16 -> x10, local copies, waits for them, and re-layouts: 5.03 us -> 2.7 us
  transfers between devices with their start and end apart: 9 -> 17, of which waited for: 5 -> 7; matrix products, arithmetic and copies ran while one was open for 8% -> 6% of each run, Pallas kernels for 2% -> 2%
where the time goes in v6:
time: 165 us; the launch traced here: 163 us
  starting transfers between devices  92.4 us (56%)
  waiting for transfers between devices  39 us (24%)
  local copies, waits for them, and re-layouts  15.6 us (9%)
  Pallas kernels  14.5 us (9%)
    ppermute x9, starting transfers between devices, swap(): return lax.ppermute(value, axis, [(0, 1), (1, 0)])  62.9 us
    ppermute x6, starting transfers between devices, shift(): lax.ppermute(value, axis, [(i, (i + step) % size) for i in range(size)])  20.2 us
    ppermute x6, waiting for transfers between devices, shift(): lax.ppermute(value, axis, [(i, (i + step) % size) for i in range(size)])  15.9 us
    all_to_all x2, waiting for transfers between devices, spread(): lax.all_to_all(jnp.broadcast_to(value[None], (AXES[axis],) + value.shape)...  12.4 us
    pallas_call x1, Pallas kernels, body(): call(block_kernel, [jax.ShapeDtypeStruct((count, 2 * BS, BS), bf16) for c...  11.5 us
    ppermute x9, waiting for transfers between devices, swap(): return lax.ppermute(value, axis, [(0, 1), (1, 0)])  10.7 us
    all_to_all x2, starting transfers between devices, spread(): lax.all_to_all(jnp.broadcast_to(value[None], (AXES[axis],) + value.shape)...  9.26 us
    reshape x2, local copies, waits for them, and re-layouts, body(): w.transpose(0, 3, 1, 2).reshape(COLS, BS, KB * BS)  6.73 us
  transfers between devices with their start and end apart: 17, of which 7 were waited for; matrix products, arithmetic and copies ran while one was open for 6% of the time, Pallas kernels for 2%

profile of v6, /device:TPU:6, one launch (start us, length us, event | category | flops | bytes accessed | tf_op | source)
XLA Modules:
  0.0 163.5 jit_solution(18223801452934690123)
XLA Ops:
  0.0 1.1 copy.12
  1.1 1.1 broadcast_in_dim.14
  2.2 4.5 %all-to-all-start = ((bf16[4,2,128,512]{3,2,1,0:T(8,128)(2,1)}), bf16[4,2,128,512]{3,2,1,0:T(8,128)(2,1)S(1)}, u32[]{:S(2)}, u32[]{:S(2)}) async-start(bf16[4,2,128,512]{3,2,1,0:T(8,128)(2,1)} %broadcast_in_dim.14), calls=%async_computation | async-start | bytes 2097152 | tf_op jit(solution)/shard_map/all_to_all | solution.py:34
  6.7 15.7 %collective-permute-start.1 = (bf16[2,128,512]{2,1,0:T(8,128)(2,1)S(1)}, bf16[2,128,512]{2,1,0:T(8,128)(2,1)S(1)}, u32[]{:S(2)}, u32[]{:S(2)}) collective-permute-start(bf16[2,128,512]{2,1,0:T(8,128)(2,1)S(1)} %bitcast.49), channel_id=1, source_target_pairs={{0,2},{2,0},{1,3},{3,1},{4,6},{6,4},{5,7},{7,5},{8,10},{10,8},{9,1... | collective-permute-start | bytes 786440 | tf_op jit(solution)/shard_map/ppermute | solution.py:25
  22.4 1.4 copy.11
  23.8 2.9 %copy.13.gate_ref = bf16[7,128,1024]{2,1,0:T(8,128)(2,1)S(1)} copy(bf16[7,128,1024]{1,2,0:T(8,128)(2,1)} %bitcast.46) | data formatting | bytes 3670016 | tf_op jit(solution)/shard_map/reshape | solution.py:138
  26.7 3.8 %copy.14.up_ref = bf16[7,128,1024]{2,1,0:T(8,128)(2,1)} copy(bf16[7,128,1024]{1,2,0:T(8,128)(2,1)} %bitcast.47) | data formatting | bytes 3670016 | tf_op jit(solution)/shard_map/reshape | solution.py:138
  32.0 3.1 %shard_map.64.place_ref = s32[56]{0:T(128)S(1)} custom-call(s32[7,8]{1,0:T(8,128)S(1)} %copy-done.2, bf16[8,1024]{1,0:T(8,128)(2,1)S(1)} %get-tuple-element.29.gate_ref, bf16[8,1024]{1,0:T(8,128)(2,1)S(1)} %get-tuple-element.28.up_ref, bf16[8,512]{1,0:T(8,128)(2,1)S(1)} %slice_bitcast_fusion.4.hidden_ref, bf16[8,512]{1,0:T(8,128)(2,1)S(1)} %slice_bitcast_fusion.3.near_ref), custom_call_target="tpu_custom_call" | custom-call | tf_op jit(solution)/shard_map/pallas_call | solution.py:141
  36.2 4.8 %all-to-all-start.1 = ((bf16[4,2,128,512]{3,2,1,0:T(8,128)(2,1)}), bf16[4,2,128,512]{3,2,1,0:T(8,128)(2,1)}, u32[]{:S(2)}, u32[]{:S(2)}) async-start(bf16[4,2,128,512]{3,2,1,0:T(8,128)(2,1)} %broadcast_in_dim.15), calls=%async_computation.1 | async-start | bytes 2097152 | tf_op jit(solution)/shard_map/all_to_all | solution.py:34
  40.9 1.9 %collective-permute-start = (bf16[4,2,128,512]{3,2,1,0:T(8,128)(2,1)S(1)}, bf16[4,2,128,512]{3,2,1,0:T(8,128)(2,1)}, u32[]{:S(2)}, u32[]{:S(2)}) collective-permute-start(bf16[4,2,128,512]{3,2,1,0:T(8,128)(2,1)S(1)} %all-to-all-done.a_ref), channel_id=1, source_target_pairs={{0,1},{1,0},{2,3},{3,2},{4,5},{5,4},{6,7},{7,6},{8,9},{9,8},{10,11... | collective-permute-start | bytes 3145736 | tf_op jit(solution)/shard_map/ppermute | solution.py:25
  42.9 12.4 %all-to-all-done.1.b_ref = bf16[4,2,128,512]{3,2,1,0:T(8,128)(2,1)} async-done(((bf16[4,2,128,512]{3,2,1,0:T(8,128)(2,1)}), bf16[4,2,128,512]{3,2,1,0:T(8,128)(2,1)}, u32[]{:S(2)}, u32[]{:S(2)}) %all-to-all-start.1) | async-done | bytes 1048608 | tf_op jit(solution)/shard_map/all_to_all | solution.py:34
  55.3 1.9 %collective-permute-start.2 = (bf16[4,2,128,512]{3,2,1,0:T(8,128)(2,1)}, bf16[4,2,128,512]{3,2,1,0:T(8,128)(2,1)S(1)}, u32[]{:S(2)}, u32[]{:S(2)}) collective-permute-start(bf16[4,2,128,512]{3,2,1,0:T(8,128)(2,1)} %all-to-all-done.1.b_ref), channel_id=1, source_target_pairs={{0,1},{1,0},{2,3},{3,2},{4,5},{5,4},{6,7},{7,6},{8,9},{9,8},{10,11... | collective-permute-start | bytes 3145736 | tf_op jit(solution)/shard_map/ppermute | solution.py:25
  57.2 2.8 %collective-permute-done.2.bc_ref = bf16[4,2,128,512]{3,2,1,0:T(8,128)(2,1)S(1)} collective-permute-done((bf16[4,2,128,512]{3,2,1,0:T(8,128)(2,1)}, bf16[4,2,128,512]{3,2,1,0:T(8,128)(2,1)S(1)}, u32[]{:S(2)}, u32[]{:S(2)}) %collective-permute-start.2) | collective-permute-done | bytes 1048608 | tf_op jit(solution)/shard_map/ppermute | solution.py:25
  60.1 1.5 copy-done
  61.6 1.2 copy-done.1
  62.7 11.5 %shard_map.65 = (bf16[16,256,128]{2,1,0:T(8,128)(2,1)S(1)}, bf16[8,256,128]{2,1,0:T(8,128)(2,1)S(1)}, bf16[8,256,128]{2,1,0:T(8,128)(2,1)S(1)}, bf16[8,256,128]{...) custom-call(bf16[4,2,128,512]{3,2,1,0:T(8,128)(2,1)S(1)} %all-to-all-done.a_ref, ...), custom_call_target="tpu_custom_call" | custom-call | flops 3758096384 | bytes 14680064 | tf_op jit(solution)/shard_map/pallas_call | solution.py:151
  74.2 2.4 %collective-permute-start.3 = (bf16[2048,128]{1,0:T(8,128)(2,1)S(1)}, bf16[2048,128]{1,0:T(8,128)(2,1)S(1)}, u32[]{:S(2)}, u32[]{:S(2)}) collective-permute-start(bf16[2048,128]{1,0:T(8,128)(2,1)S(1)} %bitcast.45), channel_id=1, source_target_pairs={{0,16},{16,32},{32,48},{48,0},{1,17},{17,33},{33,49},{49,1},{2,18}... | collective-permute-start | bytes 1572872 | tf_op jit(solution)/shard_map/ppermute | solution.py:30
  76.6 4.3 %collective-permute-start.4 = (bf16[2048,128]{1,0:T(8,128)(2,1)S(1)}, bf16[2048,128]{1,0:T(8,128)(2,1)S(1)}, u32[]{:S(2)}, u32[]{:S(2)}) collective-permute-start(bf16[2048,128]{1,0:T(8,128)(2,1)S(1)} %bitcast.44), channel_id=1, source_target_pairs={{0,32},{16,48},{32,0},{48,16},{1,33},{17,49},{33,1},{49,17},{2,34}... | collective-permute-start | bytes 1572872 | tf_op jit(solution)/shard_map/ppermute | solution.py:30
  80.9 1.9 %collective-permute-start.5 = (bf16[2048,128]{1,0:T(8,128)(2,1)S(1)}, bf16[2048,128]{1,0:T(8,128)(2,1)S(1)}, u32[]{:S(2)}, u32[]{:S(2)}) collective-permute-start(bf16[2048,128]{1,0:T(8,128)(2,1)S(1)} %bitcast.43), channel_id=1, source_target_pairs={{0,48},{16,0},{32,16},{48,32},{1,49},{17,1},{33,17},{49,33},{2,50}... | collective-permute-start | bytes 1572872 | tf_op jit(solution)/shard_map/ppermute | solution.py:30
  82.9 12.9 %collective-permute-start.9 = (bf16[4096,128]{1,0:T(8,128)(2,1)S(1)}, bf16[4096,128]{1,0:T(8,128)(2,1)S(1)}, u32[]{:S(2)}, u32[]{:S(2)}) collective-permute-start(bf16[4096,128]{1,0:T(8,128)(2,1)S(1)} %bitcast.42), channel_id=1, source_target_pairs={{0,64},{64,0},{1,65},{65,1},{2,66},{66,2},{3,67},{67,3},{4,68},{68... | collective-permute-start | bytes 3145736 | tf_op jit(solution)/shard_map/ppermute | solution.py:25
  95.8 9.1 %collective-permute-done.5 = bf16[2048,128]{1,0:T(8,128)(2,1)S(1)} collective-permute-done((bf16[2048,128]{1,0:T(8,128)(2,1)S(1)}, bf16[2048,128]{1,0:T(8,128)(2,1)S(1)}, u32[]{:S(2)}, u32[]{:S(2)}) %collective-permute-start.5) | collective-permute-done | bytes 524320 | tf_op jit(solution)/shard_map/ppermute | solution.py:30
  105.2 12.9 %collective-permute-start.6 = (bf16[1024,128]{1,0:T(8,128)(2,1)S(1)}, bf16[1024,128]{1,0:T(8,128)(2,1)S(1)}, u32[]{:S(2)}, u32[]{:S(2)}) collective-permute-start(bf16[1024,128]{1,0:T(8,128)(2,1)S(1)} %slice.143), channel_id=1, source_target_pairs={{0,64},{64,0},{1,65},{65,1},{2,66},{66,2},{3,67},{67,3},{4,68},{68... | collective-permute-start | bytes 786440 | tf_op jit(solution)/shard_map/ppermute | solution.py:25
  118.9 6.3 %collective-permute-start.10 = (bf16[1024,128]{1,0:T(8,128)(2,1)S(1)}, bf16[1024,128]{1,0:T(8,128)(2,1)S(1)}, u32[]{:S(2)}, u32[]{:S(2)}) collective-permute-start(bf16[1024,128]{1,0:T(8,128)(2,1)S(1)} %get-tuple-element.25), channel_id=1, source_target_pairs={{0,16},{16,32},{32,48},{48,0},{1,17},{17,33},{33,49},{49,1},{2,18}... | collective-permute-start | bytes 786440 | tf_op jit(solution)/shard_map/ppermute | solution.py:30
  125.2 1.9 %collective-permute-start.12 = (bf16[1024,128]{1,0:T(8,128)(2,1)S(1)}, bf16[1024,128]{1,0:T(8,128)(2,1)S(1)}, u32[]{:S(2)}, u32[]{:S(2)}) collective-permute-start(bf16[1024,128]{1,0:T(8,128)(2,1)S(1)} %get-tuple-element.26), channel_id=1, source_target_pairs={{0,48},{16,0},{32,16},{48,32},{1,49},{17,1},{33,17},{49,33},{2,50}... | collective-permute-start | bytes 786440 | tf_op jit(solution)/shard_map/ppermute | solution.py:30
  127.1 3.4 %collective-permute-start.11 = (bf16[1024,128]{1,0:T(8,128)(2,1)S(1)}, bf16[1024,128]{1,0:T(8,128)(2,1)S(1)}, u32[]{:S(2)}, u32[]{:S(2)}) collective-permute-start(bf16[1024,128]{1,0:T(8,128)(2,1)S(1)} %get-tuple-element.27), channel_id=1, source_target_pairs={{0,32},{16,48},{32,0},{48,16},{1,33},{17,49},{33,1},{49,17},{2,34}... | collective-permute-start | bytes 786440 | tf_op jit(solution)/shard_map/ppermute | solution.py:30
  130.6 1.9 %collective-permute-start.7 = (bf16[512,128]{1,0:T(8,128)(2,1)S(1)}, bf16[512,128]{1,0:T(8,128)(2,1)S(1)}, u32[]{:S(2)}, u32[]{:S(2)}) collective-permute-start(bf16[512,128]{1,0:T(8,128)(2,1)S(1)} %slice.145), channel_id=1, source_target_pairs={{0,128},{128,0},{1,129},{129,1},{2,130},{130,2},{3,131},{131,3},{4... | collective-permute-start | bytes 393224 | tf_op jit(solution)/shard_map/ppermute | solution.py:25
  132.5 6.8 %collective-permute-done.12 = bf16[1024,128]{1,0:T(8,128)(2,1)S(1)} collective-permute-done((bf16[1024,128]{1,0:T(8,128)(2,1)S(1)}, bf16[1024,128]{1,0:T(8,128)(2,1)S(1)}, u32[]{:S(2)}, u32[]{:S(2)}) %collective-permute-start.12) | collective-permute-done | bytes 262176 | tf_op jit(solution)/shard_map/ppermute | solution.py:30
  139.6 1.9 %collective-permute-start.13 = (bf16[512,128]{1,0:T(8,128)(2,1)S(1)}, bf16[512,128]{1,0:T(8,128)(2,1)S(1)}, u32[]{:S(2)}, u32[]{:S(2)}) collective-permute-start(bf16[512,128]{1,0:T(8,128)(2,1)S(1)} %slice.144), channel_id=1, source_target_pairs={{0,128},{128,0},{1,129},{129,1},{2,130},{130,2},{3,131},{131,3},{4... | collective-permute-start | bytes 393224 | tf_op jit(solution)/shard_map/ppermute | solution.py:25
  141.6 9.5 %collective-permute-start.8 = (bf16[256,128]{1,0:T(8,128)(2,1)S(1)}, bf16[256,128]{1,0:T(8,128)(2,1)S(1)}, u32[]{:S(2)}, u32[]{:S(2)}) collective-permute-start(bf16[256,128]{1,0:T(8,128)(2,1)S(1)} %slice.147), channel_id=1, source_target_pairs={{0,256},{256,0},{1,257},{257,1},{2,258},{258,2},{3,259},{259,3},{4... | collective-permute-start | bytes 196616 | tf_op jit(solution)/shard_map/ppermute | solution.py:25
  151.1 4.3 %collective-permute-start.14 = (bf16[256,128]{1,0:T(8,128)(2,1)S(1)}, bf16[256,128]{1,0:T(8,128)(2,1)S(1)}, u32[]{:S(2)}, u32[]{:S(2)}) collective-permute-start(bf16[256,128]{1,0:T(8,128)(2,1)S(1)} %slice.146), channel_id=1, source_target_pairs={{0,256},{256,0},{1,257},{257,1},{2,258},{258,2},{3,259},{259,3},{4... | collective-permute-start | bytes 196616 | tf_op jit(solution)/shard_map/ppermute | solution.py:25
  155.4 2.4 %collective-permute-done.8 = bf16[256,128]{1,0:T(8,128)(2,1)S(1)} collective-permute-done((bf16[256,128]{1,0:T(8,128)(2,1)S(1)}, bf16[256,128]{1,0:T(8,128)(2,1)S(1)}, u32[]{:S(2)}, u32[]{:S(2)}) %collective-permute-start.8) | collective-permute-done | bytes 65568 | tf_op jit(solution)/shard_map/ppermute | solution.py:25
  157.8 4.9 %collective-permute-done.14 = bf16[256,128]{1,0:T(8,128)(2,1)S(1)} collective-permute-done((bf16[256,128]{1,0:T(8,128)(2,1)S(1)}, bf16[256,128]{1,0:T(8,128)(2,1)S(1)}, u32[]{:S(2)}, u32[]{:S(2)}) %collective-permute-start.14) | collective-permute-done | bytes 65568 | tf_op jit(solution)/shard_map/ppermute | solution.py:25
  (39 shorter events, 4.8 us)
Async XLA Ops:
  1.1 21.3 %copy-start.4 = (bf16[512,896]{1,0:T(8,128)(2,1)S(1)}, bf16[512,896]{1,0:T(8,128)(2,1)}, u32[]{:S(2)}) copy-start(bf16[512,896]{1,0:T(8,128)(2,1)} %param.7) | copy-start | bytes 2752516
  2.2 29.7 %all-to-all-start = ((bf16[4,2,128,512]{3,2,1,0:T(8,128)(2,1)}), bf16[4,2,128,512]{3,2,1,0:T(8,128)(2,1)S(1)}, u32[]{:S(2)}, u32[]{:S(2)}) async-start(bf16[4,2,128,512]{3,2,1,0:T(8,128)(2,1)} %broadcast_in_dim.14), calls=%async_computation | async-start | bytes 2097152 | tf_op jit(solution)/shard_map/all_to_all | solution.py:34
  6.7 28.4 %collective-permute-start.1 = (bf16[2,128,512]{2,1,0:T(8,128)(2,1)S(1)}, bf16[2,128,512]{2,1,0:T(8,128)(2,1)S(1)}, u32[]{:S(2)}, u32[]{:S(2)}) collective-permute-start(bf16[2,128,512]{2,1,0:T(8,128)(2,1)S(1)} %bitcast.49), channel_id=1, source_target_pairs={{0,2},{2,0},{1,3},{3,1},{4,6},{6,4},{5,7},{7,5},{8,10},{10,8},{9,1... | collective-permute-start | bytes 786440 | tf_op jit(solution)/shard_map/ppermute | solution.py:25
  26.7 5.3 %copy-start.2 = (s32[7,8]{1,0:T(8,128)S(1)}, s32[7,8]{1,0:T(8,128)}, u32[]{:S(2)}) copy-start(s32[7,8]{1,0:T(8,128)} %owner_ref.1) | copy-start | bytes 676
  32.0 28.1 %copy-start.3 = (s32[7,8]{1,0:T(8,128)S(1)}, s32[7,8]{1,0:T(8,128)}, u32[]{:S(2)}) copy-start(s32[7,8]{1,0:T(8,128)} %rows_ref.1) | copy-start | bytes 676
  36.2 19.2 %all-to-all-start.1 = ((bf16[4,2,128,512]{3,2,1,0:T(8,128)(2,1)}), bf16[4,2,128,512]{3,2,1,0:T(8,128)(2,1)}, u32[]{:S(2)}, u32[]{:S(2)}) async-start(bf16[4,2,128,512]{3,2,1,0:T(8,128)(2,1)} %broadcast_in_dim.15), calls=%async_computation.1 | async-start | bytes 2097152 | tf_op jit(solution)/shard_map/all_to_all | solution.py:34
  40.9 16.3 %collective-permute-start = (bf16[4,2,128,512]{3,2,1,0:T(8,128)(2,1)S(1)}, bf16[4,2,128,512]{3,2,1,0:T(8,128)(2,1)}, u32[]{:S(2)}, u32[]{:S(2)}) collective-permute-start(bf16[4,2,128,512]{3,2,1,0:T(8,128)(2,1)S(1)} %all-to-all-done.a_ref), channel_id=1, source_target_pairs={{0,1},{1,0},{2,3},{3,2},{4,5},{5,4},{6,7},{7,6},{8,9},{9,8},{10,11... | collective-permute-start | bytes 3145736 | tf_op jit(solution)/shard_map/ppermute | solution.py:25
  55.3 4.8 %collective-permute-start.2 = (bf16[4,2,128,512]{3,2,1,0:T(8,128)(2,1)}, bf16[4,2,128,512]{3,2,1,0:T(8,128)(2,1)S(1)}, u32[]{:S(2)}, u32[]{:S(2)}) collective-permute-start(bf16[4,2,128,512]{3,2,1,0:T(8,128)(2,1)} %all-to-all-done.1.b_ref), channel_id=1, source_target_pairs={{0,1},{1,0},{2,3},{3,2},{4,5},{5,4},{6,7},{7,6},{8,9},{9,8},{10,11... | collective-permute-start | bytes 3145736 | tf_op jit(solution)/shard_map/ppermute | solution.py:25
  60.1 1.5 copy-start
  61.6 1.2 copy-start.1
  74.2 21.6 %collective-permute-start.3 = (bf16[2048,128]{1,0:T(8,128)(2,1)S(1)}, bf16[2048,128]{1,0:T(8,128)(2,1)S(1)}, u32[]{:S(2)}, u32[]{:S(2)}) collective-permute-start(bf16[2048,128]{1,0:T(8,128)(2,1)S(1)} %bitcast.45), channel_id=1, source_target_pairs={{0,16},{16,32},{32,48},{48,0},{1,17},{17,33},{33,49},{49,1},{2,18}... | collective-permute-start | bytes 1572872 | tf_op jit(solution)/shard_map/ppermute | solution.py:30
  76.6 19.2 %collective-permute-start.4 = (bf16[2048,128]{1,0:T(8,128)(2,1)S(1)}, bf16[2048,128]{1,0:T(8,128)(2,1)S(1)}, u32[]{:S(2)}, u32[]{:S(2)}) collective-permute-start(bf16[2048,128]{1,0:T(8,128)(2,1)S(1)} %bitcast.44), channel_id=1, source_target_pairs={{0,32},{16,48},{32,0},{48,16},{1,33},{17,49},{33,1},{49,17},{2,34}... | collective-permute-start | bytes 1572872 | tf_op jit(solution)/shard_map/ppermute | solution.py:30
  80.9 24.0 %collective-permute-start.5 = (bf16[2048,128]{1,0:T(8,128)(2,1)S(1)}, bf16[2048,128]{1,0:T(8,128)(2,1)S(1)}, u32[]{:S(2)}, u32[]{:S(2)}) collective-permute-start(bf16[2048,128]{1,0:T(8,128)(2,1)S(1)} %bitcast.43), channel_id=1, source_target_pairs={{0,48},{16,0},{32,16},{48,32},{1,49},{17,1},{33,17},{49,33},{2,50}... | collective-permute-start | bytes 1572872 | tf_op jit(solution)/shard_map/ppermute | solution.py:30
  82.9 35.8 %collective-permute-start.9 = (bf16[4096,128]{1,0:T(8,128)(2,1)S(1)}, bf16[4096,128]{1,0:T(8,128)(2,1)S(1)}, u32[]{:S(2)}, u32[]{:S(2)}) collective-permute-start(bf16[4096,128]{1,0:T(8,128)(2,1)S(1)} %bitcast.42), channel_id=1, source_target_pairs={{0,64},{64,0},{1,65},{65,1},{2,66},{66,2},{3,67},{67,3},{4,68},{68... | collective-permute-start | bytes 3145736 | tf_op jit(solution)/shard_map/ppermute | solution.py:25
  105.2 25.3 %collective-permute-start.6 = (bf16[1024,128]{1,0:T(8,128)(2,1)S(1)}, bf16[1024,128]{1,0:T(8,128)(2,1)S(1)}, u32[]{:S(2)}, u32[]{:S(2)}) collective-permute-start(bf16[1024,128]{1,0:T(8,128)(2,1)S(1)} %slice.143), channel_id=1, source_target_pairs={{0,64},{64,0},{1,65},{65,1},{2,66},{66,2},{3,67},{67,3},{4,68},{68... | collective-permute-start | bytes 786440 | tf_op jit(solution)/shard_map/ppermute | solution.py:25
  118.9 13.6 %collective-permute-start.10 = (bf16[1024,128]{1,0:T(8,128)(2,1)S(1)}, bf16[1024,128]{1,0:T(8,128)(2,1)S(1)}, u32[]{:S(2)}, u32[]{:S(2)}) collective-permute-start(bf16[1024,128]{1,0:T(8,128)(2,1)S(1)} %get-tuple-element.25), channel_id=1, source_target_pairs={{0,16},{16,32},{32,48},{48,0},{1,17},{17,33},{33,49},{49,1},{2,18}... | collective-permute-start | bytes 786440 | tf_op jit(solution)/shard_map/ppermute | solution.py:30
  125.2 14.2 %collective-permute-start.12 = (bf16[1024,128]{1,0:T(8,128)(2,1)S(1)}, bf16[1024,128]{1,0:T(8,128)(2,1)S(1)}, u32[]{:S(2)}, u32[]{:S(2)}) collective-permute-start(bf16[1024,128]{1,0:T(8,128)(2,1)S(1)} %get-tuple-element.26), channel_id=1, source_target_pairs={{0,48},{16,0},{32,16},{48,32},{1,49},{17,1},{33,17},{49,33},{2,50}... | collective-permute-start | bytes 786440 | tf_op jit(solution)/shard_map/ppermute | solution.py:30
  127.1 12.2 %collective-permute-start.11 = (bf16[1024,128]{1,0:T(8,128)(2,1)S(1)}, bf16[1024,128]{1,0:T(8,128)(2,1)S(1)}, u32[]{:S(2)}, u32[]{:S(2)}) collective-permute-start(bf16[1024,128]{1,0:T(8,128)(2,1)S(1)} %get-tuple-element.27), channel_id=1, source_target_pairs={{0,32},{16,48},{32,0},{48,16},{1,33},{17,49},{33,1},{49,17},{2,34}... | collective-permute-start | bytes 786440 | tf_op jit(solution)/shard_map/ppermute | solution.py:30
  130.6 10.9 %collective-permute-start.7 = (bf16[512,128]{1,0:T(8,128)(2,1)S(1)}, bf16[512,128]{1,0:T(8,128)(2,1)S(1)}, u32[]{:S(2)}, u32[]{:S(2)}) collective-permute-start(bf16[512,128]{1,0:T(8,128)(2,1)S(1)} %slice.145), channel_id=1, source_target_pairs={{0,128},{128,0},{1,129},{129,1},{2,130},{130,2},{3,131},{131,3},{4... | collective-permute-start | bytes 393224 | tf_op jit(solution)/shard_map/ppermute | solution.py:25
  139.6 11.5 %collective-permute-start.13 = (bf16[512,128]{1,0:T(8,128)(2,1)S(1)}, bf16[512,128]{1,0:T(8,128)(2,1)S(1)}, u32[]{:S(2)}, u32[]{:S(2)}) collective-permute-start(bf16[512,128]{1,0:T(8,128)(2,1)S(1)} %slice.144), channel_id=1, source_target_pairs={{0,128},{128,0},{1,129},{129,1},{2,130},{130,2},{3,131},{131,3},{4... | collective-permute-start | bytes 393224 | tf_op jit(solution)/shard_map/ppermute | solution.py:25
  141.6 16.2 %collective-permute-start.8 = (bf16[256,128]{1,0:T(8,128)(2,1)S(1)}, bf16[256,128]{1,0:T(8,128)(2,1)S(1)}, u32[]{:S(2)}, u32[]{:S(2)}) collective-permute-start(bf16[256,128]{1,0:T(8,128)(2,1)S(1)} %slice.147), channel_id=1, source_target_pairs={{0,256},{256,0},{1,257},{257,1},{2,258},{258,2},{3,259},{259,3},{4... | collective-permute-start | bytes 196616 | tf_op jit(solution)/shard_map/ppermute | solution.py:25
  151.1 11.6 %collective-permute-start.14 = (bf16[256,128]{1,0:T(8,128)(2,1)S(1)}, bf16[256,128]{1,0:T(8,128)(2,1)S(1)}, u32[]{:S(2)}, u32[]{:S(2)}) collective-permute-start(bf16[256,128]{1,0:T(8,128)(2,1)S(1)} %slice.146), channel_id=1, source_target_pairs={{0,256},{256,0},{1,257},{257,1},{2,258},{258,2},{3,259},{259,3},{4... | collective-permute-start | bytes 196616 | tf_op jit(solution)/shard_map/ppermute | solution.py:25

commit v7 on v6

--- a/solution.py
+++ b/solution.py
@@ -14,6 +14,7 @@
 TOK = 512
 ROWS = 32
 NX, NZ, CAP = 4, 8, 2
+VMEM_MIB = 40
 AXES = {"z8": 2, "z4": 2, "z2": 2, "x": 4, "y": 4, "zh": 2, "core": 2}
 VMEM = pl.BlockSpec(memory_space=pltpu.VMEM)
 HBM = pl.BlockSpec(memory_space=pltpu.HBM)
@@ -34,14 +35,14 @@
     return lax.all_to_all(jnp.broadcast_to(value[None], (AXES[axis],) + value.shape), axis, 0, 0, tiled=True)
 
 
-def call(kernel, out_shape, in_specs, out_specs, scratch=(), flops=0, bytes_accessed=0):
+def call(kernel, out_shape, in_specs, out_specs, scratch=(), flops=0, bytes_accessed=0, vmem_mib=16):
     return pl.pallas_call(
         kernel,
         out_shape=out_shape,
         in_specs=in_specs,
         out_specs=out_specs,
         scratch_shapes=list(scratch),
-        compiler_params=pltpu.CompilerParams(vmem_limit_bytes=40 * 1024 * 1024),
+        compiler_params=pltpu.CompilerParams(vmem_limit_bytes=vmem_mib * 2**20),
         cost_estimate=pl.CostEstimate(flops=flops, bytes_accessed=bytes_accessed, transcendentals=0),
     )
 
@@ -74,7 +75,7 @@
 
 def block_kernel(
     a_ref, ac_ref, b_ref, bc_ref, gate_ref, up_ref, hidden_ref, rows_ref, place_ref,
-    send_ref, first0_ref, first1_ref, first2_ref, first3_ref, keep_ref, x_ref, w_ref, h_ref, picked_ref, out_ref, x_sem, w_sem, out_sem,
+    out_ref, send_ref, x_ref, w_ref, h_ref, picked_ref, x_sem, w_sem, out_sem,
 ):
     zh = lax.axis_index("zh")
     core = lax.axis_index("core")
@@ -120,14 +121,37 @@
         for k in range(KB):
             for m in range(2):
                 out_ref[place_ref[c * KB + k], m * BS:(m + 1) * BS] = value[k * BS:(k + 1) * BS, m * BS:(m + 1) * BS]
-    places = [NX * NZ] + [i * NZ for i in range(NX)] + [NX * NZ + NX * 4]
-    out_copies = []
-    for i, ref in enumerate((send_ref, first0_ref, first1_ref, first2_ref, first3_ref, keep_ref)):
-        out_copies.append(pltpu.make_async_copy(out_ref.at[pl.ds(places[i], ref.shape[0])], ref, out_sem.at[i]))
-    for copy in out_copies:
+    copy = pltpu.make_async_copy(out_ref.at[pl.ds(NX * NZ, NX * 4)], send_ref, out_sem)
+    copy.start()
+    copy.wait()
+
+
+def split_kernel(out_ref, *refs):
+    *refs, sem = refs
+    copies = []
+    for i, ref in enumerate(refs):
+        copies.append(pltpu.make_async_copy(out_ref.at[pl.ds((i + 1) * NZ, NZ)], ref, sem.at[i]))
+    for copy in copies:
         copy.start()
-    for copy in out_copies:
+    for copy in copies:
         copy.wait()
+
+
+def add_kernel(out_ref, got_ref, order1_ref, order2_ref, order3_ref, *refs):
+    for i, ref in enumerate(refs):
+        for j in range(4):
+            at = i * 4 + j
+            total = out_ref[NX * NZ + NX * 4 + at].astype(jnp.float32) + got_ref[at].astype(jnp.float32)
+            ref[j] = total.astype(ref.dtype)
+
+
+def sum_kernel(out_ref, got1_ref, got2_ref, got3_ref, order_ref, send_ref, keep_ref):
+    for ref, at in ((keep_ref, 0), (send_ref, NZ // 2)):
+        for i in range(NZ // 2):
+            total = out_ref[at + i].astype(jnp.float32)
+            for got_ref in (got1_ref, got2_ref, got3_ref):
+                total += got_ref[at + i].astype(jnp.float32)
+            ref[i] = total.astype(ref.dtype)
 
 
 def body(x_panel, grad_hidden, gate_blocks, up_blocks, block_rows, block_owner):
@@ -147,36 +171,47 @@
     b = spread(far, "y")
     bc = swap(b, "core")
 
-    counts = (NX * 4, NZ, NZ, NZ, NZ, NX * 4)
-    send, *firsts, keep = call(
-        block_kernel, [jax.ShapeDtypeStruct((count, 2 * BS, BS), bf16) for count in counts],
-        [HBM] * 7 + [SMEM, SMEM], [ANY] * 6,
+    def places(count):
+        return jax.ShapeDtypeStruct((count, 2 * BS, BS), bf16)
+
+    out, send = call(
+        block_kernel, (places(NX * NZ * CAP), places(NX * 4)), [HBM] * 7 + [SMEM, SMEM], (VMEM, ANY),
         [
             pltpu.VMEM((ROWS, BS, TOK), bf16),
             pltpu.VMEM((COLS, 2 * BS, KB * BS), bf16),
             pltpu.VMEM((COLS, BS, TOK), bf16),
             pltpu.VMEM((2, KB * BS, TOK), bf16),
-            pltpu.VMEM((NX * NZ * CAP, 2 * BS, BS), bf16),
             pltpu.SemaphoreType.DMA((16,)),
             pltpu.SemaphoreType.DMA((3 * COLS,)),
-            pltpu.SemaphoreType.DMA((6,)),
+            pltpu.SemaphoreType.DMA,
         ],
-        flops=8 * BLOCKS * BS * BS * TOK, bytes_accessed=14 * 2**20,
+        flops=8 * BLOCKS * BS * BS * TOK, bytes_accessed=14 * 2**20, vmem_mib=VMEM_MIB,
     )(a, ac, b, bc, gate_t, up_t, hidden, block_rows, place)
+    firsts = call(
+        split_kernel, [places(NZ)] * (NX - 1), [VMEM], [ANY] * (NX - 1),
+        [pltpu.SemaphoreType.DMA((NX - 1,))], bytes_accessed=3 * 2**20,
+    )(out)
 
     def over_x(parts):
-        parts = [parts[0]] + [shift(parts[i], "x", i) for i in range(1, NX)]
-        return sum(part.astype(f32) for part in parts)
+        return [shift(part, "x", i + 1) for i, part in enumerate(parts)]
 
     def halve(keep, axis):
         half = keep.shape[0] // 2
         return keep[:half] + swap(keep[half:].astype(bf16), axis).astype(f32)
 
-    got = swap(send.reshape(-1, BS), "z2").reshape(NX, -1, BS)
-    keep = keep.reshape(NX, -1, BS)
-    first = over_x([part.reshape(-1, BS) for part in firsts])
-    second = over_x([(keep[i].astype(f32) + got[i].astype(f32)).astype(bf16) for i in range(NX)])
-    first = halve(halve(halve(first, "z2"), "z4"), "z8")
+    got = swap(send, "z2")
+    first = over_x(firsts)
+    kept, *seconds = call(
+        add_kernel, [places(4)] * NX, [VMEM] * 2 + [ANY] * 3, [VMEM] * NX, bytes_accessed=3 * 2**20,
+    )(out, got, *first)
+    second = over_x(seconds)
+    send, first = call(
+        sum_kernel, (places(4), jax.ShapeDtypeStruct((4, 2 * BS, BS), f32)), [VMEM] * NX + [ANY], (VMEM, VMEM),
+        bytes_accessed=3 * 2**20,
+    )(out, *first, kept)
+    first = first + swap(send, "z2").astype(f32)
+    first = halve(halve(first, "z4"), "z8")
+    second = kept.astype(f32) + sum(part.astype(f32) for part in second)
     second = halve(halve(second, "z4"), "z8")
     return jnp.concatenate([first, second], 0).reshape(1, 1, CAP, 2, BS, BS)
 

time: 165 us -> 170 us (1.030)
  waiting for transfers between devices: 39 us -> 58.5 us
  starting transfers between devices: 92.4 us -> 78.6 us
    ppermute x6, waiting for transfers between devices: 15.9 us -> 28.9 us  [shift(): lax.ppermute(value, axis, [(i, (i + step) % size) for i in range(size)])]
    ppermute x9, starting transfers between devices: 62.9 us -> 51.1 us  [swap(): return lax.ppermute(value, axis, [(0, 1), (1, 0)])]
    ppermute x9, waiting for transfers between devices: 10.7 us -> 17.2 us  [swap(): return lax.ppermute(value, axis, [(0, 1), (1, 0)])]
    ppermute x6, starting transfers between devices: 20.2 us -> 18.2 us  [shift(): lax.ppermute(value, axis, [(i, (i + step) % size) for i in range(size)])]
    pallas_call x1 -> x4, Pallas kernels: 11.5 us -> 11.8 us  [the longest x1 11.2 us: body(): call(block_kernel, (places(NX * NZ * CAP), places(NX * 4)), [HBM] * 7 + [...]
  transfers between devices with their start and end apart: 17 -> 17, of which waited for: 7 -> 10; matrix products, arithmetic and copies ran while one was open for 6% -> 6% of each run, Pallas kernels for 2% -> 2%
where the time goes in v7:
time: 170 us; the launch traced here: 169 us
  starting transfers between devices  78.6 us (46%)
  waiting for transfers between devices  58.5 us (34%)
  local copies, waits for them, and re-layouts  15.5 us (9%)
  Pallas kernels  14.9 us (9%)
    ppermute x9, starting transfers between devices, swap(): return lax.ppermute(value, axis, [(0, 1), (1, 0)])  51.1 us
    ppermute x6, waiting for transfers between devices, shift(): lax.ppermute(value, axis, [(i, (i + step) % size) for i in range(size)])  28.9 us
    ppermute x6, starting transfers between devices, shift(): lax.ppermute(value, axis, [(i, (i + step) % size) for i in range(size)])  18.2 us
    ppermute x9, waiting for transfers between devices, swap(): return lax.ppermute(value, axis, [(0, 1), (1, 0)])  17.2 us
    all_to_all x2, waiting for transfers between devices, spread(): lax.all_to_all(jnp.broadcast_to(value[None], (AXES[axis],) + value.shape)...  12.4 us
    pallas_call x1, Pallas kernels, body(): call(block_kernel, (places(NX * NZ * CAP), places(NX * 4)), [HBM] * 7 + [...  11.2 us
    all_to_all x2, starting transfers between devices, spread(): lax.all_to_all(jnp.broadcast_to(value[None], (AXES[axis],) + value.shape)...  9.26 us
    reshape x2, local copies, waits for them, and re-layouts, body(): w.transpose(0, 3, 1, 2).reshape(COLS, BS, KB * BS)  6.73 us
  transfers between devices with their start and end apart: 17, of which 10 were waited for; matrix products, arithmetic and copies ran while one was open for 6% of the time, Pallas kernels for 2%

profile of v7, /device:TPU:6, one launch (start us, length us, event | category | flops | bytes accessed | tf_op | source)
XLA Modules:
  0.0 168.8 jit_solution(16227867510862581041)
XLA Ops:
  2.2 4.5 %all-to-all-start = ((bf16[4,2,128,512]{3,2,1,0:T(8,128)(2,1)}), bf16[4,2,128,512]{3,2,1,0:T(8,128)(2,1)S(1)}, u32[]{:S(2)}, u32[]{:S(2)}) async-start(bf16[4,2,128,512]{3,2,1,0:T(8,128)(2,1)} %broadcast_in_dim.14), calls=%async_computation | async-start | bytes 2097152 | tf_op jit(solution)/shard_map/all_to_all | solution.py:35
  6.6 15.7 %collective-permute-start.1 = (bf16[2,128,512]{2,1,0:T(8,128)(2,1)S(1)}, bf16[2,128,512]{2,1,0:T(8,128)(2,1)S(1)}, u32[]{:S(2)}, u32[]{:S(2)}) collective-permute-start(bf16[2,128,512]{2,1,0:T(8,128)(2,1)S(1)} %bitcast.26), channel_id=1, source_target_pairs={{0,2},{2,0},{1,3},{3,1},{4,6},{6,4},{5,7},{7,5},{8,10},{10,8},{9,1... | collective-permute-start | bytes 786440 | tf_op jit(solution)/shard_map/ppermute | solution.py:26
  23.7 2.9 %copy.13.gate_ref = bf16[7,128,1024]{2,1,0:T(8,128)(2,1)S(1)} copy(bf16[7,128,1024]{1,2,0:T(8,128)(2,1)} %bitcast.23) | data formatting | bytes 3670016 | tf_op jit(solution)/shard_map/reshape | solution.py:162
  26.7 3.8 %copy.14.up_ref = bf16[7,128,1024]{2,1,0:T(8,128)(2,1)} copy(bf16[7,128,1024]{1,2,0:T(8,128)(2,1)} %bitcast.24) | data formatting | bytes 3670016 | tf_op jit(solution)/shard_map/reshape | solution.py:162
  32.0 3.1 %shard_map.64.place_ref = s32[56]{0:T(128)S(1)} custom-call(s32[7,8]{1,0:T(8,128)S(1)} %copy-done.2, bf16[8,1024]{1,0:T(8,128)(2,1)S(1)} %get-tuple-element.32.gate_ref, bf16[8,1024]{1,0:T(8,128)(2,1)S(1)} %get-tuple-element.31.up_ref, bf16[8,512]{1,0:T(8,128)(2,1)S(1)} %slice_bitcast_fusion.4.hidden_ref, bf16[8,512]{1,0:T(8,128)(2,1)S(1)} %slice_bitcast_fusion.3.near_ref), custom_call_target="tpu_custom_call" | custom-call | tf_op jit(solution)/shard_map/pallas_call | solution.py:165
  36.1 4.8 %all-to-all-start.1 = ((bf16[4,2,128,512]{3,2,1,0:T(8,128)(2,1)}), bf16[4,2,128,512]{3,2,1,0:T(8,128)(2,1)}, u32[]{:S(2)}, u32[]{:S(2)}) async-start(bf16[4,2,128,512]{3,2,1,0:T(8,128)(2,1)} %broadcast_in_dim.15), calls=%async_computation.1 | async-start | bytes 2097152 | tf_op jit(solution)/shard_map/all_to_all | solution.py:35
  40.9 1.9 %collective-permute-start = (bf16[4,2,128,512]{3,2,1,0:T(8,128)(2,1)S(1)}, bf16[4,2,128,512]{3,2,1,0:T(8,128)(2,1)}, u32[]{:S(2)}, u32[]{:S(2)}) collective-permute-start(bf16[4,2,128,512]{3,2,1,0:T(8,128)(2,1)S(1)} %all-to-all-done.a_ref), channel_id=1, source_target_pairs={{0,1},{1,0},{2,3},{3,2},{4,5},{5,4},{6,7},{7,6},{8,9},{9,8},{10,11... | collective-permute-start | bytes 3145736 | tf_op jit(solution)/shard_map/ppermute | solution.py:26
  42.8 12.4 %all-to-all-done.1.b_ref = bf16[4,2,128,512]{3,2,1,0:T(8,128)(2,1)} async-done(((bf16[4,2,128,512]{3,2,1,0:T(8,128)(2,1)}), bf16[4,2,128,512]{3,2,1,0:T(8,128)(2,1)}, u32[]{:S(2)}, u32[]{:S(2)}) %all-to-all-start.1) | async-done | bytes 1048608 | tf_op jit(solution)/shard_map/all_to_all | solution.py:35
  55.3 1.9 %collective-permute-start.2 = (bf16[4,2,128,512]{3,2,1,0:T(8,128)(2,1)}, bf16[4,2,128,512]{3,2,1,0:T(8,128)(2,1)S(1)}, u32[]{:S(2)}, u32[]{:S(2)}) collective-permute-start(bf16[4,2,128,512]{3,2,1,0:T(8,128)(2,1)} %all-to-all-done.1.b_ref), channel_id=1, source_target_pairs={{0,1},{1,0},{2,3},{3,2},{4,5},{5,4},{6,7},{7,6},{8,9},{9,8},{10,11... | collective-permute-start | bytes 3145736 | tf_op jit(solution)/shard_map/ppermute | solution.py:26
  57.2 2.8 %collective-permute-done.2.bc_ref = bf16[4,2,128,512]{3,2,1,0:T(8,128)(2,1)S(1)} collective-permute-done((bf16[4,2,128,512]{3,2,1,0:T(8,128)(2,1)}, bf16[4,2,128,512]{3,2,1,0:T(8,128)(2,1)S(1)}, u32[]{:S(2)}, u32[]{:S(2)}) %collective-permute-start.2) | collective-permute-done | bytes 1048608 | tf_op jit(solution)/shard_map/ppermute | solution.py:26
  60.0 1.5 copy-done
  62.7 11.2 %shard_map.65 = (bf16[64,256,128]{2,1,0:T(8,128)(2,1)S(1)}, bf16[16,256,128]{2,1,0:T(8,128)(2,1)S(1)}) custom-call(bf16[4,2,128,512]{3,2,1,0:T(8,128)(2,1)S(1)} %all-to-all-done.a_ref, bf16[4,2,128,512]{3,2,1,0:T(8,128)(2,1)} %collective-permute-done.ac_ref, bf16[4,2,128,512]{3,2,1,0:T(8,128)(2,1)} %all-to-all-done.1.b_ref, ...), custom_call_target="tpu_custom_call" | custom-call | flops 3758096384 | bytes 14680064 | tf_op jit(solution)/shard_map/pallas_call | solution.py:177
  73.9 12.9 %collective-permute-start.6 = (bf16[16,256,128]{2,1,0:T(8,128)(2,1)S(1)}, bf16[16,256,128]{2,1,0:T(8,128)(2,1)S(1)}, u32[]{:S(2)}, u32[]{:S(2)}) collective-permute-start(bf16[16,256,128]{2,1,0:T(8,128)(2,1)S(1)} %get-tuple-element.24), channel_id=1, source_target_pairs={{0,64},{64,0},{1,65},{65,1},{2,66},{66,2},{3,67},{67,3},{4,68},{68... | collective-permute-start | bytes 3145736 | tf_op jit(solution)/shard_map/ppermute | solution.py:26
  87.0 2.4 %collective-permute-start.3 = (bf16[8,256,128]{2,1,0:T(8,128)(2,1)S(1)}, bf16[8,256,128]{2,1,0:T(8,128)(2,1)S(1)}, u32[]{:S(2)}, u32[]{:S(2)}) collective-permute-start(bf16[8,256,128]{2,1,0:T(8,128)(2,1)S(1)} %get-tuple-element.21), channel_id=1, source_target_pairs={{0,16},{16,32},{32,48},{48,0},{1,17},{17,33},{33,49},{49,1},{2,18}... | collective-permute-start | bytes 1572872 | tf_op jit(solution)/shard_map/ppermute | solution.py:31
  89.3 4.3 %collective-permute-start.4 = (bf16[8,256,128]{2,1,0:T(8,128)(2,1)S(1)}, bf16[8,256,128]{2,1,0:T(8,128)(2,1)S(1)}, u32[]{:S(2)}, u32[]{:S(2)}) collective-permute-start(bf16[8,256,128]{2,1,0:T(8,128)(2,1)S(1)} %get-tuple-element.22), channel_id=1, source_target_pairs={{0,32},{16,48},{32,0},{48,16},{1,33},{17,49},{33,1},{49,17},{2,34}... | collective-permute-start | bytes 1572872 | tf_op jit(solution)/shard_map/ppermute | solution.py:31
  93.7 1.9 %collective-permute-start.5 = (bf16[8,256,128]{2,1,0:T(8,128)(2,1)S(1)}, bf16[8,256,128]{2,1,0:T(8,128)(2,1)S(1)}, u32[]{:S(2)}, u32[]{:S(2)}) collective-permute-start(bf16[8,256,128]{2,1,0:T(8,128)(2,1)S(1)} %get-tuple-element.23), channel_id=1, source_target_pairs={{0,48},{16,0},{32,16},{48,32},{1,49},{17,1},{33,17},{49,33},{2,50}... | collective-permute-start | bytes 1572872 | tf_op jit(solution)/shard_map/ppermute | solution.py:31
  95.6 8.1 %collective-permute-done.3.order1_ref.got1_ref = bf16[8,256,128]{2,1,0:T(8,128)(2,1)S(1)} collective-permute-done((bf16[8,256,128]{2,1,0:T(8,128)(2,1)S(1)}, bf16[8,256,128]{2,1,0:T(8,128)(2,1)S(1)}, u32[]{:S(2)}, u32[]{:S(2)}) %collective-permute-start.3) | collective-permute-done | bytes 524320 | tf_op jit(solution)/shard_map/ppermute | solution.py:31
  103.7 4.0 %collective-permute-done.4.order2_ref.got2_ref = bf16[8,256,128]{2,1,0:T(8,128)(2,1)S(1)} collective-permute-done((bf16[8,256,128]{2,1,0:T(8,128)(2,1)S(1)}, bf16[8,256,128]{2,1,0:T(8,128)(2,1)S(1)}, u32[]{:S(2)}, u32[]{:S(2)}) %collective-permute-start.4) | collective-permute-done | bytes 524320 | tf_op jit(solution)/shard_map/ppermute | solution.py:31
  107.6 9.7 %collective-permute-done.5.order3_ref.got3_ref = bf16[8,256,128]{2,1,0:T(8,128)(2,1)S(1)} collective-permute-done((bf16[8,256,128]{2,1,0:T(8,128)(2,1)S(1)}, bf16[8,256,128]{2,1,0:T(8,128)(2,1)S(1)}, u32[]{:S(2)}, u32[]{:S(2)}) %collective-permute-start.5) | collective-permute-done | bytes 524320 | tf_op jit(solution)/shard_map/ppermute | solution.py:31
  117.6 2.5 %collective-permute-start.10 = (bf16[4,256,128]{2,1,0:T(8,128)(2,1)S(1)}, bf16[4,256,128]{2,1,0:T(8,128)(2,1)S(1)}, u32[]{:S(2)}, u32[]{:S(2)}) collective-permute-start(bf16[4,256,128]{2,1,0:T(8,128)(2,1)S(1)} %get-tuple-element.28), channel_id=1, source_target_pairs={{0,16},{16,32},{32,48},{48,0},{1,17},{17,33},{33,49},{49,1},{2,18}... | collective-permute-start | bytes 786440 | tf_op jit(solution)/shard_map/ppermute | solution.py:31
  120.1 4.3 %collective-permute-start.11 = (bf16[4,256,128]{2,1,0:T(8,128)(2,1)S(1)}, bf16[4,256,128]{2,1,0:T(8,128)(2,1)S(1)}, u32[]{:S(2)}, u32[]{:S(2)}) collective-permute-start(bf16[4,256,128]{2,1,0:T(8,128)(2,1)S(1)} %get-tuple-element.29), channel_id=1, source_target_pairs={{0,32},{16,48},{32,0},{48,16},{1,33},{17,49},{33,1},{49,17},{2,34}... | collective-permute-start | bytes 786440 | tf_op jit(solution)/shard_map/ppermute | solution.py:31
  124.5 2.7 %collective-permute-start.12 = (bf16[4,256,128]{2,1,0:T(8,128)(2,1)S(1)}, bf16[4,256,128]{2,1,0:T(8,128)(2,1)S(1)}, u32[]{:S(2)}, u32[]{:S(2)}) collective-permute-start(bf16[4,256,128]{2,1,0:T(8,128)(2,1)S(1)} %get-tuple-element.30), channel_id=1, source_target_pairs={{0,48},{16,0},{32,16},{48,32},{1,49},{17,1},{33,17},{49,33},{2,50}... | collective-permute-start | bytes 786440 | tf_op jit(solution)/shard_map/ppermute | solution.py:31
  127.5 2.2 %collective-permute-start.7 = (bf16[4,256,128]{2,1,0:T(8,128)(2,1)S(1)}, bf16[4,256,128]{2,1,0:T(8,128)(2,1)S(1)}, u32[]{:S(2)}, u32[]{:S(2)}) collective-permute-start(bf16[4,256,128]{2,1,0:T(8,128)(2,1)S(1)} %get-tuple-element.27), channel_id=1, source_target_pairs={{0,64},{64,0},{1,65},{65,1},{2,66},{66,2},{3,67},{67,3},{4,68},{68... | collective-permute-start | bytes 786440 | tf_op jit(solution)/shard_map/ppermute | solution.py:26
  129.7 3.1 %collective-permute-done.11 = bf16[4,256,128]{2,1,0:T(8,128)(2,1)S(1)} collective-permute-done((bf16[4,256,128]{2,1,0:T(8,128)(2,1)S(1)}, bf16[4,256,128]{2,1,0:T(8,128)(2,1)S(1)}, u32[]{:S(2)}, u32[]{:S(2)}) %collective-permute-start.11) | collective-permute-done | bytes 262176 | tf_op jit(solution)/shard_map/ppermute | solution.py:31
  132.8 4.0 %collective-permute-done.12 = bf16[4,256,128]{2,1,0:T(8,128)(2,1)S(1)} collective-permute-done((bf16[4,256,128]{2,1,0:T(8,128)(2,1)S(1)}, bf16[4,256,128]{2,1,0:T(8,128)(2,1)S(1)}, u32[]{:S(2)}, u32[]{:S(2)}) %collective-permute-start.12) | collective-permute-done | bytes 262176 | tf_op jit(solution)/shard_map/ppermute | solution.py:31
  137.0 1.9 %collective-permute-start.13 = (bf16[2,256,128]{2,1,0:T(8,128)(2,1)S(1)}, bf16[2,256,128]{2,1,0:T(8,128)(2,1)S(1)}, u32[]{:S(2)}, u32[]{:S(2)}) collective-permute-start(bf16[2,256,128]{2,1,0:T(8,128)(2,1)S(1)} %slice.82), channel_id=1, source_target_pairs={{0,128},{128,0},{1,129},{129,1},{2,130},{130,2},{3,131},{131,3},{4... | collective-permute-start | bytes 393224 | tf_op jit(solution)/shard_map/ppermute | solution.py:26
  139.0 4.8 %collective-permute-start.8 = (bf16[2,256,128]{2,1,0:T(8,128)(2,1)S(1)}, bf16[2,256,128]{2,1,0:T(8,128)(2,1)S(1)}, u32[]{:S(2)}, u32[]{:S(2)}) collective-permute-start(bf16[2,256,128]{2,1,0:T(8,128)(2,1)S(1)} %slice.83), channel_id=1, source_target_pairs={{0,128},{128,0},{1,129},{129,1},{2,130},{130,2},{3,131},{131,3},{4... | collective-permute-start | bytes 393224 | tf_op jit(solution)/shard_map/ppermute | solution.py:26
  143.8 6.3 %collective-permute-done.13 = bf16[2,256,128]{2,1,0:T(8,128)(2,1)S(1)} collective-permute-done((bf16[2,256,128]{2,1,0:T(8,128)(2,1)S(1)}, bf16[2,256,128]{2,1,0:T(8,128)(2,1)S(1)}, u32[]{:S(2)}, u32[]{:S(2)}) %collective-permute-start.13) | collective-permute-done | bytes 131104 | tf_op jit(solution)/shard_map/ppermute | solution.py:26
  150.1 6.9 %collective-permute-start.14 = (bf16[1,256,128]{2,1,0:T(8,128)(2,1)S(1)}, bf16[1,256,128]{2,1,0:T(8,128)(2,1)S(1)}, u32[]{:S(2)}, u32[]{:S(2)}) collective-permute-start(bf16[1,256,128]{2,1,0:T(8,128)(2,1)S(1)} %slice.84), channel_id=1, source_target_pairs={{0,256},{256,0},{1,257},{257,1},{2,258},{258,2},{3,259},{259,3},{4... | collective-permute-start | bytes 196616 | tf_op jit(solution)/shard_map/ppermute | solution.py:26
  157.1 2.9 %collective-permute-start.9 = (bf16[1,256,128]{2,1,0:T(8,128)(2,1)S(1)}, bf16[1,256,128]{2,1,0:T(8,128)(2,1)S(1)}, u32[]{:S(2)}, u32[]{:S(2)}) collective-permute-start(bf16[1,256,128]{2,1,0:T(8,128)(2,1)S(1)} %slice.85), channel_id=1, source_target_pairs={{0,256},{256,0},{1,257},{257,1},{2,258},{258,2},{3,259},{259,3},{4... | collective-permute-start | bytes 196616 | tf_op jit(solution)/shard_map/ppermute | solution.py:26
  159.9 3.0 %collective-permute-done.14 = bf16[1,256,128]{2,1,0:T(8,128)(2,1)S(1)} collective-permute-done((bf16[1,256,128]{2,1,0:T(8,128)(2,1)S(1)}, bf16[1,256,128]{2,1,0:T(8,128)(2,1)S(1)}, u32[]{:S(2)}, u32[]{:S(2)}) %collective-permute-start.14) | collective-permute-done | bytes 65568 | tf_op jit(solution)/shard_map/ppermute | solution.py:26
  163.0 5.1 %collective-permute-done.9 = bf16[1,256,128]{2,1,0:T(8,128)(2,1)S(1)} collective-permute-done((bf16[1,256,128]{2,1,0:T(8,128)(2,1)S(1)}, bf16[1,256,128]{2,1,0:T(8,128)(2,1)S(1)}, u32[]{:S(2)}, u32[]{:S(2)}) %collective-permute-start.9) | collective-permute-done | bytes 65568 | tf_op jit(solution)/shard_map/ppermute | solution.py:26
  (38 shorter events, 8.9 us)
Async XLA Ops:
  1.1 21.3 %copy-start.4 = (bf16[512,896]{1,0:T(8,128)(2,1)S(1)}, bf16[512,896]{1,0:T(8,128)(2,1)}, u32[]{:S(2)}) copy-start(bf16[512,896]{1,0:T(8,128)(2,1)} %param.7) | copy-start | bytes 2752516
  2.2 29.7 %all-to-all-start = ((bf16[4,2,128,512]{3,2,1,0:T(8,128)(2,1)}), bf16[4,2,128,512]{3,2,1,0:T(8,128)(2,1)S(1)}, u32[]{:S(2)}, u32[]{:S(2)}) async-start(bf16[4,2,128,512]{3,2,1,0:T(8,128)(2,1)} %broadcast_in_dim.14), calls=%async_computation | async-start | bytes 2097152 | tf_op jit(solution)/shard_map/all_to_all | solution.py:35
  6.6 28.4 %collective-permute-start.1 = (bf16[2,128,512]{2,1,0:T(8,128)(2,1)S(1)}, bf16[2,128,512]{2,1,0:T(8,128)(2,1)S(1)}, u32[]{:S(2)}, u32[]{:S(2)}) collective-permute-start(bf16[2,128,512]{2,1,0:T(8,128)(2,1)S(1)} %bitcast.26), channel_id=1, source_target_pairs={{0,2},{2,0},{1,3},{3,1},{4,6},{6,4},{5,7},{7,5},{8,10},{10,8},{9,1... | collective-permute-start | bytes 786440 | tf_op jit(solution)/shard_map/ppermute | solution.py:26
  26.6 5.3 %copy-start.2 = (s32[7,8]{1,0:T(8,128)S(1)}, s32[7,8]{1,0:T(8,128)}, u32[]{:S(2)}) copy-start(s32[7,8]{1,0:T(8,128)} %owner_ref.1) | copy-start | bytes 676
  31.9 28.1 %copy-start.3 = (s32[7,8]{1,0:T(8,128)S(1)}, s32[7,8]{1,0:T(8,128)}, u32[]{:S(2)}) copy-start(s32[7,8]{1,0:T(8,128)} %rows_ref.1) | copy-start | bytes 676
  36.1 19.2 %all-to-all-start.1 = ((bf16[4,2,128,512]{3,2,1,0:T(8,128)(2,1)}), bf16[4,2,128,512]{3,2,1,0:T(8,128)(2,1)}, u32[]{:S(2)}, u32[]{:S(2)}) async-start(bf16[4,2,128,512]{3,2,1,0:T(8,128)(2,1)} %broadcast_in_dim.15), calls=%async_computation.1 | async-start | bytes 2097152 | tf_op jit(solution)/shard_map/all_to_all | solution.py:35
  40.9 16.3 %collective-permute-start = (bf16[4,2,128,512]{3,2,1,0:T(8,128)(2,1)S(1)}, bf16[4,2,128,512]{3,2,1,0:T(8,128)(2,1)}, u32[]{:S(2)}, u32[]{:S(2)}) collective-permute-start(bf16[4,2,128,512]{3,2,1,0:T(8,128)(2,1)S(1)} %all-to-all-done.a_ref), channel_id=1, source_target_pairs={{0,1},{1,0},{2,3},{3,2},{4,5},{5,4},{6,7},{7,6},{8,9},{9,8},{10,11... | collective-permute-start | bytes 3145736 | tf_op jit(solution)/shard_map/ppermute | solution.py:26
  55.3 4.8 %collective-permute-start.2 = (bf16[4,2,128,512]{3,2,1,0:T(8,128)(2,1)}, bf16[4,2,128,512]{3,2,1,0:T(8,128)(2,1)S(1)}, u32[]{:S(2)}, u32[]{:S(2)}) collective-permute-start(bf16[4,2,128,512]{3,2,1,0:T(8,128)(2,1)} %all-to-all-done.1.b_ref), channel_id=1, source_target_pairs={{0,1},{1,0},{2,3},{3,2},{4,5},{5,4},{6,7},{7,6},{8,9},{9,8},{10,11... | collective-permute-start | bytes 3145736 | tf_op jit(solution)/shard_map/ppermute | solution.py:26
  60.0 1.5 copy-start
  61.5 1.2 copy-start.1
  73.9 43.5 %collective-permute-start.6 = (bf16[16,256,128]{2,1,0:T(8,128)(2,1)S(1)}, bf16[16,256,128]{2,1,0:T(8,128)(2,1)S(1)}, u32[]{:S(2)}, u32[]{:S(2)}) collective-permute-start(bf16[16,256,128]{2,1,0:T(8,128)(2,1)S(1)} %get-tuple-element.24), channel_id=1, source_target_pairs={{0,64},{64,0},{1,65},{65,1},{2,66},{66,2},{3,67},{67,3},{4,68},{68... | collective-permute-start | bytes 3145736 | tf_op jit(solution)/shard_map/ppermute | solution.py:26
  87.0 16.7 %collective-permute-start.3 = (bf16[8,256,128]{2,1,0:T(8,128)(2,1)S(1)}, bf16[8,256,128]{2,1,0:T(8,128)(2,1)S(1)}, u32[]{:S(2)}, u32[]{:S(2)}) collective-permute-start(bf16[8,256,128]{2,1,0:T(8,128)(2,1)S(1)} %get-tuple-element.21), channel_id=1, source_target_pairs={{0,16},{16,32},{32,48},{48,0},{1,17},{17,33},{33,49},{49,1},{2,18}... | collective-permute-start | bytes 1572872 | tf_op jit(solution)/shard_map/ppermute | solution.py:31
  89.3 18.3 %collective-permute-start.4 = (bf16[8,256,128]{2,1,0:T(8,128)(2,1)S(1)}, bf16[8,256,128]{2,1,0:T(8,128)(2,1)S(1)}, u32[]{:S(2)}, u32[]{:S(2)}) collective-permute-start(bf16[8,256,128]{2,1,0:T(8,128)(2,1)S(1)} %get-tuple-element.22), channel_id=1, source_target_pairs={{0,32},{16,48},{32,0},{48,16},{1,33},{17,49},{33,1},{49,17},{2,34}... | collective-permute-start | bytes 1572872 | tf_op jit(solution)/shard_map/ppermute | solution.py:31
  93.7 23.7 %collective-permute-start.5 = (bf16[8,256,128]{2,1,0:T(8,128)(2,1)S(1)}, bf16[8,256,128]{2,1,0:T(8,128)(2,1)S(1)}, u32[]{:S(2)}, u32[]{:S(2)}) collective-permute-start(bf16[8,256,128]{2,1,0:T(8,128)(2,1)S(1)} %get-tuple-element.23), channel_id=1, source_target_pairs={{0,48},{16,0},{32,16},{48,32},{1,49},{17,1},{33,17},{49,33},{2,50}... | collective-permute-start | bytes 1572872 | tf_op jit(solution)/shard_map/ppermute | solution.py:31
  117.6 12.1 %collective-permute-start.10 = (bf16[4,256,128]{2,1,0:T(8,128)(2,1)S(1)}, bf16[4,256,128]{2,1,0:T(8,128)(2,1)S(1)}, u32[]{:S(2)}, u32[]{:S(2)}) collective-permute-start(bf16[4,256,128]{2,1,0:T(8,128)(2,1)S(1)} %get-tuple-element.28), channel_id=1, source_target_pairs={{0,16},{16,32},{32,48},{48,0},{1,17},{17,33},{33,49},{49,1},{2,18}... | collective-permute-start | bytes 786440 | tf_op jit(solution)/shard_map/ppermute | solution.py:31
  120.1 12.6 %collective-permute-start.11 = (bf16[4,256,128]{2,1,0:T(8,128)(2,1)S(1)}, bf16[4,256,128]{2,1,0:T(8,128)(2,1)S(1)}, u32[]{:S(2)}, u32[]{:S(2)}) collective-permute-start(bf16[4,256,128]{2,1,0:T(8,128)(2,1)S(1)} %get-tuple-element.29), channel_id=1, source_target_pairs={{0,32},{16,48},{32,0},{48,16},{1,33},{17,49},{33,1},{49,17},{2,34}... | collective-permute-start | bytes 786440 | tf_op jit(solution)/shard_map/ppermute | solution.py:31
  124.5 12.3 %collective-permute-start.12 = (bf16[4,256,128]{2,1,0:T(8,128)(2,1)S(1)}, bf16[4,256,128]{2,1,0:T(8,128)(2,1)S(1)}, u32[]{:S(2)}, u32[]{:S(2)}) collective-permute-start(bf16[4,256,128]{2,1,0:T(8,128)(2,1)S(1)} %get-tuple-element.30), channel_id=1, source_target_pairs={{0,48},{16,0},{32,16},{48,32},{1,49},{17,1},{33,17},{49,33},{2,50}... | collective-permute-start | bytes 786440 | tf_op jit(solution)/shard_map/ppermute | solution.py:31
  127.5 11.4 %collective-permute-start.7 = (bf16[4,256,128]{2,1,0:T(8,128)(2,1)S(1)}, bf16[4,256,128]{2,1,0:T(8,128)(2,1)S(1)}, u32[]{:S(2)}, u32[]{:S(2)}) collective-permute-start(bf16[4,256,128]{2,1,0:T(8,128)(2,1)S(1)} %get-tuple-element.27), channel_id=1, source_target_pairs={{0,64},{64,0},{1,65},{65,1},{2,66},{66,2},{3,67},{67,3},{4,68},{68... | collective-permute-start | bytes 786440 | tf_op jit(solution)/shard_map/ppermute | solution.py:26
  137.0 13.1 %collective-permute-start.13 = (bf16[2,256,128]{2,1,0:T(8,128)(2,1)S(1)}, bf16[2,256,128]{2,1,0:T(8,128)(2,1)S(1)}, u32[]{:S(2)}, u32[]{:S(2)}) collective-permute-start(bf16[2,256,128]{2,1,0:T(8,128)(2,1)S(1)} %slice.82), channel_id=1, source_target_pairs={{0,128},{128,0},{1,129},{129,1},{2,130},{130,2},{3,131},{131,3},{4... | collective-permute-start | bytes 393224 | tf_op jit(solution)/shard_map/ppermute | solution.py:26
  139.0 18.0 %collective-permute-start.8 = (bf16[2,256,128]{2,1,0:T(8,128)(2,1)S(1)}, bf16[2,256,128]{2,1,0:T(8,128)(2,1)S(1)}, u32[]{:S(2)}, u32[]{:S(2)}) collective-permute-start(bf16[2,256,128]{2,1,0:T(8,128)(2,1)S(1)} %slice.83), channel_id=1, source_target_pairs={{0,128},{128,0},{1,129},{129,1},{2,130},{130,2},{3,131},{131,3},{4... | collective-permute-start | bytes 393224 | tf_op jit(solution)/shard_map/ppermute | solution.py:26
  150.1 12.9 %collective-permute-start.14 = (bf16[1,256,128]{2,1,0:T(8,128)(2,1)S(1)}, bf16[1,256,128]{2,1,0:T(8,128)(2,1)S(1)}, u32[]{:S(2)}, u32[]{:S(2)}) collective-permute-start(bf16[1,256,128]{2,1,0:T(8,128)(2,1)S(1)} %slice.84), channel_id=1, source_target_pairs={{0,256},{256,0},{1,257},{257,1},{2,258},{258,2},{3,259},{259,3},{4... | collective-permute-start | bytes 196616 | tf_op jit(solution)/shard_map/ppermute | solution.py:26
  157.1 11.0 %collective-permute-start.9 = (bf16[1,256,128]{2,1,0:T(8,128)(2,1)S(1)}, bf16[1,256,128]{2,1,0:T(8,128)(2,1)S(1)}, u32[]{:S(2)}, u32[]{:S(2)}) collective-permute-start(bf16[1,256,128]{2,1,0:T(8,128)(2,1)S(1)} %slice.85), channel_id=1, source_target_pairs={{0,256},{256,0},{1,257},{257,1},{2,258},{258,2},{3,259},{259,3},{4... | collective-permute-start | bytes 196616 | tf_op jit(solution)/shard_map/ppermute | solution.py:26

commit v8 on v7

--- a/solution.py
+++ b/solution.py
@@ -14,7 +14,7 @@
 TOK = 512
 ROWS = 32
 NX, NZ, CAP = 4, 8, 2
-VMEM_MIB = 40
+VMEM_MIB = 60
 AXES = {"z8": 2, "z4": 2, "z2": 2, "x": 4, "y": 4, "zh": 2, "core": 2}
 VMEM = pl.BlockSpec(memory_space=pltpu.VMEM)
 HBM = pl.BlockSpec(memory_space=pltpu.HBM)
@@ -61,12 +61,13 @@
         owner = owner_ref[i // KB, i % KB]
         slot = seen_ref[owner]
         seen_ref[owner] = slot + 1
-        x = (owner % NX - my_x + NX) % NX
+        x = owner % NX
+        rel_x = (x - my_x + NX) % NX
         z = (owner // NX) ^ my_z
         other = z & 1
         rest = (z & 2) + (z >> 2)
         first = x * NZ + other * 4 + rest
-        second = NX * NZ + (1 - other) * (NX * 4) + x * 4 + rest
+        second = NX * NZ + (1 - other) * (NX * 4) + rel_x * 4 + rest
         place_ref[i] = jnp.where(slot == 0, first, second)
         return carry
 
@@ -75,7 +76,7 @@
 
 def block_kernel(
     a_ref, ac_ref, b_ref, bc_ref, gate_ref, up_ref, hidden_ref, rows_ref, place_ref,
-    out_ref, send_ref, x_ref, w_ref, h_ref, picked_ref, x_sem, w_sem, out_sem,
+    first_ref, send_ref, keep_ref, x_ref, w_ref, h_ref, picked_ref, act_ref, out_ref, x_sem, w_sem, out_sem,
 ):
     zh = lax.axis_index("zh")
     core = lax.axis_index("core")
@@ -102,55 +103,46 @@
     for copy in x_copies:
         copy.wait()
     for c in range(COLS):
-        now_ref = picked_ref.at[c % 2]
+        now_ref = picked_ref.at[c]
         for k in range(KB):
             now_ref[k * BS:(k + 1) * BS] = x_ref[rows_ref[c, k]]
         for copy in w_copies[c]:
             copy.wait()
-        picked = now_ref[...]
-        pre = jnp.dot(w_ref[c], picked, preferred_element_type=jnp.float32)
+        pre = jnp.dot(w_ref[c], now_ref[...], preferred_element_type=jnp.float32)
         gate, up = pre[:BS], pre[BS:]
         s = jax.nn.sigmoid(gate)
         h = h_ref[c].astype(jnp.float32)
-        grad_gate = (h * up * (s * (1.0 + gate * (1.0 - s)))).astype(jnp.bfloat16)
-        grad_up = (h * (gate * s)).astype(jnp.bfloat16)
+        act_ref[c, :BS] = (h * up * (s * (1.0 + gate * (1.0 - s)))).astype(jnp.bfloat16)
+        act_ref[c, BS:] = (h * (gate * s)).astype(jnp.bfloat16)
+    for c in range(COLS):
         value = lax.dot_general(
-            picked, jnp.concatenate([grad_gate, grad_up], 0), (((1,), (1,)), ((), ())),
-            preferred_element_type=jnp.float32,
+            picked_ref[c], act_ref[c], (((1,), (1,)), ((), ())), preferred_element_type=jnp.float32
         ).astype(jnp.bfloat16)
         for k in range(KB):
             for m in range(2):
                 out_ref[place_ref[c * KB + k], m * BS:(m + 1) * BS] = value[k * BS:(k + 1) * BS, m * BS:(m + 1) * BS]
-    copy = pltpu.make_async_copy(out_ref.at[pl.ds(NX * NZ, NX * 4)], send_ref, out_sem)
-    copy.start()
-    copy.wait()
-
-
-def split_kernel(out_ref, *refs):
-    *refs, sem = refs
-    copies = []
-    for i, ref in enumerate(refs):
-        copies.append(pltpu.make_async_copy(out_ref.at[pl.ds((i + 1) * NZ, NZ)], ref, sem.at[i]))
-    for copy in copies:
+    out_copies = []
+    for i, (ref, at) in enumerate(((send_ref, NX * NZ), (first_ref, 0), (keep_ref, NX * NZ + NX * 4))):
+        out_copies.append(pltpu.make_async_copy(out_ref.at[pl.ds(at, ref.shape[0])], ref, out_sem.at[i]))
+    for copy in out_copies:
         copy.start()
-    for copy in copies:
+    for copy in out_copies:
         copy.wait()
 
 
-def add_kernel(out_ref, got_ref, order1_ref, order2_ref, order3_ref, *refs):
+def add_kernel(keep_ref, got_ref, *refs):
     for i, ref in enumerate(refs):
         for j in range(4):
             at = i * 4 + j
-            total = out_ref[NX * NZ + NX * 4 + at].astype(jnp.float32) + got_ref[at].astype(jnp.float32)
-            ref[j] = total.astype(ref.dtype)
-
-
-def sum_kernel(out_ref, got1_ref, got2_ref, got3_ref, order_ref, send_ref, keep_ref):
+            ref[j] = (keep_ref[at].astype(jnp.float32) + got_ref[at].astype(jnp.float32)).astype(ref.dtype)
+
+
+def sum_kernel(got_ref, order_ref, send_ref, keep_ref):
     for ref, at in ((keep_ref, 0), (send_ref, NZ // 2)):
         for i in range(NZ // 2):
-            total = out_ref[at + i].astype(jnp.float32)
-            for got_ref in (got1_ref, got2_ref, got3_ref):
-                total += got_ref[at + i].astype(jnp.float32)
+            total = got_ref[at + i].astype(jnp.float32)
+            for x in range(1, NX):
+                total += got_ref[x * NZ + at + i].astype(jnp.float32)
             ref[i] = total.astype(ref.dtype)
 
 
@@ -174,41 +166,36 @@
     def places(count):
         return jax.ShapeDtypeStruct((count, 2 * BS, BS), bf16)
 
-    out, send = call(
-        block_kernel, (places(NX * NZ * CAP), places(NX * 4)), [HBM] * 7 + [SMEM, SMEM], (VMEM, ANY),
+    first, send, keep = call(
+        block_kernel, (places(NX * NZ), places(NX * 4), places(NX * 4)),
+        [HBM] * 7 + [SMEM, SMEM], (HBM, ANY, HBM),
         [
             pltpu.VMEM((ROWS, BS, TOK), bf16),
             pltpu.VMEM((COLS, 2 * BS, KB * BS), bf16),
             pltpu.VMEM((COLS, BS, TOK), bf16),
-            pltpu.VMEM((2, KB * BS, TOK), bf16),
+            pltpu.VMEM((COLS, KB * BS, TOK), bf16),
+            pltpu.VMEM((COLS, 2 * BS, TOK), bf16),
+            pltpu.VMEM((NX * NZ * CAP, 2 * BS, BS), bf16),
             pltpu.SemaphoreType.DMA((16,)),
             pltpu.SemaphoreType.DMA((3 * COLS,)),
-            pltpu.SemaphoreType.DMA,
+            pltpu.SemaphoreType.DMA((3,)),
         ],
         flops=8 * BLOCKS * BS * BS * TOK, bytes_accessed=14 * 2**20, vmem_mib=VMEM_MIB,
     )(a, ac, b, bc, gate_t, up_t, hidden, block_rows, place)
-    firsts = call(
-        split_kernel, [places(NZ)] * (NX - 1), [VMEM], [ANY] * (NX - 1),
-        [pltpu.SemaphoreType.DMA((NX - 1,))], bytes_accessed=3 * 2**20,
-    )(out)
-
-    def over_x(parts):
-        return [shift(part, "x", i + 1) for i, part in enumerate(parts)]
-
     def halve(keep, axis):
         half = keep.shape[0] // 2
         return keep[:half] + swap(keep[half:].astype(bf16), axis).astype(f32)
 
     got = swap(send, "z2")
-    first = over_x(firsts)
+    first = lax.all_to_all(first, "x", 0, 0, tiled=True)
     kept, *seconds = call(
-        add_kernel, [places(4)] * NX, [VMEM] * 2 + [ANY] * 3, [VMEM] * NX, bytes_accessed=3 * 2**20,
-    )(out, got, *first)
-    second = over_x(seconds)
+        add_kernel, [places(4)] * NX, [VMEM] * 2, [VMEM] * NX, bytes_accessed=3 * 2**20,
+    )(keep, got)
+    second = [shift(seconds[i - 1], "x", i) for i in (1, 3, 2)]
     send, first = call(
-        sum_kernel, (places(4), jax.ShapeDtypeStruct((4, 2 * BS, BS), f32)), [VMEM] * NX + [ANY], (VMEM, VMEM),
+        sum_kernel, (places(4), jax.ShapeDtypeStruct((4, 2 * BS, BS), f32)), [VMEM, ANY], (VMEM, VMEM),
         bytes_accessed=3 * 2**20,
-    )(out, *first, kept)
+    )(first, kept)
     first = first + swap(send, "z2").astype(f32)
     first = halve(halve(first, "z4"), "z8")
     second = kept.astype(f32) + sum(part.astype(f32) for part in second)

time: 170 us -> 165 us (0.971)
  starting transfers between devices: 78.6 us -> 74.9 us
  Pallas kernels: 14.9 us -> 16.8 us
    ppermute x6 -> x3, waiting for transfers between devices: 28.9 us -> 5.23 us  [shift(): lax.ppermute(value, axis, [(i, (i + step) % size) for i in range(size)])]
    ppermute x9, waiting for transfers between devices: 17.2 us -> 39.9 us  [swap(): return lax.ppermute(value, axis, [(0, 1), (1, 0)])]
    ppermute x6 -> x3, starting transfers between devices: 18.2 us -> 9.2 us  [shift(): lax.ppermute(value, axis, [(i, (i + step) % size) for i in range(size)])]
    all_to_all x0 -> x1, starting transfers between devices: none -> 4.92 us  [body(): first = lax.all_to_all(first, 'x', 0, 0, tiled=True)]
    unnamed x10 -> x14, local copies, waits for them, and re-layouts: 2.7 us -> 0.53 us
    pallas_call x3 -> x2, Pallas kernels: 11.6 us -> 13.4 us  [the longest x1 12.4 us: body(): call(block_kernel, (places(NX * NZ), places(NX * 4), places(NX * 4)), [HB...]
  transfers between devices with their start and end apart: 17 -> 15, of which waited for: 10 -> 7; matrix products, arithmetic and copies ran while one was open for 6% -> 6% of each run, Pallas kernels for 2% -> 3%
where the time goes in v8:
time: 165 us; the launch traced here: 164 us
  starting transfers between devices  74.9 us (45%)
  waiting for transfers between devices  57.5 us (35%)
  Pallas kernels  16.8 us (10%)
  local copies, waits for them, and re-layouts  13.9 us (8%)
    ppermute x9, starting transfers between devices, swap(): return lax.ppermute(value, axis, [(0, 1), (1, 0)])  51.5 us
    ppermute x9, waiting for transfers between devices, swap(): return lax.ppermute(value, axis, [(0, 1), (1, 0)])  39.9 us
    pallas_call x1, Pallas kernels, body(): call(block_kernel, (places(NX * NZ), places(NX * 4), places(NX * 4)), [HB...  12.4 us
    all_to_all x2, waiting for transfers between devices, spread(): lax.all_to_all(jnp.broadcast_to(value[None], (AXES[axis],) + value.shape)...  12.3 us
    all_to_all x2, starting transfers between devices, spread(): lax.all_to_all(jnp.broadcast_to(value[None], (AXES[axis],) + value.shape)...  9.26 us
    ppermute x3, starting transfers between devices, shift(): lax.ppermute(value, axis, [(i, (i + step) % size) for i in range(size)])  9.2 us
    reshape x2, local copies, waits for them, and re-layouts, body(): w.transpose(0, 3, 1, 2).reshape(COLS, BS, KB * BS)  7.27 us
    ppermute x3, waiting for transfers between devices, shift(): lax.ppermute(value, axis, [(i, (i + step) % size) for i in range(size)])  5.23 us
  transfers between devices with their start and end apart: 15, of which 7 were waited for; matrix products, arithmetic and copies ran while one was open for 6% of the time, Pallas kernels for 3%

profile of v8, /device:TPU:6, one launch (start us, length us, event | category | flops | bytes accessed | tf_op | source)
XLA Modules:
  0.0 164.4 jit_solution(15930390697279052238)
XLA Ops:
  0.0 1.1 copy.12
  1.1 1.1 broadcast_in_dim.14
  2.2 4.5 %all-to-all-start = ((bf16[4,2,128,512]{3,2,1,0:T(8,128)(2,1)}), bf16[4,2,128,512]{3,2,1,0:T(8,128)(2,1)S(1)}, u32[]{:S(2)}, u32[]{:S(2)}) async-start(bf16[4,2,128,512]{3,2,1,0:T(8,128)(2,1)} %broadcast_in_dim.14), calls=%async_computation | async-start | bytes 2097152 | tf_op jit(solution)/shard_map/all_to_all | solution.py:35
  6.7 15.7 %collective-permute-start.1 = (bf16[2,128,512]{2,1,0:T(8,128)(2,1)S(1)}, bf16[2,128,512]{2,1,0:T(8,128)(2,1)S(1)}, u32[]{:S(2)}, u32[]{:S(2)}) collective-permute-start(bf16[2,128,512]{2,1,0:T(8,128)(2,1)S(1)} %bitcast.24), channel_id=1, source_target_pairs={{0,2},{2,0},{1,3},{3,1},{4,6},{6,4},{5,7},{7,5},{8,10},{10,8},{9,1... | collective-permute-start | bytes 786440 | tf_op jit(solution)/shard_map/ppermute | solution.py:26
  22.4 1.4 copy.11
  23.8 2.9 %copy.13.gate_ref = bf16[7,128,1024]{2,1,0:T(8,128)(2,1)S(1)} copy(bf16[7,128,1024]{1,2,0:T(8,128)(2,1)} %bitcast.21) | data formatting | bytes 3670016 | tf_op jit(solution)/shard_map/reshape | solution.py:154
  26.7 4.4 %copy.14.up_ref = bf16[7,128,1024]{2,1,0:T(8,128)(2,1)} copy(bf16[7,128,1024]{1,2,0:T(8,128)(2,1)} %bitcast.22) | data formatting | bytes 3670016 | tf_op jit(solution)/shard_map/reshape | solution.py:154
  32.5 3.1 %shard_map.64.place_ref = s32[56]{0:T(128)S(1)} custom-call(s32[7,8]{1,0:T(8,128)S(1)} %copy-done.1, bf16[8,1024]{1,0:T(8,128)(2,1)S(1)} %get-tuple-element.28.gate_ref, bf16[8,1024]{1,0:T(8,128)(2,1)S(1)} %get-tuple-element.27.up_ref, bf16[8,512]{1,0:T(8,128)(2,1)S(1)} %slice_bitcast_fusion.4.hidden_ref, bf16[8,512]{1,0:T(8,128)(2,1)S(1)} %slice_bitcast_fusion.3.near_ref), custom_call_target="tpu_custom_call" | custom-call | tf_op jit(solution)/shard_map/pallas_call | solution.py:157
  36.1 1.1 broadcast_in_dim.15
  37.2 4.8 %all-to-all-start.1 = ((bf16[4,2,128,512]{3,2,1,0:T(8,128)(2,1)}), bf16[4,2,128,512]{3,2,1,0:T(8,128)(2,1)S(1)}, u32[]{:S(2)}, u32[]{:S(2)}) async-start(bf16[4,2,128,512]{3,2,1,0:T(8,128)(2,1)} %broadcast_in_dim.15), calls=%async_computation.1 | async-start | bytes 2097152 | tf_op jit(solution)/shard_map/all_to_all | solution.py:35
  42.0 1.9 %collective-permute-start = (bf16[4,2,128,512]{3,2,1,0:T(8,128)(2,1)S(1)}, bf16[4,2,128,512]{3,2,1,0:T(8,128)(2,1)}, u32[]{:S(2)}, u32[]{:S(2)}) collective-permute-start(bf16[4,2,128,512]{3,2,1,0:T(8,128)(2,1)S(1)} %all-to-all-done.a_ref), channel_id=1, source_target_pairs={{0,1},{1,0},{2,3},{3,2},{4,5},{5,4},{6,7},{7,6},{8,9},{9,8},{10,11... | collective-permute-start | bytes 3145736 | tf_op jit(solution)/shard_map/ppermute | solution.py:26
  44.0 12.3 %all-to-all-done.1.b_ref = bf16[4,2,128,512]{3,2,1,0:T(8,128)(2,1)S(1)} async-done(((bf16[4,2,128,512]{3,2,1,0:T(8,128)(2,1)}), bf16[4,2,128,512]{3,2,1,0:T(8,128)(2,1)S(1)}, u32[]{:S(2)}, u32[]{:S(2)}) %all-to-all-start.1) | async-done | bytes 1048608 | tf_op jit(solution)/shard_map/all_to_all | solution.py:35
  56.3 1.9 %collective-permute-start.2 = (bf16[4,2,128,512]{3,2,1,0:T(8,128)(2,1)S(1)}, bf16[4,2,128,512]{3,2,1,0:T(8,128)(2,1)}, u32[]{:S(2)}, u32[]{:S(2)}) collective-permute-start(bf16[4,2,128,512]{3,2,1,0:T(8,128)(2,1)S(1)} %all-to-all-done.1.b_ref), channel_id=1, source_target_pairs={{0,1},{1,0},{2,3},{3,2},{4,5},{5,4},{6,7},{7,6},{8,9},{9,8},{10,11... | collective-permute-start | bytes 3145736 | tf_op jit(solution)/shard_map/ppermute | solution.py:26
  58.2 2.7 %collective-permute-done.2.bc_ref = bf16[4,2,128,512]{3,2,1,0:T(8,128)(2,1)} collective-permute-done((bf16[4,2,128,512]{3,2,1,0:T(8,128)(2,1)S(1)}, bf16[4,2,128,512]{3,2,1,0:T(8,128)(2,1)}, u32[]{:S(2)}, u32[]{:S(2)}) %collective-permute-start.2) | collective-permute-done | bytes 1048608 | tf_op jit(solution)/shard_map/ppermute | solution.py:26
  61.0 12.4 %shard_map.65 = (bf16[32,256,128]{2,1,0:T(8,128)(2,1)}, bf16[16,256,128]{2,1,0:T(8,128)(2,1)}, bf16[16,256,128]{2,1,0:T(8,128)(2,1)}) custom-call(bf16[4,2,128,512]{3,2,1,0:T(8,128)(2,1)} %copy-done.4, bf16[4,2,128,512]{3,2,1,0:T(8,128)(2,1)} %collective-permute-done.ac_ref, bf16[4,2,128,512]{3,2,1,0:T(8,128)(2,1)} %copy-done.5, ...), custom_call_target="tpu_custom_call" | custom-call | flops 3758096384 | bytes 14680064 | tf_op jit(solution)/shard_map/pallas_call | solution.py:169
  73.4 4.9 %all-to-all-start.2 = ((bf16[32,256,128]{2,1,0:T(8,128)(2,1)}), bf16[32,256,128]{2,1,0:T(8,128)(2,1)S(1)}, u32[]{:S(2)}, u32[]{:S(2)}) async-start(bf16[32,256,128]{2,1,0:T(8,128)(2,1)} %get-tuple-element.18), calls=%async_computation.2 | async-start | bytes 4194304 | tf_op jit(solution)/shard_map/all_to_all | solution.py:190
  78.4 11.8 %collective-permute-start.3 = (bf16[16,256,128]{2,1,0:T(8,128)(2,1)}, bf16[16,256,128]{2,1,0:T(8,128)(2,1)S(1)}, u32[]{:S(2)}, u32[]{:S(2)}) collective-permute-start(bf16[16,256,128]{2,1,0:T(8,128)(2,1)} %get-tuple-element.20), channel_id=1, source_target_pairs={{0,64},{64,0},{1,65},{65,1},{2,66},{66,2},{3,67},{67,3},{4,68},{68... | collective-permute-start | bytes 3145736 | tf_op jit(solution)/shard_map/ppermute | solution.py:26
  90.2 23.1 %collective-permute-done.3.got_ref = bf16[16,256,128]{2,1,0:T(8,128)(2,1)S(1)} collective-permute-done((bf16[16,256,128]{2,1,0:T(8,128)(2,1)}, bf16[16,256,128]{2,1,0:T(8,128)(2,1)S(1)}, u32[]{:S(2)}, u32[]{:S(2)}) %collective-permute-start.3) | collective-permute-done | bytes 1048608 | tf_op jit(solution)/shard_map/ppermute | solution.py:26
  113.3 1.0 shard_map.66
  114.3 2.2 %collective-permute-start.7 = (bf16[4,256,128]{2,1,0:T(8,128)(2,1)}, bf16[4,256,128]{2,1,0:T(8,128)(2,1)S(1)}, u32[]{:S(2)}, u32[]{:S(2)}) collective-permute-start(bf16[4,256,128]{2,1,0:T(8,128)(2,1)} %get-tuple-element.24), channel_id=1, source_target_pairs={{0,16},{16,32},{32,48},{48,0},{1,17},{17,33},{33,49},{49,1},{2,18}... | collective-permute-start | bytes 786440 | tf_op jit(solution)/shard_map/ppermute | solution.py:31
  116.5 3.7 %collective-permute-start.8 = (bf16[4,256,128]{2,1,0:T(8,128)(2,1)}, bf16[4,256,128]{2,1,0:T(8,128)(2,1)S(1)}, u32[]{:S(2)}, u32[]{:S(2)}) collective-permute-start(bf16[4,256,128]{2,1,0:T(8,128)(2,1)} %get-tuple-element.25), channel_id=1, source_target_pairs={{0,48},{16,0},{32,16},{48,32},{1,49},{17,1},{33,17},{49,33},{2,50}... | collective-permute-start | bytes 786440 | tf_op jit(solution)/shard_map/ppermute | solution.py:31
  120.1 3.4 %collective-permute-start.9 = (bf16[4,256,128]{2,1,0:T(8,128)(2,1)}, bf16[4,256,128]{2,1,0:T(8,128)(2,1)S(1)}, u32[]{:S(2)}, u32[]{:S(2)}) collective-permute-start(bf16[4,256,128]{2,1,0:T(8,128)(2,1)} %get-tuple-element.26), channel_id=1, source_target_pairs={{0,32},{16,48},{32,0},{48,16},{1,33},{17,49},{33,1},{49,17},{2,34}... | collective-permute-start | bytes 786440 | tf_op jit(solution)/shard_map/ppermute | solution.py:31
  123.8 3.6 %collective-permute-start.4 = (bf16[4,256,128]{2,1,0:T(8,128)(2,1)S(1)}, bf16[4,256,128]{2,1,0:T(8,128)(2,1)S(1)}, u32[]{:S(2)}, u32[]{:S(2)}) collective-permute-start(bf16[4,256,128]{2,1,0:T(8,128)(2,1)S(1)} %get-tuple-element.23), channel_id=1, source_target_pairs={{0,64},{64,0},{1,65},{65,1},{2,66},{66,2},{3,67},{67,3},{4,68},{68... | collective-permute-start | bytes 786440 | tf_op jit(solution)/shard_map/ppermute | solution.py:26
  127.4 5.2 %collective-permute-done.8 = bf16[4,256,128]{2,1,0:T(8,128)(2,1)S(1)} collective-permute-done((bf16[4,256,128]{2,1,0:T(8,128)(2,1)}, bf16[4,256,128]{2,1,0:T(8,128)(2,1)S(1)}, u32[]{:S(2)}, u32[]{:S(2)}) %collective-permute-start.8) | collective-permute-done | bytes 262176 | tf_op jit(solution)/shard_map/ppermute | solution.py:31
  132.8 1.9 %collective-permute-start.10 = (bf16[2,256,128]{2,1,0:T(8,128)(2,1)S(1)}, bf16[2,256,128]{2,1,0:T(8,128)(2,1)S(1)}, u32[]{:S(2)}, u32[]{:S(2)}) collective-permute-start(bf16[2,256,128]{2,1,0:T(8,128)(2,1)S(1)} %slice.82), channel_id=1, source_target_pairs={{0,128},{128,0},{1,129},{129,1},{2,130},{130,2},{3,131},{131,3},{4... | collective-permute-start | bytes 393224 | tf_op jit(solution)/shard_map/ppermute | solution.py:26
  134.9 4.8 %collective-permute-start.5 = (bf16[2,256,128]{2,1,0:T(8,128)(2,1)S(1)}, bf16[2,256,128]{2,1,0:T(8,128)(2,1)S(1)}, u32[]{:S(2)}, u32[]{:S(2)}) collective-permute-start(bf16[2,256,128]{2,1,0:T(8,128)(2,1)S(1)} %slice.83), channel_id=1, source_target_pairs={{0,128},{128,0},{1,129},{129,1},{2,130},{130,2},{3,131},{131,3},{4... | collective-permute-start | bytes 393224 | tf_op jit(solution)/shard_map/ppermute | solution.py:26
  139.7 6.3 %collective-permute-done.10 = bf16[2,256,128]{2,1,0:T(8,128)(2,1)S(1)} collective-permute-done((bf16[2,256,128]{2,1,0:T(8,128)(2,1)S(1)}, bf16[2,256,128]{2,1,0:T(8,128)(2,1)S(1)}, u32[]{:S(2)}, u32[]{:S(2)}) %collective-permute-start.10) | collective-permute-done | bytes 131104 | tf_op jit(solution)/shard_map/ppermute | solution.py:26
  146.0 7.3 %collective-permute-start.11 = (bf16[1,256,128]{2,1,0:T(8,128)(2,1)S(1)}, bf16[1,256,128]{2,1,0:T(8,128)(2,1)S(1)}, u32[]{:S(2)}, u32[]{:S(2)}) collective-permute-start(bf16[1,256,128]{2,1,0:T(8,128)(2,1)S(1)} %slice.84), channel_id=1, source_target_pairs={{0,256},{256,0},{1,257},{257,1},{2,258},{258,2},{3,259},{259,3},{4... | collective-permute-start | bytes 196616 | tf_op jit(solution)/shard_map/ppermute | solution.py:26
  153.4 2.5 %collective-permute-start.6 = (bf16[1,256,128]{2,1,0:T(8,128)(2,1)S(1)}, bf16[1,256,128]{2,1,0:T(8,128)(2,1)S(1)}, u32[]{:S(2)}, u32[]{:S(2)}) collective-permute-start(bf16[1,256,128]{2,1,0:T(8,128)(2,1)S(1)} %slice.85), channel_id=1, source_target_pairs={{0,256},{256,0},{1,257},{257,1},{2,258},{258,2},{3,259},{259,3},{4... | collective-permute-start | bytes 196616 | tf_op jit(solution)/shard_map/ppermute | solution.py:26
  155.9 3.1 %collective-permute-done.11 = bf16[1,256,128]{2,1,0:T(8,128)(2,1)S(1)} collective-permute-done((bf16[1,256,128]{2,1,0:T(8,128)(2,1)S(1)}, bf16[1,256,128]{2,1,0:T(8,128)(2,1)S(1)}, u32[]{:S(2)}, u32[]{:S(2)}) %collective-permute-start.11) | collective-permute-done | bytes 65568 | tf_op jit(solution)/shard_map/ppermute | solution.py:26
  159.0 4.6 %collective-permute-done.6 = bf16[1,256,128]{2,1,0:T(8,128)(2,1)S(1)} collective-permute-done((bf16[1,256,128]{2,1,0:T(8,128)(2,1)S(1)}, bf16[1,256,128]{2,1,0:T(8,128)(2,1)S(1)}, u32[]{:S(2)}, u32[]{:S(2)}) %collective-permute-start.6) | collective-permute-done | bytes 65568 | tf_op jit(solution)/shard_map/ppermute | solution.py:26
  163.7 0.7 pad_maximum_fusion
  (37 shorter events, 2.6 us)
Async XLA Ops:
  1.1 21.3 %copy-start.6 = (bf16[512,896]{1,0:T(8,128)(2,1)S(1)}, bf16[512,896]{1,0:T(8,128)(2,1)}, u32[]{:S(2)}) copy-start(bf16[512,896]{1,0:T(8,128)(2,1)} %param.7) | copy-start | bytes 2752516
  2.2 30.3 %all-to-all-start = ((bf16[4,2,128,512]{3,2,1,0:T(8,128)(2,1)}), bf16[4,2,128,512]{3,2,1,0:T(8,128)(2,1)S(1)}, u32[]{:S(2)}, u32[]{:S(2)}) async-start(bf16[4,2,128,512]{3,2,1,0:T(8,128)(2,1)} %broadcast_in_dim.14), calls=%async_computation | async-start | bytes 2097152 | tf_op jit(solution)/shard_map/all_to_all | solution.py:35
  6.7 29.5 %collective-permute-start.1 = (bf16[2,128,512]{2,1,0:T(8,128)(2,1)S(1)}, bf16[2,128,512]{2,1,0:T(8,128)(2,1)S(1)}, u32[]{:S(2)}, u32[]{:S(2)}) collective-permute-start(bf16[2,128,512]{2,1,0:T(8,128)(2,1)S(1)} %bitcast.24), channel_id=1, source_target_pairs={{0,2},{2,0},{1,3},{3,1},{4,6},{6,4},{5,7},{7,5},{8,10},{10,8},{9,1... | collective-permute-start | bytes 786440 | tf_op jit(solution)/shard_map/ppermute | solution.py:26
  26.7 5.1 %copy-start.3 = (bf16[7,128,1024]{2,1,0:T(8,128)(2,1)}, bf16[7,128,1024]{2,1,0:T(8,128)(2,1)S(1)}, u32[]{:S(2)}) copy-start(bf16[7,128,1024]{2,1,0:T(8,128)(2,1)S(1)} %copy.13.gate_ref) | copy-start | bytes 5505028
  26.7 5.8 %copy-start.1 = (s32[7,8]{1,0:T(8,128)S(1)}, s32[7,8]{1,0:T(8,128)}, u32[]{:S(2)}) copy-start(s32[7,8]{1,0:T(8,128)} %owner_ref.1) | copy-start | bytes 676
  32.5 28.5 %copy-start.4 = (bf16[4,2,128,512]{3,2,1,0:T(8,128)(2,1)}, bf16[4,2,128,512]{3,2,1,0:T(8,128)(2,1)S(1)}, u32[]{:S(2)}) copy-start(bf16[4,2,128,512]{3,2,1,0:T(8,128)(2,1)S(1)} %all-to-all-done.a_ref) | copy-start | bytes 3145732
  35.6 0.5 copy-start.2
  37.2 19.1 %all-to-all-start.1 = ((bf16[4,2,128,512]{3,2,1,0:T(8,128)(2,1)}), bf16[4,2,128,512]{3,2,1,0:T(8,128)(2,1)S(1)}, u32[]{:S(2)}, u32[]{:S(2)}) async-start(bf16[4,2,128,512]{3,2,1,0:T(8,128)(2,1)} %broadcast_in_dim.15), calls=%async_computation.1 | async-start | bytes 2097152 | tf_op jit(solution)/shard_map/all_to_all | solution.py:35
  42.0 16.2 %collective-permute-start = (bf16[4,2,128,512]{3,2,1,0:T(8,128)(2,1)S(1)}, bf16[4,2,128,512]{3,2,1,0:T(8,128)(2,1)}, u32[]{:S(2)}, u32[]{:S(2)}) collective-permute-start(bf16[4,2,128,512]{3,2,1,0:T(8,128)(2,1)S(1)} %all-to-all-done.a_ref), channel_id=1, source_target_pairs={{0,1},{1,0},{2,3},{3,2},{4,5},{5,4},{6,7},{7,6},{8,9},{9,8},{10,11... | collective-permute-start | bytes 3145736 | tf_op jit(solution)/shard_map/ppermute | solution.py:26
  56.3 4.7 %copy-start.5 = (bf16[4,2,128,512]{3,2,1,0:T(8,128)(2,1)}, bf16[4,2,128,512]{3,2,1,0:T(8,128)(2,1)S(1)}, u32[]{:S(2)}) copy-start(bf16[4,2,128,512]{3,2,1,0:T(8,128)(2,1)S(1)} %all-to-all-done.1.b_ref) | copy-start | bytes 3145732
  56.3 4.7 %collective-permute-start.2 = (bf16[4,2,128,512]{3,2,1,0:T(8,128)(2,1)S(1)}, bf16[4,2,128,512]{3,2,1,0:T(8,128)(2,1)}, u32[]{:S(2)}, u32[]{:S(2)}) collective-permute-start(bf16[4,2,128,512]{3,2,1,0:T(8,128)(2,1)S(1)} %all-to-all-done.1.b_ref), channel_id=1, source_target_pairs={{0,1},{1,0},{2,3},{3,2},{4,5},{5,4},{6,7},{7,6},{8,9},{9,8},{10,11... | collective-permute-start | bytes 3145736 | tf_op jit(solution)/shard_map/ppermute | solution.py:26
  73.4 39.9 %copy-start = (bf16[16,256,128]{2,1,0:T(8,128)(2,1)S(1)}, bf16[16,256,128]{2,1,0:T(8,128)(2,1)}, u32[]{:S(2)}) copy-start(bf16[16,256,128]{2,1,0:T(8,128)(2,1)} %get-tuple-element.19.keep_ref) | copy-start | bytes 3145732
  73.4 50.1 %all-to-all-start.2 = ((bf16[32,256,128]{2,1,0:T(8,128)(2,1)}), bf16[32,256,128]{2,1,0:T(8,128)(2,1)S(1)}, u32[]{:S(2)}, u32[]{:S(2)}) async-start(bf16[32,256,128]{2,1,0:T(8,128)(2,1)} %get-tuple-element.18), calls=%async_computation.2 | async-start | bytes 4194304 | tf_op jit(solution)/shard_map/all_to_all | solution.py:190
  78.4 34.9 %collective-permute-start.3 = (bf16[16,256,128]{2,1,0:T(8,128)(2,1)}, bf16[16,256,128]{2,1,0:T(8,128)(2,1)S(1)}, u32[]{:S(2)}, u32[]{:S(2)}) collective-permute-start(bf16[16,256,128]{2,1,0:T(8,128)(2,1)} %get-tuple-element.20), channel_id=1, source_target_pairs={{0,64},{64,0},{1,65},{65,1},{2,66},{66,2},{3,67},{67,3},{4,68},{68... | collective-permute-start | bytes 3145736 | tf_op jit(solution)/shard_map/ppermute | solution.py:26
  114.3 13.1 %collective-permute-start.7 = (bf16[4,256,128]{2,1,0:T(8,128)(2,1)}, bf16[4,256,128]{2,1,0:T(8,128)(2,1)S(1)}, u32[]{:S(2)}, u32[]{:S(2)}) collective-permute-start(bf16[4,256,128]{2,1,0:T(8,128)(2,1)} %get-tuple-element.24), channel_id=1, source_target_pairs={{0,16},{16,32},{32,48},{48,0},{1,17},{17,33},{33,49},{49,1},{2,18}... | collective-permute-start | bytes 786440 | tf_op jit(solution)/shard_map/ppermute | solution.py:31
  116.5 16.2 %collective-permute-start.8 = (bf16[4,256,128]{2,1,0:T(8,128)(2,1)}, bf16[4,256,128]{2,1,0:T(8,128)(2,1)S(1)}, u32[]{:S(2)}, u32[]{:S(2)}) collective-permute-start(bf16[4,256,128]{2,1,0:T(8,128)(2,1)} %get-tuple-element.25), channel_id=1, source_target_pairs={{0,48},{16,0},{32,16},{48,32},{1,49},{17,1},{33,17},{49,33},{2,50}... | collective-permute-start | bytes 786440 | tf_op jit(solution)/shard_map/ppermute | solution.py:31
  120.1 12.5 %collective-permute-start.9 = (bf16[4,256,128]{2,1,0:T(8,128)(2,1)}, bf16[4,256,128]{2,1,0:T(8,128)(2,1)S(1)}, u32[]{:S(2)}, u32[]{:S(2)}) collective-permute-start(bf16[4,256,128]{2,1,0:T(8,128)(2,1)} %get-tuple-element.26), channel_id=1, source_target_pairs={{0,32},{16,48},{32,0},{48,16},{1,33},{17,49},{33,1},{49,17},{2,34}... | collective-permute-start | bytes 786440 | tf_op jit(solution)/shard_map/ppermute | solution.py:31
  123.8 11.0 %collective-permute-start.4 = (bf16[4,256,128]{2,1,0:T(8,128)(2,1)S(1)}, bf16[4,256,128]{2,1,0:T(8,128)(2,1)S(1)}, u32[]{:S(2)}, u32[]{:S(2)}) collective-permute-start(bf16[4,256,128]{2,1,0:T(8,128)(2,1)S(1)} %get-tuple-element.23), channel_id=1, source_target_pairs={{0,64},{64,0},{1,65},{65,1},{2,66},{66,2},{3,67},{67,3},{4,68},{68... | collective-permute-start | bytes 786440 | tf_op jit(solution)/shard_map/ppermute | solution.py:26
  132.8 13.2 %collective-permute-start.10 = (bf16[2,256,128]{2,1,0:T(8,128)(2,1)S(1)}, bf16[2,256,128]{2,1,0:T(8,128)(2,1)S(1)}, u32[]{:S(2)}, u32[]{:S(2)}) collective-permute-start(bf16[2,256,128]{2,1,0:T(8,128)(2,1)S(1)} %slice.82), channel_id=1, source_target_pairs={{0,128},{128,0},{1,129},{129,1},{2,130},{130,2},{3,131},{131,3},{4... | collective-permute-start | bytes 393224 | tf_op jit(solution)/shard_map/ppermute | solution.py:26
  134.9 18.5 %collective-permute-start.5 = (bf16[2,256,128]{2,1,0:T(8,128)(2,1)S(1)}, bf16[2,256,128]{2,1,0:T(8,128)(2,1)S(1)}, u32[]{:S(2)}, u32[]{:S(2)}) collective-permute-start(bf16[2,256,128]{2,1,0:T(8,128)(2,1)S(1)} %slice.83), channel_id=1, source_target_pairs={{0,128},{128,0},{1,129},{129,1},{2,130},{130,2},{3,131},{131,3},{4... | collective-permute-start | bytes 393224 | tf_op jit(solution)/shard_map/ppermute | solution.py:26
  146.0 13.0 %collective-permute-start.11 = (bf16[1,256,128]{2,1,0:T(8,128)(2,1)S(1)}, bf16[1,256,128]{2,1,0:T(8,128)(2,1)S(1)}, u32[]{:S(2)}, u32[]{:S(2)}) collective-permute-start(bf16[1,256,128]{2,1,0:T(8,128)(2,1)S(1)} %slice.84), channel_id=1, source_target_pairs={{0,256},{256,0},{1,257},{257,1},{2,258},{258,2},{3,259},{259,3},{4... | collective-permute-start | bytes 196616 | tf_op jit(solution)/shard_map/ppermute | solution.py:26
  153.4 10.3 %collective-permute-start.6 = (bf16[1,256,128]{2,1,0:T(8,128)(2,1)S(1)}, bf16[1,256,128]{2,1,0:T(8,128)(2,1)S(1)}, u32[]{:S(2)}, u32[]{:S(2)}) collective-permute-start(bf16[1,256,128]{2,1,0:T(8,128)(2,1)S(1)} %slice.85), channel_id=1, source_target_pairs={{0,256},{256,0},{1,257},{257,1},{2,258},{258,2},{3,259},{259,3},{4... | collective-permute-start | bytes 196616 | tf_op jit(solution)/shard_map/ppermute | solution.py:26

commit v9 on v8

--- a/solution.py
+++ b/solution.py
@@ -130,14 +130,14 @@
         copy.wait()
 
 
-def add_kernel(keep_ref, got_ref, *refs):
+def add_kernel(keep_ref, got_ref, order_ref, *refs):
     for i, ref in enumerate(refs):
         for j in range(4):
             at = i * 4 + j
             ref[j] = (keep_ref[at].astype(jnp.float32) + got_ref[at].astype(jnp.float32)).astype(ref.dtype)
 
 
-def sum_kernel(got_ref, order_ref, send_ref, keep_ref):
+def sum_kernel(got_ref, send_ref, keep_ref):
     for ref, at in ((keep_ref, 0), (send_ref, NZ // 2)):
         for i in range(NZ // 2):
             total = got_ref[at + i].astype(jnp.float32)
@@ -188,15 +188,16 @@
 
     got = swap(send, "z2")
     first = lax.all_to_all(first, "x", 0, 0, tiled=True)
+    send, first = call(
+        sum_kernel, (places(4), jax.ShapeDtypeStruct((4, 2 * BS, BS), f32)), [VMEM], (VMEM, VMEM),
+        bytes_accessed=3 * 2**20,
+    )(first)
+    got_first = swap(send, "z2")
     kept, *seconds = call(
-        add_kernel, [places(4)] * NX, [VMEM] * 2, [VMEM] * NX, bytes_accessed=3 * 2**20,
-    )(keep, got)
+        add_kernel, [places(4)] * NX, [VMEM] * 2 + [ANY], [VMEM] * NX, bytes_accessed=3 * 2**20,
+    )(keep, got, got_first)
     second = [shift(seconds[i - 1], "x", i) for i in (1, 3, 2)]
-    send, first = call(
-        sum_kernel, (places(4), jax.ShapeDtypeStruct((4, 2 * BS, BS), f32)), [VMEM, ANY], (VMEM, VMEM),
-        bytes_accessed=3 * 2**20,
-    )(first, kept)
-    first = first + swap(send, "z2").astype(f32)
+    first = first + got_first.astype(f32)
     first = halve(halve(first, "z4"), "z8")
     second = kept.astype(f32) + sum(part.astype(f32) for part in second)
     second = halve(halve(second, "z4"), "z8")

time: 165 us -> 166 us (level)
  waiting for transfers between devices: 57.5 us -> 47.2 us
  starting transfers between devices: 74.9 us -> 85.1 us
    ppermute x9, waiting for transfers between devices: 39.9 us -> 15.1 us  [swap(): return lax.ppermute(value, axis, [(0, 1), (1, 0)])]
    all_to_all x1, waiting for transfers between devices: 0.01 us -> 12.6 us  [body(): first = lax.all_to_all(first, 'x', 0, 0, tiled=True)]
    ppermute x9, starting transfers between devices: 51.5 us -> 61.3 us  [swap(): return lax.ppermute(value, axis, [(0, 1), (1, 0)])]
    ppermute x3, waiting for transfers between devices: 5.23 us -> 7.14 us  [shift(): lax.ppermute(value, axis, [(i, (i + step) % size) for i in range(size)])]
  transfers between devices with their start and end apart: 15 -> 15, of which waited for: 7 -> 6; matrix products, arithmetic and copies ran while one was open for 6% -> 6% of each run, Pallas kernels for 3% -> 2%
where the time goes in v9:
time: 166 us; the launch traced here: 165 us
  starting transfers between devices  85.1 us (51%)
  waiting for transfers between devices  47.2 us (28%)
  Pallas kernels  17.2 us (10%)
  local copies, waits for them, and re-layouts  13.9 us (8%)
    ppermute x9, starting transfers between devices, swap(): return lax.ppermute(value, axis, [(0, 1), (1, 0)])  61.3 us
    ppermute x9, waiting for transfers between devices, swap(): return lax.ppermute(value, axis, [(0, 1), (1, 0)])  15.1 us
    all_to_all x1, waiting for transfers between devices, body(): first = lax.all_to_all(first, 'x', 0, 0, tiled=True)  12.6 us
    pallas_call x1, Pallas kernels, body(): call(block_kernel, (places(NX * NZ), places(NX * 4), places(NX * 4)), [HB...  12.4 us
    all_to_all x2, waiting for transfers between devices, spread(): lax.all_to_all(jnp.broadcast_to(value[None], (AXES[axis],) + value.shape)...  12.3 us
    ppermute x3, starting transfers between devices, shift(): lax.ppermute(value, axis, [(i, (i + step) % size) for i in range(size)])  9.82 us
    all_to_all x2, starting transfers between devices, spread(): lax.all_to_all(jnp.broadcast_to(value[None], (AXES[axis],) + value.shape)...  9.26 us
    reshape x2, local copies, waits for them, and re-layouts, body(): w.transpose(0, 3, 1, 2).reshape(COLS, BS, KB * BS)  7.27 us
  transfers between devices with their start and end apart: 15, of which 6 were waited for; matrix products, arithmetic and copies ran while one was open for 6% of the time, Pallas kernels for 2%

profile of v9, /device:TPU:6, one launch (start us, length us, event | category | flops | bytes accessed | tf_op | source)
XLA Modules:
  0.0 164.7 jit_solution(14691329339492517010)
XLA Ops:
  0.0 1.1 copy.12
  1.1 1.1 broadcast_in_dim.14
  2.2 4.5 %all-to-all-start = ((bf16[4,2,128,512]{3,2,1,0:T(8,128)(2,1)}), bf16[4,2,128,512]{3,2,1,0:T(8,128)(2,1)S(1)}, u32[]{:S(2)}, u32[]{:S(2)}) async-start(bf16[4,2,128,512]{3,2,1,0:T(8,128)(2,1)} %broadcast_in_dim.14), calls=%async_computation | async-start | bytes 2097152 | tf_op jit(solution)/shard_map/all_to_all | solution.py:35
  6.7 15.7 %collective-permute-start.1 = (bf16[2,128,512]{2,1,0:T(8,128)(2,1)S(1)}, bf16[2,128,512]{2,1,0:T(8,128)(2,1)S(1)}, u32[]{:S(2)}, u32[]{:S(2)}) collective-permute-start(bf16[2,128,512]{2,1,0:T(8,128)(2,1)S(1)} %bitcast.24), channel_id=1, source_target_pairs={{0,2},{2,0},{1,3},{3,1},{4,6},{6,4},{5,7},{7,5},{8,10},{10,8},{9,1... | collective-permute-start | bytes 786440 | tf_op jit(solution)/shard_map/ppermute | solution.py:26
  22.4 1.4 copy.11
  23.8 2.9 %copy.13.gate_ref = bf16[7,128,1024]{2,1,0:T(8,128)(2,1)S(1)} copy(bf16[7,128,1024]{1,2,0:T(8,128)(2,1)} %bitcast.21) | data formatting | bytes 3670016 | tf_op jit(solution)/shard_map/reshape | solution.py:154
  26.7 4.4 %copy.14.up_ref = bf16[7,128,1024]{2,1,0:T(8,128)(2,1)} copy(bf16[7,128,1024]{1,2,0:T(8,128)(2,1)} %bitcast.22) | data formatting | bytes 3670016 | tf_op jit(solution)/shard_map/reshape | solution.py:154
  31.8 0.7 slice_bitcast_fusion.1
  32.5 3.1 %shard_map.64.place_ref = s32[56]{0:T(128)S(1)} custom-call(s32[7,8]{1,0:T(8,128)S(1)} %copy-done.1, bf16[8,1024]{1,0:T(8,128)(2,1)S(1)} %get-tuple-element.28.gate_ref, bf16[8,1024]{1,0:T(8,128)(2,1)S(1)} %get-tuple-element.27.up_ref, bf16[8,512]{1,0:T(8,128)(2,1)S(1)} %slice_bitcast_fusion.4.hidden_ref, bf16[8,512]{1,0:T(8,128)(2,1)S(1)} %slice_bitcast_fusion.3.near_ref), custom_call_target="tpu_custom_call" | custom-call | tf_op jit(solution)/shard_map/pallas_call | solution.py:157
  36.1 1.1 broadcast_in_dim.15
  37.2 4.8 %all-to-all-start.1 = ((bf16[4,2,128,512]{3,2,1,0:T(8,128)(2,1)}), bf16[4,2,128,512]{3,2,1,0:T(8,128)(2,1)S(1)}, u32[]{:S(2)}, u32[]{:S(2)}) async-start(bf16[4,2,128,512]{3,2,1,0:T(8,128)(2,1)} %broadcast_in_dim.15), calls=%async_computation.1 | async-start | bytes 2097152 | tf_op jit(solution)/shard_map/all_to_all | solution.py:35
  42.0 1.9 %collective-permute-start = (bf16[4,2,128,512]{3,2,1,0:T(8,128)(2,1)S(1)}, bf16[4,2,128,512]{3,2,1,0:T(8,128)(2,1)}, u32[]{:S(2)}, u32[]{:S(2)}) collective-permute-start(bf16[4,2,128,512]{3,2,1,0:T(8,128)(2,1)S(1)} %all-to-all-done.a_ref), channel_id=1, source_target_pairs={{0,1},{1,0},{2,3},{3,2},{4,5},{5,4},{6,7},{7,6},{8,9},{9,8},{10,11... | collective-permute-start | bytes 3145736 | tf_op jit(solution)/shard_map/ppermute | solution.py:26
  44.0 12.3 %all-to-all-done.1.b_ref = bf16[4,2,128,512]{3,2,1,0:T(8,128)(2,1)S(1)} async-done(((bf16[4,2,128,512]{3,2,1,0:T(8,128)(2,1)}), bf16[4,2,128,512]{3,2,1,0:T(8,128)(2,1)S(1)}, u32[]{:S(2)}, u32[]{:S(2)}) %all-to-all-start.1) | async-done | bytes 1048608 | tf_op jit(solution)/shard_map/all_to_all | solution.py:35
  56.3 1.9 %collective-permute-start.2 = (bf16[4,2,128,512]{3,2,1,0:T(8,128)(2,1)S(1)}, bf16[4,2,128,512]{3,2,1,0:T(8,128)(2,1)}, u32[]{:S(2)}, u32[]{:S(2)}) collective-permute-start(bf16[4,2,128,512]{3,2,1,0:T(8,128)(2,1)S(1)} %all-to-all-done.1.b_ref), channel_id=1, source_target_pairs={{0,1},{1,0},{2,3},{3,2},{4,5},{5,4},{6,7},{7,6},{8,9},{9,8},{10,11... | collective-permute-start | bytes 3145736 | tf_op jit(solution)/shard_map/ppermute | solution.py:26
  58.2 2.7 %collective-permute-done.2.bc_ref = bf16[4,2,128,512]{3,2,1,0:T(8,128)(2,1)} collective-permute-done((bf16[4,2,128,512]{3,2,1,0:T(8,128)(2,1)S(1)}, bf16[4,2,128,512]{3,2,1,0:T(8,128)(2,1)}, u32[]{:S(2)}, u32[]{:S(2)}) %collective-permute-start.2) | collective-permute-done | bytes 1048608 | tf_op jit(solution)/shard_map/ppermute | solution.py:26
  61.0 12.4 %shard_map.65 = (bf16[32,256,128]{2,1,0:T(8,128)(2,1)}, bf16[16,256,128]{2,1,0:T(8,128)(2,1)}, bf16[16,256,128]{2,1,0:T(8,128)(2,1)}) custom-call(bf16[4,2,128,512]{3,2,1,0:T(8,128)(2,1)} %copy-done.4, bf16[4,2,128,512]{3,2,1,0:T(8,128)(2,1)} %collective-permute-done.ac_ref, bf16[4,2,128,512]{3,2,1,0:T(8,128)(2,1)} %copy-done.5, ...), custom_call_target="tpu_custom_call" | custom-call | flops 3758096384 | bytes 14680064 | tf_op jit(solution)/shard_map/pallas_call | solution.py:169
  73.3 4.8 %all-to-all-start.2 = ((bf16[32,256,128]{2,1,0:T(8,128)(2,1)}), bf16[32,256,128]{2,1,0:T(8,128)(2,1)S(1)}, u32[]{:S(2)}, u32[]{:S(2)}) async-start(bf16[32,256,128]{2,1,0:T(8,128)(2,1)} %get-tuple-element.18), calls=%async_computation.2 | async-start | bytes 4194304 | tf_op jit(solution)/shard_map/all_to_all | solution.py:190
  78.1 11.9 %collective-permute-start.6 = (bf16[16,256,128]{2,1,0:T(8,128)(2,1)}, bf16[16,256,128]{2,1,0:T(8,128)(2,1)}, u32[]{:S(2)}, u32[]{:S(2)}) collective-permute-start(bf16[16,256,128]{2,1,0:T(8,128)(2,1)} %get-tuple-element.22), channel_id=1, source_target_pairs={{0,64},{64,0},{1,65},{65,1},{2,66},{66,2},{3,67},{67,3},{4,68},{68... | collective-permute-start | bytes 3145736 | tf_op jit(solution)/shard_map/ppermute | solution.py:26
  90.1 12.6 %all-to-all-done.2.got_ref = bf16[32,256,128]{2,1,0:T(8,128)(2,1)S(1)} async-done(((bf16[32,256,128]{2,1,0:T(8,128)(2,1)}), bf16[32,256,128]{2,1,0:T(8,128)(2,1)S(1)}, u32[]{:S(2)}, u32[]{:S(2)}) %all-to-all-start.2) | async-done | bytes 2097184 | tf_op jit(solution)/shard_map/all_to_all | solution.py:190
  102.9 11.9 %collective-permute-start.3 = (bf16[4,256,128]{2,1,0:T(8,128)(2,1)S(1)}, bf16[4,256,128]{2,1,0:T(8,128)(2,1)S(1)}, u32[]{:S(2)}, u32[]{:S(2)}) collective-permute-start(bf16[4,256,128]{2,1,0:T(8,128)(2,1)S(1)} %get-tuple-element.20), channel_id=1, source_target_pairs={{0,64},{64,0},{1,65},{65,1},{2,66},{66,2},{3,67},{67,3},{4,68},{68... | collective-permute-start | bytes 786440 | tf_op jit(solution)/shard_map/ppermute | solution.py:26
  114.8 5.5 %collective-permute-done.3.order_ref = bf16[4,256,128]{2,1,0:T(8,128)(2,1)S(1)} collective-permute-done((bf16[4,256,128]{2,1,0:T(8,128)(2,1)S(1)}, bf16[4,256,128]{2,1,0:T(8,128)(2,1)S(1)}, u32[]{:S(2)}, u32[]{:S(2)}) %collective-permute-start.3) | collective-permute-done | bytes 262176 | tf_op jit(solution)/shard_map/ppermute | solution.py:26
  120.3 1.5 shard_map.67
  121.7 4.0 %collective-permute-start.7 = (bf16[4,256,128]{2,1,0:T(8,128)(2,1)S(1)}, bf16[4,256,128]{2,1,0:T(8,128)(2,1)S(1)}, u32[]{:S(2)}, u32[]{:S(2)}) collective-permute-start(bf16[4,256,128]{2,1,0:T(8,128)(2,1)S(1)} %get-tuple-element.24), channel_id=1, source_target_pairs={{0,16},{16,32},{32,48},{48,0},{1,17},{17,33},{33,49},{49,1},{2,18}... | collective-permute-start | bytes 786440 | tf_op jit(solution)/shard_map/ppermute | solution.py:31
  125.7 1.9 %collective-permute-start.8 = (bf16[4,256,128]{2,1,0:T(8,128)(2,1)S(1)}, bf16[4,256,128]{2,1,0:T(8,128)(2,1)S(1)}, u32[]{:S(2)}, u32[]{:S(2)}) collective-permute-start(bf16[4,256,128]{2,1,0:T(8,128)(2,1)S(1)} %get-tuple-element.25), channel_id=1, source_target_pairs={{0,48},{16,0},{32,16},{48,32},{1,49},{17,1},{33,17},{49,33},{2,50}... | collective-permute-start | bytes 786440 | tf_op jit(solution)/shard_map/ppermute | solution.py:31
  127.7 3.9 %collective-permute-start.9 = (bf16[4,256,128]{2,1,0:T(8,128)(2,1)S(1)}, bf16[4,256,128]{2,1,0:T(8,128)(2,1)S(1)}, u32[]{:S(2)}, u32[]{:S(2)}) collective-permute-start(bf16[4,256,128]{2,1,0:T(8,128)(2,1)S(1)} %get-tuple-element.26), channel_id=1, source_target_pairs={{0,32},{16,48},{32,0},{48,16},{1,33},{17,49},{33,1},{49,17},{2,34}... | collective-permute-start | bytes 786440 | tf_op jit(solution)/shard_map/ppermute | solution.py:31
  131.7 1.9 %collective-permute-start.4 = (bf16[2,256,128]{2,1,0:T(8,128)(2,1)S(1)}, bf16[2,256,128]{2,1,0:T(8,128)(2,1)S(1)}, u32[]{:S(2)}, u32[]{:S(2)}) collective-permute-start(bf16[2,256,128]{2,1,0:T(8,128)(2,1)S(1)} %slice.83), channel_id=1, source_target_pairs={{0,128},{128,0},{1,129},{129,1},{2,130},{130,2},{3,131},{131,3},{4... | collective-permute-start | bytes 393224 | tf_op jit(solution)/shard_map/ppermute | solution.py:26
  133.6 7.1 %collective-permute-done.8 = bf16[4,256,128]{2,1,0:T(8,128)(2,1)S(1)} collective-permute-done((bf16[4,256,128]{2,1,0:T(8,128)(2,1)S(1)}, bf16[4,256,128]{2,1,0:T(8,128)(2,1)S(1)}, u32[]{:S(2)}, u32[]{:S(2)}) %collective-permute-start.8) | collective-permute-done | bytes 262176 | tf_op jit(solution)/shard_map/ppermute | solution.py:31
  140.9 1.9 %collective-permute-start.10 = (bf16[2,256,128]{2,1,0:T(8,128)(2,1)S(1)}, bf16[2,256,128]{2,1,0:T(8,128)(2,1)S(1)}, u32[]{:S(2)}, u32[]{:S(2)}) collective-permute-start(bf16[2,256,128]{2,1,0:T(8,128)(2,1)S(1)} %slice.82), channel_id=1, source_target_pairs={{0,128},{128,0},{1,129},{129,1},{2,130},{130,2},{3,131},{131,3},{4... | collective-permute-start | bytes 393224 | tf_op jit(solution)/shard_map/ppermute | solution.py:26
  142.9 9.4 %collective-permute-start.5 = (bf16[1,256,128]{2,1,0:T(8,128)(2,1)S(1)}, bf16[1,256,128]{2,1,0:T(8,128)(2,1)S(1)}, u32[]{:S(2)}, u32[]{:S(2)}) collective-permute-start(bf16[1,256,128]{2,1,0:T(8,128)(2,1)S(1)} %slice.85), channel_id=1, source_target_pairs={{0,256},{256,0},{1,257},{257,1},{2,258},{258,2},{3,259},{259,3},{4... | collective-permute-start | bytes 196616 | tf_op jit(solution)/shard_map/ppermute | solution.py:26
  152.4 4.7 %collective-permute-start.11 = (bf16[1,256,128]{2,1,0:T(8,128)(2,1)S(1)}, bf16[1,256,128]{2,1,0:T(8,128)(2,1)S(1)}, u32[]{:S(2)}, u32[]{:S(2)}) collective-permute-start(bf16[1,256,128]{2,1,0:T(8,128)(2,1)S(1)} %slice.84), channel_id=1, source_target_pairs={{0,256},{256,0},{1,257},{257,1},{2,258},{258,2},{3,259},{259,3},{4... | collective-permute-start | bytes 196616 | tf_op jit(solution)/shard_map/ppermute | solution.py:26
  157.1 6.9 %collective-permute-done.11 = bf16[1,256,128]{2,1,0:T(8,128)(2,1)S(1)} collective-permute-done((bf16[1,256,128]{2,1,0:T(8,128)(2,1)S(1)}, bf16[1,256,128]{2,1,0:T(8,128)(2,1)S(1)}, u32[]{:S(2)}, u32[]{:S(2)}) %collective-permute-start.11) | collective-permute-done | bytes 65568 | tf_op jit(solution)/shard_map/ppermute | solution.py:26
  164.0 0.7 pad_maximum_fusion
  (37 shorter events, 1.8 us)
Async XLA Ops:
  1.1 21.3 %copy-start.6 = (bf16[512,896]{1,0:T(8,128)(2,1)S(1)}, bf16[512,896]{1,0:T(8,128)(2,1)}, u32[]{:S(2)}) copy-start(bf16[512,896]{1,0:T(8,128)(2,1)} %param.7) | copy-start | bytes 2752516
  2.2 30.3 %all-to-all-start = ((bf16[4,2,128,512]{3,2,1,0:T(8,128)(2,1)}), bf16[4,2,128,512]{3,2,1,0:T(8,128)(2,1)S(1)}, u32[]{:S(2)}, u32[]{:S(2)}) async-start(bf16[4,2,128,512]{3,2,1,0:T(8,128)(2,1)} %broadcast_in_dim.14), calls=%async_computation | async-start | bytes 2097152 | tf_op jit(solution)/shard_map/all_to_all | solution.py:35
  6.7 29.5 %collective-permute-start.1 = (bf16[2,128,512]{2,1,0:T(8,128)(2,1)S(1)}, bf16[2,128,512]{2,1,0:T(8,128)(2,1)S(1)}, u32[]{:S(2)}, u32[]{:S(2)}) collective-permute-start(bf16[2,128,512]{2,1,0:T(8,128)(2,1)S(1)} %bitcast.24), channel_id=1, source_target_pairs={{0,2},{2,0},{1,3},{3,1},{4,6},{6,4},{5,7},{7,5},{8,10},{10,8},{9,1... | collective-permute-start | bytes 786440 | tf_op jit(solution)/shard_map/ppermute | solution.py:26
  26.7 5.1 %copy-start.3 = (bf16[7,128,1024]{2,1,0:T(8,128)(2,1)}, bf16[7,128,1024]{2,1,0:T(8,128)(2,1)S(1)}, u32[]{:S(2)}) copy-start(bf16[7,128,1024]{2,1,0:T(8,128)(2,1)S(1)} %copy.13.gate_ref) | copy-start | bytes 5505028
  26.7 5.8 %copy-start.1 = (s32[7,8]{1,0:T(8,128)S(1)}, s32[7,8]{1,0:T(8,128)}, u32[]{:S(2)}) copy-start(s32[7,8]{1,0:T(8,128)} %owner_ref.1) | copy-start | bytes 676
  32.5 28.5 %copy-start.4 = (bf16[4,2,128,512]{3,2,1,0:T(8,128)(2,1)}, bf16[4,2,128,512]{3,2,1,0:T(8,128)(2,1)S(1)}, u32[]{:S(2)}) copy-start(bf16[4,2,128,512]{3,2,1,0:T(8,128)(2,1)S(1)} %all-to-all-done.a_ref) | copy-start | bytes 3145732
  35.6 0.5 copy-start.2
  37.2 19.1 %all-to-all-start.1 = ((bf16[4,2,128,512]{3,2,1,0:T(8,128)(2,1)}), bf16[4,2,128,512]{3,2,1,0:T(8,128)(2,1)S(1)}, u32[]{:S(2)}, u32[]{:S(2)}) async-start(bf16[4,2,128,512]{3,2,1,0:T(8,128)(2,1)} %broadcast_in_dim.15), calls=%async_computation.1 | async-start | bytes 2097152 | tf_op jit(solution)/shard_map/all_to_all | solution.py:35
  42.0 16.2 %collective-permute-start = (bf16[4,2,128,512]{3,2,1,0:T(8,128)(2,1)S(1)}, bf16[4,2,128,512]{3,2,1,0:T(8,128)(2,1)}, u32[]{:S(2)}, u32[]{:S(2)}) collective-permute-start(bf16[4,2,128,512]{3,2,1,0:T(8,128)(2,1)S(1)} %all-to-all-done.a_ref), channel_id=1, source_target_pairs={{0,1},{1,0},{2,3},{3,2},{4,5},{5,4},{6,7},{7,6},{8,9},{9,8},{10,11... | collective-permute-start | bytes 3145736 | tf_op jit(solution)/shard_map/ppermute | solution.py:26
  56.3 4.7 %copy-start.5 = (bf16[4,2,128,512]{3,2,1,0:T(8,128)(2,1)}, bf16[4,2,128,512]{3,2,1,0:T(8,128)(2,1)S(1)}, u32[]{:S(2)}) copy-start(bf16[4,2,128,512]{3,2,1,0:T(8,128)(2,1)S(1)} %all-to-all-done.1.b_ref) | copy-start | bytes 3145732
  56.3 4.7 %collective-permute-start.2 = (bf16[4,2,128,512]{3,2,1,0:T(8,128)(2,1)S(1)}, bf16[4,2,128,512]{3,2,1,0:T(8,128)(2,1)}, u32[]{:S(2)}, u32[]{:S(2)}) collective-permute-start(bf16[4,2,128,512]{3,2,1,0:T(8,128)(2,1)S(1)} %all-to-all-done.1.b_ref), channel_id=1, source_target_pairs={{0,1},{1,0},{2,3},{3,2},{4,5},{5,4},{6,7},{7,6},{8,9},{9,8},{10,11... | collective-permute-start | bytes 3145736 | tf_op jit(solution)/shard_map/ppermute | solution.py:26
  73.3 29.3 %all-to-all-start.2 = ((bf16[32,256,128]{2,1,0:T(8,128)(2,1)}), bf16[32,256,128]{2,1,0:T(8,128)(2,1)S(1)}, u32[]{:S(2)}, u32[]{:S(2)}) async-start(bf16[32,256,128]{2,1,0:T(8,128)(2,1)} %get-tuple-element.18), calls=%async_computation.2 | async-start | bytes 4194304 | tf_op jit(solution)/shard_map/all_to_all | solution.py:190
  78.1 42.1 %copy-start = (bf16[16,256,128]{2,1,0:T(8,128)(2,1)S(1)}, bf16[16,256,128]{2,1,0:T(8,128)(2,1)}, u32[]{:S(2)}) copy-start(bf16[16,256,128]{2,1,0:T(8,128)(2,1)} %get-tuple-element.21.keep_ref) | copy-start | bytes 3145732
  78.1 36.7 %collective-permute-start.6 = (bf16[16,256,128]{2,1,0:T(8,128)(2,1)}, bf16[16,256,128]{2,1,0:T(8,128)(2,1)}, u32[]{:S(2)}, u32[]{:S(2)}) collective-permute-start(bf16[16,256,128]{2,1,0:T(8,128)(2,1)} %get-tuple-element.22), channel_id=1, source_target_pairs={{0,64},{64,0},{1,65},{65,1},{2,66},{66,2},{3,67},{67,3},{4,68},{68... | collective-permute-start | bytes 3145736 | tf_op jit(solution)/shard_map/ppermute | solution.py:26
  102.9 17.3 %collective-permute-start.3 = (bf16[4,256,128]{2,1,0:T(8,128)(2,1)S(1)}, bf16[4,256,128]{2,1,0:T(8,128)(2,1)S(1)}, u32[]{:S(2)}, u32[]{:S(2)}) collective-permute-start(bf16[4,256,128]{2,1,0:T(8,128)(2,1)S(1)} %get-tuple-element.20), channel_id=1, source_target_pairs={{0,64},{64,0},{1,65},{65,1},{2,66},{66,2},{3,67},{67,3},{4,68},{68... | collective-permute-start | bytes 786440 | tf_op jit(solution)/shard_map/ppermute | solution.py:26
  121.7 11.9 %collective-permute-start.7 = (bf16[4,256,128]{2,1,0:T(8,128)(2,1)S(1)}, bf16[4,256,128]{2,1,0:T(8,128)(2,1)S(1)}, u32[]{:S(2)}, u32[]{:S(2)}) collective-permute-start(bf16[4,256,128]{2,1,0:T(8,128)(2,1)S(1)} %get-tuple-element.24), channel_id=1, source_target_pairs={{0,16},{16,32},{32,48},{48,0},{1,17},{17,33},{33,49},{49,1},{2,18}... | collective-permute-start | bytes 786440 | tf_op jit(solution)/shard_map/ppermute | solution.py:31
  125.7 15.0 %collective-permute-start.8 = (bf16[4,256,128]{2,1,0:T(8,128)(2,1)S(1)}, bf16[4,256,128]{2,1,0:T(8,128)(2,1)S(1)}, u32[]{:S(2)}, u32[]{:S(2)}) collective-permute-start(bf16[4,256,128]{2,1,0:T(8,128)(2,1)S(1)} %get-tuple-element.25), channel_id=1, source_target_pairs={{0,48},{16,0},{32,16},{48,32},{1,49},{17,1},{33,17},{49,33},{2,50}... | collective-permute-start | bytes 786440 | tf_op jit(solution)/shard_map/ppermute | solution.py:31
  127.7 13.1 %collective-permute-start.9 = (bf16[4,256,128]{2,1,0:T(8,128)(2,1)S(1)}, bf16[4,256,128]{2,1,0:T(8,128)(2,1)S(1)}, u32[]{:S(2)}, u32[]{:S(2)}) collective-permute-start(bf16[4,256,128]{2,1,0:T(8,128)(2,1)S(1)} %get-tuple-element.26), channel_id=1, source_target_pairs={{0,32},{16,48},{32,0},{48,16},{1,33},{17,49},{33,1},{49,17},{2,34}... | collective-permute-start | bytes 786440 | tf_op jit(solution)/shard_map/ppermute | solution.py:31
  131.7 11.2 %collective-permute-start.4 = (bf16[2,256,128]{2,1,0:T(8,128)(2,1)S(1)}, bf16[2,256,128]{2,1,0:T(8,128)(2,1)S(1)}, u32[]{:S(2)}, u32[]{:S(2)}) collective-permute-start(bf16[2,256,128]{2,1,0:T(8,128)(2,1)S(1)} %slice.83), channel_id=1, source_target_pairs={{0,128},{128,0},{1,129},{129,1},{2,130},{130,2},{3,131},{131,3},{4... | collective-permute-start | bytes 393224 | tf_op jit(solution)/shard_map/ppermute | solution.py:26
  140.9 11.4 %collective-permute-start.10 = (bf16[2,256,128]{2,1,0:T(8,128)(2,1)S(1)}, bf16[2,256,128]{2,1,0:T(8,128)(2,1)S(1)}, u32[]{:S(2)}, u32[]{:S(2)}) collective-permute-start(bf16[2,256,128]{2,1,0:T(8,128)(2,1)S(1)} %slice.82), channel_id=1, source_target_pairs={{0,128},{128,0},{1,129},{129,1},{2,130},{130,2},{3,131},{131,3},{4... | collective-permute-start | bytes 393224 | tf_op jit(solution)/shard_map/ppermute | solution.py:26
  142.9 14.2 %collective-permute-start.5 = (bf16[1,256,128]{2,1,0:T(8,128)(2,1)S(1)}, bf16[1,256,128]{2,1,0:T(8,128)(2,1)S(1)}, u32[]{:S(2)}, u32[]{:S(2)}) collective-permute-start(bf16[1,256,128]{2,1,0:T(8,128)(2,1)S(1)} %slice.85), channel_id=1, source_target_pairs={{0,256},{256,0},{1,257},{257,1},{2,258},{258,2},{3,259},{259,3},{4... | collective-permute-start | bytes 196616 | tf_op jit(solution)/shard_map/ppermute | solution.py:26
  152.4 11.6 %collective-permute-start.11 = (bf16[1,256,128]{2,1,0:T(8,128)(2,1)S(1)}, bf16[1,256,128]{2,1,0:T(8,128)(2,1)S(1)}, u32[]{:S(2)}, u32[]{:S(2)}) collective-permute-start(bf16[1,256,128]{2,1,0:T(8,128)(2,1)S(1)} %slice.84), channel_id=1, source_target_pairs={{0,256},{256,0},{1,257},{257,1},{2,258},{258,2},{3,259},{259,3},{4... | collective-permute-start | bytes 196616 | tf_op jit(solution)/shard_map/ppermute | solution.py:26

commit v10 on v6

--- a/solution.py
+++ b/solution.py
@@ -14,6 +14,7 @@
 TOK = 512
 ROWS = 32
 NX, NZ, CAP = 4, 8, 2
+VMEM_MIB = 60
 AXES = {"z8": 2, "z4": 2, "z2": 2, "x": 4, "y": 4, "zh": 2, "core": 2}
 VMEM = pl.BlockSpec(memory_space=pltpu.VMEM)
 HBM = pl.BlockSpec(memory_space=pltpu.HBM)
@@ -34,14 +35,14 @@
     return lax.all_to_all(jnp.broadcast_to(value[None], (AXES[axis],) + value.shape), axis, 0, 0, tiled=True)
 
 
-def call(kernel, out_shape, in_specs, out_specs, scratch=(), flops=0, bytes_accessed=0):
+def call(kernel, out_shape, in_specs, out_specs, scratch=(), flops=0, bytes_accessed=0, vmem_mib=16):
     return pl.pallas_call(
         kernel,
         out_shape=out_shape,
         in_specs=in_specs,
         out_specs=out_specs,
         scratch_shapes=list(scratch),
-        compiler_params=pltpu.CompilerParams(vmem_limit_bytes=40 * 1024 * 1024),
+        compiler_params=pltpu.CompilerParams(vmem_limit_bytes=vmem_mib * 2**20),
         cost_estimate=pl.CostEstimate(flops=flops, bytes_accessed=bytes_accessed, transcendentals=0),
     )
 
@@ -161,11 +162,11 @@
             pltpu.SemaphoreType.DMA((3 * COLS,)),
             pltpu.SemaphoreType.DMA((6,)),
         ],
-        flops=8 * BLOCKS * BS * BS * TOK, bytes_accessed=14 * 2**20,
+        flops=8 * BLOCKS * BS * BS * TOK, bytes_accessed=14 * 2**20, vmem_mib=VMEM_MIB,
     )(a, ac, b, bc, gate_t, up_t, hidden, block_rows, place)
 
     def over_x(parts):
-        parts = [parts[0]] + [shift(parts[i], "x", i) for i in range(1, NX)]
+        parts = [parts[0]] + [shift(parts[i], "x", i) for i in (1, 3, 2)]
         return sum(part.astype(f32) for part in parts)
 
     def halve(keep, axis):

time: 165 us -> 164 us (level)
  starting transfers between devices: 92.4 us -> 88.9 us
  Pallas kernels: 14.5 us -> 17.6 us
    pallas_call x1, Pallas kernels: 11.5 us -> 14.5 us  [body(): call(block_kernel, [jax.ShapeDtypeStruct((count, 2 * BS, BS), bf16) for c...]
    unnamed x10 -> x16, local copies, waits for them, and re-layouts: 2.7 us -> 0.54 us
    ppermute x9, starting transfers between devices: 62.9 us -> 61.1 us  [swap(): return lax.ppermute(value, axis, [(0, 1), (1, 0)])]
    ppermute x9, waiting for transfers between devices: 10.7 us -> 12.4 us  [swap(): return lax.ppermute(value, axis, [(0, 1), (1, 0)])]
    ppermute x6, starting transfers between devices: 20.2 us -> 18.5 us  [shift(): lax.ppermute(value, axis, [(i, (i + step) % size) for i in range(size)])]
  transfers between devices with their start and end apart: 17 -> 17, of which waited for: 7 -> 9; matrix products, arithmetic and copies ran while one was open for 6% -> 7% of each run, Pallas kernels for 2% -> 2%
where the time goes in v10:
time: 164 us; the launch traced here: 163 us
  starting transfers between devices  88.9 us (54%)
  waiting for transfers between devices  39.8 us (24%)
  Pallas kernels  17.6 us (11%)
  local copies, waits for them, and re-layouts  15.1 us (9%)
    ppermute x9, starting transfers between devices, swap(): return lax.ppermute(value, axis, [(0, 1), (1, 0)])  61.1 us
    ppermute x6, starting transfers between devices, shift(): lax.ppermute(value, axis, [(i, (i + step) % size) for i in range(size)])  18.5 us
    ppermute x6, waiting for transfers between devices, shift(): lax.ppermute(value, axis, [(i, (i + step) % size) for i in range(size)])  15.1 us
    pallas_call x1, Pallas kernels, body(): call(block_kernel, [jax.ShapeDtypeStruct((count, 2 * BS, BS), bf16) for c...  14.5 us
    ppermute x9, waiting for transfers between devices, swap(): return lax.ppermute(value, axis, [(0, 1), (1, 0)])  12.4 us
    all_to_all x2, waiting for transfers between devices, spread(): lax.all_to_all(jnp.broadcast_to(value[None], (AXES[axis],) + value.shape)...  12.3 us
    all_to_all x2, starting transfers between devices, spread(): lax.all_to_all(jnp.broadcast_to(value[None], (AXES[axis],) + value.shape)...  9.26 us
    reshape x2, local copies, waits for them, and re-layouts, body(): w.transpose(0, 3, 1, 2).reshape(COLS, BS, KB * BS)  7.25 us
  transfers between devices with their start and end apart: 17, of which 9 were waited for; matrix products, arithmetic and copies ran while one was open for 7% of the time, Pallas kernels for 2%

profile of v10, /device:TPU:6, one launch (start us, length us, event | category | flops | bytes accessed | tf_op | source)
XLA Modules:
  0.0 163.4 jit_solution(11251597554743523635)
XLA Ops:
  2.2 4.5 %all-to-all-start = ((bf16[4,2,128,512]{3,2,1,0:T(8,128)(2,1)}), bf16[4,2,128,512]{3,2,1,0:T(8,128)(2,1)S(1)}, u32[]{:S(2)}, u32[]{:S(2)}) async-start(bf16[4,2,128,512]{3,2,1,0:T(8,128)(2,1)} %broadcast_in_dim.14), calls=%async_computation | async-start | bytes 2097152 | tf_op jit(solution)/shard_map/all_to_all | solution.py:35
  6.6 15.7 %collective-permute-start.1 = (bf16[2,128,512]{2,1,0:T(8,128)(2,1)S(1)}, bf16[2,128,512]{2,1,0:T(8,128)(2,1)S(1)}, u32[]{:S(2)}, u32[]{:S(2)}) collective-permute-start(bf16[2,128,512]{2,1,0:T(8,128)(2,1)S(1)} %bitcast.43), channel_id=1, source_target_pairs={{0,2},{2,0},{1,3},{3,1},{4,6},{6,4},{5,7},{7,5},{8,10},{10,8},{9,1... | collective-permute-start | bytes 786440 | tf_op jit(solution)/shard_map/ppermute | solution.py:26
  22.4 1.3 copy.11
  23.7 2.9 %copy.13.gate_ref = bf16[7,128,1024]{2,1,0:T(8,128)(2,1)S(1)} copy(bf16[7,128,1024]{1,2,0:T(8,128)(2,1)} %bitcast.40) | data formatting | bytes 3670016 | tf_op jit(solution)/shard_map/reshape | solution.py:139
  26.6 4.4 %copy.14.up_ref = bf16[7,128,1024]{2,1,0:T(8,128)(2,1)} copy(bf16[7,128,1024]{1,2,0:T(8,128)(2,1)} %bitcast.41) | data formatting | bytes 3670016 | tf_op jit(solution)/shard_map/reshape | solution.py:139
  32.4 3.1 %shard_map.64.place_ref = s32[56]{0:T(128)S(1)} custom-call(s32[7,8]{1,0:T(8,128)S(1)} %copy-done, bf16[8,1024]{1,0:T(8,128)(2,1)S(1)} %get-tuple-element.29.gate_ref, bf16[8,1024]{1,0:T(8,128)(2,1)S(1)} %get-tuple-element.28.up_ref, bf16[8,512]{1,0:T(8,128)(2,1)S(1)} %slice_bitcast_fusion.4.hidden_ref, bf16[8,512]{1,0:T(8,128)(2,1)S(1)} %slice_bitcast_fusion.3.near_ref), custom_call_target="tpu_custom_call" | custom-call | tf_op jit(solution)/shard_map/pallas_call | solution.py:142
  37.1 4.8 %all-to-all-start.1 = ((bf16[4,2,128,512]{3,2,1,0:T(8,128)(2,1)}), bf16[4,2,128,512]{3,2,1,0:T(8,128)(2,1)S(1)}, u32[]{:S(2)}, u32[]{:S(2)}) async-start(bf16[4,2,128,512]{3,2,1,0:T(8,128)(2,1)} %broadcast_in_dim.15), calls=%async_computation.1 | async-start | bytes 2097152 | tf_op jit(solution)/shard_map/all_to_all | solution.py:35
  41.9 1.9 %collective-permute-start = (bf16[4,2,128,512]{3,2,1,0:T(8,128)(2,1)S(1)}, bf16[4,2,128,512]{3,2,1,0:T(8,128)(2,1)S(1)}, u32[]{:S(2)}, u32[]{:S(2)}) collective-permute-start(bf16[4,2,128,512]{3,2,1,0:T(8,128)(2,1)S(1)} %all-to-all-done.a_ref), channel_id=1, source_target_pairs={{0,1},{1,0},{2,3},{3,2},{4,5},{5,4},{6,7},{7,6},{8,9},{9,8},{10,11... | collective-permute-start | bytes 3145736 | tf_op jit(solution)/shard_map/ppermute | solution.py:26
  43.9 12.3 %all-to-all-done.1.b_ref = bf16[4,2,128,512]{3,2,1,0:T(8,128)(2,1)S(1)} async-done(((bf16[4,2,128,512]{3,2,1,0:T(8,128)(2,1)}), bf16[4,2,128,512]{3,2,1,0:T(8,128)(2,1)S(1)}, u32[]{:S(2)}, u32[]{:S(2)}) %all-to-all-start.1) | async-done | bytes 1048608 | tf_op jit(solution)/shard_map/all_to_all | solution.py:35
  56.2 1.9 %collective-permute-start.2 = (bf16[4,2,128,512]{3,2,1,0:T(8,128)(2,1)S(1)}, bf16[4,2,128,512]{3,2,1,0:T(8,128)(2,1)}, u32[]{:S(2)}, u32[]{:S(2)}) collective-permute-start(bf16[4,2,128,512]{3,2,1,0:T(8,128)(2,1)S(1)} %all-to-all-done.1.b_ref), channel_id=1, source_target_pairs={{0,1},{1,0},{2,3},{3,2},{4,5},{5,4},{6,7},{7,6},{8,9},{9,8},{10,11... | collective-permute-start | bytes 3145736 | tf_op jit(solution)/shard_map/ppermute | solution.py:26
  58.1 2.7 %collective-permute-done.2.bc_ref = bf16[4,2,128,512]{3,2,1,0:T(8,128)(2,1)} collective-permute-done((bf16[4,2,128,512]{3,2,1,0:T(8,128)(2,1)S(1)}, bf16[4,2,128,512]{3,2,1,0:T(8,128)(2,1)}, u32[]{:S(2)}, u32[]{:S(2)}) %collective-permute-start.2) | collective-permute-done | bytes 1048608 | tf_op jit(solution)/shard_map/ppermute | solution.py:26
  60.9 14.5 %shard_map.65 = (bf16[16,256,128]{2,1,0:T(8,128)(2,1)}, bf16[8,256,128]{2,1,0:T(8,128)(2,1)}, bf16[8,256,128]{2,1,0:T(8,128)(2,1)}, bf16[8,256,128]{2,1,0:T(8,12...) custom-call(bf16[4,2,128,512]{3,2,1,0:T(8,128)(2,1)} %copy-done.3, ...), custom_call_target="tpu_custom_call" | custom-call | flops 3758096384 | bytes 14680064 | tf_op jit(solution)/shard_map/pallas_call | solution.py:152
  75.4 2.5 %collective-permute-start.3 = (bf16[2048,128]{1,0:T(8,128)(2,1)}, bf16[2048,128]{1,0:T(8,128)(2,1)S(1)}, u32[]{:S(2)}, u32[]{:S(2)}) collective-permute-start(bf16[2048,128]{1,0:T(8,128)(2,1)} %bitcast.51), channel_id=1, source_target_pairs={{0,16},{16,32},{32,48},{48,0},{1,17},{17,33},{33,49},{49,1},{2,18}... | collective-permute-start | bytes 1572872 | tf_op jit(solution)/shard_map/ppermute | solution.py:31
  78.0 3.5 %collective-permute-start.4 = (bf16[2048,128]{1,0:T(8,128)(2,1)}, bf16[2048,128]{1,0:T(8,128)(2,1)S(1)}, u32[]{:S(2)}, u32[]{:S(2)}) collective-permute-start(bf16[2048,128]{1,0:T(8,128)(2,1)} %bitcast.50), channel_id=1, source_target_pairs={{0,48},{16,0},{32,16},{48,32},{1,49},{17,1},{33,17},{49,33},{2,50}... | collective-permute-start | bytes 1572872 | tf_op jit(solution)/shard_map/ppermute | solution.py:31
  81.4 3.3 %collective-permute-start.5 = (bf16[2048,128]{1,0:T(8,128)(2,1)}, bf16[2048,128]{1,0:T(8,128)(2,1)S(1)}, u32[]{:S(2)}, u32[]{:S(2)}) collective-permute-start(bf16[2048,128]{1,0:T(8,128)(2,1)} %bitcast.49), channel_id=1, source_target_pairs={{0,32},{16,48},{32,0},{48,16},{1,33},{17,49},{33,1},{49,17},{2,34}... | collective-permute-start | bytes 1572872 | tf_op jit(solution)/shard_map/ppermute | solution.py:31
  84.7 11.9 %collective-permute-start.9 = (bf16[4096,128]{1,0:T(8,128)(2,1)}, bf16[4096,128]{1,0:T(8,128)(2,1)S(1)}, u32[]{:S(2)}, u32[]{:S(2)}) collective-permute-start(bf16[4096,128]{1,0:T(8,128)(2,1)} %bitcast.48), channel_id=1, source_target_pairs={{0,64},{64,0},{1,65},{65,1},{2,66},{66,2},{3,67},{67,3},{4,68},{68... | collective-permute-start | bytes 3145736 | tf_op jit(solution)/shard_map/ppermute | solution.py:26
  96.7 1.3 fusion.6
  97.9 8.2 %collective-permute-done.4 = bf16[2048,128]{1,0:T(8,128)(2,1)S(1)} collective-permute-done((bf16[2048,128]{1,0:T(8,128)(2,1)}, bf16[2048,128]{1,0:T(8,128)(2,1)S(1)}, u32[]{:S(2)}, u32[]{:S(2)}) %collective-permute-start.4) | collective-permute-done | bytes 524320 | tf_op jit(solution)/shard_map/ppermute | solution.py:31
  106.5 11.9 %collective-permute-start.6 = (bf16[1024,128]{1,0:T(8,128)(2,1)S(1)}, bf16[1024,128]{1,0:T(8,128)(2,1)S(1)}, u32[]{:S(2)}, u32[]{:S(2)}) collective-permute-start(bf16[1024,128]{1,0:T(8,128)(2,1)S(1)} %slice.143), channel_id=1, source_target_pairs={{0,64},{64,0},{1,65},{65,1},{2,66},{66,2},{3,67},{67,3},{4,68},{68... | collective-permute-start | bytes 786440 | tf_op jit(solution)/shard_map/ppermute | solution.py:26
  118.4 2.5 %collective-permute-done.9 = bf16[4096,128]{1,0:T(8,128)(2,1)S(1)} collective-permute-done((bf16[4096,128]{1,0:T(8,128)(2,1)}, bf16[4096,128]{1,0:T(8,128)(2,1)S(1)}, u32[]{:S(2)}, u32[]{:S(2)}) %collective-permute-start.9) | collective-permute-done | bytes 1048608 | tf_op jit(solution)/shard_map/ppermute | solution.py:26
  121.2 4.0 %collective-permute-start.10 = (bf16[1024,128]{1,0:T(8,128)(2,1)S(1)}, bf16[1024,128]{1,0:T(8,128)(2,1)S(1)}, u32[]{:S(2)}, u32[]{:S(2)}) collective-permute-start(bf16[1024,128]{1,0:T(8,128)(2,1)S(1)} %get-tuple-element.25), channel_id=1, source_target_pairs={{0,16},{16,32},{32,48},{48,0},{1,17},{17,33},{33,49},{49,1},{2,18}... | collective-permute-start | bytes 786440 | tf_op jit(solution)/shard_map/ppermute | solution.py:31
  125.2 3.0 %collective-permute-start.12 = (bf16[1024,128]{1,0:T(8,128)(2,1)S(1)}, bf16[1024,128]{1,0:T(8,128)(2,1)S(1)}, u32[]{:S(2)}, u32[]{:S(2)}) collective-permute-start(bf16[1024,128]{1,0:T(8,128)(2,1)S(1)} %get-tuple-element.26), channel_id=1, source_target_pairs={{0,32},{16,48},{32,0},{48,16},{1,33},{17,49},{33,1},{49,17},{2,34}... | collective-permute-start | bytes 786440 | tf_op jit(solution)/shard_map/ppermute | solution.py:31
  128.2 2.2 %collective-permute-start.11 = (bf16[1024,128]{1,0:T(8,128)(2,1)S(1)}, bf16[1024,128]{1,0:T(8,128)(2,1)S(1)}, u32[]{:S(2)}, u32[]{:S(2)}) collective-permute-start(bf16[1024,128]{1,0:T(8,128)(2,1)S(1)} %get-tuple-element.27), channel_id=1, source_target_pairs={{0,48},{16,0},{32,16},{48,32},{1,49},{17,1},{33,17},{49,33},{2,50}... | collective-permute-start | bytes 786440 | tf_op jit(solution)/shard_map/ppermute | solution.py:31
  130.6 1.9 %collective-permute-start.7 = (bf16[512,128]{1,0:T(8,128)(2,1)S(1)}, bf16[512,128]{1,0:T(8,128)(2,1)S(1)}, u32[]{:S(2)}, u32[]{:S(2)}) collective-permute-start(bf16[512,128]{1,0:T(8,128)(2,1)S(1)} %slice.145), channel_id=1, source_target_pairs={{0,128},{128,0},{1,129},{129,1},{2,130},{130,2},{3,131},{131,3},{4... | collective-permute-start | bytes 393224 | tf_op jit(solution)/shard_map/ppermute | solution.py:26
  132.5 1.3 collective-permute-done.10
  133.8 2.8 %collective-permute-done.12 = bf16[1024,128]{1,0:T(8,128)(2,1)S(1)} collective-permute-done((bf16[1024,128]{1,0:T(8,128)(2,1)S(1)}, bf16[1024,128]{1,0:T(8,128)(2,1)S(1)}, u32[]{:S(2)}, u32[]{:S(2)}) %collective-permute-start.12) | collective-permute-done | bytes 262176 | tf_op jit(solution)/shard_map/ppermute | solution.py:31
  136.6 2.7 %collective-permute-done.11 = bf16[1024,128]{1,0:T(8,128)(2,1)S(1)} collective-permute-done((bf16[1024,128]{1,0:T(8,128)(2,1)S(1)}, bf16[1024,128]{1,0:T(8,128)(2,1)S(1)}, u32[]{:S(2)}, u32[]{:S(2)}) %collective-permute-start.11) | collective-permute-done | bytes 262176 | tf_op jit(solution)/shard_map/ppermute | solution.py:31
  139.5 1.9 %collective-permute-start.13 = (bf16[512,128]{1,0:T(8,128)(2,1)S(1)}, bf16[512,128]{1,0:T(8,128)(2,1)S(1)}, u32[]{:S(2)}, u32[]{:S(2)}) collective-permute-start(bf16[512,128]{1,0:T(8,128)(2,1)S(1)} %slice.144), channel_id=1, source_target_pairs={{0,128},{128,0},{1,129},{129,1},{2,130},{130,2},{3,131},{131,3},{4... | collective-permute-start | bytes 393224 | tf_op jit(solution)/shard_map/ppermute | solution.py:26
  141.5 9.4 %collective-permute-start.8 = (bf16[256,128]{1,0:T(8,128)(2,1)S(1)}, bf16[256,128]{1,0:T(8,128)(2,1)S(1)}, u32[]{:S(2)}, u32[]{:S(2)}) collective-permute-start(bf16[256,128]{1,0:T(8,128)(2,1)S(1)} %slice.147), channel_id=1, source_target_pairs={{0,256},{256,0},{1,257},{257,1},{2,258},{258,2},{3,259},{259,3},{4... | collective-permute-start | bytes 196616 | tf_op jit(solution)/shard_map/ppermute | solution.py:26
  151.0 4.5 %collective-permute-start.14 = (bf16[256,128]{1,0:T(8,128)(2,1)S(1)}, bf16[256,128]{1,0:T(8,128)(2,1)S(1)}, u32[]{:S(2)}, u32[]{:S(2)}) collective-permute-start(bf16[256,128]{1,0:T(8,128)(2,1)S(1)} %slice.146), channel_id=1, source_target_pairs={{0,256},{256,0},{1,257},{257,1},{2,258},{258,2},{3,259},{259,3},{4... | collective-permute-start | bytes 196616 | tf_op jit(solution)/shard_map/ppermute | solution.py:26
  155.5 2.0 %collective-permute-done.8 = bf16[256,128]{1,0:T(8,128)(2,1)S(1)} collective-permute-done((bf16[256,128]{1,0:T(8,128)(2,1)S(1)}, bf16[256,128]{1,0:T(8,128)(2,1)S(1)}, u32[]{:S(2)}, u32[]{:S(2)}) %collective-permute-start.8) | collective-permute-done | bytes 65568 | tf_op jit(solution)/shard_map/ppermute | solution.py:26
  157.5 5.1 %collective-permute-done.14 = bf16[256,128]{1,0:T(8,128)(2,1)S(1)} collective-permute-done((bf16[256,128]{1,0:T(8,128)(2,1)S(1)}, bf16[256,128]{1,0:T(8,128)(2,1)S(1)}, u32[]{:S(2)}, u32[]{:S(2)}) %collective-permute-start.14) | collective-permute-done | bytes 65568 | tf_op jit(solution)/shard_map/ppermute | solution.py:26
  (45 shorter events, 6.9 us)
Async XLA Ops:
  1.1 21.3 %copy-start.5 = (bf16[512,896]{1,0:T(8,128)(2,1)S(1)}, bf16[512,896]{1,0:T(8,128)(2,1)}, u32[]{:S(2)}) copy-start(bf16[512,896]{1,0:T(8,128)(2,1)} %param.7) | copy-start | bytes 2752516
  2.2 30.2 %all-to-all-start = ((bf16[4,2,128,512]{3,2,1,0:T(8,128)(2,1)}), bf16[4,2,128,512]{3,2,1,0:T(8,128)(2,1)S(1)}, u32[]{:S(2)}, u32[]{:S(2)}) async-start(bf16[4,2,128,512]{3,2,1,0:T(8,128)(2,1)} %broadcast_in_dim.14), calls=%async_computation | async-start | bytes 2097152 | tf_op jit(solution)/shard_map/all_to_all | solution.py:35
  6.6 29.4 %collective-permute-start.1 = (bf16[2,128,512]{2,1,0:T(8,128)(2,1)S(1)}, bf16[2,128,512]{2,1,0:T(8,128)(2,1)S(1)}, u32[]{:S(2)}, u32[]{:S(2)}) collective-permute-start(bf16[2,128,512]{2,1,0:T(8,128)(2,1)S(1)} %bitcast.43), channel_id=1, source_target_pairs={{0,2},{2,0},{1,3},{3,1},{4,6},{6,4},{5,7},{7,5},{8,10},{10,8},{9,1... | collective-permute-start | bytes 786440 | tf_op jit(solution)/shard_map/ppermute | solution.py:26
  26.6 5.1 %copy-start.2 = (bf16[7,128,1024]{2,1,0:T(8,128)(2,1)}, bf16[7,128,1024]{2,1,0:T(8,128)(2,1)S(1)}, u32[]{:S(2)}) copy-start(bf16[7,128,1024]{2,1,0:T(8,128)(2,1)S(1)} %copy.13.gate_ref) | copy-start | bytes 5505028
  26.6 5.8 %copy-start = (s32[7,8]{1,0:T(8,128)S(1)}, s32[7,8]{1,0:T(8,128)}, u32[]{:S(2)}) copy-start(s32[7,8]{1,0:T(8,128)} %owner_ref.1) | copy-start | bytes 676
  32.4 28.5 %copy-start.3 = (bf16[4,2,128,512]{3,2,1,0:T(8,128)(2,1)}, bf16[4,2,128,512]{3,2,1,0:T(8,128)(2,1)S(1)}, u32[]{:S(2)}) copy-start(bf16[4,2,128,512]{3,2,1,0:T(8,128)(2,1)S(1)} %all-to-all-done.a_ref) | copy-start | bytes 3145732
  35.5 0.5 copy-start.1
  37.1 19.1 %all-to-all-start.1 = ((bf16[4,2,128,512]{3,2,1,0:T(8,128)(2,1)}), bf16[4,2,128,512]{3,2,1,0:T(8,128)(2,1)S(1)}, u32[]{:S(2)}, u32[]{:S(2)}) async-start(bf16[4,2,128,512]{3,2,1,0:T(8,128)(2,1)} %broadcast_in_dim.15), calls=%async_computation.1 | async-start | bytes 2097152 | tf_op jit(solution)/shard_map/all_to_all | solution.py:35
  41.9 16.2 %collective-permute-start = (bf16[4,2,128,512]{3,2,1,0:T(8,128)(2,1)S(1)}, bf16[4,2,128,512]{3,2,1,0:T(8,128)(2,1)S(1)}, u32[]{:S(2)}, u32[]{:S(2)}) collective-permute-start(bf16[4,2,128,512]{3,2,1,0:T(8,128)(2,1)S(1)} %all-to-all-done.a_ref), channel_id=1, source_target_pairs={{0,1},{1,0},{2,3},{3,2},{4,5},{5,4},{6,7},{7,6},{8,9},{9,8},{10,11... | collective-permute-start | bytes 3145736 | tf_op jit(solution)/shard_map/ppermute | solution.py:26
  56.2 4.7 %copy-start.4 = (bf16[4,2,128,512]{3,2,1,0:T(8,128)(2,1)}, bf16[4,2,128,512]{3,2,1,0:T(8,128)(2,1)S(1)}, u32[]{:S(2)}) copy-start(bf16[4,2,128,512]{3,2,1,0:T(8,128)(2,1)S(1)} %all-to-all-done.1.b_ref) | copy-start | bytes 3145732
  56.2 4.7 %collective-permute-start.2 = (bf16[4,2,128,512]{3,2,1,0:T(8,128)(2,1)S(1)}, bf16[4,2,128,512]{3,2,1,0:T(8,128)(2,1)}, u32[]{:S(2)}, u32[]{:S(2)}) collective-permute-start(bf16[4,2,128,512]{3,2,1,0:T(8,128)(2,1)S(1)} %all-to-all-done.1.b_ref), channel_id=1, source_target_pairs={{0,1},{1,0},{2,3},{3,2},{4,5},{5,4},{6,7},{7,6},{8,9},{9,8},{10,11... | collective-permute-start | bytes 3145736 | tf_op jit(solution)/shard_map/ppermute | solution.py:26
  58.1 2.8 %copy-start.7 = (bf16[4,2,128,512]{3,2,1,0:T(8,128)(2,1)}, bf16[4,2,128,512]{3,2,1,0:T(8,128)(2,1)S(1)}, u32[]{:S(2)}) copy-start(bf16[4,2,128,512]{3,2,1,0:T(8,128)(2,1)S(1)} %collective-permute-done.ac_ref) | copy-start | bytes 3145732
  75.4 30.8 %copy-start.6 = (bf16[8,256,128]{2,1,0:T(8,128)(2,1)S(1)}, bf16[8,256,128]{2,1,0:T(8,128)(2,1)}, u32[]{:S(2)}) copy-start(bf16[8,256,128]{2,1,0:T(8,128)(2,1)} %get-tuple-element.15) | copy-start | bytes 1572868
  75.4 22.5 %collective-permute-start.3 = (bf16[2048,128]{1,0:T(8,128)(2,1)}, bf16[2048,128]{1,0:T(8,128)(2,1)S(1)}, u32[]{:S(2)}, u32[]{:S(2)}) collective-permute-start(bf16[2048,128]{1,0:T(8,128)(2,1)} %bitcast.51), channel_id=1, source_target_pairs={{0,16},{16,32},{32,48},{48,0},{1,17},{17,33},{33,49},{49,1},{2,18}... | collective-permute-start | bytes 1572872 | tf_op jit(solution)/shard_map/ppermute | solution.py:31
  78.0 28.2 %collective-permute-start.4 = (bf16[2048,128]{1,0:T(8,128)(2,1)}, bf16[2048,128]{1,0:T(8,128)(2,1)S(1)}, u32[]{:S(2)}, u32[]{:S(2)}) collective-permute-start(bf16[2048,128]{1,0:T(8,128)(2,1)} %bitcast.50), channel_id=1, source_target_pairs={{0,48},{16,0},{32,16},{48,32},{1,49},{17,1},{33,17},{49,33},{2,50}... | collective-permute-start | bytes 1572872 | tf_op jit(solution)/shard_map/ppermute | solution.py:31
  81.4 24.8 %collective-permute-start.5 = (bf16[2048,128]{1,0:T(8,128)(2,1)}, bf16[2048,128]{1,0:T(8,128)(2,1)S(1)}, u32[]{:S(2)}, u32[]{:S(2)}) collective-permute-start(bf16[2048,128]{1,0:T(8,128)(2,1)} %bitcast.49), channel_id=1, source_target_pairs={{0,32},{16,48},{32,0},{48,16},{1,33},{17,49},{33,1},{49,17},{2,34}... | collective-permute-start | bytes 1572872 | tf_op jit(solution)/shard_map/ppermute | solution.py:31
  84.7 36.2 %collective-permute-start.9 = (bf16[4096,128]{1,0:T(8,128)(2,1)}, bf16[4096,128]{1,0:T(8,128)(2,1)S(1)}, u32[]{:S(2)}, u32[]{:S(2)}) collective-permute-start(bf16[4096,128]{1,0:T(8,128)(2,1)} %bitcast.48), channel_id=1, source_target_pairs={{0,64},{64,0},{1,65},{65,1},{2,66},{66,2},{3,67},{67,3},{4,68},{68... | collective-permute-start | bytes 3145736 | tf_op jit(solution)/shard_map/ppermute | solution.py:26
  106.5 24.0 %collective-permute-start.6 = (bf16[1024,128]{1,0:T(8,128)(2,1)S(1)}, bf16[1024,128]{1,0:T(8,128)(2,1)S(1)}, u32[]{:S(2)}, u32[]{:S(2)}) collective-permute-start(bf16[1024,128]{1,0:T(8,128)(2,1)S(1)} %slice.143), channel_id=1, source_target_pairs={{0,64},{64,0},{1,65},{65,1},{2,66},{66,2},{3,67},{67,3},{4,68},{68... | collective-permute-start | bytes 786440 | tf_op jit(solution)/shard_map/ppermute | solution.py:26
  121.2 12.6 %collective-permute-start.10 = (bf16[1024,128]{1,0:T(8,128)(2,1)S(1)}, bf16[1024,128]{1,0:T(8,128)(2,1)S(1)}, u32[]{:S(2)}, u32[]{:S(2)}) collective-permute-start(bf16[1024,128]{1,0:T(8,128)(2,1)S(1)} %get-tuple-element.25), channel_id=1, source_target_pairs={{0,16},{16,32},{32,48},{48,0},{1,17},{17,33},{33,49},{49,1},{2,18}... | collective-permute-start | bytes 786440 | tf_op jit(solution)/shard_map/ppermute | solution.py:31
  125.2 11.4 %collective-permute-start.12 = (bf16[1024,128]{1,0:T(8,128)(2,1)S(1)}, bf16[1024,128]{1,0:T(8,128)(2,1)S(1)}, u32[]{:S(2)}, u32[]{:S(2)}) collective-permute-start(bf16[1024,128]{1,0:T(8,128)(2,1)S(1)} %get-tuple-element.26), channel_id=1, source_target_pairs={{0,32},{16,48},{32,0},{48,16},{1,33},{17,49},{33,1},{49,17},{2,34}... | collective-permute-start | bytes 786440 | tf_op jit(solution)/shard_map/ppermute | solution.py:31
  128.2 11.1 %collective-permute-start.11 = (bf16[1024,128]{1,0:T(8,128)(2,1)S(1)}, bf16[1024,128]{1,0:T(8,128)(2,1)S(1)}, u32[]{:S(2)}, u32[]{:S(2)}) collective-permute-start(bf16[1024,128]{1,0:T(8,128)(2,1)S(1)} %get-tuple-element.27), channel_id=1, source_target_pairs={{0,48},{16,0},{32,16},{48,32},{1,49},{17,1},{33,17},{49,33},{2,50}... | collective-permute-start | bytes 786440 | tf_op jit(solution)/shard_map/ppermute | solution.py:31
  130.6 10.9 %collective-permute-start.7 = (bf16[512,128]{1,0:T(8,128)(2,1)S(1)}, bf16[512,128]{1,0:T(8,128)(2,1)S(1)}, u32[]{:S(2)}, u32[]{:S(2)}) collective-permute-start(bf16[512,128]{1,0:T(8,128)(2,1)S(1)} %slice.145), channel_id=1, source_target_pairs={{0,128},{128,0},{1,129},{129,1},{2,130},{130,2},{3,131},{131,3},{4... | collective-permute-start | bytes 393224 | tf_op jit(solution)/shard_map/ppermute | solution.py:26
  139.5 11.4 %collective-permute-start.13 = (bf16[512,128]{1,0:T(8,128)(2,1)S(1)}, bf16[512,128]{1,0:T(8,128)(2,1)S(1)}, u32[]{:S(2)}, u32[]{:S(2)}) collective-permute-start(bf16[512,128]{1,0:T(8,128)(2,1)S(1)} %slice.144), channel_id=1, source_target_pairs={{0,128},{128,0},{1,129},{129,1},{2,130},{130,2},{3,131},{131,3},{4... | collective-permute-start | bytes 393224 | tf_op jit(solution)/shard_map/ppermute | solution.py:26
  141.5 16.0 %collective-permute-start.8 = (bf16[256,128]{1,0:T(8,128)(2,1)S(1)}, bf16[256,128]{1,0:T(8,128)(2,1)S(1)}, u32[]{:S(2)}, u32[]{:S(2)}) collective-permute-start(bf16[256,128]{1,0:T(8,128)(2,1)S(1)} %slice.147), channel_id=1, source_target_pairs={{0,256},{256,0},{1,257},{257,1},{2,258},{258,2},{3,259},{259,3},{4... | collective-permute-start | bytes 196616 | tf_op jit(solution)/shard_map/ppermute | solution.py:26
  151.0 11.6 %collective-permute-start.14 = (bf16[256,128]{1,0:T(8,128)(2,1)S(1)}, bf16[256,128]{1,0:T(8,128)(2,1)S(1)}, u32[]{:S(2)}, u32[]{:S(2)}) collective-permute-start(bf16[256,128]{1,0:T(8,128)(2,1)S(1)} %slice.146), channel_id=1, source_target_pairs={{0,256},{256,0},{1,257},{257,1},{2,258},{258,2},{3,259},{259,3},{4... | collective-permute-start | bytes 196616 | tf_op jit(solution)/shard_map/ppermute | solution.py:26

commit v11 on v10

--- a/solution.py
+++ b/solution.py
@@ -14,7 +14,7 @@
 TOK = 512
 ROWS = 32
 NX, NZ, CAP = 4, 8, 2
-VMEM_MIB = 60
+VMEM_MIB = 50
 AXES = {"z8": 2, "z4": 2, "z2": 2, "x": 4, "y": 4, "zh": 2, "core": 2}
 VMEM = pl.BlockSpec(memory_space=pltpu.VMEM)
 HBM = pl.BlockSpec(memory_space=pltpu.HBM)
@@ -75,7 +75,7 @@
 
 def block_kernel(
     a_ref, ac_ref, b_ref, bc_ref, gate_ref, up_ref, hidden_ref, rows_ref, place_ref,
-    send_ref, first0_ref, first1_ref, first2_ref, first3_ref, keep_ref, x_ref, w_ref, h_ref, picked_ref, out_ref, x_sem, w_sem, out_sem,
+    send_ref, first0_ref, first1_ref, first2_ref, first3_ref, keep_ref, x_ref, w_ref, h_ref, picked_ref, act_ref, out_ref, x_sem, w_sem, out_sem,
 ):
     zh = lax.axis_index("zh")
     core = lax.axis_index("core")
@@ -102,21 +102,20 @@
     for copy in x_copies:
         copy.wait()
     for c in range(COLS):
-        now_ref = picked_ref.at[c % 2]
+        now_ref = picked_ref.at[c]
         for k in range(KB):
             now_ref[k * BS:(k + 1) * BS] = x_ref[rows_ref[c, k]]
         for copy in w_copies[c]:
             copy.wait()
-        picked = now_ref[...]
-        pre = jnp.dot(w_ref[c], picked, preferred_element_type=jnp.float32)
+        pre = jnp.dot(w_ref[c], now_ref[...], preferred_element_type=jnp.float32)
         gate, up = pre[:BS], pre[BS:]
         s = jax.nn.sigmoid(gate)
         h = h_ref[c].astype(jnp.float32)
-        grad_gate = (h * up * (s * (1.0 + gate * (1.0 - s)))).astype(jnp.bfloat16)
-        grad_up = (h * (gate * s)).astype(jnp.bfloat16)
+        act_ref[c, :BS] = (h * up * (s * (1.0 + gate * (1.0 - s)))).astype(jnp.bfloat16)
+        act_ref[c, BS:] = (h * (gate * s)).astype(jnp.bfloat16)
+    for c in range(COLS):
         value = lax.dot_general(
-            picked, jnp.concatenate([grad_gate, grad_up], 0), (((1,), (1,)), ((), ())),
-            preferred_element_type=jnp.float32,
+            picked_ref[c], act_ref[c], (((1,), (1,)), ((), ())), preferred_element_type=jnp.float32
         ).astype(jnp.bfloat16)
         for k in range(KB):
             for m in range(2):
@@ -156,7 +155,8 @@
             pltpu.VMEM((ROWS, BS, TOK), bf16),
             pltpu.VMEM((COLS, 2 * BS, KB * BS), bf16),
             pltpu.VMEM((COLS, BS, TOK), bf16),
-            pltpu.VMEM((2, KB * BS, TOK), bf16),
+            pltpu.VMEM((COLS, KB * BS, TOK), bf16),
+            pltpu.VMEM((COLS, 2 * BS, TOK), bf16),
             pltpu.VMEM((NX * NZ * CAP, 2 * BS, BS), bf16),
             pltpu.SemaphoreType.DMA((16,)),
             pltpu.SemaphoreType.DMA((3 * COLS,)),

time: 164 us -> 161 us (0.982)
  Pallas kernels: 17.6 us -> 13.5 us
  starting transfers between devices: 88.9 us -> 90.6 us
    pallas_call x1, Pallas kernels: 14.5 us -> 10.4 us  [body(): call(block_kernel, [jax.ShapeDtypeStruct((count, 2 * BS, BS), bf16) for c...]
    ppermute x9, starting transfers between devices: 61.1 us -> 63 us  [swap(): return lax.ppermute(value, axis, [(0, 1), (1, 0)])]
where the time goes in v11:
time: 161 us; the launch traced here: 160 us
  starting transfers between devices  90.6 us (56%)
  waiting for transfers between devices  38.6 us (24%)
  local copies, waits for them, and re-layouts  15.1 us (9%)
  Pallas kernels  13.5 us (8%)
    ppermute x9, starting transfers between devices, swap(): return lax.ppermute(value, axis, [(0, 1), (1, 0)])  63 us
    ppermute x6, starting transfers between devices, shift(): lax.ppermute(value, axis, [(i, (i + step) % size) for i in range(size)])  18.4 us
    ppermute x6, waiting for transfers between devices, shift(): lax.ppermute(value, axis, [(i, (i + step) % size) for i in range(size)])  13.9 us
    ppermute x9, waiting for transfers between devices, swap(): return lax.ppermute(value, axis, [(0, 1), (1, 0)])  12.4 us
    all_to_all x2, waiting for transfers between devices, spread(): lax.all_to_all(jnp.broadcast_to(value[None], (AXES[axis],) + value.shape)...  12.4 us
    pallas_call x1, Pallas kernels, body(): call(block_kernel, [jax.ShapeDtypeStruct((count, 2 * BS, BS), bf16) for c...  10.4 us
    all_to_all x2, starting transfers between devices, spread(): lax.all_to_all(jnp.broadcast_to(value[None], (AXES[axis],) + value.shape)...  9.26 us
    reshape x2, local copies, waits for them, and re-layouts, body(): w.transpose(0, 3, 1, 2).reshape(COLS, BS, KB * BS)  7.27 us
  transfers between devices with their start and end apart: 17, of which 9 were waited for; matrix products, arithmetic and copies ran while one was open for 7% of the time, Pallas kernels for 2%

profile of v11, /device:TPU:6, one launch (start us, length us, event | category | flops | bytes accessed | tf_op | source)
XLA Modules:
  0.0 159.8 jit_solution(2231228517800836268)
XLA Ops:
  1.1 1.1 broadcast_in_dim.14
  2.2 4.5 %all-to-all-start = ((bf16[4,2,128,512]{3,2,1,0:T(8,128)(2,1)}), bf16[4,2,128,512]{3,2,1,0:T(8,128)(2,1)}, u32[]{:S(2)}, u32[]{:S(2)}) async-start(bf16[4,2,128,512]{3,2,1,0:T(8,128)(2,1)} %broadcast_in_dim.14), calls=%async_computation | async-start | bytes 2097152 | tf_op jit(solution)/shard_map/all_to_all | solution.py:35
  6.7 15.7 %collective-permute-start.1 = (bf16[2,128,512]{2,1,0:T(8,128)(2,1)S(1)}, bf16[2,128,512]{2,1,0:T(8,128)(2,1)S(1)}, u32[]{:S(2)}, u32[]{:S(2)}) collective-permute-start(bf16[2,128,512]{2,1,0:T(8,128)(2,1)S(1)} %bitcast.49), channel_id=1, source_target_pairs={{0,2},{2,0},{1,3},{3,1},{4,6},{6,4},{5,7},{7,5},{8,10},{10,8},{9,1... | collective-permute-start | bytes 786440 | tf_op jit(solution)/shard_map/ppermute | solution.py:26
  22.9 2.9 %copy.13.gate_ref = bf16[7,128,1024]{2,1,0:T(8,128)(2,1)S(1)} copy(bf16[7,128,1024]{1,2,0:T(8,128)(2,1)} %bitcast.46) | data formatting | bytes 3670016 | tf_op jit(solution)/shard_map/reshape | solution.py:138
  25.9 4.4 %copy.14.up_ref = bf16[7,128,1024]{2,1,0:T(8,128)(2,1)} copy(bf16[7,128,1024]{1,2,0:T(8,128)(2,1)} %bitcast.47) | data formatting | bytes 3670016 | tf_op jit(solution)/shard_map/reshape | solution.py:138
  32.0 3.1 %shard_map.64.place_ref = s32[56]{0:T(128)S(1)} custom-call(s32[7,8]{1,0:T(8,128)S(1)} %copy-done, bf16[8,1024]{1,0:T(8,128)(2,1)S(1)} %get-tuple-element.29.gate_ref, bf16[8,1024]{1,0:T(8,128)(2,1)S(1)} %get-tuple-element.28.up_ref, bf16[8,512]{1,0:T(8,128)(2,1)S(1)} %slice_bitcast_fusion.4.hidden_ref, bf16[8,512]{1,0:T(8,128)(2,1)S(1)} %slice_bitcast_fusion.3.near_ref), custom_call_target="tpu_custom_call" | custom-call | tf_op jit(solution)/shard_map/pallas_call | solution.py:141
  36.2 4.8 %all-to-all-start.1 = ((bf16[4,2,128,512]{3,2,1,0:T(8,128)(2,1)}), bf16[4,2,128,512]{3,2,1,0:T(8,128)(2,1)S(1)}, u32[]{:S(2)}, u32[]{:S(2)}) async-start(bf16[4,2,128,512]{3,2,1,0:T(8,128)(2,1)} %broadcast_in_dim.15), calls=%async_computation.1 | async-start | bytes 2097152 | tf_op jit(solution)/shard_map/all_to_all | solution.py:35
  41.0 1.9 %collective-permute-start = (bf16[4,2,128,512]{3,2,1,0:T(8,128)(2,1)}, bf16[4,2,128,512]{3,2,1,0:T(8,128)(2,1)S(1)}, u32[]{:S(2)}, u32[]{:S(2)}) collective-permute-start(bf16[4,2,128,512]{3,2,1,0:T(8,128)(2,1)} %all-to-all-done.a_ref), channel_id=1, source_target_pairs={{0,1},{1,0},{2,3},{3,2},{4,5},{5,4},{6,7},{7,6},{8,9},{9,8},{10,11... | collective-permute-start | bytes 3145736 | tf_op jit(solution)/shard_map/ppermute | solution.py:26
  42.9 12.4 %all-to-all-done.1.b_ref = bf16[4,2,128,512]{3,2,1,0:T(8,128)(2,1)S(1)} async-done(((bf16[4,2,128,512]{3,2,1,0:T(8,128)(2,1)}), bf16[4,2,128,512]{3,2,1,0:T(8,128)(2,1)S(1)}, u32[]{:S(2)}, u32[]{:S(2)}) %all-to-all-start.1) | async-done | bytes 1048608 | tf_op jit(solution)/shard_map/all_to_all | solution.py:35
  55.2 1.9 %collective-permute-start.2 = (bf16[4,2,128,512]{3,2,1,0:T(8,128)(2,1)S(1)}, bf16[4,2,128,512]{3,2,1,0:T(8,128)(2,1)S(1)}, u32[]{:S(2)}, u32[]{:S(2)}) collective-permute-start(bf16[4,2,128,512]{3,2,1,0:T(8,128)(2,1)S(1)} %all-to-all-done.1.b_ref), channel_id=1, source_target_pairs={{0,1},{1,0},{2,3},{3,2},{4,5},{5,4},{6,7},{7,6},{8,9},{9,8},{10,11... | collective-permute-start | bytes 3145736 | tf_op jit(solution)/shard_map/ppermute | solution.py:26
  57.2 2.6 %collective-permute-done.2.bc_ref = bf16[4,2,128,512]{3,2,1,0:T(8,128)(2,1)S(1)} collective-permute-done((bf16[4,2,128,512]{3,2,1,0:T(8,128)(2,1)S(1)}, bf16[4,2,128,512]{3,2,1,0:T(8,128)(2,1)S(1)}, u32[]{:S(2)}, u32[]{:S(2)}) %collective-permute-start.2) | collective-permute-done | bytes 1048608 | tf_op jit(solution)/shard_map/ppermute | solution.py:26
  60.8 10.4 %shard_map.65 = (bf16[16,256,128]{2,1,0:T(8,128)(2,1)S(1)}, bf16[8,256,128]{2,1,0:T(8,128)(2,1)S(1)}, bf16[8,256,128]{2,1,0:T(8,128)(2,1)S(1)}, bf16[8,256,128]{...) custom-call(bf16[4,2,128,512]{3,2,1,0:T(8,128)(2,1)} %all-to-all-done.a_ref, ...), custom_call_target="tpu_custom_call" | custom-call | flops 3758096384 | bytes 14680064 | tf_op jit(solution)/shard_map/pallas_call | solution.py:151
  71.2 2.4 %collective-permute-start.3 = (bf16[2048,128]{1,0:T(8,128)(2,1)S(1)}, bf16[2048,128]{1,0:T(8,128)(2,1)S(1)}, u32[]{:S(2)}, u32[]{:S(2)}) collective-permute-start(bf16[2048,128]{1,0:T(8,128)(2,1)S(1)} %bitcast.45), channel_id=1, source_target_pairs={{0,16},{16,32},{32,48},{48,0},{1,17},{17,33},{33,49},{49,1},{2,18}... | collective-permute-start | bytes 1572872 | tf_op jit(solution)/shard_map/ppermute | solution.py:31
  73.6 3.5 %collective-permute-start.4 = (bf16[2048,128]{1,0:T(8,128)(2,1)S(1)}, bf16[2048,128]{1,0:T(8,128)(2,1)S(1)}, u32[]{:S(2)}, u32[]{:S(2)}) collective-permute-start(bf16[2048,128]{1,0:T(8,128)(2,1)S(1)} %bitcast.44), channel_id=1, source_target_pairs={{0,48},{16,0},{32,16},{48,32},{1,49},{17,1},{33,17},{49,33},{2,50}... | collective-permute-start | bytes 1572872 | tf_op jit(solution)/shard_map/ppermute | solution.py:31
  77.1 3.3 %collective-permute-start.5 = (bf16[2048,128]{1,0:T(8,128)(2,1)S(1)}, bf16[2048,128]{1,0:T(8,128)(2,1)S(1)}, u32[]{:S(2)}, u32[]{:S(2)}) collective-permute-start(bf16[2048,128]{1,0:T(8,128)(2,1)S(1)} %bitcast.43), channel_id=1, source_target_pairs={{0,32},{16,48},{32,0},{48,16},{1,33},{17,49},{33,1},{49,17},{2,34}... | collective-permute-start | bytes 1572872 | tf_op jit(solution)/shard_map/ppermute | solution.py:31
  80.4 12.9 %collective-permute-start.9 = (bf16[4096,128]{1,0:T(8,128)(2,1)S(1)}, bf16[4096,128]{1,0:T(8,128)(2,1)S(1)}, u32[]{:S(2)}, u32[]{:S(2)}) collective-permute-start(bf16[4096,128]{1,0:T(8,128)(2,1)S(1)} %bitcast.42), channel_id=1, source_target_pairs={{0,64},{64,0},{1,65},{65,1},{2,66},{66,2},{3,67},{67,3},{4,68},{68... | collective-permute-start | bytes 3145736 | tf_op jit(solution)/shard_map/ppermute | solution.py:26
  93.3 1.3 fusion.6
  94.6 7.0 %collective-permute-done.4 = bf16[2048,128]{1,0:T(8,128)(2,1)S(1)} collective-permute-done((bf16[2048,128]{1,0:T(8,128)(2,1)S(1)}, bf16[2048,128]{1,0:T(8,128)(2,1)S(1)}, u32[]{:S(2)}, u32[]{:S(2)}) %collective-permute-start.4) | collective-permute-done | bytes 524320 | tf_op jit(solution)/shard_map/ppermute | solution.py:31
  101.9 12.9 %collective-permute-start.6 = (bf16[1024,128]{1,0:T(8,128)(2,1)S(1)}, bf16[1024,128]{1,0:T(8,128)(2,1)S(1)}, u32[]{:S(2)}, u32[]{:S(2)}) collective-permute-start(bf16[1024,128]{1,0:T(8,128)(2,1)S(1)} %slice.143), channel_id=1, source_target_pairs={{0,64},{64,0},{1,65},{65,1},{2,66},{66,2},{3,67},{67,3},{4,68},{68... | collective-permute-start | bytes 786440 | tf_op jit(solution)/shard_map/ppermute | solution.py:26
  114.9 2.5 %collective-permute-done.9 = bf16[4096,128]{1,0:T(8,128)(2,1)S(1)} collective-permute-done((bf16[4096,128]{1,0:T(8,128)(2,1)S(1)}, bf16[4096,128]{1,0:T(8,128)(2,1)S(1)}, u32[]{:S(2)}, u32[]{:S(2)}) %collective-permute-start.9) | collective-permute-done | bytes 1048608 | tf_op jit(solution)/shard_map/ppermute | solution.py:26
  117.6 4.0 %collective-permute-start.10 = (bf16[1024,128]{1,0:T(8,128)(2,1)S(1)}, bf16[1024,128]{1,0:T(8,128)(2,1)S(1)}, u32[]{:S(2)}, u32[]{:S(2)}) collective-permute-start(bf16[1024,128]{1,0:T(8,128)(2,1)S(1)} %get-tuple-element.25), channel_id=1, source_target_pairs={{0,16},{16,32},{32,48},{48,0},{1,17},{17,33},{33,49},{49,1},{2,18}... | collective-permute-start | bytes 786440 | tf_op jit(solution)/shard_map/ppermute | solution.py:31
  121.6 3.0 %collective-permute-start.12 = (bf16[1024,128]{1,0:T(8,128)(2,1)S(1)}, bf16[1024,128]{1,0:T(8,128)(2,1)S(1)}, u32[]{:S(2)}, u32[]{:S(2)}) collective-permute-start(bf16[1024,128]{1,0:T(8,128)(2,1)S(1)} %get-tuple-element.26), channel_id=1, source_target_pairs={{0,32},{16,48},{32,0},{48,16},{1,33},{17,49},{33,1},{49,17},{2,34}... | collective-permute-start | bytes 786440 | tf_op jit(solution)/shard_map/ppermute | solution.py:31
  124.7 2.2 %collective-permute-start.11 = (bf16[1024,128]{1,0:T(8,128)(2,1)S(1)}, bf16[1024,128]{1,0:T(8,128)(2,1)S(1)}, u32[]{:S(2)}, u32[]{:S(2)}) collective-permute-start(bf16[1024,128]{1,0:T(8,128)(2,1)S(1)} %get-tuple-element.27), channel_id=1, source_target_pairs={{0,48},{16,0},{32,16},{48,32},{1,49},{17,1},{33,17},{49,33},{2,50}... | collective-permute-start | bytes 786440 | tf_op jit(solution)/shard_map/ppermute | solution.py:31
  127.0 1.9 %collective-permute-start.7 = (bf16[512,128]{1,0:T(8,128)(2,1)S(1)}, bf16[512,128]{1,0:T(8,128)(2,1)S(1)}, u32[]{:S(2)}, u32[]{:S(2)}) collective-permute-start(bf16[512,128]{1,0:T(8,128)(2,1)S(1)} %slice.145), channel_id=1, source_target_pairs={{0,128},{128,0},{1,129},{129,1},{2,130},{130,2},{3,131},{131,3},{4... | collective-permute-start | bytes 393224 | tf_op jit(solution)/shard_map/ppermute | solution.py:26
  128.9 1.3 collective-permute-done.10
  130.3 2.8 %collective-permute-done.12 = bf16[1024,128]{1,0:T(8,128)(2,1)S(1)} collective-permute-done((bf16[1024,128]{1,0:T(8,128)(2,1)S(1)}, bf16[1024,128]{1,0:T(8,128)(2,1)S(1)}, u32[]{:S(2)}, u32[]{:S(2)}) %collective-permute-start.12) | collective-permute-done | bytes 262176 | tf_op jit(solution)/shard_map/ppermute | solution.py:31
  133.1 2.7 %collective-permute-done.11 = bf16[1024,128]{1,0:T(8,128)(2,1)S(1)} collective-permute-done((bf16[1024,128]{1,0:T(8,128)(2,1)S(1)}, bf16[1024,128]{1,0:T(8,128)(2,1)S(1)}, u32[]{:S(2)}, u32[]{:S(2)}) %collective-permute-start.11) | collective-permute-done | bytes 262176 | tf_op jit(solution)/shard_map/ppermute | solution.py:31
  136.0 1.9 %collective-permute-start.13 = (bf16[512,128]{1,0:T(8,128)(2,1)S(1)}, bf16[512,128]{1,0:T(8,128)(2,1)S(1)}, u32[]{:S(2)}, u32[]{:S(2)}) collective-permute-start(bf16[512,128]{1,0:T(8,128)(2,1)S(1)} %slice.144), channel_id=1, source_target_pairs={{0,128},{128,0},{1,129},{129,1},{2,130},{130,2},{3,131},{131,3},{4... | collective-permute-start | bytes 393224 | tf_op jit(solution)/shard_map/ppermute | solution.py:26
  137.9 9.5 %collective-permute-start.8 = (bf16[256,128]{1,0:T(8,128)(2,1)S(1)}, bf16[256,128]{1,0:T(8,128)(2,1)S(1)}, u32[]{:S(2)}, u32[]{:S(2)}) collective-permute-start(bf16[256,128]{1,0:T(8,128)(2,1)S(1)} %slice.147), channel_id=1, source_target_pairs={{0,256},{256,0},{1,257},{257,1},{2,258},{258,2},{3,259},{259,3},{4... | collective-permute-start | bytes 196616 | tf_op jit(solution)/shard_map/ppermute | solution.py:26
  147.5 4.3 %collective-permute-start.14 = (bf16[256,128]{1,0:T(8,128)(2,1)S(1)}, bf16[256,128]{1,0:T(8,128)(2,1)S(1)}, u32[]{:S(2)}, u32[]{:S(2)}) collective-permute-start(bf16[256,128]{1,0:T(8,128)(2,1)S(1)} %slice.146), channel_id=1, source_target_pairs={{0,256},{256,0},{1,257},{257,1},{2,258},{258,2},{3,259},{259,3},{4... | collective-permute-start | bytes 196616 | tf_op jit(solution)/shard_map/ppermute | solution.py:26
  151.8 2.4 %collective-permute-done.8 = bf16[256,128]{1,0:T(8,128)(2,1)S(1)} collective-permute-done((bf16[256,128]{1,0:T(8,128)(2,1)S(1)}, bf16[256,128]{1,0:T(8,128)(2,1)S(1)}, u32[]{:S(2)}, u32[]{:S(2)}) %collective-permute-start.8) | collective-permute-done | bytes 65568 | tf_op jit(solution)/shard_map/ppermute | solution.py:26
  154.1 5.0 %collective-permute-done.14 = bf16[256,128]{1,0:T(8,128)(2,1)S(1)} collective-permute-done((bf16[256,128]{1,0:T(8,128)(2,1)S(1)}, bf16[256,128]{1,0:T(8,128)(2,1)S(1)}, u32[]{:S(2)}, u32[]{:S(2)}) %collective-permute-start.14) | collective-permute-done | bytes 65568 | tf_op jit(solution)/shard_map/ppermute | solution.py:26
  (43 shorter events, 7.1 us)
Async XLA Ops:
  1.1 21.3 %copy-start.4 = (bf16[512,896]{1,0:T(8,128)(2,1)S(1)}, bf16[512,896]{1,0:T(8,128)(2,1)}, u32[]{:S(2)}) copy-start(bf16[512,896]{1,0:T(8,128)(2,1)} %param.7) | copy-start | bytes 2752516
  2.2 28.8 %all-to-all-start = ((bf16[4,2,128,512]{3,2,1,0:T(8,128)(2,1)}), bf16[4,2,128,512]{3,2,1,0:T(8,128)(2,1)}, u32[]{:S(2)}, u32[]{:S(2)}) async-start(bf16[4,2,128,512]{3,2,1,0:T(8,128)(2,1)} %broadcast_in_dim.14), calls=%async_computation | async-start | bytes 2097152 | tf_op jit(solution)/shard_map/all_to_all | solution.py:35
  6.7 28.4 %collective-permute-start.1 = (bf16[2,128,512]{2,1,0:T(8,128)(2,1)S(1)}, bf16[2,128,512]{2,1,0:T(8,128)(2,1)S(1)}, u32[]{:S(2)}, u32[]{:S(2)}) collective-permute-start(bf16[2,128,512]{2,1,0:T(8,128)(2,1)S(1)} %bitcast.49), channel_id=1, source_target_pairs={{0,2},{2,0},{1,3},{3,1},{4,6},{6,4},{5,7},{7,5},{8,10},{10,8},{9,1... | collective-permute-start | bytes 786440 | tf_op jit(solution)/shard_map/ppermute | solution.py:26
  25.9 4.4 %copy-start.2 = (bf16[7,128,1024]{2,1,0:T(8,128)(2,1)}, bf16[7,128,1024]{2,1,0:T(8,128)(2,1)S(1)}, u32[]{:S(2)}) copy-start(bf16[7,128,1024]{2,1,0:T(8,128)(2,1)S(1)} %copy.13.gate_ref) | copy-start | bytes 5505028
  25.9 6.1 %copy-start = (s32[7,8]{1,0:T(8,128)S(1)}, s32[7,8]{1,0:T(8,128)}, u32[]{:S(2)}) copy-start(s32[7,8]{1,0:T(8,128)} %owner_ref.1) | copy-start | bytes 676
  31.9 28.8 %copy-start.1 = (s32[7,8]{1,0:T(8,128)S(1)}, s32[7,8]{1,0:T(8,128)}, u32[]{:S(2)}) copy-start(s32[7,8]{1,0:T(8,128)} %rows_ref.1) | copy-start | bytes 676
  36.2 19.1 %all-to-all-start.1 = ((bf16[4,2,128,512]{3,2,1,0:T(8,128)(2,1)}), bf16[4,2,128,512]{3,2,1,0:T(8,128)(2,1)S(1)}, u32[]{:S(2)}, u32[]{:S(2)}) async-start(bf16[4,2,128,512]{3,2,1,0:T(8,128)(2,1)} %broadcast_in_dim.15), calls=%async_computation.1 | async-start | bytes 2097152 | tf_op jit(solution)/shard_map/all_to_all | solution.py:35
  41.0 16.2 %collective-permute-start = (bf16[4,2,128,512]{3,2,1,0:T(8,128)(2,1)}, bf16[4,2,128,512]{3,2,1,0:T(8,128)(2,1)S(1)}, u32[]{:S(2)}, u32[]{:S(2)}) collective-permute-start(bf16[4,2,128,512]{3,2,1,0:T(8,128)(2,1)} %all-to-all-done.a_ref), channel_id=1, source_target_pairs={{0,1},{1,0},{2,3},{3,2},{4,5},{5,4},{6,7},{7,6},{8,9},{9,8},{10,11... | collective-permute-start | bytes 3145736 | tf_op jit(solution)/shard_map/ppermute | solution.py:26
  55.2 4.5 %copy-start.3 = (bf16[4,2,128,512]{3,2,1,0:T(8,128)(2,1)}, bf16[4,2,128,512]{3,2,1,0:T(8,128)(2,1)S(1)}, u32[]{:S(2)}) copy-start(bf16[4,2,128,512]{3,2,1,0:T(8,128)(2,1)S(1)} %all-to-all-done.1.b_ref) | copy-start | bytes 3145732
  55.2 4.5 %collective-permute-start.2 = (bf16[4,2,128,512]{3,2,1,0:T(8,128)(2,1)S(1)}, bf16[4,2,128,512]{3,2,1,0:T(8,128)(2,1)S(1)}, u32[]{:S(2)}, u32[]{:S(2)}) collective-permute-start(bf16[4,2,128,512]{3,2,1,0:T(8,128)(2,1)S(1)} %all-to-all-done.1.b_ref), channel_id=1, source_target_pairs={{0,1},{1,0},{2,3},{3,2},{4,5},{5,4},{6,7},{7,6},{8,9},{9,8},{10,11... | collective-permute-start | bytes 3145736 | tf_op jit(solution)/shard_map/ppermute | solution.py:26
  57.2 2.6 %copy-start.5 = (bf16[4,2,128,512]{3,2,1,0:T(8,128)(2,1)}, bf16[4,2,128,512]{3,2,1,0:T(8,128)(2,1)S(1)}, u32[]{:S(2)}) copy-start(bf16[4,2,128,512]{3,2,1,0:T(8,128)(2,1)S(1)} %collective-permute-done.ac_ref) | copy-start | bytes 3145732
  59.8 1.0 copy-start.6
  71.2 23.4 %collective-permute-start.3 = (bf16[2048,128]{1,0:T(8,128)(2,1)S(1)}, bf16[2048,128]{1,0:T(8,128)(2,1)S(1)}, u32[]{:S(2)}, u32[]{:S(2)}) collective-permute-start(bf16[2048,128]{1,0:T(8,128)(2,1)S(1)} %bitcast.45), channel_id=1, source_target_pairs={{0,16},{16,32},{32,48},{48,0},{1,17},{17,33},{33,49},{49,1},{2,18}... | collective-permute-start | bytes 1572872 | tf_op jit(solution)/shard_map/ppermute | solution.py:31
  73.6 28.0 %collective-permute-start.4 = (bf16[2048,128]{1,0:T(8,128)(2,1)S(1)}, bf16[2048,128]{1,0:T(8,128)(2,1)S(1)}, u32[]{:S(2)}, u32[]{:S(2)}) collective-permute-start(bf16[2048,128]{1,0:T(8,128)(2,1)S(1)} %bitcast.44), channel_id=1, source_target_pairs={{0,48},{16,0},{32,16},{48,32},{1,49},{17,1},{33,17},{49,33},{2,50}... | collective-permute-start | bytes 1572872 | tf_op jit(solution)/shard_map/ppermute | solution.py:31
  77.1 24.5 %collective-permute-start.5 = (bf16[2048,128]{1,0:T(8,128)(2,1)S(1)}, bf16[2048,128]{1,0:T(8,128)(2,1)S(1)}, u32[]{:S(2)}, u32[]{:S(2)}) collective-permute-start(bf16[2048,128]{1,0:T(8,128)(2,1)S(1)} %bitcast.43), channel_id=1, source_target_pairs={{0,32},{16,48},{32,0},{48,16},{1,33},{17,49},{33,1},{49,17},{2,34}... | collective-permute-start | bytes 1572872 | tf_op jit(solution)/shard_map/ppermute | solution.py:31
  80.4 37.0 %collective-permute-start.9 = (bf16[4096,128]{1,0:T(8,128)(2,1)S(1)}, bf16[4096,128]{1,0:T(8,128)(2,1)S(1)}, u32[]{:S(2)}, u32[]{:S(2)}) collective-permute-start(bf16[4096,128]{1,0:T(8,128)(2,1)S(1)} %bitcast.42), channel_id=1, source_target_pairs={{0,64},{64,0},{1,65},{65,1},{2,66},{66,2},{3,67},{67,3},{4,68},{68... | collective-permute-start | bytes 3145736 | tf_op jit(solution)/shard_map/ppermute | solution.py:26
  101.9 25.0 %collective-permute-start.6 = (bf16[1024,128]{1,0:T(8,128)(2,1)S(1)}, bf16[1024,128]{1,0:T(8,128)(2,1)S(1)}, u32[]{:S(2)}, u32[]{:S(2)}) collective-permute-start(bf16[1024,128]{1,0:T(8,128)(2,1)S(1)} %slice.143), channel_id=1, source_target_pairs={{0,64},{64,0},{1,65},{65,1},{2,66},{66,2},{3,67},{67,3},{4,68},{68... | collective-permute-start | bytes 786440 | tf_op jit(solution)/shard_map/ppermute | solution.py:26
  117.6 12.7 %collective-permute-start.10 = (bf16[1024,128]{1,0:T(8,128)(2,1)S(1)}, bf16[1024,128]{1,0:T(8,128)(2,1)S(1)}, u32[]{:S(2)}, u32[]{:S(2)}) collective-permute-start(bf16[1024,128]{1,0:T(8,128)(2,1)S(1)} %get-tuple-element.25), channel_id=1, source_target_pairs={{0,16},{16,32},{32,48},{48,0},{1,17},{17,33},{33,49},{49,1},{2,18}... | collective-permute-start | bytes 786440 | tf_op jit(solution)/shard_map/ppermute | solution.py:31
  121.6 11.4 %collective-permute-start.12 = (bf16[1024,128]{1,0:T(8,128)(2,1)S(1)}, bf16[1024,128]{1,0:T(8,128)(2,1)S(1)}, u32[]{:S(2)}, u32[]{:S(2)}) collective-permute-start(bf16[1024,128]{1,0:T(8,128)(2,1)S(1)} %get-tuple-element.26), channel_id=1, source_target_pairs={{0,32},{16,48},{32,0},{48,16},{1,33},{17,49},{33,1},{49,17},{2,34}... | collective-permute-start | bytes 786440 | tf_op jit(solution)/shard_map/ppermute | solution.py:31
  124.7 11.1 %collective-permute-start.11 = (bf16[1024,128]{1,0:T(8,128)(2,1)S(1)}, bf16[1024,128]{1,0:T(8,128)(2,1)S(1)}, u32[]{:S(2)}, u32[]{:S(2)}) collective-permute-start(bf16[1024,128]{1,0:T(8,128)(2,1)S(1)} %get-tuple-element.27), channel_id=1, source_target_pairs={{0,48},{16,0},{32,16},{48,32},{1,49},{17,1},{33,17},{49,33},{2,50}... | collective-permute-start | bytes 786440 | tf_op jit(solution)/shard_map/ppermute | solution.py:31
  127.0 10.9 %collective-permute-start.7 = (bf16[512,128]{1,0:T(8,128)(2,1)S(1)}, bf16[512,128]{1,0:T(8,128)(2,1)S(1)}, u32[]{:S(2)}, u32[]{:S(2)}) collective-permute-start(bf16[512,128]{1,0:T(8,128)(2,1)S(1)} %slice.145), channel_id=1, source_target_pairs={{0,128},{128,0},{1,129},{129,1},{2,130},{130,2},{3,131},{131,3},{4... | collective-permute-start | bytes 393224 | tf_op jit(solution)/shard_map/ppermute | solution.py:26
  136.0 11.5 %collective-permute-start.13 = (bf16[512,128]{1,0:T(8,128)(2,1)S(1)}, bf16[512,128]{1,0:T(8,128)(2,1)S(1)}, u32[]{:S(2)}, u32[]{:S(2)}) collective-permute-start(bf16[512,128]{1,0:T(8,128)(2,1)S(1)} %slice.144), channel_id=1, source_target_pairs={{0,128},{128,0},{1,129},{129,1},{2,130},{130,2},{3,131},{131,3},{4... | collective-permute-start | bytes 393224 | tf_op jit(solution)/shard_map/ppermute | solution.py:26
  137.9 16.2 %collective-permute-start.8 = (bf16[256,128]{1,0:T(8,128)(2,1)S(1)}, bf16[256,128]{1,0:T(8,128)(2,1)S(1)}, u32[]{:S(2)}, u32[]{:S(2)}) collective-permute-start(bf16[256,128]{1,0:T(8,128)(2,1)S(1)} %slice.147), channel_id=1, source_target_pairs={{0,256},{256,0},{1,257},{257,1},{2,258},{258,2},{3,259},{259,3},{4... | collective-permute-start | bytes 196616 | tf_op jit(solution)/shard_map/ppermute | solution.py:26
  147.5 11.6 %collective-permute-start.14 = (bf16[256,128]{1,0:T(8,128)(2,1)S(1)}, bf16[256,128]{1,0:T(8,128)(2,1)S(1)}, u32[]{:S(2)}, u32[]{:S(2)}) collective-permute-start(bf16[256,128]{1,0:T(8,128)(2,1)S(1)} %slice.146), channel_id=1, source_target_pairs={{0,256},{256,0},{1,257},{257,1},{2,258},{258,2},{3,259},{259,3},{4... | collective-permute-start | bytes 196616 | tf_op jit(solution)/shard_map/ppermute | solution.py:26

commit v12 on v11

--- a/solution.py
+++ b/solution.py
@@ -14,7 +14,7 @@
 TOK = 512
 ROWS = 32
 NX, NZ, CAP = 4, 8, 2
-VMEM_MIB = 50
+VMEM_MIB = 45
 AXES = {"z8": 2, "z4": 2, "z2": 2, "x": 4, "y": 4, "zh": 2, "core": 2}
 VMEM = pl.BlockSpec(memory_space=pltpu.VMEM)
 HBM = pl.BlockSpec(memory_space=pltpu.HBM)

time: 161 us -> 158 us (0.981)
  local copies, waits for them, and re-layouts: 15.1 us -> 12.4 us
  transfers between devices with their start and end apart: 17 -> 17, of which waited for: 9 -> 9; matrix products, arithmetic and copies ran while one was open for 7% -> 6% of each run, Pallas kernels for 2% -> 2%
where the time goes in v12:
time: 158 us
  starting transfers between devices  91.9 us (58%)
  waiting for transfers between devices  39.1 us (25%)
  local copies, waits for them, and re-layouts  12.4 us (8%)
  Pallas kernels  12.3 us (8%)
    ppermute x9, starting transfers between devices, swap(): return lax.ppermute(value, axis, [(0, 1), (1, 0)])  64.3 us
    ppermute x6, starting transfers between devices, shift(): lax.ppermute(value, axis, [(i, (i + step) % size) for i in range(size)])  18.4 us
    ppermute x6, waiting for transfers between devices, shift(): lax.ppermute(value, axis, [(i, (i + step) % size) for i in range(size)])  14.5 us
    all_to_all x2, waiting for transfers between devices, spread(): lax.all_to_all(jnp.broadcast_to(value[None], (AXES[axis],) + value.shape)...  12.3 us
    ppermute x9, waiting for transfers between devices, swap(): return lax.ppermute(value, axis, [(0, 1), (1, 0)])  12.3 us
    all_to_all x2, starting transfers between devices, spread(): lax.all_to_all(jnp.broadcast_to(value[None], (AXES[axis],) + value.shape)...  9.26 us
    pallas_call x1, Pallas kernels, body(): call(block_kernel, [jax.ShapeDtypeStruct((count, 2 * BS, BS), bf16) for c...  9.23 us
    reshape x2, local copies, waits for them, and re-layouts, body(): w.transpose(0, 3, 1, 2).reshape(COLS, BS, KB * BS)  7.67 us
  transfers between devices with their start and end apart: 17, of which 9 were waited for; matrix products, arithmetic and copies ran while one was open for 6% of the time, Pallas kernels for 2%

profile of v12, /device:TPU:6, one launch (start us, length us, event | category | flops | bytes accessed | tf_op | source)
XLA Modules:
  0.0 157.6 jit_solution(5430398845300380046)
XLA Ops:
  0.0 1.1 copy.12
  1.1 1.1 broadcast_in_dim.14
  2.2 4.5 %all-to-all-start = ((bf16[4,2,128,512]{3,2,1,0:T(8,128)(2,1)}), bf16[4,2,128,512]{3,2,1,0:T(8,128)(2,1)S(1)}, u32[]{:S(2)}, u32[]{:S(2)}) async-start(bf16[4,2,128,512]{3,2,1,0:T(8,128)(2,1)} %broadcast_in_dim.14), calls=%async_computation | async-start | bytes 2097152 | tf_op jit(solution)/shard_map/all_to_all | solution.py:35
  6.6 15.7 %collective-permute-start.1 = (bf16[2,128,512]{2,1,0:T(8,128)(2,1)S(1)}, bf16[2,128,512]{2,1,0:T(8,128)(2,1)S(1)}, u32[]{:S(2)}, u32[]{:S(2)}) collective-permute-start(bf16[2,128,512]{2,1,0:T(8,128)(2,1)S(1)} %bitcast.49), channel_id=1, source_target_pairs={{0,2},{2,0},{1,3},{3,1},{4,6},{6,4},{5,7},{7,5},{8,10},{10,8},{9,1... | collective-permute-start | bytes 786440 | tf_op jit(solution)/shard_map/ppermute | solution.py:26
  22.9 3.8 %copy.13.gate_ref = bf16[7,128,1024]{2,1,0:T(8,128)(2,1)} copy(bf16[7,128,1024]{1,2,0:T(8,128)(2,1)} %bitcast.46) | data formatting | bytes 3670016 | tf_op jit(solution)/shard_map/reshape | solution.py:138
  26.7 3.8 %copy.14.up_ref = bf16[7,128,1024]{2,1,0:T(8,128)(2,1)} copy(bf16[7,128,1024]{1,2,0:T(8,128)(2,1)} %bitcast.47) | data formatting | bytes 3670016 | tf_op jit(solution)/shard_map/reshape | solution.py:138
  31.4 3.1 %shard_map.64.place_ref = s32[56]{0:T(128)S(1)} custom-call(s32[7,8]{1,0:T(8,128)S(1)} %copy-done, bf16[8,1024]{1,0:T(8,128)(2,1)S(1)} %get-tuple-element.29.gate_ref, bf16[8,1024]{1,0:T(8,128)(2,1)S(1)} %get-tuple-element.28.up_ref, bf16[8,512]{1,0:T(8,128)(2,1)S(1)} %slice_bitcast_fusion.4.hidden_ref, bf16[8,512]{1,0:T(8,128)(2,1)S(1)} %slice_bitcast_fusion.3.near_ref), custom_call_target="tpu_custom_call" | custom-call | tf_op jit(solution)/shard_map/pallas_call | solution.py:141
  34.5 1.1 broadcast_in_dim.15
  35.6 4.8 %all-to-all-start.1 = ((bf16[4,2,128,512]{3,2,1,0:T(8,128)(2,1)}), bf16[4,2,128,512]{3,2,1,0:T(8,128)(2,1)S(1)}, u32[]{:S(2)}, u32[]{:S(2)}) async-start(bf16[4,2,128,512]{3,2,1,0:T(8,128)(2,1)} %broadcast_in_dim.15), calls=%async_computation.1 | async-start | bytes 2097152 | tf_op jit(solution)/shard_map/all_to_all | solution.py:35
  40.4 1.9 %collective-permute-start = (bf16[4,2,128,512]{3,2,1,0:T(8,128)(2,1)S(1)}, bf16[4,2,128,512]{3,2,1,0:T(8,128)(2,1)}, u32[]{:S(2)}, u32[]{:S(2)}) collective-permute-start(bf16[4,2,128,512]{3,2,1,0:T(8,128)(2,1)S(1)} %all-to-all-done.a_ref), channel_id=1, source_target_pairs={{0,1},{1,0},{2,3},{3,2},{4,5},{5,4},{6,7},{7,6},{8,9},{9,8},{10,11... | collective-permute-start | bytes 3145736 | tf_op jit(solution)/shard_map/ppermute | solution.py:26
  42.3 12.3 %all-to-all-done.1.b_ref = bf16[4,2,128,512]{3,2,1,0:T(8,128)(2,1)S(1)} async-done(((bf16[4,2,128,512]{3,2,1,0:T(8,128)(2,1)}), bf16[4,2,128,512]{3,2,1,0:T(8,128)(2,1)S(1)}, u32[]{:S(2)}, u32[]{:S(2)}) %all-to-all-start.1) | async-done | bytes 1048608 | tf_op jit(solution)/shard_map/all_to_all | solution.py:35
  54.6 1.9 %collective-permute-start.2 = (bf16[4,2,128,512]{3,2,1,0:T(8,128)(2,1)S(1)}, bf16[4,2,128,512]{3,2,1,0:T(8,128)(2,1)S(1)}, u32[]{:S(2)}, u32[]{:S(2)}) collective-permute-start(bf16[4,2,128,512]{3,2,1,0:T(8,128)(2,1)S(1)} %all-to-all-done.1.b_ref), channel_id=1, source_target_pairs={{0,1},{1,0},{2,3},{3,2},{4,5},{5,4},{6,7},{7,6},{8,9},{9,8},{10,11... | collective-permute-start | bytes 3145736 | tf_op jit(solution)/shard_map/ppermute | solution.py:26
  56.5 2.6 %collective-permute-done.2.bc_ref = bf16[4,2,128,512]{3,2,1,0:T(8,128)(2,1)S(1)} collective-permute-done((bf16[4,2,128,512]{3,2,1,0:T(8,128)(2,1)S(1)}, bf16[4,2,128,512]{3,2,1,0:T(8,128)(2,1)S(1)}, u32[]{:S(2)}, u32[]{:S(2)}) %collective-permute-start.2) | collective-permute-done | bytes 1048608 | tf_op jit(solution)/shard_map/ppermute | solution.py:26
  59.2 9.2 %shard_map.65 = (bf16[16,256,128]{2,1,0:T(8,128)(2,1)S(1)}, bf16[8,256,128]{2,1,0:T(8,128)(2,1)S(1)}, bf16[8,256,128]{2,1,0:T(8,128)(2,1)S(1)}, bf16[8,256,128]{...) custom-call(bf16[4,2,128,512]{3,2,1,0:T(8,128)(2,1)S(1)} %all-to-all-done.a_ref, ...), custom_call_target="tpu_custom_call" | custom-call | flops 3758096384 | bytes 14680064 | tf_op jit(solution)/shard_map/pallas_call | solution.py:151
  68.4 2.4 %collective-permute-start.3 = (bf16[2048,128]{1,0:T(8,128)(2,1)S(1)}, bf16[2048,128]{1,0:T(8,128)(2,1)S(1)}, u32[]{:S(2)}, u32[]{:S(2)}) collective-permute-start(bf16[2048,128]{1,0:T(8,128)(2,1)S(1)} %bitcast.45), channel_id=1, source_target_pairs={{0,16},{16,32},{32,48},{48,0},{1,17},{17,33},{33,49},{49,1},{2,18}... | collective-permute-start | bytes 1572872 | tf_op jit(solution)/shard_map/ppermute | solution.py:31
  70.8 3.5 %collective-permute-start.4 = (bf16[2048,128]{1,0:T(8,128)(2,1)S(1)}, bf16[2048,128]{1,0:T(8,128)(2,1)S(1)}, u32[]{:S(2)}, u32[]{:S(2)}) collective-permute-start(bf16[2048,128]{1,0:T(8,128)(2,1)S(1)} %bitcast.44), channel_id=1, source_target_pairs={{0,48},{16,0},{32,16},{48,32},{1,49},{17,1},{33,17},{49,33},{2,50}... | collective-permute-start | bytes 1572872 | tf_op jit(solution)/shard_map/ppermute | solution.py:31
  74.3 3.3 %collective-permute-start.5 = (bf16[2048,128]{1,0:T(8,128)(2,1)S(1)}, bf16[2048,128]{1,0:T(8,128)(2,1)S(1)}, u32[]{:S(2)}, u32[]{:S(2)}) collective-permute-start(bf16[2048,128]{1,0:T(8,128)(2,1)S(1)} %bitcast.43), channel_id=1, source_target_pairs={{0,32},{16,48},{32,0},{48,16},{1,33},{17,49},{33,1},{49,17},{2,34}... | collective-permute-start | bytes 1572872 | tf_op jit(solution)/shard_map/ppermute | solution.py:31
  77.6 13.5 %collective-permute-start.9 = (bf16[4096,128]{1,0:T(8,128)(2,1)S(1)}, bf16[4096,128]{1,0:T(8,128)(2,1)S(1)}, u32[]{:S(2)}, u32[]{:S(2)}) collective-permute-start(bf16[4096,128]{1,0:T(8,128)(2,1)S(1)} %bitcast.42), channel_id=1, source_target_pairs={{0,64},{64,0},{1,65},{65,1},{2,66},{66,2},{3,67},{67,3},{4,68},{68... | collective-permute-start | bytes 3145736 | tf_op jit(solution)/shard_map/ppermute | solution.py:26
  91.1 7.7 %collective-permute-done.4 = bf16[2048,128]{1,0:T(8,128)(2,1)S(1)} collective-permute-done((bf16[2048,128]{1,0:T(8,128)(2,1)S(1)}, bf16[2048,128]{1,0:T(8,128)(2,1)S(1)}, u32[]{:S(2)}, u32[]{:S(2)}) %collective-permute-start.4) | collective-permute-done | bytes 524320 | tf_op jit(solution)/shard_map/ppermute | solution.py:31
  99.1 13.5 %collective-permute-start.6 = (bf16[1024,128]{1,0:T(8,128)(2,1)S(1)}, bf16[1024,128]{1,0:T(8,128)(2,1)S(1)}, u32[]{:S(2)}, u32[]{:S(2)}) collective-permute-start(bf16[1024,128]{1,0:T(8,128)(2,1)S(1)} %slice.143), channel_id=1, source_target_pairs={{0,64},{64,0},{1,65},{65,1},{2,66},{66,2},{3,67},{67,3},{4,68},{68... | collective-permute-start | bytes 786440 | tf_op jit(solution)/shard_map/ppermute | solution.py:26
  112.6 2.5 %collective-permute-done.9 = bf16[4096,128]{1,0:T(8,128)(2,1)S(1)} collective-permute-done((bf16[4096,128]{1,0:T(8,128)(2,1)S(1)}, bf16[4096,128]{1,0:T(8,128)(2,1)S(1)}, u32[]{:S(2)}, u32[]{:S(2)}) %collective-permute-start.9) | collective-permute-done | bytes 1048608 | tf_op jit(solution)/shard_map/ppermute | solution.py:26
  115.4 4.0 %collective-permute-start.10 = (bf16[1024,128]{1,0:T(8,128)(2,1)S(1)}, bf16[1024,128]{1,0:T(8,128)(2,1)S(1)}, u32[]{:S(2)}, u32[]{:S(2)}) collective-permute-start(bf16[1024,128]{1,0:T(8,128)(2,1)S(1)} %get-tuple-element.25), channel_id=1, source_target_pairs={{0,16},{16,32},{32,48},{48,0},{1,17},{17,33},{33,49},{49,1},{2,18}... | collective-permute-start | bytes 786440 | tf_op jit(solution)/shard_map/ppermute | solution.py:31
  119.4 3.0 %collective-permute-start.12 = (bf16[1024,128]{1,0:T(8,128)(2,1)S(1)}, bf16[1024,128]{1,0:T(8,128)(2,1)S(1)}, u32[]{:S(2)}, u32[]{:S(2)}) collective-permute-start(bf16[1024,128]{1,0:T(8,128)(2,1)S(1)} %get-tuple-element.26), channel_id=1, source_target_pairs={{0,32},{16,48},{32,0},{48,16},{1,33},{17,49},{33,1},{49,17},{2,34}... | collective-permute-start | bytes 786440 | tf_op jit(solution)/shard_map/ppermute | solution.py:31
  122.4 2.2 %collective-permute-start.11 = (bf16[1024,128]{1,0:T(8,128)(2,1)S(1)}, bf16[1024,128]{1,0:T(8,128)(2,1)S(1)}, u32[]{:S(2)}, u32[]{:S(2)}) collective-permute-start(bf16[1024,128]{1,0:T(8,128)(2,1)S(1)} %get-tuple-element.27), channel_id=1, source_target_pairs={{0,48},{16,0},{32,16},{48,32},{1,49},{17,1},{33,17},{49,33},{2,50}... | collective-permute-start | bytes 786440 | tf_op jit(solution)/shard_map/ppermute | solution.py:31
  124.7 1.9 %collective-permute-start.7 = (bf16[512,128]{1,0:T(8,128)(2,1)S(1)}, bf16[512,128]{1,0:T(8,128)(2,1)S(1)}, u32[]{:S(2)}, u32[]{:S(2)}) collective-permute-start(bf16[512,128]{1,0:T(8,128)(2,1)S(1)} %slice.145), channel_id=1, source_target_pairs={{0,128},{128,0},{1,129},{129,1},{2,130},{130,2},{3,131},{131,3},{4... | collective-permute-start | bytes 393224 | tf_op jit(solution)/shard_map/ppermute | solution.py:26
  126.7 1.3 collective-permute-done.10
  128.0 2.8 %collective-permute-done.12 = bf16[1024,128]{1,0:T(8,128)(2,1)S(1)} collective-permute-done((bf16[1024,128]{1,0:T(8,128)(2,1)S(1)}, bf16[1024,128]{1,0:T(8,128)(2,1)S(1)}, u32[]{:S(2)}, u32[]{:S(2)}) %collective-permute-start.12) | collective-permute-done | bytes 262176 | tf_op jit(solution)/shard_map/ppermute | solution.py:31
  130.8 2.7 %collective-permute-done.11 = bf16[1024,128]{1,0:T(8,128)(2,1)S(1)} collective-permute-done((bf16[1024,128]{1,0:T(8,128)(2,1)S(1)}, bf16[1024,128]{1,0:T(8,128)(2,1)S(1)}, u32[]{:S(2)}, u32[]{:S(2)}) %collective-permute-start.11) | collective-permute-done | bytes 262176 | tf_op jit(solution)/shard_map/ppermute | solution.py:31
  133.7 1.9 %collective-permute-start.13 = (bf16[512,128]{1,0:T(8,128)(2,1)S(1)}, bf16[512,128]{1,0:T(8,128)(2,1)S(1)}, u32[]{:S(2)}, u32[]{:S(2)}) collective-permute-start(bf16[512,128]{1,0:T(8,128)(2,1)S(1)} %slice.144), channel_id=1, source_target_pairs={{0,128},{128,0},{1,129},{129,1},{2,130},{130,2},{3,131},{131,3},{4... | collective-permute-start | bytes 393224 | tf_op jit(solution)/shard_map/ppermute | solution.py:26
  135.7 9.5 %collective-permute-start.8 = (bf16[256,128]{1,0:T(8,128)(2,1)S(1)}, bf16[256,128]{1,0:T(8,128)(2,1)S(1)}, u32[]{:S(2)}, u32[]{:S(2)}) collective-permute-start(bf16[256,128]{1,0:T(8,128)(2,1)S(1)} %slice.147), channel_id=1, source_target_pairs={{0,256},{256,0},{1,257},{257,1},{2,258},{258,2},{3,259},{259,3},{4... | collective-permute-start | bytes 196616 | tf_op jit(solution)/shard_map/ppermute | solution.py:26
  145.3 4.5 %collective-permute-start.14 = (bf16[256,128]{1,0:T(8,128)(2,1)S(1)}, bf16[256,128]{1,0:T(8,128)(2,1)S(1)}, u32[]{:S(2)}, u32[]{:S(2)}) collective-permute-start(bf16[256,128]{1,0:T(8,128)(2,1)S(1)} %slice.146), channel_id=1, source_target_pairs={{0,256},{256,0},{1,257},{257,1},{2,258},{258,2},{3,259},{259,3},{4... | collective-permute-start | bytes 196616 | tf_op jit(solution)/shard_map/ppermute | solution.py:26
  150.3 6.6 %collective-permute-done.14 = bf16[256,128]{1,0:T(8,128)(2,1)S(1)} collective-permute-done((bf16[256,128]{1,0:T(8,128)(2,1)S(1)}, bf16[256,128]{1,0:T(8,128)(2,1)S(1)}, u32[]{:S(2)}, u32[]{:S(2)}) %collective-permute-start.14) | collective-permute-done | bytes 65568 | tf_op jit(solution)/shard_map/ppermute | solution.py:26
  (35 shorter events, 3.6 us)
Async XLA Ops:
  1.1 21.3 %copy-start.2 = (bf16[512,896]{1,0:T(8,128)(2,1)S(1)}, bf16[512,896]{1,0:T(8,128)(2,1)}, u32[]{:S(2)}) copy-start(bf16[512,896]{1,0:T(8,128)(2,1)} %param.7) | copy-start | bytes 2752516
  2.2 29.2 %all-to-all-start = ((bf16[4,2,128,512]{3,2,1,0:T(8,128)(2,1)}), bf16[4,2,128,512]{3,2,1,0:T(8,128)(2,1)S(1)}, u32[]{:S(2)}, u32[]{:S(2)}) async-start(bf16[4,2,128,512]{3,2,1,0:T(8,128)(2,1)} %broadcast_in_dim.14), calls=%async_computation | async-start | bytes 2097152 | tf_op jit(solution)/shard_map/all_to_all | solution.py:35
  6.6 27.8 %collective-permute-start.1 = (bf16[2,128,512]{2,1,0:T(8,128)(2,1)S(1)}, bf16[2,128,512]{2,1,0:T(8,128)(2,1)S(1)}, u32[]{:S(2)}, u32[]{:S(2)}) collective-permute-start(bf16[2,128,512]{2,1,0:T(8,128)(2,1)S(1)} %bitcast.49), channel_id=1, source_target_pairs={{0,2},{2,0},{1,3},{3,1},{4,6},{6,4},{5,7},{7,5},{8,10},{10,8},{9,1... | collective-permute-start | bytes 786440 | tf_op jit(solution)/shard_map/ppermute | solution.py:26
  26.7 4.6 %copy-start = (s32[7,8]{1,0:T(8,128)S(1)}, s32[7,8]{1,0:T(8,128)}, u32[]{:S(2)}) copy-start(s32[7,8]{1,0:T(8,128)} %owner_ref.1) | copy-start | bytes 676
  31.3 27.8 %copy-start.1 = (s32[7,8]{1,0:T(8,128)S(1)}, s32[7,8]{1,0:T(8,128)}, u32[]{:S(2)}) copy-start(s32[7,8]{1,0:T(8,128)} %rows_ref.1) | copy-start | bytes 676
  35.6 19.1 %all-to-all-start.1 = ((bf16[4,2,128,512]{3,2,1,0:T(8,128)(2,1)}), bf16[4,2,128,512]{3,2,1,0:T(8,128)(2,1)S(1)}, u32[]{:S(2)}, u32[]{:S(2)}) async-start(bf16[4,2,128,512]{3,2,1,0:T(8,128)(2,1)} %broadcast_in_dim.15), calls=%async_computation.1 | async-start | bytes 2097152 | tf_op jit(solution)/shard_map/all_to_all | solution.py:35
  40.4 16.2 %collective-permute-start = (bf16[4,2,128,512]{3,2,1,0:T(8,128)(2,1)S(1)}, bf16[4,2,128,512]{3,2,1,0:T(8,128)(2,1)}, u32[]{:S(2)}, u32[]{:S(2)}) collective-permute-start(bf16[4,2,128,512]{3,2,1,0:T(8,128)(2,1)S(1)} %all-to-all-done.a_ref), channel_id=1, source_target_pairs={{0,1},{1,0},{2,3},{3,2},{4,5},{5,4},{6,7},{7,6},{8,9},{9,8},{10,11... | collective-permute-start | bytes 3145736 | tf_op jit(solution)/shard_map/ppermute | solution.py:26
  54.6 4.5 %collective-permute-start.2 = (bf16[4,2,128,512]{3,2,1,0:T(8,128)(2,1)S(1)}, bf16[4,2,128,512]{3,2,1,0:T(8,128)(2,1)S(1)}, u32[]{:S(2)}, u32[]{:S(2)}) collective-permute-start(bf16[4,2,128,512]{3,2,1,0:T(8,128)(2,1)S(1)} %all-to-all-done.1.b_ref), channel_id=1, source_target_pairs={{0,1},{1,0},{2,3},{3,2},{4,5},{5,4},{6,7},{7,6},{8,9},{9,8},{10,11... | collective-permute-start | bytes 3145736 | tf_op jit(solution)/shard_map/ppermute | solution.py:26
  68.4 22.7 %collective-permute-start.3 = (bf16[2048,128]{1,0:T(8,128)(2,1)S(1)}, bf16[2048,128]{1,0:T(8,128)(2,1)S(1)}, u32[]{:S(2)}, u32[]{:S(2)}) collective-permute-start(bf16[2048,128]{1,0:T(8,128)(2,1)S(1)} %bitcast.45), channel_id=1, source_target_pairs={{0,16},{16,32},{32,48},{48,0},{1,17},{17,33},{33,49},{49,1},{2,18}... | collective-permute-start | bytes 1572872 | tf_op jit(solution)/shard_map/ppermute | solution.py:31
  70.8 28.0 %collective-permute-start.4 = (bf16[2048,128]{1,0:T(8,128)(2,1)S(1)}, bf16[2048,128]{1,0:T(8,128)(2,1)S(1)}, u32[]{:S(2)}, u32[]{:S(2)}) collective-permute-start(bf16[2048,128]{1,0:T(8,128)(2,1)S(1)} %bitcast.44), channel_id=1, source_target_pairs={{0,48},{16,0},{32,16},{48,32},{1,49},{17,1},{33,17},{49,33},{2,50}... | collective-permute-start | bytes 1572872 | tf_op jit(solution)/shard_map/ppermute | solution.py:31
  74.3 24.6 %collective-permute-start.5 = (bf16[2048,128]{1,0:T(8,128)(2,1)S(1)}, bf16[2048,128]{1,0:T(8,128)(2,1)S(1)}, u32[]{:S(2)}, u32[]{:S(2)}) collective-permute-start(bf16[2048,128]{1,0:T(8,128)(2,1)S(1)} %bitcast.43), channel_id=1, source_target_pairs={{0,32},{16,48},{32,0},{48,16},{1,33},{17,49},{33,1},{49,17},{2,34}... | collective-permute-start | bytes 1572872 | tf_op jit(solution)/shard_map/ppermute | solution.py:31
  77.6 37.5 %collective-permute-start.9 = (bf16[4096,128]{1,0:T(8,128)(2,1)S(1)}, bf16[4096,128]{1,0:T(8,128)(2,1)S(1)}, u32[]{:S(2)}, u32[]{:S(2)}) collective-permute-start(bf16[4096,128]{1,0:T(8,128)(2,1)S(1)} %bitcast.42), channel_id=1, source_target_pairs={{0,64},{64,0},{1,65},{65,1},{2,66},{66,2},{3,67},{67,3},{4,68},{68... | collective-permute-start | bytes 3145736 | tf_op jit(solution)/shard_map/ppermute | solution.py:26
  99.1 25.5 %collective-permute-start.6 = (bf16[1024,128]{1,0:T(8,128)(2,1)S(1)}, bf16[1024,128]{1,0:T(8,128)(2,1)S(1)}, u32[]{:S(2)}, u32[]{:S(2)}) collective-permute-start(bf16[1024,128]{1,0:T(8,128)(2,1)S(1)} %slice.143), channel_id=1, source_target_pairs={{0,64},{64,0},{1,65},{65,1},{2,66},{66,2},{3,67},{67,3},{4,68},{68... | collective-permute-start | bytes 786440 | tf_op jit(solution)/shard_map/ppermute | solution.py:26
  115.4 12.6 %collective-permute-start.10 = (bf16[1024,128]{1,0:T(8,128)(2,1)S(1)}, bf16[1024,128]{1,0:T(8,128)(2,1)S(1)}, u32[]{:S(2)}, u32[]{:S(2)}) collective-permute-start(bf16[1024,128]{1,0:T(8,128)(2,1)S(1)} %get-tuple-element.25), channel_id=1, source_target_pairs={{0,16},{16,32},{32,48},{48,0},{1,17},{17,33},{33,49},{49,1},{2,18}... | collective-permute-start | bytes 786440 | tf_op jit(solution)/shard_map/ppermute | solution.py:31
  119.4 11.5 %collective-permute-start.12 = (bf16[1024,128]{1,0:T(8,128)(2,1)S(1)}, bf16[1024,128]{1,0:T(8,128)(2,1)S(1)}, u32[]{:S(2)}, u32[]{:S(2)}) collective-permute-start(bf16[1024,128]{1,0:T(8,128)(2,1)S(1)} %get-tuple-element.26), channel_id=1, source_target_pairs={{0,32},{16,48},{32,0},{48,16},{1,33},{17,49},{33,1},{49,17},{2,34}... | collective-permute-start | bytes 786440 | tf_op jit(solution)/shard_map/ppermute | solution.py:31
  122.4 11.1 %collective-permute-start.11 = (bf16[1024,128]{1,0:T(8,128)(2,1)S(1)}, bf16[1024,128]{1,0:T(8,128)(2,1)S(1)}, u32[]{:S(2)}, u32[]{:S(2)}) collective-permute-start(bf16[1024,128]{1,0:T(8,128)(2,1)S(1)} %get-tuple-element.27), channel_id=1, source_target_pairs={{0,48},{16,0},{32,16},{48,32},{1,49},{17,1},{33,17},{49,33},{2,50}... | collective-permute-start | bytes 786440 | tf_op jit(solution)/shard_map/ppermute | solution.py:31
  124.7 10.9 %collective-permute-start.7 = (bf16[512,128]{1,0:T(8,128)(2,1)S(1)}, bf16[512,128]{1,0:T(8,128)(2,1)S(1)}, u32[]{:S(2)}, u32[]{:S(2)}) collective-permute-start(bf16[512,128]{1,0:T(8,128)(2,1)S(1)} %slice.145), channel_id=1, source_target_pairs={{0,128},{128,0},{1,129},{129,1},{2,130},{130,2},{3,131},{131,3},{4... | collective-permute-start | bytes 393224 | tf_op jit(solution)/shard_map/ppermute | solution.py:26
  133.7 11.5 %collective-permute-start.13 = (bf16[512,128]{1,0:T(8,128)(2,1)S(1)}, bf16[512,128]{1,0:T(8,128)(2,1)S(1)}, u32[]{:S(2)}, u32[]{:S(2)}) collective-permute-start(bf16[512,128]{1,0:T(8,128)(2,1)S(1)} %slice.144), channel_id=1, source_target_pairs={{0,128},{128,0},{1,129},{129,1},{2,130},{130,2},{3,131},{131,3},{4... | collective-permute-start | bytes 393224 | tf_op jit(solution)/shard_map/ppermute | solution.py:26
  135.7 14.6 %collective-permute-start.8 = (bf16[256,128]{1,0:T(8,128)(2,1)S(1)}, bf16[256,128]{1,0:T(8,128)(2,1)S(1)}, u32[]{:S(2)}, u32[]{:S(2)}) collective-permute-start(bf16[256,128]{1,0:T(8,128)(2,1)S(1)} %slice.147), channel_id=1, source_target_pairs={{0,256},{256,0},{1,257},{257,1},{2,258},{258,2},{3,259},{259,3},{4... | collective-permute-start | bytes 196616 | tf_op jit(solution)/shard_map/ppermute | solution.py:26
  145.3 11.6 %collective-permute-start.14 = (bf16[256,128]{1,0:T(8,128)(2,1)S(1)}, bf16[256,128]{1,0:T(8,128)(2,1)S(1)}, u32[]{:S(2)}, u32[]{:S(2)}) collective-permute-start(bf16[256,128]{1,0:T(8,128)(2,1)S(1)} %slice.146), channel_id=1, source_target_pairs={{0,256},{256,0},{1,257},{257,1},{2,258},{258,2},{3,259},{259,3},{4... | collective-permute-start | bytes 196616 | tf_op jit(solution)/shard_map/ppermute | solution.py:26

commit v13 on v12

--- a/solution.py
+++ b/solution.py
@@ -177,9 +177,11 @@
     keep = keep.reshape(NX, -1, BS)
     first = over_x([part.reshape(-1, BS) for part in firsts])
     second = over_x([(keep[i].astype(f32) + got[i].astype(f32)).astype(bf16) for i in range(NX)])
-    first = halve(halve(halve(first, "z2"), "z4"), "z8")
-    second = halve(halve(second, "z4"), "z8")
-    return jnp.concatenate([first, second], 0).reshape(1, 1, CAP, 2, BS, BS)
+    first = halve(halve(first, "z2"), "z4")
+    second = halve(second, "z4")
+    half = first.shape[0] // 2
+    got = swap(jnp.concatenate([first[half:], second[half:]], 0).astype(bf16), "z8")
+    return (jnp.concatenate([first[:half], second[:half]], 0) + got.astype(f32)).reshape(1, 1, CAP, 2, BS, BS)
 
 
 def solution(mesh):

time: 158 us -> 160 us (1.013)
  waiting for transfers between devices: 39.1 us -> 46.1 us
  starting transfers between devices: 91.9 us -> 85.6 us
    ppermute x9 -> x8, waiting for transfers between devices: 12.3 us -> 19.2 us  [swap(): return lax.ppermute(value, axis, [(0, 1), (1, 0)])]
    ppermute x9 -> x8, starting transfers between devices: 64.3 us -> 57.9 us  [swap(): return lax.ppermute(value, axis, [(0, 1), (1, 0)])]
  transfers between devices with their start and end apart: 17 -> 16, of which waited for: 9 -> 9; matrix products, arithmetic and copies ran while one was open for 6% -> 6% of each run, Pallas kernels for 2% -> 2%
where the time goes in v13:
time: 160 us; the launch traced here: 158 us
  starting transfers between devices  85.6 us (54%)
  waiting for transfers between devices  46.1 us (29%)
  local copies, waits for them, and re-layouts  12.4 us (8%)
  Pallas kernels  12.3 us (8%)
    ppermute x8, starting transfers between devices, swap(): return lax.ppermute(value, axis, [(0, 1), (1, 0)])  57.9 us
    ppermute x8, waiting for transfers between devices, swap(): return lax.ppermute(value, axis, [(0, 1), (1, 0)])  19.2 us
    ppermute x6, starting transfers between devices, shift(): lax.ppermute(value, axis, [(i, (i + step) % size) for i in range(size)])  18.4 us
    ppermute x6, waiting for transfers between devices, shift(): lax.ppermute(value, axis, [(i, (i + step) % size) for i in range(size)])  14.6 us
    all_to_all x2, waiting for transfers between devices, spread(): lax.all_to_all(jnp.broadcast_to(value[None], (AXES[axis],) + value.shape)...  12.3 us
    all_to_all x2, starting transfers between devices, spread(): lax.all_to_all(jnp.broadcast_to(value[None], (AXES[axis],) + value.shape)...  9.26 us
    pallas_call x1, Pallas kernels, body(): call(block_kernel, [jax.ShapeDtypeStruct((count, 2 * BS, BS), bf16) for c...  9.24 us
    reshape x2, local copies, waits for them, and re-layouts, body(): w.transpose(0, 3, 1, 2).reshape(COLS, BS, KB * BS)  7.68 us
  transfers between devices with their start and end apart: 16, of which 9 were waited for; matrix products, arithmetic and copies ran while one was open for 6% of the time, Pallas kernels for 2%

profile of v13, /device:TPU:6, one launch (start us, length us, event | category | flops | bytes accessed | tf_op | source)
XLA Modules:
  0.0 158.3 jit_solution(4508555437018339981)
XLA Ops:
  0.0 1.1 copy.12
  1.1 1.1 broadcast_in_dim.14
  2.2 4.5 %all-to-all-start = ((bf16[4,2,128,512]{3,2,1,0:T(8,128)(2,1)}), bf16[4,2,128,512]{3,2,1,0:T(8,128)(2,1)S(1)}, u32[]{:S(2)}, u32[]{:S(2)}) async-start(bf16[4,2,128,512]{3,2,1,0:T(8,128)(2,1)} %broadcast_in_dim.14), calls=%async_computation | async-start | bytes 2097152 | tf_op jit(solution)/shard_map/all_to_all | solution.py:35
  6.6 15.7 %collective-permute-start.1 = (bf16[2,128,512]{2,1,0:T(8,128)(2,1)S(1)}, bf16[2,128,512]{2,1,0:T(8,128)(2,1)S(1)}, u32[]{:S(2)}, u32[]{:S(2)}) collective-permute-start(bf16[2,128,512]{2,1,0:T(8,128)(2,1)S(1)} %bitcast.49), channel_id=1, source_target_pairs={{0,2},{2,0},{1,3},{3,1},{4,6},{6,4},{5,7},{7,5},{8,10},{10,8},{9,1... | collective-permute-start | bytes 786440 | tf_op jit(solution)/shard_map/ppermute | solution.py:26
  22.9 3.8 %copy.13.gate_ref = bf16[7,128,1024]{2,1,0:T(8,128)(2,1)} copy(bf16[7,128,1024]{1,2,0:T(8,128)(2,1)} %bitcast.46) | data formatting | bytes 3670016 | tf_op jit(solution)/shard_map/reshape | solution.py:138
  26.8 3.8 %copy.14.up_ref = bf16[7,128,1024]{2,1,0:T(8,128)(2,1)} copy(bf16[7,128,1024]{1,2,0:T(8,128)(2,1)} %bitcast.47) | data formatting | bytes 3670016 | tf_op jit(solution)/shard_map/reshape | solution.py:138
  31.4 3.1 %shard_map.64.place_ref = s32[56]{0:T(128)S(1)} custom-call(s32[7,8]{1,0:T(8,128)S(1)} %copy-done, bf16[8,1024]{1,0:T(8,128)(2,1)S(1)} %get-tuple-element.29.gate_ref, bf16[8,1024]{1,0:T(8,128)(2,1)S(1)} %get-tuple-element.28.up_ref, bf16[8,512]{1,0:T(8,128)(2,1)S(1)} %slice_bitcast_fusion.4.hidden_ref, bf16[8,512]{1,0:T(8,128)(2,1)S(1)} %slice_bitcast_fusion.3.near_ref), custom_call_target="tpu_custom_call" | custom-call | tf_op jit(solution)/shard_map/pallas_call | solution.py:141
  34.5 1.1 broadcast_in_dim.15
  35.6 4.8 %all-to-all-start.1 = ((bf16[4,2,128,512]{3,2,1,0:T(8,128)(2,1)}), bf16[4,2,128,512]{3,2,1,0:T(8,128)(2,1)S(1)}, u32[]{:S(2)}, u32[]{:S(2)}) async-start(bf16[4,2,128,512]{3,2,1,0:T(8,128)(2,1)} %broadcast_in_dim.15), calls=%async_computation.1 | async-start | bytes 2097152 | tf_op jit(solution)/shard_map/all_to_all | solution.py:35
  40.4 1.9 %collective-permute-start = (bf16[4,2,128,512]{3,2,1,0:T(8,128)(2,1)S(1)}, bf16[4,2,128,512]{3,2,1,0:T(8,128)(2,1)}, u32[]{:S(2)}, u32[]{:S(2)}) collective-permute-start(bf16[4,2,128,512]{3,2,1,0:T(8,128)(2,1)S(1)} %all-to-all-done.a_ref), channel_id=1, source_target_pairs={{0,1},{1,0},{2,3},{3,2},{4,5},{5,4},{6,7},{7,6},{8,9},{9,8},{10,11... | collective-permute-start | bytes 3145736 | tf_op jit(solution)/shard_map/ppermute | solution.py:26
  42.3 12.3 %all-to-all-done.1.b_ref = bf16[4,2,128,512]{3,2,1,0:T(8,128)(2,1)S(1)} async-done(((bf16[4,2,128,512]{3,2,1,0:T(8,128)(2,1)}), bf16[4,2,128,512]{3,2,1,0:T(8,128)(2,1)S(1)}, u32[]{:S(2)}, u32[]{:S(2)}) %all-to-all-start.1) | async-done | bytes 1048608 | tf_op jit(solution)/shard_map/all_to_all | solution.py:35
  54.6 1.9 %collective-permute-start.2 = (bf16[4,2,128,512]{3,2,1,0:T(8,128)(2,1)S(1)}, bf16[4,2,128,512]{3,2,1,0:T(8,128)(2,1)S(1)}, u32[]{:S(2)}, u32[]{:S(2)}) collective-permute-start(bf16[4,2,128,512]{3,2,1,0:T(8,128)(2,1)S(1)} %all-to-all-done.1.b_ref), channel_id=1, source_target_pairs={{0,1},{1,0},{2,3},{3,2},{4,5},{5,4},{6,7},{7,6},{8,9},{9,8},{10,11... | collective-permute-start | bytes 3145736 | tf_op jit(solution)/shard_map/ppermute | solution.py:26
  56.6 2.6 %collective-permute-done.2.bc_ref = bf16[4,2,128,512]{3,2,1,0:T(8,128)(2,1)S(1)} collective-permute-done((bf16[4,2,128,512]{3,2,1,0:T(8,128)(2,1)S(1)}, bf16[4,2,128,512]{3,2,1,0:T(8,128)(2,1)S(1)}, u32[]{:S(2)}, u32[]{:S(2)}) %collective-permute-start.2) | collective-permute-done | bytes 1048608 | tf_op jit(solution)/shard_map/ppermute | solution.py:26
  59.2 9.2 %shard_map.65 = (bf16[16,256,128]{2,1,0:T(8,128)(2,1)S(1)}, bf16[8,256,128]{2,1,0:T(8,128)(2,1)S(1)}, bf16[8,256,128]{2,1,0:T(8,128)(2,1)S(1)}, bf16[8,256,128]{...) custom-call(bf16[4,2,128,512]{3,2,1,0:T(8,128)(2,1)S(1)} %all-to-all-done.a_ref, ...), custom_call_target="tpu_custom_call" | custom-call | flops 3758096384 | bytes 14680064 | tf_op jit(solution)/shard_map/pallas_call | solution.py:151
  68.4 2.4 %collective-permute-start.3 = (bf16[2048,128]{1,0:T(8,128)(2,1)S(1)}, bf16[2048,128]{1,0:T(8,128)(2,1)S(1)}, u32[]{:S(2)}, u32[]{:S(2)}) collective-permute-start(bf16[2048,128]{1,0:T(8,128)(2,1)S(1)} %bitcast.45), channel_id=1, source_target_pairs={{0,16},{16,32},{32,48},{48,0},{1,17},{17,33},{33,49},{49,1},{2,18}... | collective-permute-start | bytes 1572872 | tf_op jit(solution)/shard_map/ppermute | solution.py:31
  70.8 3.5 %collective-permute-start.4 = (bf16[2048,128]{1,0:T(8,128)(2,1)S(1)}, bf16[2048,128]{1,0:T(8,128)(2,1)S(1)}, u32[]{:S(2)}, u32[]{:S(2)}) collective-permute-start(bf16[2048,128]{1,0:T(8,128)(2,1)S(1)} %bitcast.44), channel_id=1, source_target_pairs={{0,48},{16,0},{32,16},{48,32},{1,49},{17,1},{33,17},{49,33},{2,50}... | collective-permute-start | bytes 1572872 | tf_op jit(solution)/shard_map/ppermute | solution.py:31
  74.3 3.3 %collective-permute-start.5 = (bf16[2048,128]{1,0:T(8,128)(2,1)S(1)}, bf16[2048,128]{1,0:T(8,128)(2,1)S(1)}, u32[]{:S(2)}, u32[]{:S(2)}) collective-permute-start(bf16[2048,128]{1,0:T(8,128)(2,1)S(1)} %bitcast.43), channel_id=1, source_target_pairs={{0,32},{16,48},{32,0},{48,16},{1,33},{17,49},{33,1},{49,17},{2,34}... | collective-permute-start | bytes 1572872 | tf_op jit(solution)/shard_map/ppermute | solution.py:31
  77.6 13.5 %collective-permute-start.8 = (bf16[4096,128]{1,0:T(8,128)(2,1)S(1)}, bf16[4096,128]{1,0:T(8,128)(2,1)S(1)}, u32[]{:S(2)}, u32[]{:S(2)}) collective-permute-start(bf16[4096,128]{1,0:T(8,128)(2,1)S(1)} %bitcast.42), channel_id=1, source_target_pairs={{0,64},{64,0},{1,65},{65,1},{2,66},{66,2},{3,67},{67,3},{4,68},{68... | collective-permute-start | bytes 3145736 | tf_op jit(solution)/shard_map/ppermute | solution.py:26
  91.2 7.7 %collective-permute-done.4 = bf16[2048,128]{1,0:T(8,128)(2,1)S(1)} collective-permute-done((bf16[2048,128]{1,0:T(8,128)(2,1)S(1)}, bf16[2048,128]{1,0:T(8,128)(2,1)S(1)}, u32[]{:S(2)}, u32[]{:S(2)}) %collective-permute-start.4) | collective-permute-done | bytes 524320 | tf_op jit(solution)/shard_map/ppermute | solution.py:31
  99.2 13.5 %collective-permute-start.6 = (bf16[1024,128]{1,0:T(8,128)(2,1)S(1)}, bf16[1024,128]{1,0:T(8,128)(2,1)S(1)}, u32[]{:S(2)}, u32[]{:S(2)}) collective-permute-start(bf16[1024,128]{1,0:T(8,128)(2,1)S(1)} %slice.141), channel_id=1, source_target_pairs={{0,64},{64,0},{1,65},{65,1},{2,66},{66,2},{3,67},{67,3},{4,68},{68... | collective-permute-start | bytes 786440 | tf_op jit(solution)/shard_map/ppermute | solution.py:26
  112.6 2.5 %collective-permute-done.8 = bf16[4096,128]{1,0:T(8,128)(2,1)S(1)} collective-permute-done((bf16[4096,128]{1,0:T(8,128)(2,1)S(1)}, bf16[4096,128]{1,0:T(8,128)(2,1)S(1)}, u32[]{:S(2)}, u32[]{:S(2)}) %collective-permute-start.8) | collective-permute-done | bytes 1048608 | tf_op jit(solution)/shard_map/ppermute | solution.py:26
  115.4 4.0 %collective-permute-start.9 = (bf16[1024,128]{1,0:T(8,128)(2,1)S(1)}, bf16[1024,128]{1,0:T(8,128)(2,1)S(1)}, u32[]{:S(2)}, u32[]{:S(2)}) collective-permute-start(bf16[1024,128]{1,0:T(8,128)(2,1)S(1)} %get-tuple-element.25), channel_id=1, source_target_pairs={{0,16},{16,32},{32,48},{48,0},{1,17},{17,33},{33,49},{49,1},{2,18}... | collective-permute-start | bytes 786440 | tf_op jit(solution)/shard_map/ppermute | solution.py:31
  119.4 3.0 %collective-permute-start.11 = (bf16[1024,128]{1,0:T(8,128)(2,1)S(1)}, bf16[1024,128]{1,0:T(8,128)(2,1)S(1)}, u32[]{:S(2)}, u32[]{:S(2)}) collective-permute-start(bf16[1024,128]{1,0:T(8,128)(2,1)S(1)} %get-tuple-element.26), channel_id=1, source_target_pairs={{0,32},{16,48},{32,0},{48,16},{1,33},{17,49},{33,1},{49,17},{2,34}... | collective-permute-start | bytes 786440 | tf_op jit(solution)/shard_map/ppermute | solution.py:31
  122.4 2.3 %collective-permute-start.10 = (bf16[1024,128]{1,0:T(8,128)(2,1)S(1)}, bf16[1024,128]{1,0:T(8,128)(2,1)S(1)}, u32[]{:S(2)}, u32[]{:S(2)}) collective-permute-start(bf16[1024,128]{1,0:T(8,128)(2,1)S(1)} %get-tuple-element.27), channel_id=1, source_target_pairs={{0,48},{16,0},{32,16},{48,32},{1,49},{17,1},{33,17},{49,33},{2,50}... | collective-permute-start | bytes 786440 | tf_op jit(solution)/shard_map/ppermute | solution.py:31
  124.8 1.9 %collective-permute-start.7 = (bf16[512,128]{1,0:T(8,128)(2,1)S(1)}, bf16[512,128]{1,0:T(8,128)(2,1)S(1)}, u32[]{:S(2)}, u32[]{:S(2)}) collective-permute-start(bf16[512,128]{1,0:T(8,128)(2,1)S(1)} %slice.143), channel_id=1, source_target_pairs={{0,128},{128,0},{1,129},{129,1},{2,130},{130,2},{3,131},{131,3},{4... | collective-permute-start | bytes 393224 | tf_op jit(solution)/shard_map/ppermute | solution.py:26
  126.7 1.3 collective-permute-done.9
  128.0 2.8 %collective-permute-done.11 = bf16[1024,128]{1,0:T(8,128)(2,1)S(1)} collective-permute-done((bf16[1024,128]{1,0:T(8,128)(2,1)S(1)}, bf16[1024,128]{1,0:T(8,128)(2,1)S(1)}, u32[]{:S(2)}, u32[]{:S(2)}) %collective-permute-start.11) | collective-permute-done | bytes 262176 | tf_op jit(solution)/shard_map/ppermute | solution.py:31
  130.9 2.7 %collective-permute-done.10 = bf16[1024,128]{1,0:T(8,128)(2,1)S(1)} collective-permute-done((bf16[1024,128]{1,0:T(8,128)(2,1)S(1)}, bf16[1024,128]{1,0:T(8,128)(2,1)S(1)}, u32[]{:S(2)}, u32[]{:S(2)}) %collective-permute-start.10) | collective-permute-done | bytes 262176 | tf_op jit(solution)/shard_map/ppermute | solution.py:31
  133.8 1.9 %collective-permute-start.12 = (bf16[512,128]{1,0:T(8,128)(2,1)S(1)}, bf16[512,128]{1,0:T(8,128)(2,1)S(1)}, u32[]{:S(2)}, u32[]{:S(2)}) collective-permute-start(bf16[512,128]{1,0:T(8,128)(2,1)S(1)} %slice.142), channel_id=1, source_target_pairs={{0,128},{128,0},{1,129},{129,1},{2,130},{130,2},{3,131},{131,3},{4... | collective-permute-start | bytes 393224 | tf_op jit(solution)/shard_map/ppermute | solution.py:26
  135.7 7.2 %collective-permute-done.12 = bf16[512,128]{1,0:T(8,128)(2,1)S(1)} collective-permute-done((bf16[512,128]{1,0:T(8,128)(2,1)S(1)}, bf16[512,128]{1,0:T(8,128)(2,1)S(1)}, u32[]{:S(2)}, u32[]{:S(2)}) %collective-permute-start.12) | collective-permute-done | bytes 131104 | tf_op jit(solution)/shard_map/ppermute | solution.py:26
  143.0 7.6 %collective-permute-start.13 = (bf16[512,128]{1,0:T(8,128)(2,1)S(1)}, bf16[512,128]{1,0:T(8,128)(2,1)S(1)}, u32[]{:S(2)}, u32[]{:S(2)}) collective-permute-start(bf16[512,128]{1,0:T(8,128)(2,1)S(1)} %pad_maximum_fusion), channel_id=1, source_target_pairs={{0,256},{256,0},{1,257},{257,1},{2,258},{258,2},{3,259},{259,3},{4... | collective-permute-start | bytes 393224 | tf_op jit(solution)/shard_map/ppermute | solution.py:26
  150.6 6.9 %collective-permute-done.13 = bf16[512,128]{1,0:T(8,128)(2,1)S(1)} collective-permute-done((bf16[512,128]{1,0:T(8,128)(2,1)S(1)}, bf16[512,128]{1,0:T(8,128)(2,1)S(1)}, u32[]{:S(2)}, u32[]{:S(2)}) %collective-permute-start.13) | collective-permute-done | bytes 131104 | tf_op jit(solution)/shard_map/ppermute | solution.py:26
  (34 shorter events, 3.0 us)
Async XLA Ops:
  1.1 21.3 %copy-start.2 = (bf16[512,896]{1,0:T(8,128)(2,1)S(1)}, bf16[512,896]{1,0:T(8,128)(2,1)}, u32[]{:S(2)}) copy-start(bf16[512,896]{1,0:T(8,128)(2,1)} %param.7) | copy-start | bytes 2752516
  2.2 29.2 %all-to-all-start = ((bf16[4,2,128,512]{3,2,1,0:T(8,128)(2,1)}), bf16[4,2,128,512]{3,2,1,0:T(8,128)(2,1)S(1)}, u32[]{:S(2)}, u32[]{:S(2)}) async-start(bf16[4,2,128,512]{3,2,1,0:T(8,128)(2,1)} %broadcast_in_dim.14), calls=%async_computation | async-start | bytes 2097152 | tf_op jit(solution)/shard_map/all_to_all | solution.py:35
  6.6 27.8 %collective-permute-start.1 = (bf16[2,128,512]{2,1,0:T(8,128)(2,1)S(1)}, bf16[2,128,512]{2,1,0:T(8,128)(2,1)S(1)}, u32[]{:S(2)}, u32[]{:S(2)}) collective-permute-start(bf16[2,128,512]{2,1,0:T(8,128)(2,1)S(1)} %bitcast.49), channel_id=1, source_target_pairs={{0,2},{2,0},{1,3},{3,1},{4,6},{6,4},{5,7},{7,5},{8,10},{10,8},{9,1... | collective-permute-start | bytes 786440 | tf_op jit(solution)/shard_map/ppermute | solution.py:26
  26.8 4.6 %copy-start = (s32[7,8]{1,0:T(8,128)S(1)}, s32[7,8]{1,0:T(8,128)}, u32[]{:S(2)}) copy-start(s32[7,8]{1,0:T(8,128)} %owner_ref.1) | copy-start | bytes 676
  31.4 27.8 %copy-start.1 = (s32[7,8]{1,0:T(8,128)S(1)}, s32[7,8]{1,0:T(8,128)}, u32[]{:S(2)}) copy-start(s32[7,8]{1,0:T(8,128)} %rows_ref.1) | copy-start | bytes 676
  35.6 19.1 %all-to-all-start.1 = ((bf16[4,2,128,512]{3,2,1,0:T(8,128)(2,1)}), bf16[4,2,128,512]{3,2,1,0:T(8,128)(2,1)S(1)}, u32[]{:S(2)}, u32[]{:S(2)}) async-start(bf16[4,2,128,512]{3,2,1,0:T(8,128)(2,1)} %broadcast_in_dim.15), calls=%async_computation.1 | async-start | bytes 2097152 | tf_op jit(solution)/shard_map/all_to_all | solution.py:35
  40.4 16.2 %collective-permute-start = (bf16[4,2,128,512]{3,2,1,0:T(8,128)(2,1)S(1)}, bf16[4,2,128,512]{3,2,1,0:T(8,128)(2,1)}, u32[]{:S(2)}, u32[]{:S(2)}) collective-permute-start(bf16[4,2,128,512]{3,2,1,0:T(8,128)(2,1)S(1)} %all-to-all-done.a_ref), channel_id=1, source_target_pairs={{0,1},{1,0},{2,3},{3,2},{4,5},{5,4},{6,7},{7,6},{8,9},{9,8},{10,11... | collective-permute-start | bytes 3145736 | tf_op jit(solution)/shard_map/ppermute | solution.py:26
  54.6 4.5 %collective-permute-start.2 = (bf16[4,2,128,512]{3,2,1,0:T(8,128)(2,1)S(1)}, bf16[4,2,128,512]{3,2,1,0:T(8,128)(2,1)S(1)}, u32[]{:S(2)}, u32[]{:S(2)}) collective-permute-start(bf16[4,2,128,512]{3,2,1,0:T(8,128)(2,1)S(1)} %all-to-all-done.1.b_ref), channel_id=1, source_target_pairs={{0,1},{1,0},{2,3},{3,2},{4,5},{5,4},{6,7},{7,6},{8,9},{9,8},{10,11... | collective-permute-start | bytes 3145736 | tf_op jit(solution)/shard_map/ppermute | solution.py:26
  68.4 22.7 %collective-permute-start.3 = (bf16[2048,128]{1,0:T(8,128)(2,1)S(1)}, bf16[2048,128]{1,0:T(8,128)(2,1)S(1)}, u32[]{:S(2)}, u32[]{:S(2)}) collective-permute-start(bf16[2048,128]{1,0:T(8,128)(2,1)S(1)} %bitcast.45), channel_id=1, source_target_pairs={{0,16},{16,32},{32,48},{48,0},{1,17},{17,33},{33,49},{49,1},{2,18}... | collective-permute-start | bytes 1572872 | tf_op jit(solution)/shard_map/ppermute | solution.py:31
  70.8 28.0 %collective-permute-start.4 = (bf16[2048,128]{1,0:T(8,128)(2,1)S(1)}, bf16[2048,128]{1,0:T(8,128)(2,1)S(1)}, u32[]{:S(2)}, u32[]{:S(2)}) collective-permute-start(bf16[2048,128]{1,0:T(8,128)(2,1)S(1)} %bitcast.44), channel_id=1, source_target_pairs={{0,48},{16,0},{32,16},{48,32},{1,49},{17,1},{33,17},{49,33},{2,50}... | collective-permute-start | bytes 1572872 | tf_op jit(solution)/shard_map/ppermute | solution.py:31
  74.3 24.6 %collective-permute-start.5 = (bf16[2048,128]{1,0:T(8,128)(2,1)S(1)}, bf16[2048,128]{1,0:T(8,128)(2,1)S(1)}, u32[]{:S(2)}, u32[]{:S(2)}) collective-permute-start(bf16[2048,128]{1,0:T(8,128)(2,1)S(1)} %bitcast.43), channel_id=1, source_target_pairs={{0,32},{16,48},{32,0},{48,16},{1,33},{17,49},{33,1},{49,17},{2,34}... | collective-permute-start | bytes 1572872 | tf_op jit(solution)/shard_map/ppermute | solution.py:31
  77.6 37.5 %collective-permute-start.8 = (bf16[4096,128]{1,0:T(8,128)(2,1)S(1)}, bf16[4096,128]{1,0:T(8,128)(2,1)S(1)}, u32[]{:S(2)}, u32[]{:S(2)}) collective-permute-start(bf16[4096,128]{1,0:T(8,128)(2,1)S(1)} %bitcast.42), channel_id=1, source_target_pairs={{0,64},{64,0},{1,65},{65,1},{2,66},{66,2},{3,67},{67,3},{4,68},{68... | collective-permute-start | bytes 3145736 | tf_op jit(solution)/shard_map/ppermute | solution.py:26
  99.2 25.5 %collective-permute-start.6 = (bf16[1024,128]{1,0:T(8,128)(2,1)S(1)}, bf16[1024,128]{1,0:T(8,128)(2,1)S(1)}, u32[]{:S(2)}, u32[]{:S(2)}) collective-permute-start(bf16[1024,128]{1,0:T(8,128)(2,1)S(1)} %slice.141), channel_id=1, source_target_pairs={{0,64},{64,0},{1,65},{65,1},{2,66},{66,2},{3,67},{67,3},{4,68},{68... | collective-permute-start | bytes 786440 | tf_op jit(solution)/shard_map/ppermute | solution.py:26
  115.4 12.6 %collective-permute-start.9 = (bf16[1024,128]{1,0:T(8,128)(2,1)S(1)}, bf16[1024,128]{1,0:T(8,128)(2,1)S(1)}, u32[]{:S(2)}, u32[]{:S(2)}) collective-permute-start(bf16[1024,128]{1,0:T(8,128)(2,1)S(1)} %get-tuple-element.25), channel_id=1, source_target_pairs={{0,16},{16,32},{32,48},{48,0},{1,17},{17,33},{33,49},{49,1},{2,18}... | collective-permute-start | bytes 786440 | tf_op jit(solution)/shard_map/ppermute | solution.py:31
  119.4 11.5 %collective-permute-start.11 = (bf16[1024,128]{1,0:T(8,128)(2,1)S(1)}, bf16[1024,128]{1,0:T(8,128)(2,1)S(1)}, u32[]{:S(2)}, u32[]{:S(2)}) collective-permute-start(bf16[1024,128]{1,0:T(8,128)(2,1)S(1)} %get-tuple-element.26), channel_id=1, source_target_pairs={{0,32},{16,48},{32,0},{48,16},{1,33},{17,49},{33,1},{49,17},{2,34}... | collective-permute-start | bytes 786440 | tf_op jit(solution)/shard_map/ppermute | solution.py:31
  122.4 11.1 %collective-permute-start.10 = (bf16[1024,128]{1,0:T(8,128)(2,1)S(1)}, bf16[1024,128]{1,0:T(8,128)(2,1)S(1)}, u32[]{:S(2)}, u32[]{:S(2)}) collective-permute-start(bf16[1024,128]{1,0:T(8,128)(2,1)S(1)} %get-tuple-element.27), channel_id=1, source_target_pairs={{0,48},{16,0},{32,16},{48,32},{1,49},{17,1},{33,17},{49,33},{2,50}... | collective-permute-start | bytes 786440 | tf_op jit(solution)/shard_map/ppermute | solution.py:31
  124.8 10.9 %collective-permute-start.7 = (bf16[512,128]{1,0:T(8,128)(2,1)S(1)}, bf16[512,128]{1,0:T(8,128)(2,1)S(1)}, u32[]{:S(2)}, u32[]{:S(2)}) collective-permute-start(bf16[512,128]{1,0:T(8,128)(2,1)S(1)} %slice.143), channel_id=1, source_target_pairs={{0,128},{128,0},{1,129},{129,1},{2,130},{130,2},{3,131},{131,3},{4... | collective-permute-start | bytes 393224 | tf_op jit(solution)/shard_map/ppermute | solution.py:26
  133.8 9.2 %collective-permute-start.12 = (bf16[512,128]{1,0:T(8,128)(2,1)S(1)}, bf16[512,128]{1,0:T(8,128)(2,1)S(1)}, u32[]{:S(2)}, u32[]{:S(2)}) collective-permute-start(bf16[512,128]{1,0:T(8,128)(2,1)S(1)} %slice.142), channel_id=1, source_target_pairs={{0,128},{128,0},{1,129},{129,1},{2,130},{130,2},{3,131},{131,3},{4... | collective-permute-start | bytes 393224 | tf_op jit(solution)/shard_map/ppermute | solution.py:26
  143.0 14.6 %collective-permute-start.13 = (bf16[512,128]{1,0:T(8,128)(2,1)S(1)}, bf16[512,128]{1,0:T(8,128)(2,1)S(1)}, u32[]{:S(2)}, u32[]{:S(2)}) collective-permute-start(bf16[512,128]{1,0:T(8,128)(2,1)S(1)} %pad_maximum_fusion), channel_id=1, source_target_pairs={{0,256},{256,0},{1,257},{257,1},{2,258},{258,2},{3,259},{259,3},{4... | collective-permute-start | bytes 393224 | tf_op jit(solution)/shard_map/ppermute | solution.py:26
